TPU v7x, 32 devices: a whole 2x2x4 slice. The times are simulated.
32 devices in a mesh: dp: 8 (over y, x, core), mp: 4 (over z).
Axes of the slice: x: 2, y: 2, z: 4, core: 2. Of those that a mesh axis runs over, the one named last changes fastest.
Arguments:
- block_input: bfloat16 [2016, 12544], P('mp', 'dp'), may hold values from -12 to 12
- output_grad: bfloat16 [2016, 12544], P('mp', 'dp'), may hold values from -1.2e-05 to 1.2e-05
- w_reduce: float32 [2016, 2016], P('dp', 'mp')
- w_group: float32 [2016, 504], P('dp')
- w_squeeze: float32 [2016, 504], P(None, 'mp')
- w_excite: float32 [504, 2016], P(None, 'mp')
- w_expand: float32 [2016, 2016], P('dp', 'mp')
- w_project: float32 [2016, 256], P(None, 'mp')
- prototypes: float32 [256, 3000], P(None, 'mp')
- bn_gains: float32 [3, 2016], P(None, 'mp'), may hold values from 0.5 to 1.5
- bn_biases: float32 [3, 2016], P(None, 'mp'), may hold values from -4 to 4
- m_reduce: float32 [2016, 2016], P('dp', 'mp'), may hold values from -0.00030517578 to 0.00030517578
- m_group: float32 [2016, 504], P('dp'), may hold values from -0.00061035156 to 0.00061035156
- m_squeeze: float32 [2016, 504], P(None, 'mp'), may hold values from -0.00030517578 to 0.00030517578
- m_excite: float32 [504, 2016], P(None, 'mp'), may hold values from -0.0029296875 to 0.0029296875
- m_expand: float32 [2016, 2016], P('dp', 'mp'), may hold values from -0.00030517578 to 0.00030517578
- m_project: float32 [2016, 256], P(None, 'mp'), may hold values from -0.00030517578 to 0.00030517578
- m_protos: float32 [256, 3000], P(None, 'mp'), may hold values from -0.0014648438 to 0.0014648438
- m_gains: float32 [3, 2016], P(None, 'mp'), may hold values from -0.015625 to 0.015625
- m_biases: float32 [3, 2016], P(None, 'mp'), may hold values from -0.00390625 to 0.00390625
- queue_store: float32 [1024, 256], P('dp'), may hold values from -0.7 to 0.7
- queue_slots: int32 [8, 128], P('dp'), may hold values from 0 to 127
- crop_perm: int32 [8, 8], P('dp'), may hold values from 0 to 7, each once within a row
Outputs:
- block_output: bfloat16 [2016, 12544], P('mp', 'dp')
- loss: float32 [], replicated
- input_grad: float32 [2016, 12544], P('mp', 'dp')
- mom_reduce: float32 [2016, 2016], P('dp', 'mp')
- mom_group: float32 [2016, 504], P('dp')
- mom_squeeze: float32 [2016, 504], P(None, 'mp')
- mom_excite: float32 [504, 2016], P(None, 'mp')
- mom_expand: float32 [2016, 2016], P('dp', 'mp')
- mom_project: float32 [2016, 256], P(None, 'mp')
- mom_protos: float32 [256, 3000], P(None, 'mp')
- mom_gains: float32 [3, 2016], P(None, 'mp')
- mom_biases: float32 [3, 2016], P(None, 'mp')
- param_norms: float32 [13, 2], replicated
Inputs may be any that keep to these rules, and one draw needn't show every extreme that they name: `queue_slots`: each entry picks one of the 128 rows of queue_store that share the entry's index of dp; a row may be picked more than once. `crop_perm`: each row lists 0 to 7 once.
All inputs are finite; a program needn't handle non-finite values.
Results may differ from a plain program's by a relative error of at most 0.018.
Values may be sent and summed in bfloat16 or wider, within the bound.
No kernel may reach another device: no remote copies, remote signals or barrier semaphores. Data moves between devices by JAX's collectives and lax.ppermute only.
A program may use at most 512 MiB of HBM per device.

v0:
```python
import functools

import jax
import jax.numpy as jnp
import numpy as np
from jax import lax
from jax.experimental import pallas as pl
from jax.experimental.pallas import tpu as pltpu
from jax.sharding import PartitionSpec as P

HW = 14
PIXELS = HW * HW
SINK = 3
EPS_BN = 1e-05
EPS_NORM = 1e-06
EPS_SINK = 0.05
SOFTMAX_TEMPER = 0.1
TRUST = 0.001
DECAY = 1e-06
MOMENTUM = 0.9

QUADS = 4
QUAD = 504
HALF = 252
LANES = 512
GAP = LANES - QUAD
GROUP = 56
SE_PART = 63
SE_LANES = 64
PITCH = 16
VMEM_BYTES = 48 * 1024 * 1024
f32 = jnp.float32
bf16 = jnp.bfloat16
NN = (((1,), (0,)), ((), ()))
NT = (((1,), (1,)), ((), ()))
TN = (((0,), (0,)), ((), ()))


def dot(a, b, dims=NN):
    return lax.dot_general(a, b, dims, preferred_element_type=f32)


def widen(v, axis):
    first = lax.slice_in_dim(v, 0, HALF, axis=axis)
    last = lax.slice_in_dim(v, HALF, QUAD, axis=axis)
    shape = list(v.shape)
    shape[axis] = GAP
    return jnp.concatenate([first, jnp.zeros(shape, v.dtype), last], axis)


def narrow(v, axis):
    first = lax.slice_in_dim(v, 0, HALF, axis=axis)
    last = lax.slice_in_dim(v, HALF + GAP, LANES, axis=axis)
    return jnp.concatenate([first, last], axis)


def spread_channels(v):
    lead = v.shape[:-1]
    return widen(v.reshape(lead + (QUADS, QUAD)), len(lead) + 1).reshape(lead + (QUADS * LANES,))


def pack_channels(v):
    lead = v.shape[:-1]
    return narrow(v.reshape(lead + (QUADS, LANES)), len(lead) + 1).reshape(lead + (QUADS * QUAD,))


def half_rows(v, position):
    pad = 256 - HALF
    padded = jnp.pad(v, ((pad, pad),) + ((0, 0),) * (v.ndim - 1))
    return lax.dynamic_slice_in_dim(padded, pad * (1 - position % 2), 256, 0)


def unhalf_rows(v, position):
    return lax.dynamic_slice_in_dim(v, (256 - HALF) * (position % 2), HALF, 0)


def spread_inner(v):
    lead = v.shape[:-1]
    parts = v.shape[-1] // SE_PART
    v = v.reshape(lead + (parts, SE_PART))
    v = jnp.pad(v, ((0, 0),) * (v.ndim - 1) + ((0, SE_LANES - SE_PART),))
    return v.reshape(lead + (parts * SE_LANES,))


def pack_inner(v):
    lead = v.shape[:-1]
    parts = v.shape[-1] // SE_LANES
    return v.reshape(lead + (parts, SE_LANES))[..., :SE_PART].reshape(lead + (parts * SE_PART,))


def flips(axis, bit):
    return [(i, i ^ bit) for i in range(lax.axis_size(axis))]


def spread(v, axis):
    n = lax.axis_size(axis)
    return lax.all_to_all(
        jnp.broadcast_to(v[None], (n,) + v.shape), axis, split_axis=0, concat_axis=0, tiled=True
    )


def total(v):
    return jnp.sum(spread(jnp.sum(spread(v, "dp"), 0), "mp"), 0)


def tie(*values):
    return lax.optimization_barrier(values)


def gather_all(v):
    n = lax.axis_size("dp") * lax.axis_size("mp")
    out = lax.all_to_all(
        jnp.broadcast_to(v[None], (n,) + v.shape),
        ("dp", "mp"),
        split_axis=0,
        concat_axis=0,
        tiled=True,
    )
    return out


def in_order(parts, me):
    out = []
    for j in range(len(parts)):
        v = parts[0]
        for k in range(1, len(parts)):
            v = jnp.where((me ^ k) == j, parts[k], v)
        out.append(v)
    return jnp.stack(out)


def exchange(blocks):
    return lax.all_to_all(blocks, "mp", split_axis=0, concat_axis=0, tiled=True)


def parts_mp(v):
    return [v] + [lax.ppermute(v, "mp", flips("mp", k)) for k in range(1, lax.axis_size("mp"))]


def gather_mp(v):
    return in_order(parts_mp(v), lax.axis_index("mp"))


def diagonal(axis_size):
    return [(i, i ^ 4 if i % 2 == 0 else i ^ 2) for i in range(axis_size)]


def gather_sides(v):
    return lax.ppermute(v, "dp", flips("dp", 2)), lax.ppermute(v, "dp", flips("dp", 4))


def gather_corner(across, up):
    even = lax.axis_index("dp") % 2 == 0
    return lax.ppermute(jnp.where(even, across, up), "dp", diagonal(8))


def gather_twins(own, across, up, corner):
    pieces = []
    for got in (own, across, up, corner):
        pieces += [got, lax.ppermute(got, "dp", flips("dp", 1))]
    return pieces


def gather_dp(v):
    across, up = gather_sides(v)
    return gather_twins(v, across, up, gather_corner(across, up))


def scatter_corner(kept, got):
    (last,) = twin_sums(kept, got, (3,))
    corner = lax.ppermute(last, "dp", diagonal(8))
    own, across, up = twin_sums(kept, got, (0, 1, 2))
    return (own, across, up), corner


def from_twin(sent):
    return lax.ppermute(sent, "dp", flips("dp", 1))


def scatter_sides(across, up):
    return lax.ppermute(across, "dp", flips("dp", 2)), lax.ppermute(up, "dp", flips("dp", 4))


def scatter_mp(own, parts):
    return [own] + [lax.ppermute(v, "mp", flips("mp", k + 1)) for k, v in enumerate(parts)]


def quick_mesh():
    return lax.axis_size("dp") == 2 * QUADS and lax.axis_size("mp") == QUADS


def slab_blocks(v):
    n = lax.axis_size("mp")
    blocks = v.T.reshape(n, v.shape[1] // n, v.shape[0])
    return widen(blocks, 2) if quick_mesh() else blocks


def quad_blocks(blocks):
    if quick_mesh():
        return blocks
    rows = blocks.shape[1]
    full = spread_channels(blocks.transpose(1, 0, 2).reshape(rows, -1))
    return full.reshape(rows, QUADS, LANES).transpose(1, 0, 2)


def out_blocks(blocks):
    if quick_mesh():
        return blocks
    n = lax.axis_size("mp")
    rows = blocks.shape[1]
    full = pack_channels(blocks.transpose(1, 0, 2).reshape(rows, -1))
    return full.reshape(rows, n, -1).transpose(1, 0, 2)


def out_channels(blocks, channels, dtype):
    if quick_mesh():
        blocks = join_rows(blocks, dtype)
    return blocks.astype(dtype).reshape(-1, channels).T


def shard_square(w):
    return half_rows(widen(w.astype(bf16), 1), lax.axis_index("dp")).T


def gather_square(w):
    full = lax.all_gather(w.astype(bf16), "mp", axis=1, tiled=True)
    full = lax.all_gather(full, "dp", axis=0, tiled=True)
    full = spread_channels(spread_channels(full).T)
    return full.reshape(QUADS, LANES, 2 * QUADS, 256).transpose(2, 0, 1, 3)


def scatter_square(kept, sent):
    g = jnp.stack([kept, sent], 1).reshape((8,) + kept.shape[1:])
    full = g.transpose(1, 2, 0, 3).reshape(QUADS * LANES, 2 * QUADS * 256)
    full = pack_channels(pack_channels(full).T)
    part = lax.psum_scatter(full, "dp", scatter_dimension=0, tiled=True)
    return lax.psum_scatter(part, "mp", scatter_dimension=1, tiled=True).astype(f32)


def gather_kernel(w):
    low = w.astype(bf16)
    if quick_mesh():
        return gather_dp(half_rows(low, lax.axis_index("dp")).T)
    full = lax.all_gather(low, "dp", axis=0, tiled=True)
    return spread_channels(full.T).reshape(-1, 2 * QUADS, 256).transpose(1, 0, 2)


def scatter_kernel(kept, sent):
    g = jnp.stack([kept, sent], 1).reshape((8,) + kept.shape[1:])
    full = pack_channels(g.transpose(1, 0, 2).reshape(g.shape[1], -1)).T
    part = lax.psum_scatter(full, "dp", scatter_dimension=0, tiled=True).astype(f32)
    return lax.psum(part, "mp")


SE_ROWS = 256
SE_OFFSET = QUADS * LANES
HEAD_ROWS = 208
PROTO_ROWS = 96
QUEUE_ROWS = 32


def shard_excitation(w_squeeze, w_excite):
    d = lax.axis_index("dp")
    squeeze = lax.dynamic_slice_in_dim(w_squeeze, d * HALF, HALF, 0).astype(bf16)
    squeeze = spread_inner(half_rows(squeeze, d))
    excite = lax.dynamic_slice_in_dim(w_excite, d * SE_PART, SE_PART, 0).astype(bf16)
    excite = jnp.pad(widen(excite, 1), ((0, SE_LANES - SE_PART), (0, 0)))
    excite = jnp.concatenate([excite[:, 128 * i : 128 * (i + 1)] for i in range(4)], 0)
    return jnp.concatenate([squeeze, excite], 1)


def shard_head(w_project, prototypes, queue_rows, pairing):
    d = lax.axis_index("dp")
    m = lax.axis_index("mp")
    project = lax.dynamic_slice_in_dim(w_project, d * HALF, HALF, 0).astype(bf16)
    project = half_rows(project, d).T
    protos = jnp.pad(prototypes.T, ((0, 2 * QUADS * PROTO_ROWS - prototypes.shape[1]), (0, 0)))
    protos = lax.dynamic_slice_in_dim(protos, d * PROTO_ROWS, PROTO_ROWS, 0).astype(bf16)
    queue = lax.dynamic_slice_in_dim(queue_rows, m * QUEUE_ROWS, QUEUE_ROWS, 0)
    size = pairing.shape[0]
    lane = lax.broadcasted_iota(jnp.int32, (size, 256), 1)
    pairing = jnp.where(lane // size == d, jnp.tile(pairing, (1, 256 // size)), 0.0)
    pairing = jnp.pad(pairing.astype(bf16), ((0, 16 - size), (0, 0)))
    return jnp.concatenate([project, protos, queue, pairing], 0)


def gather_excitation(w_squeeze, w_excite):
    squeeze = lax.all_gather(w_squeeze.astype(bf16), "mp", axis=1, tiled=True)
    excite = lax.all_gather(w_excite.astype(bf16), "mp", axis=1, tiled=True)
    squeeze = spread_channels(spread_inner(squeeze).T).T
    excite = spread_inner(spread_channels(excite).T).T
    squeeze = squeeze.reshape(8, 256, 4, 128).transpose(0, 2, 1, 3)
    excite = excite.reshape(8, 64, 4, 4, 128).transpose(0, 2, 3, 1, 4).reshape(8, 4, 256, 128)
    return jnp.concatenate([squeeze, excite], 3)


def gather_head(w_project, prototypes, queue_rows, pairing):
    project = lax.all_gather(w_project.astype(bf16), "mp", axis=1, tiled=True)
    protos = lax.all_gather(prototypes.astype(bf16), "mp", axis=1, tiled=True)
    queue = lax.all_gather(queue_rows, "dp", axis=0, tiled=True)
    pairs = lax.all_gather(pairing, "dp")
    return spread_channels(project.T).T, protos, queue, pairs


def block_diagonal(pairs):
    images, size = pairs.shape[:2]
    return (
        jnp.eye(images, dtype=f32)[:, None, :, None] * pairs.astype(f32)[:, :, None, :]
    ).reshape(images * size, images * size)


BRIEF = pl.CostEstimate(flops=1, bytes_accessed=1, transcendentals=0)


def params(*semantics):
    return pltpu.CompilerParams(vmem_limit_bytes=VMEM_BYTES)


def column_sums(stats_ref, a, b):
    stats_ref[0:1, :] = jnp.sum(a, 0, keepdims=True)
    stats_ref[1:2, :] = jnp.sum(b, 0, keepdims=True)


def index_scalar(axis):
    quick = quick_mesh()
    return (lax.axis_index(axis) if quick else jnp.zeros((), jnp.int32)).astype(jnp.int32)[None]


SCALAR = pl.BlockSpec(memory_space=pltpu.SMEM)


def half_block(index):
    return pl.ds(pl.multiple_of(index * 256, 256), 256)


def join_rows_kernel(blocks_ref, out_ref):
    for j in range(QUADS):
        v = blocks_ref[j].astype(f32)
        v = jnp.concatenate([v[:, :HALF], v[:, HALF + GAP :]], 1)
        out_ref[j] = v.astype(out_ref.dtype)


def join_rows(blocks, dtype):
    return pl.pallas_call(
        join_rows_kernel,
        out_shape=jax.ShapeDtypeStruct(blocks.shape[:2] + (QUAD,), dtype),
        compiler_params=params(),
        cost_estimate=BRIEF,
        name="join_rows",
    )(blocks)


def piece_list(w):
    return w if isinstance(w, list) else [w[b].reshape(-1, 256) for b in range(8)]


def half_of(ref, index):
    return ref[index // 2, :, half_block(index % 2)]


def mix_kernel(me_ref, x_ref, *refs):
    out_ref, stats_ref = refs[8:]
    turned = jnp.concatenate([half_of(x_ref, me_ref[0] ^ b) for b in range(8)], 1)
    acc = dot(turned, jnp.concatenate([refs[b][...] for b in range(8)], 1), NT)
    out_ref[...] = acc
    column_sums(stats_ref, acc, acc * acc)


def mix(x, w):
    _, rows, _ = x.shape
    width = QUADS * LANES
    return pl.pallas_call(
        mix_kernel,
        grid=(QUADS,),
        in_specs=[SCALAR, pl.BlockSpec(x.shape, lambda m: (0, 0, 0))]
        + [pl.BlockSpec((LANES, 256), lambda m: (m, 0))] * 8,
        out_specs=[
            pl.BlockSpec((rows, LANES), lambda m: (0, m)),
            pl.BlockSpec((2, LANES), lambda m: (0, m)),
        ],
        out_shape=[
            jax.ShapeDtypeStruct((rows, width), f32),
            jax.ShapeDtypeStruct((2, width), f32),
        ],
        compiler_params=params(),
        cost_estimate=BRIEF,
        name="mix",
    )(index_scalar("dp"), x, *piece_list(w))


def mix_back_kernel(rest, me_ref, g_ref, *refs):
    out_ref, hold_ref, sems = refs[8 + rest :]

    def copy(b):
        source = refs[b].at[pl.ds(0, QUADS * LANES)]
        return pltpu.make_async_copy(source, hold_ref.at[b], sems.at[b])

    for b in range(8):
        copy(b).start()
    for b in range(8):
        index = me_ref[0] ^ b
        copy(b).wait()
        acc = dot(g_ref[...], hold_ref[b])
        if rest:
            acc = acc + refs[8][:, half_block(index)]
            out_ref[index // 2, :, half_block(index % 2)] = acc.astype(bf16)
        else:
            out_ref[:, half_block(index)] = acc


def mix_back(g, w, rest=None):
    rows, width = g.shape
    if rest is None:
        more, out = [], jax.ShapeDtypeStruct((rows, width), f32)
    else:
        more, out = [rest], jax.ShapeDtypeStruct((QUADS, rows, LANES), bf16)
    return pl.pallas_call(
        functools.partial(mix_back_kernel, len(more)),
        in_specs=[SCALAR, pl.BlockSpec(memory_space=pltpu.VMEM)]
        + [pl.BlockSpec(memory_space=pl.ANY)] * 8
        + [pl.BlockSpec(memory_space=pltpu.VMEM)] * len(more),
        out_specs=pl.BlockSpec(memory_space=pltpu.VMEM),
        out_shape=out,
        scratch_shapes=[
            pltpu.VMEM((8, QUADS * LANES, 256), bf16),
            pltpu.SemaphoreType.DMA((8,)),
        ],
        compiler_params=params(),
        cost_estimate=BRIEF,
        name="mix_back",
    )(index_scalar("dp"), g, *piece_list(w), *more)


def weight_grad_kernel(me_ref, x_ref, g_ref, kept_ref, sent_ref):
    turned = g_ref[...].T
    for odd, out_ref in ((1, sent_ref), (0, kept_ref)):
        wanted = jnp.concatenate(
            [half_of(x_ref, me_ref[0] ^ (2 * i + odd)) for i in range(4)], 1
        )
        result = dot(turned, wanted)
        for i in range(4):
            out_ref[i, 0] = result[:, 256 * i : 256 * (i + 1)].astype(bf16)


def weight_grad(x, g):
    rows, width = g.shape
    return pl.pallas_call(
        weight_grad_kernel,
        grid=(QUADS,),
        in_specs=[
            SCALAR,
            pl.BlockSpec(x.shape, lambda m: (0, 0, 0)),
            pl.BlockSpec((rows, LANES), lambda m: (0, m)),
        ],
        out_specs=[pl.BlockSpec((4, 1, LANES, 256), lambda m: (0, m, 0, 0))] * 2,
        out_shape=[jax.ShapeDtypeStruct((4, QUADS, LANES, 256), bf16)] * 2,
        compiler_params=params(),
        cost_estimate=BRIEF,
        name="weight_grad",
    )(index_scalar("dp"), x, g)


def twin_sums_kernel(count, *refs):
    for i in range(count):
        refs[2 * count + i][...] = (
            refs[i][...].astype(f32) + refs[count + i][...].astype(f32)
        ).astype(bf16)


def twin_sums(kept, got, picks):
    shape = kept.shape[1:]
    specs = [
        pl.BlockSpec((None, 1) + shape[1:], lambda m, i=i: (i, m, 0, 0)) for i in picks
    ]
    return pl.pallas_call(
        functools.partial(twin_sums_kernel, len(picks)),
        grid=shape[:1],
        in_specs=specs * 2,
        out_specs=[pl.BlockSpec((1,) + shape[1:], lambda m: (m, 0, 0))] * len(picks),
        out_shape=[jax.ShapeDtypeStruct(shape, bf16)] * len(picks),
        compiler_params=params(),
        cost_estimate=BRIEF,
        name="twin_sums",
    )(*([kept] * len(picks) + [got] * len(picks)))


def corner_sums_kernel(me_ref, across_ref, up_ref, corner_ref, across_out, up_out):
    even = me_ref[0] % 2 == 0
    corner = corner_ref[...].astype(f32)
    across_out[...] = (across_ref[...].astype(f32) + jnp.where(even, corner, 0.0)).astype(bf16)
    up_out[...] = (up_ref[...].astype(f32) + jnp.where(even, 0.0, corner)).astype(bf16)


def corner_sums(across, up, corner):
    block = pl.BlockSpec((1,) + across.shape[1:], lambda m: (m, 0, 0))
    return pl.pallas_call(
        corner_sums_kernel,
        grid=across.shape[:1],
        in_specs=[SCALAR, block, block, block],
        out_specs=[block, block],
        out_shape=[jax.ShapeDtypeStruct(across.shape, bf16)] * 2,
        compiler_params=params(),
        cost_estimate=BRIEF,
        name="corner_sums",
    )(index_scalar("dp"), across, up, corner)


def side_sums_kernel(me_ref, own_ref, across_ref, up_ref, out_ref, *parts):
    for k in range(len(parts) + 1):
        j = me_ref[0] ^ k
        value = (
            own_ref[j].astype(f32) + across_ref[j].astype(f32) + up_ref[j].astype(f32)
        )
        if k:
            parts[k - 1][...] = value.astype(bf16)
        else:
            out_ref[...] = value


def side_sums(own, across, up):
    n, *shape = own.shape
    me = index_scalar("mp") if n > 1 else jnp.zeros((1,), jnp.int32)
    return pl.pallas_call(
        side_sums_kernel,
        in_specs=[SCALAR] + [pl.BlockSpec(memory_space=pltpu.VMEM)] * 3,
        out_shape=[jax.ShapeDtypeStruct(shape, f32)] + [jax.ShapeDtypeStruct(shape, bf16)] * (n - 1),
        compiler_params=params(),
        cost_estimate=BRIEF,
        name="side_sums",
    )(me, own, across, up)


def own_square_kernel(me_ref, own_ref, *refs):
    out_ref, square_ref = refs[-2:]
    value = own_ref[...]
    for part in refs[:-2]:
        value = value + part[...].astype(f32)
    row = lax.broadcasted_iota(jnp.int32, (QUAD, 1), 0)
    value = jnp.where(row < HALF, value[:QUAD], value[GAP:])
    value = jnp.where(me_ref[0] % 2 == 1, value[:, 256 - HALF :], value[:, :HALF])
    out_ref[...] = value
    square_ref[...] = jnp.sum(jnp.sum(value * value, 1, keepdims=True), 0, keepdims=True)


def own_square(parts):
    return pl.pallas_call(
        own_square_kernel,
        in_specs=[SCALAR] + [pl.BlockSpec(memory_space=pltpu.VMEM)] * len(parts),
        out_shape=[
            jax.ShapeDtypeStruct((QUAD, HALF), f32), jax.ShapeDtypeStruct((1, 1), f32),
        ],
        compiler_params=params(),
        cost_estimate=BRIEF,
        name="own_square",
    )(index_scalar("dp"), *parts)


def affine(sums, norms, k, count):
    mean = sums[0:1] / count
    inverse = lax.rsqrt(sums[1:2] / count - mean * mean + EPS_BN)
    scale = inverse * norms[k : k + 1]
    return mean, inverse, scale, norms[3 + k : 4 + k] - mean * scale


def quad_spec(rows):
    return pl.BlockSpec((rows, LANES), lambda q: (0, q))


def block_spec(rows):
    return pl.BlockSpec((None, rows, LANES), lambda q: (q, 0, 0))


def crop_totals(ref, crops):
    return jnp.concatenate(
        [jnp.sum(ref[pl.ds(PIXELS * c, PIXELS), :], 0, keepdims=True) for c in range(crops)], 0
    )


def value_kernel(crops, count, x_ref, a_ref, sums_ref, norms_ref, y_ref, summary_ref, work_ref):
    _, _, scale, shift = affine(sums_ref[...], norms_ref[...], 2, count)
    work_ref[...] = swish(x_ref[...].astype(f32) + a_ref[...] * scale + shift)
    y_ref[...] = work_ref[...].astype(bf16)
    summary_ref[...] = (crop_totals(work_ref, crops) / PIXELS).astype(bf16)


def block_value(x, a, sums, norms, count):
    rows, width = a.shape
    crops = rows // PIXELS
    return pl.pallas_call(
        functools.partial(value_kernel, crops, count),
        grid=(QUADS,),
        in_specs=[block_spec(rows), quad_spec(rows), quad_spec(2), quad_spec(6)],
        out_specs=[block_spec(rows), quad_spec(crops)],
        out_shape=[
            jax.ShapeDtypeStruct((QUADS, rows, LANES), bf16),
            jax.ShapeDtypeStruct((crops, width), bf16),
        ],
        scratch_shapes=[pltpu.VMEM((rows, LANES), f32)],
        compiler_params=params(),
        cost_estimate=BRIEF,
        name="value",
    )(x, a, sums, norms)


def value_back_kernel(
    crops, count, first_ref, x_ref, a_ref, sums_ref, norms_ref, dy_ref, do_ref, out_ref, stats_ref
):
    mean, inverse, scale, shift = affine(sums_ref[...], norms_ref[...], 2, count)
    values = a_ref[...]
    row = lax.broadcasted_iota(jnp.int32, (do_ref.shape[0], 1), 0)
    own = jnp.concatenate(
        [
            jnp.sum(jnp.where(row == first_ref[0] + c, do_ref[...], 0.0), 0, keepdims=True)
            for c in range(crops)
        ],
        0,
    )
    slope = swish_slope(x_ref[...].astype(f32) + values * scale + shift)
    grad = (dy_ref[...].astype(f32) + rows_of_crops(own / PIXELS, values.shape[0])) * slope
    out_ref[...] = grad
    column_sums(stats_ref, grad, grad * ((values - mean) * inverse))


def value_back(first, x, a, sums, norms, dy, do, count):
    rows, width = a.shape
    return pl.pallas_call(
        functools.partial(value_back_kernel, rows // PIXELS, count),
        grid=(QUADS,),
        in_specs=[
            SCALAR, block_spec(rows), quad_spec(rows), quad_spec(2), quad_spec(6),
            block_spec(rows), quad_spec(do.shape[0]),
        ],
        out_specs=[quad_spec(rows), quad_spec(2)],
        out_shape=[
            jax.ShapeDtypeStruct((rows, width), f32), jax.ShapeDtypeStruct((2, width), f32),
        ],
        compiler_params=params(),
        cost_estimate=BRIEF,
        name="value_back",
    )(first, x, a, sums, norms, dy, do)


def norm_back(grad, values, sums, norms, k, grad_sums, count):
    mean, inverse, scale, _ = affine(sums, norms, k, count)
    centred = (values - mean) * inverse
    return scale * (grad - (grad_sums[0:1] + centred * grad_sums[1:2]) / count)


def norm_back_kernel(k, sloped, count, g_ref, a_ref, sums_ref, norms_ref, grad_sums_ref, out_ref):
    grad, values = g_ref[...].astype(f32), a_ref[...]
    if sloped:
        _, _, scale, shift = affine(sums_ref[...], norms_ref[...], k, count)
        grad = grad * swish_slope(values * scale + shift)
    out_ref[...] = norm_back(
        grad, values, sums_ref[...], norms_ref[...], k, grad_sums_ref[...], count
    ).astype(bf16)


def norm_backward(g, a, sums, norms, k, grad_sums, count, sloped):
    rows, width = a.shape
    return pl.pallas_call(
        functools.partial(norm_back_kernel, k, sloped, count),
        grid=(QUADS,),
        in_specs=[quad_spec(rows), quad_spec(rows), quad_spec(2), quad_spec(6), quad_spec(2)],
        out_specs=quad_spec(rows),
        out_shape=jax.ShapeDtypeStruct((rows, width), bf16),
        compiler_params=params(),
        cost_estimate=BRIEF,
        name="norm_backward",
    )(g, a, sums, norms, grad_sums)


def lane_mask(low, high, rows=GROUP):
    lane = lax.broadcasted_iota(jnp.int32, (rows, 256), 1)
    return (lane >= low) & (lane < high)


def dense_kernel(me_ref, *refs):
    out_ref, hold_ref = refs[8:]

    @pl.when(pl.program_id(0) == 0)
    def _():
        for b in range(8):
            hold_ref[me_ref[0] ^ b] = refs[b][...]

    even = hold_ref[2 * pl.program_id(0)].astype(f32)
    odd = hold_ref[2 * pl.program_id(0) + 1].astype(f32)
    row = lax.broadcasted_iota(jnp.int32, (256, 256), 0)
    edge = jnp.zeros((32, 256), f32)
    centre = lane_mask(96, 124) | lane_mask(132, 160)
    for tap in range(9):
        e = even[GROUP * tap : GROUP * (tap + 1)]
        o = odd[GROUP * tap : GROUP * (tap + 1)]
        first = [jnp.where(lane_mask(GROUP * g, GROUP * (g + 1)), e, 0.0) for g in range(4)]
        last = [
            jnp.where(lane_mask(32 + GROUP * g, 32 + GROUP * (g + 1)), o, 0.0) for g in range(4)
        ]
        out_ref[0, 0, tap] = jnp.concatenate(first + [edge], 0).astype(bf16)
        out_ref[0, 1, tap] = jnp.concatenate([edge] + last, 0).astype(bf16)
        across = jnp.where(centre, jnp.concatenate([e[:, 128:], o[:, :128]], 1), 0.0)
        upper = jnp.concatenate(
            [jnp.zeros((96, 256), f32), across, jnp.zeros((104, 256), f32)], 0
        )
        lower = jnp.concatenate(
            [jnp.zeros((104, 256), f32), across, jnp.zeros((96, 256), f32)], 0
        )
        out_ref[0, 2, tap] = (
            jnp.where(row < 124, upper, 0.0) + jnp.where(row >= 132, lower, 0.0)
        ).astype(bf16)


def dense_windows(kernel):
    pieces = [kernel[b] for b in range(8)]
    return pl.pallas_call(
        dense_kernel,
        grid=(QUADS,),
        in_specs=[SCALAR] + [pl.BlockSpec(memory_space=pltpu.VMEM)] * 8,
        out_specs=pl.BlockSpec((1, 3, 9, 256, 256), lambda q: (q, 0, 0, 0, 0)),
        out_shape=jax.ShapeDtypeStruct((QUADS, 3, 9, 256, 256), bf16),
        scratch_shapes=[pltpu.VMEM((8,) + pieces[0].shape, bf16)],
        compiler_params=params(),
        cost_estimate=BRIEF,
        name="dense_windows",
    )(index_scalar("dp"), *pieces)


WINDOWS = (0, 256, 128)


def place_pixels(pad_ref, moved_ref, source_ref, crops):
    for crop in range(crops):
        for row in range(HW):
            pad_ref[pl.ds(PITCH + 256 * crop + PITCH * (row + 1), HW), :] = source_ref[
                pl.ds(PIXELS * crop + HW * row, HW), :
            ]
    for shift in range(3):
        moved_ref[shift] = pad_ref[pl.ds(PITCH - 1 + shift, 256 * crops), :].astype(bf16)


def tap_rows(moved_ref, dy, dx, low, crops):
    return jnp.concatenate(
        [
            moved_ref[dx, pl.ds(256 * crop + PITCH * dy, PITCH * HW), pl.ds(low, 256)]
            for crop in range(crops)
        ],
        0,
    )


def take_pixels(target_ref, source_ref, crops):
    for crop in range(crops):
        for row in range(HW):
            target_ref[pl.ds(PIXELS * crop + HW * row, HW), :] = source_ref[
                pl.ds(PITCH * HW * crop + PITCH * row, HW), :
            ]


def swish(v):
    return v / (1.0 + jnp.exp(-v))


def swish_slope(v):
    sigma = 1.0 / (1.0 + jnp.exp(-v))
    return sigma * (1.0 + v * (1.0 - sigma))


def conv_kernel(crops, count, a_ref, sums_ref, norms_ref, w_ref, out_ref, stats_ref, pad_ref, moved_ref, wide_ref, act_ref):
    @pl.when(pl.program_id(0) == 0)
    def _():
        pad_ref[...] = jnp.zeros_like(pad_ref)

    _, _, scale, shift = affine(sums_ref[...], norms_ref[...], 0, count)
    act = swish(a_ref[...] * scale + shift)
    act_ref[...] = act.astype(bf16).astype(f32)
    place_pixels(pad_ref, moved_ref, act_ref, crops)
    for window, low in enumerate(WINDOWS):
        taps = [tap_rows(moved_ref, tap // 3, tap % 3, low, crops) for tap in range(9)]
        acc = dot(jnp.concatenate(taps, 1), w_ref[0, window].reshape(9 * 256, 256))
        if window < 2:
            wide_ref[:, pl.ds(low, 256)] = acc
        else:
            wide_ref[:, pl.ds(low, 256)] += acc
    take_pixels(act_ref, wide_ref, crops)
    result = act_ref[...].astype(bf16)
    out_ref[...] = result
    result = result.astype(f32)
    column_sums(stats_ref, result, result * result)


def conv(a, sums, norms, windows, count):
    rows, width = a.shape
    crops = rows // PIXELS
    return pl.pallas_call(
        functools.partial(conv_kernel, crops, count),
        grid=(QUADS,),
        in_specs=[
            quad_spec(rows), quad_spec(2), quad_spec(6),
            pl.BlockSpec((1, 3, 9, 256, 256), lambda q: (q, 0, 0, 0, 0)),
        ],
        out_specs=[
            pl.BlockSpec((rows, LANES), lambda q: (0, q)),
            pl.BlockSpec((2, LANES), lambda q: (0, q)),
        ],
        out_shape=[
            jax.ShapeDtypeStruct((rows, width), bf16),
            jax.ShapeDtypeStruct((2, width), f32),
        ],
        scratch_shapes=[
            pltpu.VMEM((2 * PITCH + 256 * crops, LANES), f32),
            pltpu.VMEM((3, 256 * crops, LANES), bf16),
            pltpu.VMEM((PITCH * HW * crops, LANES), f32),
            pltpu.VMEM((rows, LANES), f32),
        ],
        compiler_params=params(),
        cost_estimate=BRIEF,
        name="conv",
    )(a, sums, norms, windows)


def conv_back_kernel(
    crops, count, me_ref, g_ref, a2_ref, sums2_ref, grad_sums_ref, a_ref, sums_ref, norms_ref, w_ref,
    out_ref, kept_ref, sent_ref, stats_ref,
    pad_ref, moved_ref, pad_x_ref, moved_x_ref, wide_ref, act_ref, hold_ref,
):
    @pl.when(pl.program_id(0) == 0)
    def _():
        pad_ref[...] = jnp.zeros_like(pad_ref)
        pad_x_ref[...] = jnp.zeros_like(pad_x_ref)

    norms = norms_ref[...]
    grad = norm_back(
        g_ref[...], a2_ref[...].astype(f32), sums2_ref[...], norms, 1, grad_sums_ref[...], count
    )
    act_ref[...] = grad.astype(bf16).astype(f32)
    place_pixels(pad_ref, moved_ref, act_ref, crops)
    values = a_ref[...]
    mean, inverse, scale, shift = affine(sums_ref[...], norms, 0, count)
    normed = values * scale + shift
    act_ref[...] = swish(normed).astype(bf16).astype(f32)
    place_pixels(pad_x_ref, moved_x_ref, act_ref, crops)
    for window, low in enumerate(WINDOWS):
        taps = [tap_rows(moved_ref, 2 - tap // 3, 2 - tap % 3, low, crops) for tap in range(9)]
        weight = jnp.concatenate([w_ref[0, window, tap] for tap in range(9)], 1)
        acc = dot(jnp.concatenate(taps, 1), weight, NT)
        if window < 2:
            wide_ref[:, pl.ds(low, 256)] = acc
        else:
            wide_ref[:, pl.ds(low, 256)] += acc
    take_pixels(act_ref, wide_ref, crops)
    result = act_ref[...].astype(bf16)
    out_ref[...] = result
    grad = result.astype(f32) * swish_slope(normed)
    column_sums(stats_ref, grad, grad * ((values - mean) * inverse))
    centre = lane_mask(96, 124) | lane_mask(132, 160)
    row = lax.broadcasted_iota(jnp.int32, (GROUP, 256), 0)
    mids = [
        tap_rows(moved_ref, 1, 1, low, crops) for low in WINDOWS
    ]
    for tap in range(9):
        pieces = []
        for window, low in enumerate(WINDOWS):
            pieces.append(
                dot(tap_rows(moved_x_ref, tap // 3, tap % 3, low, crops), mids[window], TN)
            )
        even = sum(
            jnp.where(lane_mask(GROUP * g, GROUP * (g + 1)), pieces[0][GROUP * g : GROUP * (g + 1)], 0.0)
            for g in range(4)
        )
        odd = sum(
            jnp.where(
                lane_mask(32 + GROUP * g, 32 + GROUP * (g + 1)),
                pieces[1][32 + GROUP * g : 32 + GROUP * (g + 1)],
                0.0,
            )
            for g in range(4)
        )
        across = jnp.where(
            centre, jnp.where(row < GROUP // 2, pieces[2][96:152], pieces[2][104:160]), 0.0
        )
        nothing = jnp.zeros((GROUP, 128), f32)
        even = even + jnp.concatenate([nothing, across[:, :128]], 1)
        odd = odd + jnp.concatenate([across[:, 128:], nothing], 1)
        twin = me_ref[0] % 2 == 1
        hold_ref[0, pl.ds(GROUP * tap, GROUP), :] = jnp.where(twin, odd, even)
        hold_ref[1, pl.ds(GROUP * tap, GROUP), :] = jnp.where(twin, even, odd)
    kept_ref[0, 0] = hold_ref[0].astype(bf16)
    sent_ref[0, 0] = hold_ref[1].astype(bf16)


def conv_back(g, a2, sums2, grad_sums, a, sums, norms, windows, count):
    rows, width = a.shape
    crops = rows // PIXELS
    piece = pl.BlockSpec((1, 1, 9 * GROUP, 256), lambda q, me: (q ^ (me[0] // 2), 0, 0, 0))

    def quad(n):
        return pl.BlockSpec((n, LANES), lambda q, me: (0, q))

    spec = pltpu.PrefetchScalarGridSpec(
        num_scalar_prefetch=1,
        grid=(QUADS,),
        in_specs=[
            quad(rows), quad(rows), quad(2), quad(2), quad(rows), quad(2), quad(6),
            pl.BlockSpec((1, 3, 9, 256, 256), lambda q, me: (q, 0, 0, 0, 0)),
        ],
        out_specs=[quad(rows), piece, piece, quad(2)],
        scratch_shapes=[
            pltpu.VMEM((2 * PITCH + 256 * crops, LANES), f32),
            pltpu.VMEM((3, 256 * crops, LANES), bf16),
            pltpu.VMEM((2 * PITCH + 256 * crops, LANES), f32),
            pltpu.VMEM((3, 256 * crops, LANES), bf16),
            pltpu.VMEM((PITCH * HW * crops, LANES), f32),
            pltpu.VMEM((rows, LANES), f32),
            pltpu.VMEM((2, 9 * GROUP, 256), f32),
        ],
    )
    return pl.pallas_call(
        functools.partial(conv_back_kernel, crops, count),
        grid_spec=spec,
        out_shape=[
            jax.ShapeDtypeStruct((rows, width), bf16),
            jax.ShapeDtypeStruct((QUADS, 1, 9 * GROUP, 256), bf16),
            jax.ShapeDtypeStruct((QUADS, 1, 9 * GROUP, 256), bf16),
            jax.ShapeDtypeStruct((2, width), f32),
        ],
        compiler_params=params(),
        cost_estimate=BRIEF,
        name="conv_back",
    )(index_scalar("dp"), g, a2, sums2, grad_sums, a, sums, norms, windows)


def squeeze_weight(se_ref, d):
    return jnp.concatenate([se_ref[d, m, :, :128] for m in range(QUADS)], 1)


def excite_weight(se_ref, m):
    return jnp.concatenate(
        [
            jnp.concatenate(
                [se_ref[d, m, 64 * i : 64 * (i + 1), 128:] for i in range(4)], 1
            )
            for d in range(2 * QUADS)
        ],
        0,
    )


def rows_of_crops(values, rows):
    row = lax.broadcasted_iota(jnp.int32, (rows, 1), 0)
    out = values[0:1]
    for c in range(1, values.shape[0]):
        out = jnp.where(row >= PIXELS * c, values[c : c + 1], out)
    return out


def fetch_pieces(me_ref, pieces, hold_ref, sems, offset):
    size = hold_ref.shape[2]
    copies = [
        pltpu.make_async_copy(
            piece.at[pl.ds(offset + m * size, size)],
            hold_ref.at[me_ref[0] ^ b, m],
            sems.at[b * QUADS + m],
        )
        for b, piece in enumerate(pieces)
        for m in range(QUADS)
    ]
    for copy in copies:
        copy.start()
    return copies


def fetch_scratch(size):
    return [
        pltpu.VMEM((2 * QUADS, QUADS, size, 256), bf16),
        pltpu.SemaphoreType.DMA((8 * QUADS,)),
    ]


def gate_kernel(crops, count, me_ref, a_ref, sums_ref, norms_ref, *refs):
    h_ref, pooled_ref, squeezed_ref, act_ref, gate_ref, f2_ref, se_ref, sems = refs[8:]
    copies = fetch_pieces(me_ref, refs[:8], se_ref, sems, SE_OFFSET)
    rows = a_ref.shape[0]
    _, _, scale, shift = affine(sums_ref[...], norms_ref[...], 1, count)
    f2_ref[...] = swish(a_ref[...].astype(f32) * scale + shift)
    pooled = jnp.concatenate(
        [
            jnp.sum(f2_ref[pl.ds(PIXELS * c, PIXELS), :], 0, keepdims=True) / PIXELS
            for c in range(crops)
        ],
        0,
    ).astype(bf16)
    pooled_ref[...] = pooled
    for copy in copies:
        copy.wait()
    squeezed = sum(
        dot(pooled[:, 256 * d : 256 * (d + 1)], squeeze_weight(se_ref, d)) for d in range(8)
    )
    squeezed_ref[...] = squeezed
    act = swish(squeezed).astype(bf16)
    act_ref[...] = act
    for m in range(QUADS):
        lanes = pl.ds(m * LANES, LANES)
        gate = 1.0 / (1.0 + jnp.exp(-dot(act, excite_weight(se_ref, m))))
        gate_ref[:, lanes] = gate
        h_ref[m] = (f2_ref[:, lanes] * rows_of_crops(gate, rows)).astype(bf16)


def gate(a, sums, norms, se, count):
    rows, width = a.shape
    crops = rows // PIXELS
    return pl.pallas_call(
        functools.partial(gate_kernel, crops, count),
        in_specs=[SCALAR] + [pl.BlockSpec(memory_space=pltpu.VMEM)] * 3
        + [pl.BlockSpec(memory_space=pl.ANY)] * 8,
        out_shape=[
            jax.ShapeDtypeStruct((QUADS, rows, LANES), bf16),
            jax.ShapeDtypeStruct((crops, width), bf16),
            jax.ShapeDtypeStruct((crops, 512), f32),
            jax.ShapeDtypeStruct((crops, 512), bf16),
            jax.ShapeDtypeStruct((crops, width), f32),
        ],
        scratch_shapes=[pltpu.VMEM((rows, width), f32)] + fetch_scratch(SE_ROWS),
        compiler_params=params(),
        cost_estimate=BRIEF,
        name="gate",
    )(index_scalar("dp"), a, sums, norms, *se)


def gate_back_kernel(
    crops, count, me_ref, dh_ref, a_ref, sums_ref, norms_ref, gate_ref, squeezed_ref, *refs
):
    q_ref, stats_ref, excite_grad_ref, squeeze_grad_ref, work_ref, se_ref, sems = refs[8:]
    copies = fetch_pieces(me_ref, refs[:8], se_ref, sems, SE_OFFSET)
    rows = a_ref.shape[0]
    for m in range(QUADS):
        lanes = pl.ds(m * LANES, LANES)
        _, _, scale, shift = affine(sums_ref[:, lanes], norms_ref[:, lanes], 1, count)
        normed = a_ref[:, lanes].astype(f32) * scale + shift
        work_ref[:, lanes] = dh_ref[:, lanes] * swish(normed)
    sums = jnp.concatenate(
        [
            jnp.sum(work_ref[pl.ds(PIXELS * c, PIXELS), :], 0, keepdims=True)
            for c in range(crops)
        ],
        0,
    )
    gates = gate_ref[...]
    excite_grad = (sums * gates * (1.0 - gates)).astype(bf16)
    excite_grad_ref[...] = excite_grad
    for copy in copies:
        copy.wait()
    act_grad = sum(
        dot(excite_grad[:, m * LANES : (m + 1) * LANES], excite_weight(se_ref, m), NT)
        for m in range(QUADS)
    )
    squeeze_grad = (act_grad * swish_slope(squeezed_ref[...])).astype(bf16)
    squeeze_grad_ref[...] = squeeze_grad
    for d in range(8):
        lanes = pl.ds(d * 256, 256)
        pooled_grad = dot(squeeze_grad, squeeze_weight(se_ref, d), NT) / PIXELS
        values = a_ref[:, lanes].astype(f32)
        mean, inverse, scale, shift = affine(sums_ref[:, lanes], norms_ref[:, lanes], 1, count)
        normed = values * scale + shift
        q = (
            dh_ref[:, lanes] * rows_of_crops(gate_ref[:, lanes], rows)
            + rows_of_crops(pooled_grad, rows)
        ) * swish_slope(normed)
        q_ref[:, lanes] = q
        centred = (values - mean) * inverse
        stats_ref[0:1, lanes] = jnp.sum(q, 0, keepdims=True)
        stats_ref[1:2, lanes] = jnp.sum(q * centred, 0, keepdims=True)


def gate_back(dh, a, sums, norms, gates, squeezed, se, count):
    rows, width = a.shape
    crops = rows // PIXELS
    return pl.pallas_call(
        functools.partial(gate_back_kernel, crops, count),
        in_specs=[SCALAR] + [pl.BlockSpec(memory_space=pltpu.VMEM)] * 6
        + [pl.BlockSpec(memory_space=pl.ANY)] * 8,
        out_shape=[
            jax.ShapeDtypeStruct((rows, width), f32),
            jax.ShapeDtypeStruct((2, width), f32),
            jax.ShapeDtypeStruct((crops, width), bf16),
            jax.ShapeDtypeStruct((crops, 512), bf16),
        ],
        scratch_shapes=[pltpu.VMEM((rows, width), f32)] + fetch_scratch(SE_ROWS),
        compiler_params=params(),
        cost_estimate=BRIEF,
        name="gate_back",
    )(index_scalar("dp"), dh, a, sums, norms, gates, squeezed, *se)


def head_kernel(
    width, me_ref, summary_ref, *refs
):
    (
        loss_ref, unit_ref, score_grad_ref, embed_grad_ref, summary_grad_ref, all_ref,
        hold_ref, plan_ref, protos_ref, queue_ref, project_ref, bundle_ref, sems,
    ) = refs[8:]
    copies = fetch_pieces(me_ref, refs[:8], bundle_ref, sems, 0)
    crops = all_ref.shape[0]
    each = summary_ref.shape[1]
    for i in range(summary_ref.shape[0]):
        hold_ref[pl.ds(each * i, each), :] = summary_ref[i].astype(f32)
    all_ref[...] = hold_ref[...].astype(bf16)
    for copy in copies:
        copy.wait()
    parts = 2 * QUADS * QUADS
    blocks = parts * QUEUE_ROWS // crops
    for i in range(parts):
        d, m = i // QUADS, i % QUADS
        low = 64
        project_ref[d, pl.ds(64 * m, 64), :] = bundle_ref[d, m, 0:low, :]
        protos_ref[pl.ds(PROTO_ROWS * i, PROTO_ROWS), :] = bundle_ref[d, m, low : low + PROTO_ROWS, :]
        low = low + PROTO_ROWS
        queue_ref[pl.ds(QUEUE_ROWS * i, QUEUE_ROWS), :] = bundle_ref[d, m, low : low + QUEUE_ROWS, :]
    protos = protos_ref[...]
    embedded = sum(
        dot(all_ref[:, 256 * d : 256 * (d + 1)], project_ref[d], NT) for d in range(8)
    )
    scale = lax.rsqrt(jnp.sum(embedded * embedded, 1, keepdims=True) + EPS_NORM)
    unit = (embedded * scale).astype(bf16)
    unit_ref[...] = unit
    scores = dot(unit, protos, NT)
    lane = lax.broadcasted_iota(jnp.int32, (1, parts * PROTO_ROWS), 1)
    block = lane // PROTO_ROWS
    there = (block // QUADS) * PROTO_ROWS + (lane - block * PROTO_ROWS) < width
    first = jnp.where(there, jnp.exp(scores / EPS_SINK), 0.0)
    plan_ref[pl.ds(0, crops), :] = first

    def fill(i, column):
        rows = queue_ref[pl.ds(pl.multiple_of(i * crops, crops), crops), :]
        value = jnp.exp(dot(rows, protos, NT) / EPS_SINK)
        plan_ref[pl.ds(pl.multiple_of((i + 1) * crops, crops), crops), :] = value
        return column + jnp.sum(value, 0, keepdims=True)

    column = lax.fori_loop(0, blocks, fill, jnp.sum(first, 0, keepdims=True))
    inverse = jnp.where(there, 1.0 / column, 0.0)
    for sweep in range(SINK - 1):

        def pass_rows(i, column, inverse=inverse):
            place = pl.ds(pl.multiple_of(i * crops, crops), crops)
            value = plan_ref[place, :] * inverse
            value = value * (1.0 / jnp.sum(value, 1, keepdims=True))
            plan_ref[place, :] = value
            return column + jnp.sum(value, 0, keepdims=True)

        column = lax.fori_loop(0, blocks + 1, pass_rows, jnp.zeros_like(column))
        inverse = jnp.where(there, 1.0 / column, 0.0)
    value = plan_ref[pl.ds(0, crops), :] * inverse
    value = value / jnp.sum(value, 1, keepdims=True)
    pairs = jnp.concatenate(
        [bundle_ref[d, 0, HEAD_ROWS - 16 : HEAD_ROWS, :].astype(f32)[:8, :crops] for d in range(8)], 0
    )
    plan = lax.dot_general(
        pairs, value, NN, precision=lax.Precision.HIGHEST, preferred_element_type=f32
    )
    logits = scores / SOFTMAX_TEMPER
    top = jnp.max(jnp.where(there, logits, -jnp.inf), 1, keepdims=True)
    power = jnp.where(there, jnp.exp(logits - top), 0.0)
    mass = jnp.sum(power, 1, keepdims=True)
    entropy = jnp.sum(plan * (logits - (top + jnp.log(mass))), 1, keepdims=True)
    loss_ref[...] = -jnp.sum(entropy, 0, keepdims=True) / crops
    score_grad = ((power / mass - plan) / (SOFTMAX_TEMPER * crops)).astype(bf16)
    score_grad_ref[...] = score_grad.T
    unit_grad = dot(score_grad, protos)
    inner = jnp.sum(embedded * unit_grad, 1, keepdims=True)
    embed_grad = (scale * unit_grad - embedded * (scale * scale * scale * inner)).astype(bf16)
    embed_grad_ref[...] = embed_grad
    for d in range(8):
        summary_grad_ref[:, 256 * d : 256 * (d + 1)] = dot(embed_grad, project_ref[d])


def head(summary, bundle, width):
    devices, each, channels = summary.shape
    crops = devices * each
    parts = 2 * QUADS * QUADS
    return pl.pallas_call(
        functools.partial(head_kernel, width),
        in_specs=[SCALAR, pl.BlockSpec(memory_space=pltpu.VMEM)]
        + [pl.BlockSpec(memory_space=pl.ANY)] * 8,
        out_shape=[
            jax.ShapeDtypeStruct((1, 1), f32),
            jax.ShapeDtypeStruct((crops, 256), bf16),
            jax.ShapeDtypeStruct((parts * PROTO_ROWS, crops), bf16),
            jax.ShapeDtypeStruct((crops, 256), bf16),
            jax.ShapeDtypeStruct((crops, channels), f32),
            jax.ShapeDtypeStruct((crops, channels), bf16),
        ],
        scratch_shapes=[
            pltpu.VMEM((crops, channels), f32),
            pltpu.VMEM((crops + parts * QUEUE_ROWS, parts * PROTO_ROWS), f32),
            pltpu.VMEM((parts * PROTO_ROWS, 256), bf16),
            pltpu.VMEM((parts * QUEUE_ROWS, 256), bf16),
            pltpu.VMEM((8, 256, 256), bf16),
        ]
        + fetch_scratch(HEAD_ROWS),
        compiler_params=params(),
        cost_estimate=BRIEF,
        name="head",
    )(index_scalar("dp"), summary, *bundle)


def plain_head(summary, project, protos, queue, pairs):
    crops = summary.shape[0]
    embedded = dot(summary, project)
    scale = lax.rsqrt(jnp.sum(embedded * embedded, 1, keepdims=True) + EPS_NORM)
    unit = (embedded * scale).astype(bf16)
    scores = dot(unit, protos)
    plan = jnp.exp(jnp.concatenate([scores, dot(queue, protos)], 0) / EPS_SINK)
    for sweep in range(SINK):
        plan = plan / jnp.sum(plan, 0, keepdims=True)
        plan = plan / jnp.sum(plan, 1, keepdims=True)
    plan = lax.dot_general(
        pairs, plan[:crops], NN, precision=lax.Precision.HIGHEST, preferred_element_type=f32
    )
    logits = scores / SOFTMAX_TEMPER
    loss = -jnp.sum(plan * jax.nn.log_softmax(logits, axis=1)) / crops
    score_grad = ((jax.nn.softmax(logits, axis=1) - plan) / (SOFTMAX_TEMPER * crops)).astype(bf16)
    unit_grad = dot(score_grad, protos, NT)
    inner = jnp.sum(embedded * unit_grad, 1, keepdims=True)
    embed_grad = (scale * unit_grad - embedded * (scale * scale * scale * inner)).astype(bf16)
    return loss.reshape(1, 1), unit, score_grad, embed_grad, dot(embed_grad, project, NT)


def picks(rows, columns, source):
    row = lax.broadcasted_iota(jnp.int32, (rows, columns), 0)
    column = lax.broadcasted_iota(jnp.int32, (rows, columns), 1)
    return jnp.where(row == source(column), 1.0, 0.0).astype(bf16)


def narrow_lanes(v):
    return jnp.concatenate([v[:, :HALF], v[:, HALF + GAP :]], 1)


def square_sum(v):
    return jnp.sum(jnp.sum(v * v, 1, keepdims=True), 0, keepdims=True)


def small_grads_kernel(
    m_ref, small_ref, summary_ref, embed_grad_ref, score_grad_ref, unit_ref,
    squeeze_ref, excite_ref, project_ref, protos_ref, squares_ref, hold_ref,
):
    m = m_ref[0]
    devices, each, _ = small_ref.shape
    for i in range(devices):
        hold_ref[pl.ds(each * i, each), :] = small_ref[i].astype(f32)
    wide, inner = QUADS * LANES, 8 * SE_LANES

    def rows_of(base, size):
        return hold_ref[:, pl.ds(pl.multiple_of(base, 128), size)]

    squeeze_grad = rows_of(wide + inner + 128 * m, 128).astype(bf16)
    squeeze_grad = dot(
        squeeze_grad, picks(128, 2 * SE_PART, lambda c: (c // SE_PART) * SE_LANES + c % SE_PART)
    ).astype(bf16)
    squares = []
    total_square = jnp.zeros((1, 1), f32)
    for q in range(QUADS):
        pooled = narrow_lanes(rows_of(q * LANES, LANES)).astype(bf16)
        part = dot(pooled, squeeze_grad, TN)
        squeeze_ref[pl.ds(QUAD * q, QUAD), :] = part
        total_square = total_square + square_sum(part)
    squares.append(total_square)
    act = rows_of(wide, inner).astype(bf16)
    act = dot(act, picks(inner, QUAD, lambda c: (c // SE_PART) * SE_LANES + c % SE_PART)).astype(bf16)
    excite_grad = narrow_lanes(rows_of(wide + 2 * inner + LANES * m, LANES)).astype(bf16)
    part = dot(act, excite_grad, TN)
    excite_ref[...] = part
    squares.append(square_sum(part))
    embed_grad = dot(embed_grad_ref[...], picks(256, 64, lambda c: 64 * m + c)).astype(bf16)
    summary = jnp.concatenate(
        [
            narrow_lanes(summary_ref[:, q * LANES : (q + 1) * LANES].astype(f32))
            for q in range(QUADS)
        ],
        1,
    ).astype(bf16)
    part = dot(embed_grad, summary, TN)
    project_ref[...] = part
    squares.append(square_sum(part))
    total_square = jnp.zeros((1, 1), f32)
    last = protos_ref.shape[0]
    for d in range(8):
        place = pl.ds(pl.multiple_of((QUADS * d + m) * PROTO_ROWS, PROTO_ROWS), PROTO_ROWS)
        part = dot(score_grad_ref[place, :], unit_ref[...])
        size = min(PROTO_ROWS, last - PROTO_ROWS * d)
        protos_ref[pl.ds(PROTO_ROWS * d, size), :] = part[:size]
        total_square = total_square + square_sum(part)
    squares.append(total_square)
    lane = lax.broadcasted_iota(jnp.int32, (1, 128), 1)
    squares_ref[...] = sum(jnp.where(lane == i, v, 0.0) for i, v in enumerate(squares))


def small_grads(small, summary, embed_grad, score_grad, unit, width):
    crops = summary.shape[0]
    return pl.pallas_call(
        small_grads_kernel,
        in_specs=[SCALAR] + [pl.BlockSpec(memory_space=pltpu.VMEM)] * 5,
        out_shape=[
            jax.ShapeDtypeStruct((QUADS * QUAD, 2 * SE_PART), f32),
            jax.ShapeDtypeStruct((QUAD, QUAD), f32),
            jax.ShapeDtypeStruct((64, QUADS * QUAD), f32),
            jax.ShapeDtypeStruct((width, 256), f32),
            jax.ShapeDtypeStruct((1, 128), f32),
        ],
        scratch_shapes=[pltpu.VMEM((crops, small.shape[2]), f32)],
        compiler_params=params(),
        cost_estimate=BRIEF,
        name="small_grads",
    )(index_scalar("mp"), small, summary, embed_grad, score_grad, unit)


def own_kernel_kernel(me_ref, v_ref, out_ref, square_ref):
    value = v_ref[: 9 * GROUP].astype(f32)
    value = jnp.where(me_ref[0] % 2 == 1, value[:, 256 - HALF :], value[:, :HALF])
    out_ref[...] = value
    square_ref[...] = square_sum(value)


def own_kernel(v):
    return pl.pallas_call(
        own_kernel_kernel,
        in_specs=[SCALAR, pl.BlockSpec(memory_space=pltpu.VMEM)],
        out_shape=[
            jax.ShapeDtypeStruct((9 * GROUP, HALF), f32), jax.ShapeDtypeStruct((1, 1), f32),
        ],
        compiler_params=params(),
        cost_estimate=BRIEF,
        name="own_kernel",
    )(index_scalar("dp"), v)


def weight_sums_kernel(*refs):
    lane = lax.broadcasted_iota(jnp.int32, (1, 128), 1)
    refs[-1][...] = sum(
        jnp.where(lane == i, square_sum(ref[...]), 0.0) for i, ref in enumerate(refs[:-1])
    )


def weight_sums(weights):
    values = [w if w.shape[1] == 2 * SE_PART or w.shape[0] == w.shape[1] else w.T for w in weights]
    return pl.pallas_call(
        weight_sums_kernel,
        out_shape=jax.ShapeDtypeStruct((1, 128), f32),
        compiler_params=params(),
        cost_estimate=BRIEF,
        name="weight_sums",
    )(*values)


def squares_kernel(
    n_dp, n_mp, weights_ref, norms_ref, small_ref, reduce_ref, expand_ref, kernel_ref,
    g1_ref, g2_ref, g3_ref, out_ref,
):
    lane = lax.broadcasted_iota(jnp.int32, (1, 128), 1)

    def at(i, v):
        return jnp.where(lane == i, v, 0.0)

    portions = at(0, 1.0) + at(1, 1.0 / n_mp) + at(4, 1.0)
    for i in (2, 3, 5, 6):
        portions = portions + at(i, 1.0 / n_dp)
    weights = weights_ref[...] * portions
    small = small_ref[...]
    grads = at(0, reduce_ref[...]) + at(1, kernel_ref[...] / n_mp) + at(4, expand_ref[...])
    for i, k in enumerate((2, 3, 5, 6)):
        grads = grads + at(k, small[:, i : i + 1] / n_dp)
    everywhere = 1.0 / (n_dp * n_mp)
    for k, ref in enumerate((g1_ref, g2_ref, g3_ref)):
        for row, first in ((1, 7), (0, 10)):
            grads = grads + at(first + k, square_sum(ref[row : row + 1, :]) * everywhere)
        weights = weights + at(7 + k, square_sum(norms_ref[k : k + 1, :]) * everywhere)
        weights = weights + at(10 + k, square_sum(norms_ref[3 + k : 4 + k, :]) * everywhere)
    out_ref[0:1, :] = weights
    out_ref[1:2, :] = grads


def squares(n_dp, n_mp, *values):
    return pl.pallas_call(
        functools.partial(squares_kernel, n_dp, n_mp),
        out_shape=jax.ShapeDtypeStruct((2, 128), f32),
        compiler_params=params(),
        cost_estimate=BRIEF,
        name="squares",
    )(*values)


def rate_of(norm_squares, i):
    norms = jnp.sqrt(norm_squares[:, i : i + 1] + EPS_NORM)
    return TRUST * norms[0:1] / (norms[1:2] + DECAY * norms[0:1])


def step(weight, gradient, momentum, norm_squares, i):
    return MOMENTUM * momentum + rate_of(norm_squares, i) * (gradient + DECAY * weight)


def lars_prepare_kernel(*refs):
    n = len(refs) // 5
    for i in range(n):
        weight, gradient, momentum = (refs[3 * i + j] for j in range(3))
        refs[3 * n + 2 * i][...] = gradient[...] + DECAY * weight[...]
        refs[3 * n + 2 * i + 1][...] = MOMENTUM * momentum[...]


def lars_prepare(items):
    return pl.pallas_call(
        lars_prepare_kernel,
        out_shape=[jax.ShapeDtypeStruct(w.shape, f32) for w, _, _ in items for _ in range(2)],
        compiler_params=params(),
        cost_estimate=BRIEF,
        name="lars_prepare",
    )(*[v for item in items for v in item])


def lars_kernel(squares_ref, weight_ref, gradient_ref, momentum_ref, *refs):
    norm_squares = squares_ref[...]
    n = len(refs) // 3
    refs[2 * n][...] = step(
        weight_ref[...], gradient_ref[...], momentum_ref[...], norm_squares, 0
    )
    for i in range(n):
        refs[2 * n + 1 + i][...] = (
            refs[2 * i + 1][...] + rate_of(norm_squares, i + 1) * refs[2 * i][...]
        )


def lars(norm_squares, weight, gradient, momentum, prepared):
    shapes = [weight.shape] + [v.shape for v in prepared[::2]]
    return pl.pallas_call(
        lars_kernel,
        out_shape=[jax.ShapeDtypeStruct(shape, f32) for shape in shapes],
        compiler_params=params(),
        cost_estimate=BRIEF,
        name="lars",
    )(norm_squares, weight, gradient, momentum, *prepared)


def lars_norms_kernel(
    m_ref, squares_ref, gains_ref, biases_ref, m_gains_ref, m_biases_ref, g1_ref, g2_ref, g3_ref,
    gains_out, biases_out,
):
    norm_squares = squares_ref[...]
    lanes = pl.ds(pl.multiple_of(m_ref[0] * LANES, LANES), LANES)
    for k, ref in enumerate((g1_ref, g2_ref, g3_ref)):
        own = narrow_lanes(ref[:, lanes])
        row = slice(k, k + 1)
        gains_out[row, :] = step(gains_ref[row, :], own[1:2], m_gains_ref[row, :], norm_squares, 7 + k)
        biases_out[row, :] = step(
            biases_ref[row, :], own[0:1], m_biases_ref[row, :], norm_squares, 10 + k
        )


def lars_norms(norm_squares, *values):
    return pl.pallas_call(
        lars_norms_kernel,
        in_specs=[SCALAR] + [pl.BlockSpec(memory_space=pltpu.VMEM)] * 8,
        out_shape=[jax.ShapeDtypeStruct(values[0].shape, f32)] * 2,
        compiler_params=params(),
        cost_estimate=BRIEF,
        name="lars_norms",
    )(index_scalar("mp"), norm_squares, *values)


def plain_finish(
    small, summary, unit, score_grad, embed_grad, grad_sums, channels_here, big_grads, weights, moments
):
    n_dp, n_mp, m_index = lax.axis_size("dp"), lax.axis_size("mp"), lax.axis_index("mp")
    w_reduce, w_group, w_squeeze, w_excite, w_expand, w_project, prototypes, bn_gains, bn_biases = weights
    small = small.reshape(-1, small.shape[-1])
    wide, inner = QUADS * LANES, 8 * SE_LANES
    pooled_all = pack_channels(small[:, :wide])
    act_all = pack_inner(small[:, wide : wide + inner])
    squeeze_all = pack_inner(small[:, wide + inner : wide + 2 * inner])
    excite_all = pack_channels(small[:, wide + 2 * inner :])

    def own(v, width):
        return lax.dynamic_slice_in_dim(v, m_index * width, width, 1)

    reduce_grad, kernel_grad, expand_grad = big_grads
    gain_part = own(pack_channels(jnp.stack([v[1] for v in grad_sums])), channels_here)
    bias_part = own(pack_channels(jnp.stack([v[0] for v in grad_sums])), channels_here)
    grads = [
        reduce_grad,
        kernel_grad,
        dot(pooled_all, own(squeeze_all, w_squeeze.shape[1]), TN),
        dot(act_all, own(excite_all, w_excite.shape[1]), TN),
        expand_grad,
        dot(pack_channels(summary), own(embed_grad, w_project.shape[1]), TN),
        dot(unit, own(score_grad, prototypes.shape[1]), TN),
    ]
    portions = [1.0, 1.0 / n_mp, 1.0 / n_dp, 1.0 / n_dp, 1.0, 1.0 / n_dp, 1.0 / n_dp]

    def shares(arrays, gain, bias):
        return jnp.concatenate(
            [
                jnp.stack([jnp.sum(a * a) * p for a, p in zip(arrays, portions)]),
                jnp.sum(gain * gain, 1) / n_dp,
                jnp.sum(bias * bias, 1) / n_dp,
            ]
        )

    norms = total(
        jnp.stack([shares(weights[:7], bn_gains, bn_biases), shares(grads, gain_part, bias_part)])
    )
    stepped = [
        step(w, g, m, norms, i) for i, (w, g, m) in enumerate(zip(weights[:7], grads, moments[:7]))
    ]
    for values, part, momentum, first in (
        (bn_gains, gain_part, moments[7], 7), (bn_biases, bias_part, moments[8], 10),
    ):
        stepped.append(
            jnp.concatenate(
                [
                    step(values[k : k + 1], part[k : k + 1], momentum[k : k + 1], norms, first + k)
                    for k in range(3)
                ]
            )
        )
    return stepped, norms


def body(
    block_input, output_grad, w_reduce, w_group, w_squeeze, w_excite, w_expand, w_project,
    prototypes, bn_gains, bn_biases, m_reduce, m_group, m_squeeze, m_excite, m_expand,
    m_project, m_protos, m_gains, m_biases, queue_store, queue_slots, crop_perm,
):
    n_dp = lax.axis_size("dp")
    n_mp = lax.axis_size("mp")
    m_index = lax.axis_index("mp")
    channels_here = block_input.shape[0]
    rows = block_input.shape[1] // n_mp
    crops = rows // PIXELS
    count = rows * n_dp * n_mp
    all_crops = crops * n_dp * n_mp
    quick = quick_mesh()
    weights = [
        w_reduce, w_group, w_squeeze, w_excite, w_expand, w_project, prototypes, bn_gains, bn_biases,
    ]
    moments = [
        m_reduce, m_group, m_squeeze, m_excite, m_expand, m_project, m_protos, m_gains, m_biases,
    ]

    slot_table = (
        queue_slots[0][:, None]
        == lax.broadcasted_iota(jnp.int32, (queue_slots.shape[1], queue_store.shape[0]), 1)
    ).astype(bf16)
    queue_rows = dot(slot_table, queue_store.astype(bf16)).astype(bf16)
    order = crop_perm[0]
    pairing = (order[None, :] == jnp.bitwise_xor(order, 1)[:, None]).astype(f32)
    kernel_low = gather_kernel(w_group)
    x_blocks = slab_blocks(block_input)
    y_grad_blocks = slab_blocks(output_grad)
    norms = spread(jnp.concatenate([bn_gains, bn_biases], 0), "mp")
    norms = spread_channels(norms.transpose(1, 0, 2).reshape(norms.shape[1], -1))
    if quick:
        reduce_quads = gather_mp(shard_square(w_reduce)).reshape(-1, 256)
        rest = jnp.concatenate([shard_square(w_expand), shard_excitation(w_squeeze, w_excite)], 0)
        reduce_quads, rest, norms, *kernel_low = tie(reduce_quads, rest, norms, *kernel_low)
        across, up = gather_sides(reduce_quads)
        rest_parts = parts_mp(rest)
        windows = dense_windows(kernel_low)
        across, up, windows, x_blocks = tie(across, up, windows, x_blocks)
        corner = gather_corner(across, up)
        x_blocks, corner, *rest_parts = tie(x_blocks, corner, *rest_parts)
        x_blocks = exchange(x_blocks)
        rest = in_order(rest_parts, m_index)
        rest = jnp.concatenate(
            [rest[:, :LANES].reshape(-1, 256), rest[:, LANES:].reshape(-1, 256)], 0
        )
        rest_across, rest_up = gather_sides(rest)
        reduce_pieces = gather_twins(reduce_quads, across, up, corner)
        head_values = tie(w_project, prototypes, queue_rows, pairing, corner)
        bundle = shard_head(*head_values[:4])
    else:
        x_blocks = exchange(x_blocks)
        y_grad_blocks = exchange(y_grad_blocks)
        reduce_pieces = gather_square(w_reduce)
        rest_pieces = gather_excitation(w_squeeze, w_excite)
        expand_pieces = gather_square(w_expand)
        rest_pieces = jnp.concatenate(
            [expand_pieces.reshape(8, -1, 256), rest_pieces.reshape(8, -1, 256)], 1
        )
        rest_pieces = [rest_pieces[b] for b in range(8)]
        project_low, protos_low, queue_low, pairs = gather_head(
            w_project, prototypes, queue_rows, pairing
        )
        pairs = block_diagonal(pairs)
        windows = dense_windows(kernel_low)
    x = quad_blocks(x_blocks)

    reduced, sums1 = mix(x, reduce_pieces)
    if quick:
        sums1, rest_across, rest_up = tie(sums1, rest_across, rest_up)
        rest_corner = gather_corner(rest_across, rest_up)
    sums1 = total(sums1)
    if quick:
        sums1, bundle, rest_corner = tie(sums1, bundle, rest_corner)
        bundle = gather_mp(bundle).reshape(-1, 256)
    grouped, sums2 = conv(reduced, sums1, norms, windows, count)
    if quick:
        sums2, bundle = tie(sums2, bundle)
    sums2 = total(sums2)
    if quick:
        weight_squares = weight_sums(weights[:7])
        sums2, weight_squares = tie(sums2, weight_squares)
        rest_pieces = expand_pieces = gather_twins(rest, rest_across, rest_up, rest_corner)
    gated, pooled, squeezed, squeeze_act, gates = gate(grouped, sums2, norms, rest_pieces, count)
    if quick:
        gated, bundle = tie(gated, bundle)
        across, up = gather_sides(bundle)
    expanded, sums3 = mix(gated, expand_pieces)
    if quick:
        sums3, across, up = tie(sums3, across, up)
        corner = gather_corner(across, up)
    sums3 = total(sums3)
    if quick:
        sums3, corner = tie(sums3, corner)
        bundle = gather_twins(bundle, across, up, corner)
    y_blocks, summary = block_value(x, expanded, sums3, norms, count)
    summary = gather_all(summary)

    first_crop = ((lax.axis_index("dp") * n_mp + m_index) * crops).astype(jnp.int32)[None]
    if quick:
        summary, y_grad_blocks = tie(summary, y_grad_blocks)
        y_grad_blocks = exchange(y_grad_blocks)
        loss, unit, score_grad, embed_grad, summary_grad, summary = head(
            summary, bundle, prototypes.shape[1]
        )
    else:
        summary = summary.reshape(all_crops, -1)
        loss, unit, score_grad, embed_grad, summary_grad = plain_head(
            summary, project_low, protos_low, queue_low, pairs
        )

    joined_grad, grad_sums3 = value_back(
        first_crop, x, expanded, sums3, norms, quad_blocks(y_grad_blocks), summary_grad, count
    )
    grad_sums3 = total(grad_sums3)
    expanded_grad = norm_backward(joined_grad, expanded, sums3, norms, 2, grad_sums3, count, False)
    expand_kept, expand_sent = weight_grad(gated, expanded_grad)
    if quick:
        expand_got = from_twin(expand_sent)
    gated_grad = mix_back(expanded_grad, expand_pieces)
    if quick:
        gated_grad, expand_got = tie(gated_grad, expand_got)
        expand_sums, expand_corner = scatter_corner(expand_kept, expand_got)
    act2_grad, grad_sums2, excite_grad, squeeze_grad = gate_back(
        gated_grad, grouped, sums2, norms, gates, squeezed, rest_pieces, count
    )
    small = jnp.concatenate([pooled, squeeze_act, squeeze_grad, excite_grad], 1)
    if quick:
        grad_sums2, expand_corner = tie(grad_sums2, expand_corner)
    grad_sums2 = total(grad_sums2)
    grad_sums2, y_blocks = tie(grad_sums2, y_blocks)
    y_blocks = exchange(out_blocks(y_blocks))
    if quick:
        expand_own, across, up = expand_sums
        across, up = corner_sums(across, up, expand_corner)
        across, up = scatter_sides(across, up)
    act1_grad, kernel_kept, kernel_sent, grad_sums1 = conv_back(
        act2_grad, grouped, sums2, grad_sums2, reduced, sums1, norms, windows, count
    )
    if quick:
        grad_sums1, across, up, kernel_kept, kernel_sent, y_blocks = tie(
            grad_sums1, across, up, kernel_kept, kernel_sent, y_blocks
        )
        expand_own, *expand_parts = side_sums(expand_own, across, up)
        expand_parts = scatter_mp(expand_own, expand_parts)
        kernel_sums, kernel_corner = scatter_corner(kernel_kept, from_twin(kernel_sent))
        kernel_own, across, up = kernel_sums
        kernel_across, kernel_up = corner_sums(across, up, kernel_corner)
        grad_sums1 = jnp.sum(spread(grad_sums1, "dp"), 0)
        grad_sums1, expand_parts, kernel_across, kernel_up = tie(
            grad_sums1, expand_parts, kernel_across, kernel_up
        )
        kernel_across, kernel_up = scatter_sides(kernel_across, kernel_up)
        grad_sums1 = jnp.sum(spread(grad_sums1, "mp"), 0)
    else:
        grad_sums1 = total(grad_sums1)
    reduced_grad = norm_backward(act1_grad, reduced, sums1, norms, 0, grad_sums1, count, True)
    if quick:
        reduced_grad, kernel_across, kernel_up, small = tie(
            reduced_grad, kernel_across, kernel_up, small
        )
        kernel_sum = side_sums(kernel_own, kernel_across, kernel_up)[0].astype(bf16)
        kernel_sum = kernel_sum + lax.ppermute(kernel_sum, "mp", flips("mp", 1))
    small = gather_all(small)
    reduce_kept, reduce_sent = weight_grad(x, reduced_grad)
    if quick:
        reduce_got = from_twin(reduce_sent)
        reduce_got, kernel_sum = tie(reduce_got, kernel_sum)
        kernel_sum = kernel_sum + lax.ppermute(kernel_sum, "mp", flips("mp", 2))
    x_grad = out_blocks(mix_back(reduced_grad, reduce_pieces, joined_grad))
    if quick:
        x_grad, reduce_got, kernel_sum, small = tie(x_grad, reduce_got, kernel_sum, small)
        (own, across, up), corner = scatter_corner(reduce_kept, reduce_got)
        x_grad = exchange(x_grad)
        across, up = corner_sums(across, up, corner)
        across, up, small, kernel_sum = tie(across, up, small, kernel_sum)
        across, up = scatter_sides(across, up)
        squeeze_part, excite_part, project_part, protos_part, small_squares = small_grads(
            small, summary, embed_grad, score_grad, unit, prototypes.shape[1]
        )
        expand_grad, expand_square = own_square(expand_parts)
        kernel_grad, kernel_square = own_kernel(kernel_sum)
        across, up, x_grad, small_squares, expand_square, kernel_square = tie(
            across, up, x_grad, small_squares, expand_square, kernel_square
        )
        own, *parts = side_sums(own, across, up)
        parts = scatter_mp(own, parts)
        input_grad = out_channels(x_grad, channels_here, f32)
        block_output = out_channels(y_blocks, channels_here, bf16)
        prepared = lars_prepare(
            [
                (w_group.T, kernel_grad, m_group.T),
                (w_squeeze, squeeze_part, m_squeeze),
                (w_excite, excite_part, m_excite),
                (w_expand.T, expand_grad, m_expand.T),
                (w_project.T, project_part, m_project.T),
                (prototypes.T, protos_part, m_protos.T),
            ]
        )
        parts, input_grad, block_output, *prepared = tie(
            parts, input_grad, block_output, *prepared
        )
        reduce_grad, reduce_square = own_square(parts)
        norm_squares = total(
            squares(
                n_dp, n_mp, weight_squares, norms, small_squares, reduce_square, expand_square,
                kernel_square, grad_sums1, grad_sums2, grad_sums3,
            )
        )
        mom_reduce, mom_group, mom_squeeze, mom_excite, mom_expand, mom_project, mom_protos = lars(
            norm_squares, w_reduce.T, reduce_grad, m_reduce.T, prepared
        )
        mom_gains, mom_biases = lars_norms(
            norm_squares, bn_gains, bn_biases, m_gains, m_biases, grad_sums1, grad_sums2, grad_sums3
        )
        stepped = [
            mom_reduce.T, mom_group.T, mom_squeeze, mom_excite, mom_expand.T, mom_project.T,
            mom_protos.T, mom_gains, mom_biases,
        ]
    else:
        input_grad = out_channels(exchange(x_grad), channels_here, f32)
        block_output = out_channels(y_blocks, channels_here, bf16)
        big_grads = (
            scatter_square(reduce_kept, reduce_sent),
            scatter_kernel(kernel_kept[:, 0], kernel_sent[:, 0]),
            scatter_square(expand_kept, expand_sent),
        )
        stepped, norm_squares = plain_finish(
            small, summary, unit, score_grad, embed_grad, (grad_sums1, grad_sums2, grad_sums3),
            channels_here, big_grads, weights, moments,
        )
    param_norms = jnp.sqrt(norm_squares[:, :13].T + EPS_NORM)
    return (block_output, loss[0, 0], input_grad, *stepped, param_norms)


def solution(mesh):
    split = P("dp", "mp")
    turned = P("mp", "dp")
    rows = P("dp", None)
    columns = P(None, "mp")
    return jax.shard_map(
        body,
        mesh=mesh,
        in_specs=(
            turned, turned, split, rows, columns, columns, split, columns, columns, columns, columns,
            split, rows, columns, columns, split, columns, columns, columns, columns, rows, rows, rows,
        ),
        out_specs=(
            turned, P(), turned, split, rows, columns, columns, split, columns, columns, columns,
            columns, P(),
        ),
        check_vma=False,
    )
```

profile of v0, /device:TPU:0, one launch (start us, length us, event | category | flops | bytes accessed | tf_op | source)
XLA Modules:
  0.0 677.6 jit_solution(3296085579593971289)
XLA Ops:
  3.5 5.1 collective-permute-start
  13.3 4.9 all-to-all-start
  21.9 10.3 %all-to-all-done = f32[4,6,504]{2,1,0:T(8,128)S(1)} async-done(((f32[4,6,504]{2,1,0:T(8,128)}), f32[4,6,504]{2,1,0:T(8,128)S(1)}, u32[]{:S(2)}, u32[]{:S(2)}) %all-to-all-start) | async-done | bytes 48416 | tf_op jit(solution)/shard_map/all_to_all | solution.py:97
  38.7 2.8 pad_maximum_fusion.1
  41.5 5.4 dense_windows.1.w_ref
  47.0 13.6 %collective-permute-done.10.refs_2_ = bf16[2048,256]{1,0:T(8,128)(2,1)} collective-permute-done((bf16[2048,256]{1,0:T(8,128)(2,1)}, bf16[2048,256]{1,0:T(8,128)(2,1)}, u32[]{:S(2)}, u32[]{:S(2)}) %collective-permute-start.10) | collective-permute-done | bytes 1048608 | tf_op jit(solution)/shard_map/ppermute | solution.py:149
  65.1 2.7 collective-permute-start.14
  69.2 11.9 %collective-permute-done.13 = bf16[768,256]{1,0:T(8,128)(2,1)S(1)} collective-permute-done((bf16[768,256]{1,0:T(8,128)(2,1)S(1)}, bf16[768,256]{1,0:T(8,128)(2,1)S(1)}, u32[]{:S(2)}, u32[]{:S(2)}) %collective-permute-start.13) | collective-permute-done | bytes 393248 | tf_op jit(solution)/shard_map/ppermute | solution.py:137
  81.0 13.9 %collective-permute-done.14 = bf16[768,256]{1,0:T(8,128)(2,1)S(1)} collective-permute-done((bf16[768,256]{1,0:T(8,128)(2,1)S(1)}, bf16[768,256]{1,0:T(8,128)(2,1)S(1)}, u32[]{:S(2)}, u32[]{:S(2)}) %collective-permute-start.14) | collective-permute-done | bytes 393248 | tf_op jit(solution)/shard_map/ppermute | solution.py:137
  96.5 7.5 %all-to-all-start.1 = ((bf16[4,392,512]{2,1,0:T(8,128)(2,1)}), bf16[4,392,512]{2,1,0:T(8,128)(2,1)S(1)}, u32[]{:S(2)}, u32[]{:S(2)}) async-start(bf16[4,392,512]{2,1,0:T(8,128)(2,1)} %get-tuple-element.215), calls=%async_computation.1 | async-start | bytes 3211264 | tf_op jit(solution)/shard_map/all_to_all | solution.py:133
  113.7 25.1 %all-to-all-done.1.x_ref = bf16[4,392,512]{2,1,0:T(8,128)(2,1)S(1)} async-done(((bf16[4,392,512]{2,1,0:T(8,128)(2,1)}), bf16[4,392,512]{2,1,0:T(8,128)(2,1)S(1)}, u32[]{:S(2)}, u32[]{:S(2)}) %all-to-all-start.1) | async-done | bytes 1605664 | tf_op jit(solution)/shard_map/all_to_all | solution.py:133
  140.0 8.4 %mix.2 = (f32[392,2048]{1,0:T(8,128)}, f32[2,2048]{1,0:T(2,128)S(1)}) custom-call(s32[1]{0:T(128)} %bitcast.1.me_ref, bf16[4,392,512]{2,1,0:T(8,128)(2,1)} %copy-done.2, bf16[2048,256]{1,0:T(8,128)(2,1)} %bitcast.7.refs_0_, bf16[2048,256]{1,0:T(8,128)(2,1)} %collective-permute-done.16.refs_1_, bf16[2048,256]{1,0:T(8,128)(2,1)} %collective-permute-done.10.refs_2_, ...), custom_call_target="tpu_custom_call" | custom-call | flops 1 | bytes 1 | tf_op jit(solution)/shard_map/mix/pallas_call | solution.py:372
  148.5 2.8 broadcast_select_fusion
  156.1 3.7 all-to-all-start.2
  160.8 13.2 %all-to-all-done.2 = f32[8,2,2048]{2,1,0:T(2,128)S(1)} async-done(((f32[8,2,2048]{2,1,0:T(2,128)}), f32[8,2,2048]{2,1,0:T(2,128)S(1)}, u32[]{:S(2)}, u32[]{:S(2)}) %all-to-all-start.2) | async-done | bytes 131104 | tf_op jit(solution)/shard_map/all_to_all | solution.py:97
  174.7 13.5 %all-to-all-start.3 = ((f32[4,2,2048]{2,1,0:T(2,128)}), f32[4,2,2048]{2,1,0:T(2,128)S(1)}, u32[]{:S(2)}, u32[]{:S(2)}) async-start(f32[4,2,2048]{2,1,0:T(2,128)} %broadcast_in_dim.55), calls=%async_computation.3 | async-start | bytes 131072 | tf_op jit(solution)/shard_map/all_to_all | solution.py:97
  188.7 4.8 all-to-all-done.3
  194.8 6.2 collective-permute-done.23
  202.1 6.5 collective-permute-done.24
  210.6 11.5 %conv.1 = (bf16[392,2048]{1,0:T(8,128)(2,1)S(1)}, f32[2,2048]{1,0:T(2,128)S(1)}) custom-call(f32[392,2048]{1,0:T(8,128)S(1)} %copy-done.4, f32[2,2048]{1,0:T(2,128)S(1)} %reduce_sum.127.sums_ref, f32[6,2048]{1,0:T(8,128)S(1)} %bitcast.83, bf16[4,3,9,256,256]{4,3,2,1,0:T(8,128)(2,1)} %dense_windows.1.w_ref), custom_call_target="tpu_custom_call" | custom-call | flops 1 | bytes 1 | tf_op jit(solution)/shard_map/conv/pallas_call | solution.py:793
  224.1 10.3 %all_to_all.105 = f32[8,2,2048]{2,1,0:T(2,128)S(1)} all-to-all(f32[8,2,2048]{2,1,0:T(2,128)S(1)} %broadcast_in_dim.57), channel_id=1, replica_groups=mesh['dp'=8,'mp'=4] {'dp'}, dimensions={0} | all-to-all | bytes 262144 | tf_op jit(solution)/shard_map/all_to_all | solution.py:97
  235.1 3.3 all-to-all-start.5
  247.0 7.7 %gate.1 = (bf16[4,392,512]{2,1,0:T(8,128)(2,1)}, bf16[2,2048]{1,0:T(2,128)(2,1)S(1)}, f32[2,512]{1,0:T(2,128)S(1)}, bf16[2,512]{1,0:T(2,128)(2,1)S(1)}, f32[2,2048]{1,0:T(2,128)S(1)}) custom-call(s32[1]{0:T(128)} %bitcast.1.me_ref, bf16[392,2048]{1,0:T(8,128)(2,1)} %copy-done.10, f32[2,2048]{1,0:T(2,128)S(1)} %reduce_sum.129.sums_ref.sums2_ref, ...), custom_call_target="tpu_custom_call" | custom-call | flops 1 | bytes 1 | tf_op jit(solution)/shard_map/gate/pallas_call | solution.py:1010
  258.1 8.0 %mix.3 = (f32[392,2048]{1,0:T(8,128)}, f32[2,2048]{1,0:T(2,128)S(1)}) custom-call(s32[1]{0:T(128)} %bitcast.1.me_ref, bf16[4,392,512]{2,1,0:T(8,128)(2,1)} %get-tuple-element.241.x_ref, bf16[3072,256]{1,0:T(8,128)(2,1)S(1)} %pad_maximum_fusion.3.refs_0_, bf16[3072,256]{1,0:T(8,128)(2,1)S(1)} %collective-permute-done.26.refs_1_, ...), custom_call_target="tpu_custom_call" | custom-call | flops 1 | bytes 1 | tf_op jit(solution)/shard_map/mix/pallas_call | solution.py:372
  270.5 9.1 %all_to_all.106 = f32[8,2,2048]{2,1,0:T(2,128)S(1)} all-to-all(f32[8,2,2048]{2,1,0:T(2,128)S(1)} %broadcast_in_dim.59), channel_id=1, replica_groups=mesh['dp'=8,'mp'=4] {'dp'}, dimensions={0} | all-to-all | bytes 262144 | tf_op jit(solution)/shard_map/all_to_all | solution.py:97
  279.8 10.3 %all_to_all.107 = f32[4,2,2048]{2,1,0:T(2,128)S(1)} all-to-all(f32[4,2,2048]{2,1,0:T(2,128)S(1)} %broadcast_in_dim.60), channel_id=1, replica_groups=mesh['dp'=8,'mp'=4] {'mp'}, dimensions={0} | all-to-all | bytes 131072 | tf_op jit(solution)/shard_map/all_to_all | solution.py:97
  290.1 3.7 value.1
  295.2 11.9 %all_to_all.108.summary_ref = bf16[32,2,2048]{2,1,0:T(2,128)(2,1)S(1)} all-to-all(bf16[32,2,2048]{2,1,0:T(2,128)(2,1)S(1)} %broadcast_in_dim.61), channel_id=1, replica_groups=mesh['dp'=8,'mp'=4] {'dp','mp'}, dimensions={0} | all-to-all | bytes 524288 | tf_op jit(solution)/shard_map/all_to_all | solution.py:112
  307.1 4.4 all-to-all-start.9
  318.5 24.3 %head.1 = (f32[1,1]{1,0:T(1,128)}, bf16[64,256]{1,0:T(8,128)(2,1)S(1)}, bf16[3072,64]{1,0:T(8,128)(2,1)S(1)}, bf16[64,256]{1,0:T(8,128)(2,1)S(1)}, f32[64,2048]{1,0:T(8,128)S(1)}, /*index=5*/bf16[64,2048]{1,0:T(8,128)(2,1)S(1)}) custom-call(s32[1]{0:T(128)} %bitcast.1.me_ref, bf16[32,2,2048]{2,1,0:T(2,128)(2,1)S(1)} %all_to_all.108.summary_ref, ...), custom_call_target="tpu_custom_call" | custom-call | flops 1 | bytes 1 | tf_op jit(solution)/shard_map/head/pallas_call | solution.py:1178
  346.4 3.7 all-to-all-done.9.dy_ref
  351.1 5.7 value_back.1
  356.9 7.9 %all_to_all.109 = f32[8,2,2048]{2,1,0:T(2,128)S(1)} all-to-all(f32[8,2,2048]{2,1,0:T(2,128)S(1)} %broadcast_in_dim.62), channel_id=1, replica_groups=mesh['dp'=8,'mp'=4] {'dp'}, dimensions={0} | all-to-all | bytes 262144 | tf_op jit(solution)/shard_map/all_to_all | solution.py:97
  364.9 8.5 %all_to_all.110 = f32[4,2,2048]{2,1,0:T(2,128)S(1)} all-to-all(f32[4,2,2048]{2,1,0:T(2,128)S(1)} %broadcast_in_dim.63), channel_id=1, replica_groups=mesh['dp'=8,'mp'=4] {'mp'}, dimensions={0} | all-to-all | bytes 131072 | tf_op jit(solution)/shard_map/all_to_all | solution.py:97
  375.3 3.4 norm_backward.2.g_ref
  378.7 6.7 weight_grad.2
  385.4 11.4 %mix_back.2.dh_ref = f32[392,2048]{1,0:T(8,128)} custom-call(s32[1]{0:T(128)} %bitcast.1.me_ref, bf16[392,2048]{1,0:T(8,128)(2,1)} %copy-done.9, bf16[3072,256]{1,0:T(8,128)(2,1)S(1)} %pad_maximum_fusion.3.refs_0_, bf16[3072,256]{1,0:T(8,128)(2,1)S(1)} %copy-done.6, bf16[3072,256]{1,0:T(8,128)(2,1)} %collective-permute-done.20.refs_2_, ...), custom_call_target="tpu_custom_call" | custom-call | flops 1 | bytes 1 | tf_op jit(solution)/shard_map/mix_back/pallas_call | solution.py:417
  401.6 11.6 %gate_back.1 = (f32[392,2048]{1,0:T(8,128)}, f32[2,2048]{1,0:T(2,128)S(1)}, bf16[2,2048]{1,0:T(2,128)(2,1)S(1)}, bf16[2,512]{1,0:T(2,128)(2,1)S(1)}) custom-call(s32[1]{0:T(128)} %bitcast.1.me_ref, f32[392,2048]{1,0:T(8,128)} %mix_back.2.dh_ref, bf16[392,2048]{1,0:T(8,128)(2,1)} %copy-done.10, f32[2,2048]{1,0:T(2,128)S(1)} %reduce_sum.129.sums_ref.sums2_ref, ...), custom_call_target="tpu_custom_call" | custom-call | flops 1 | bytes 1 | tf_op jit(solution)/shard_map/gate_back/pallas_call | solution.py:1076
  413.2 2.6 collective-permute-done.38.corner_ref
  416.8 7.9 %all_to_all.111 = f32[8,2,2048]{2,1,0:T(2,128)S(1)} all-to-all(f32[8,2,2048]{2,1,0:T(2,128)S(1)} %broadcast_in_dim.64), channel_id=1, replica_groups=mesh['dp'=8,'mp'=4] {'dp'}, dimensions={0} | all-to-all | bytes 262144 | tf_op jit(solution)/shard_map/all_to_all | solution.py:97
  424.8 8.1 %all_to_all.112 = f32[4,2,2048]{2,1,0:T(2,128)S(1)} all-to-all(f32[4,2,2048]{2,1,0:T(2,128)S(1)} %broadcast_in_dim.65), channel_id=1, replica_groups=mesh['dp'=8,'mp'=4] {'mp'}, dimensions={0} | all-to-all | bytes 131072 | tf_op jit(solution)/shard_map/all_to_all | solution.py:97
  433.0 4.8 all-to-all-start.14
  437.8 3.8 twin_sums.7
  444.4 22.2 %conv_back.1 = (bf16[392,2048]{1,0:T(8,128)(2,1)S(1)}, bf16[4,1,504,256]{3,2,1,0:T(8,128)(2,1)S(1)}, bf16[4,1,504,256]{3,2,1,0:T(8,128)(2,1)S(1)}, f32[2,2048]{1,0:T(2,128)S(1)}) custom-call(s32[1]{0:T(128)} %bitcast.1.me_ref, f32[392,2048]{1,0:T(8,128)} %get-tuple-element.260.g_ref, bf16[392,2048]{1,0:T(8,128)(2,1)S(1)} %copy-done.11, ...), custom_call_target="tpu_custom_call" | custom-call | flops 1 | bytes 1 | tf_op jit(solution)/shard_map/conv_back/pallas_call | solution.py:916
  470.8 3.6 all-to-all-done.14.blocks_ref
  486.7 8.2 %all_to_all.113 = f32[8,2,2048]{2,1,0:T(2,128)S(1)} all-to-all(f32[8,2,2048]{2,1,0:T(2,128)S(1)} %broadcast_in_dim.66), channel_id=1, replica_groups=mesh['dp'=8,'mp'=4] {'dp'}, dimensions={0} | all-to-all | bytes 262144 | tf_op jit(solution)/shard_map/all_to_all | solution.py:97
  498.2 3.4 collective-permute-done.42.refs_1_
  502.2 7.1 %all-to-all-start.16 = ((f32[4,2,2048]{2,1,0:T(2,128)}), f32[4,2,2048]{2,1,0:T(2,128)S(1)}, u32[]{:S(2)}, u32[]{:S(2)}) async-start(f32[4,2,2048]{2,1,0:T(2,128)} %broadcast_in_dim.67), calls=%async_computation.16 | async-start | bytes 131072 | tf_op jit(solution)/shard_map/all_to_all | solution.py:97
  511.2 3.8 all-to-all-done.16
  516.5 4.2 norm_backward.3.g_ref
  520.7 6.8 weight_grad.3
  528.7 2.8 all-to-all-start.17
  533.5 16.8 %collective-permute-done.49 = bf16[504,256]{1,0:T(8,128)(2,1)S(1)} collective-permute-done((bf16[504,256]{1,0:T(8,128)(2,1)S(1)}, bf16[504,256]{1,0:T(8,128)(2,1)S(1)}, u32[]{:S(2)}, u32[]{:S(2)}) %collective-permute-start.49) | collective-permute-done | bytes 258080 | tf_op jit(solution)/shard_map/ppermute | solution.py:1687
  552.9 12.8 %mix_back.3 = bf16[4,392,512]{2,1,0:T(8,128)(2,1)} custom-call(s32[1]{0:T(128)} %bitcast.1.me_ref, bf16[392,2048]{1,0:T(8,128)(2,1)} %copy-done.12, bf16[2048,256]{1,0:T(8,128)(2,1)} %bitcast.7.refs_0_, bf16[2048,256]{1,0:T(8,128)(2,1)} %collective-permute-done.16.refs_1_, bf16[2048,256]{1,0:T(8,128)(2,1)} %collective-permute-done.10.refs_2_, ...), custom_call_target="tpu_custom_call" | custom-call | flops 1 | bytes 1 | tf_op jit(solution)/shard_map/mix_back/pallas_call | solution.py:417
  566.5 3.6 all-to-all-start.18
  576.0 3.7 twin_sums.10
  579.7 9.6 %collective-permute-done.51.corner_ref = bf16[4,512,256]{2,1,0:T(8,128)(2,1)S(1)} collective-permute-done((bf16[4,512,256]{2,1,0:T(8,128)(2,1)S(1)}, bf16[4,512,256]{2,1,0:T(8,128)(2,1)S(1)}, u32[]{:S(2)}, u32[]{:S(2)}) %collective-permute-start.51) | collective-permute-done | bytes 1048608 | tf_op jit(solution)/shard_map/ppermute | solution.py:171
  604.1 9.6 %collective-permute-done.52.across_ref = bf16[4,512,256]{2,1,0:T(8,128)(2,1)S(1)} collective-permute-done((bf16[4,512,256]{2,1,0:T(8,128)(2,1)S(1)}, bf16[4,512,256]{2,1,0:T(8,128)(2,1)S(1)}, u32[]{:S(2)}, u32[]{:S(2)}) %collective-permute-start.52) | collective-permute-done | bytes 1048608 | tf_op jit(solution)/shard_map/ppermute | solution.py:181
  623.2 3.1 join_rows.3
  626.4 6.6 lars_prepare.1
  635.3 5.1 collective-permute-done.55.refs_1_
  644.6 8.2 %all_to_all.114 = f32[8,2,128]{2,1,0:T(2,128)S(1)} all-to-all(f32[8,2,128]{2,1,0:T(2,128)S(1)} %broadcast_in_dim.69), channel_id=1, replica_groups=mesh['dp'=8,'mp'=4] {'dp'}, dimensions={0} | all-to-all | bytes 16384 | tf_op jit(solution)/shard_map/all_to_all | solution.py:97
  652.8 10.9 %all_to_all.115 = f32[4,2,128]{2,1,0:T(2,128)S(1)} all-to-all(f32[4,2,128]{2,1,0:T(2,128)S(1)} %broadcast_in_dim.70), channel_id=1, replica_groups=mesh['dp'=8,'mp'=4] {'mp'}, dimensions={0} | all-to-all | bytes 8192 | tf_op jit(solution)/shard_map/all_to_all | solution.py:97
  672.7 4.7 lars.1
  (452 shorter events, 165.7 us)
Async XLA Ops:
  3.5 29.0 %collective-permute-start = (bf16[512,256]{1,0:T(8,128)(2,1)S(1)}, bf16[512,256]{1,0:T(8,128)(2,1)S(1)}, u32[]{:S(2)}, u32[]{:S(2)}) collective-permute-start(bf16[512,256]{1,0:T(8,128)(2,1)S(1)} %fusion), channel_id=1, source_target_pairs={{0,3},{1,2},{2,1},{3,0},{4,7},{5,6},{6,5},{7,4},{8,11},{9,10},{10,... | collective-permute-start | bytes 786440 | tf_op jit(solution)/shard_map/ppermute | solution.py:137
  8.6 24.0 %collective-permute-start.1 = (bf16[512,256]{1,0:T(8,128)(2,1)S(1)}, bf16[512,256]{1,0:T(8,128)(2,1)S(1)}, u32[]{:S(2)}, u32[]{:S(2)}) collective-permute-start(bf16[512,256]{1,0:T(8,128)(2,1)S(1)} %fusion), channel_id=1, source_target_pairs={{0,2},{1,3},{2,0},{3,1},{4,6},{5,7},{6,4},{7,5},{8,10},{9,11},{10,... | collective-permute-start | bytes 786440 | tf_op jit(solution)/shard_map/ppermute | solution.py:137
  8.6 24.6 %collective-permute-start.2 = (bf16[512,256]{1,0:T(8,128)(2,1)S(1)}, bf16[512,256]{1,0:T(8,128)(2,1)S(1)}, u32[]{:S(2)}, u32[]{:S(2)}) collective-permute-start(bf16[512,256]{1,0:T(8,128)(2,1)S(1)} %fusion), channel_id=1, source_target_pairs={{0,1},{1,0},{2,3},{3,2},{4,5},{5,4},{6,7},{7,6},{8,9},{9,8},{10,11... | collective-permute-start | bytes 786440 | tf_op jit(solution)/shard_map/ppermute | solution.py:137
  9.4 11.8 %collective-permute-start.4 = (bf16[504,256]{1,0:T(8,128)(2,1)S(1)}, bf16[504,256]{1,0:T(8,128)(2,1)S(1)}, u32[]{:S(2)}, u32[]{:S(2)}) collective-permute-start(bf16[504,256]{1,0:T(8,128)(2,1)S(1)} %fusion.2.refs_0_), channel_id=1, source_target_pairs={{0,8},{4,12},{8,0},{12,4},{16,24},{20,28},{24,16},{28,20},{1,9},{5... | collective-permute-start | bytes 774152 | tf_op jit(solution)/shard_map/ppermute | solution.py:149
  11.1 10.2 %collective-permute-start.6 = (bf16[504,256]{1,0:T(8,128)(2,1)S(1)}, bf16[504,256]{1,0:T(8,128)(2,1)S(1)}, u32[]{:S(2)}, u32[]{:S(2)}) collective-permute-start(bf16[504,256]{1,0:T(8,128)(2,1)S(1)} %fusion.2.refs_0_), channel_id=1, source_target_pairs={{0,16},{4,20},{8,24},{12,28},{16,0},{20,4},{24,8},{28,12},{1,17},{... | collective-permute-start | bytes 774152 | tf_op jit(solution)/shard_map/ppermute | solution.py:149
  13.3 19.0 %all-to-all-start = ((f32[4,6,504]{2,1,0:T(8,128)}), f32[4,6,504]{2,1,0:T(8,128)S(1)}, u32[]{:S(2)}, u32[]{:S(2)}) async-start(f32[4,6,504]{2,1,0:T(8,128)} %broadcast_in_dim.51), calls=%async_computation | async-start | bytes 131072 | tf_op jit(solution)/shard_map/all_to_all | solution.py:97
  21.2 13.5 %collective-permute-start.3 = (bf16[504,256]{1,0:T(8,128)(2,1)S(1)}, bf16[504,256]{1,0:T(8,128)(2,1)S(1)}, u32[]{:S(2)}, u32[]{:S(2)}) collective-permute-start(bf16[504,256]{1,0:T(8,128)(2,1)S(1)} %fusion.2.refs_0_), channel_id=1, source_target_pairs={{0,4},{4,0},{8,12},{12,8},{16,20},{20,16},{24,28},{28,24},{1,5},{5... | collective-permute-start | bytes 774152 | tf_op jit(solution)/shard_map/ppermute | solution.py:160
  21.4 11.7 %collective-permute-start.8 = (bf16[504,256]{1,0:T(8,128)(2,1)S(1)}, bf16[504,256]{1,0:T(8,128)(2,1)S(1)}, u32[]{:S(2)}, u32[]{:S(2)}) collective-permute-start(bf16[504,256]{1,0:T(8,128)(2,1)S(1)} %broadcast_select_fusion.3), channel_id=1, source_target_pairs={{0,16},{4,12},{8,24},{12,4},{16,0},{20,28},{24,8},{28,20},{1,17},{... | collective-permute-start | bytes 774152 | tf_op jit(solution)/shard_map/ppermute | solution.py:154
  32.5 2.2 collective-permute-start.5
  34.8 25.8 %collective-permute-start.10 = (bf16[2048,256]{1,0:T(8,128)(2,1)}, bf16[2048,256]{1,0:T(8,128)(2,1)}, u32[]{:S(2)}, u32[]{:S(2)}) collective-permute-start(bf16[2048,256]{1,0:T(8,128)(2,1)} %bitcast.7.refs_0_), channel_id=1, source_target_pairs={{0,8},{4,12},{8,0},{12,4},{16,24},{20,28},{24,16},{28,20},{1,9},{5... | collective-permute-start | bytes 3145736 | tf_op jit(solution)/shard_map/ppermute | solution.py:149
  36.3 25.5 %collective-permute-start.11 = (bf16[2048,256]{1,0:T(8,128)(2,1)}, bf16[2048,256]{1,0:T(8,128)(2,1)}, u32[]{:S(2)}, u32[]{:S(2)}) collective-permute-start(bf16[2048,256]{1,0:T(8,128)(2,1)} %bitcast.7.refs_0_), channel_id=1, source_target_pairs={{0,16},{4,20},{8,24},{12,28},{16,0},{20,4},{24,8},{28,12},{1,17},{... | collective-permute-start | bytes 3145736 | tf_op jit(solution)/shard_map/ppermute | solution.py:149
  63.2 33.3 %collective-permute-start.12 = (bf16[2048,256]{1,0:T(8,128)(2,1)S(1)}, bf16[2048,256]{1,0:T(8,128)(2,1)}, u32[]{:S(2)}, u32[]{:S(2)}) collective-permute-start(bf16[2048,256]{1,0:T(8,128)(2,1)S(1)} %broadcast_select_fusion.1), channel_id=1, source_target_pairs={{0,16},{4,12},{8,24},{12,4},{16,0},{20,28},{24,8},{28,20},{1,17},{... | collective-permute-start | bytes 3145736 | tf_op jit(solution)/shard_map/ppermute | solution.py:154
  64.8 16.3 %collective-permute-start.13 = (bf16[768,256]{1,0:T(8,128)(2,1)S(1)}, bf16[768,256]{1,0:T(8,128)(2,1)S(1)}, u32[]{:S(2)}, u32[]{:S(2)}) collective-permute-start(bf16[768,256]{1,0:T(8,128)(2,1)S(1)} %pad_maximum_fusion.7), channel_id=1, source_target_pairs={{0,1},{1,0},{2,3},{3,2},{4,5},{5,4},{6,7},{7,6},{8,9},{9,8},{10,11... | collective-permute-start | bytes 1179656 | tf_op jit(solution)/shard_map/ppermute | solution.py:137
  65.1 29.8 %collective-permute-start.14 = (bf16[768,256]{1,0:T(8,128)(2,1)S(1)}, bf16[768,256]{1,0:T(8,128)(2,1)S(1)}, u32[]{:S(2)}, u32[]{:S(2)}) collective-permute-start(bf16[768,256]{1,0:T(8,128)(2,1)S(1)} %pad_maximum_fusion.7), channel_id=1, source_target_pairs={{0,2},{1,3},{2,0},{3,1},{4,6},{5,7},{6,4},{7,5},{8,10},{9,11},{10,... | collective-permute-start | bytes 1179656 | tf_op jit(solution)/shard_map/ppermute | solution.py:137
  67.8 27.2 %collective-permute-start.15 = (bf16[768,256]{1,0:T(8,128)(2,1)S(1)}, bf16[768,256]{1,0:T(8,128)(2,1)S(1)}, u32[]{:S(2)}, u32[]{:S(2)}) collective-permute-start(bf16[768,256]{1,0:T(8,128)(2,1)S(1)} %pad_maximum_fusion.7), channel_id=1, source_target_pairs={{0,3},{1,2},{2,1},{3,0},{4,7},{5,6},{6,5},{7,4},{8,11},{9,10},{10,... | collective-permute-start | bytes 1179656 | tf_op jit(solution)/shard_map/ppermute | solution.py:137
  69.1 39.0 %collective-permute-start.16 = (bf16[2048,256]{1,0:T(8,128)(2,1)}, bf16[2048,256]{1,0:T(8,128)(2,1)}, u32[]{:S(2)}, u32[]{:S(2)}) collective-permute-start(bf16[2048,256]{1,0:T(8,128)(2,1)} %bitcast.7.refs_0_), channel_id=1, source_target_pairs={{0,4},{4,0},{8,12},{12,8},{16,20},{20,16},{24,28},{28,24},{1,5},{5... | collective-permute-start | bytes 3145736 | tf_op jit(solution)/shard_map/ppermute | solution.py:160
  96.5 42.3 %all-to-all-start.1 = ((bf16[4,392,512]{2,1,0:T(8,128)(2,1)}), bf16[4,392,512]{2,1,0:T(8,128)(2,1)S(1)}, u32[]{:S(2)}, u32[]{:S(2)}) async-start(bf16[4,392,512]{2,1,0:T(8,128)(2,1)} %get-tuple-element.215), calls=%async_computation.1 | async-start | bytes 3211264 | tf_op jit(solution)/shard_map/all_to_all | solution.py:133
  104.6 43.8 %collective-permute-start.20 = (bf16[3072,256]{1,0:T(8,128)(2,1)S(1)}, bf16[3072,256]{1,0:T(8,128)(2,1)}, u32[]{:S(2)}, u32[]{:S(2)}) collective-permute-start(bf16[3072,256]{1,0:T(8,128)(2,1)S(1)} %pad_maximum_fusion.3.refs_0_), channel_id=1, source_target_pairs={{0,8},{4,12},{8,0},{12,4},{16,24},{20,28},{24,16},{28,20},{1,9},{5... | collective-permute-start | bytes 4718600 | tf_op jit(solution)/shard_map/ppermute | solution.py:149
  106.1 42.3 %collective-permute-start.21 = (bf16[3072,256]{1,0:T(8,128)(2,1)S(1)}, bf16[3072,256]{1,0:T(8,128)(2,1)}, u32[]{:S(2)}, u32[]{:S(2)}) collective-permute-start(bf16[3072,256]{1,0:T(8,128)(2,1)S(1)} %pad_maximum_fusion.3.refs_0_), channel_id=1, source_target_pairs={{0,16},{4,20},{8,24},{12,28},{16,0},{20,4},{24,8},{28,12},{1,17},{... | collective-permute-start | bytes 4718600 | tf_op jit(solution)/shard_map/ppermute | solution.py:149
  107.7 3.0 collective-permute-start.17
  107.7 4.5 collective-permute-start.18
  108.2 5.5 collective-permute-start.19
  151.3 42.3 %collective-permute-start.22 = (bf16[3072,256]{1,0:T(8,128)(2,1)}, bf16[3072,256]{1,0:T(8,128)(2,1)}, u32[]{:S(2)}, u32[]{:S(2)}) collective-permute-start(bf16[3072,256]{1,0:T(8,128)(2,1)} %broadcast_select_fusion), channel_id=1, source_target_pairs={{0,16},{4,12},{8,24},{12,4},{16,0},{20,28},{24,8},{28,20},{1,17},{... | collective-permute-start | bytes 4718600 | tf_op jit(solution)/shard_map/ppermute | solution.py:154
  154.1 92.8 %collective-permute-start.26 = (bf16[3072,256]{1,0:T(8,128)(2,1)S(1)}, bf16[3072,256]{1,0:T(8,128)(2,1)S(1)}, u32[]{:S(2)}, u32[]{:S(2)}) collective-permute-start(bf16[3072,256]{1,0:T(8,128)(2,1)S(1)} %pad_maximum_fusion.3.refs_0_), channel_id=1, source_target_pairs={{0,4},{4,0},{8,12},{12,8},{16,20},{20,16},{24,28},{28,24},{1,5},{5... | collective-permute-start | bytes 4718600 | tf_op jit(solution)/shard_map/ppermute | solution.py:160
  156.1 17.8 %all-to-all-start.2 = ((f32[8,2,2048]{2,1,0:T(2,128)}), f32[8,2,2048]{2,1,0:T(2,128)S(1)}, u32[]{:S(2)}, u32[]{:S(2)}) async-start(f32[8,2,2048]{2,1,0:T(2,128)} %broadcast_in_dim.54), calls=%async_computation.2 | async-start | bytes 262144 | tf_op jit(solution)/shard_map/all_to_all | solution.py:97
  174.7 18.9 %all-to-all-start.3 = ((f32[4,2,2048]{2,1,0:T(2,128)}), f32[4,2,2048]{2,1,0:T(2,128)S(1)}, u32[]{:S(2)}, u32[]{:S(2)}) async-start(f32[4,2,2048]{2,1,0:T(2,128)} %broadcast_in_dim.55), calls=%async_computation.3 | async-start | bytes 131072 | tf_op jit(solution)/shard_map/all_to_all | solution.py:97
  188.2 58.8 %collective-permute-start.27 = (bf16[3072,256]{1,0:T(8,128)(2,1)}, bf16[3072,256]{1,0:T(8,128)(2,1)}, u32[]{:S(2)}, u32[]{:S(2)}) collective-permute-start(bf16[3072,256]{1,0:T(8,128)(2,1)} %collective-permute-done.20.refs_2_), channel_id=1, source_target_pairs={{0,4},{4,0},{8,12},{12,8},{16,20},{20,16},{24,28},{28,24},{1,5},{5... | collective-permute-start | bytes 4718600 | tf_op jit(solution)/shard_map/ppermute | solution.py:160
  188.2 58.7 %collective-permute-start.28 = (bf16[3072,256]{1,0:T(8,128)(2,1)}, bf16[3072,256]{1,0:T(8,128)(2,1)}, u32[]{:S(2)}, u32[]{:S(2)}) collective-permute-start(bf16[3072,256]{1,0:T(8,128)(2,1)} %collective-permute-done.21.refs_4_), channel_id=1, source_target_pairs={{0,4},{4,0},{8,12},{12,8},{16,20},{20,16},{24,28},{28,24},{1,5},{5... | collective-permute-start | bytes 4718600 | tf_op jit(solution)/shard_map/ppermute | solution.py:160
  193.6 53.3 %collective-permute-start.29 = (bf16[3072,256]{1,0:T(8,128)(2,1)}, bf16[3072,256]{1,0:T(8,128)(2,1)}, u32[]{:S(2)}, u32[]{:S(2)}) collective-permute-start(bf16[3072,256]{1,0:T(8,128)(2,1)} %collective-permute-done.22.refs_6_), channel_id=1, source_target_pairs={{0,4},{4,0},{8,12},{12,8},{16,20},{20,16},{24,28},{28,24},{1,5},{5... | collective-permute-start | bytes 4718600 | tf_op jit(solution)/shard_map/ppermute | solution.py:160
  193.7 7.3 %collective-permute-start.23 = (bf16[208,256]{1,0:T(8,128)(2,1)S(1)}, bf16[208,256]{1,0:T(8,128)(2,1)S(1)}, u32[]{:S(2)}, u32[]{:S(2)}) collective-permute-start(bf16[208,256]{1,0:T(8,128)(2,1)S(1)} %fusion.4), channel_id=1, source_target_pairs={{0,3},{1,2},{2,1},{3,0},{4,7},{5,6},{6,5},{7,4},{8,11},{9,10},{10,... | collective-permute-start | bytes 319496 | tf_op jit(solution)/shard_map/ppermute | solution.py:137
  201.0 7.7 %collective-permute-start.24 = (bf16[208,256]{1,0:T(8,128)(2,1)S(1)}, bf16[208,256]{1,0:T(8,128)(2,1)S(1)}, u32[]{:S(2)}, u32[]{:S(2)}) collective-permute-start(bf16[208,256]{1,0:T(8,128)(2,1)S(1)} %fusion.4), channel_id=1, source_target_pairs={{0,2},{1,3},{2,0},{3,1},{4,6},{5,7},{6,4},{7,5},{8,10},{9,11},{10,... | collective-permute-start | bytes 319496 | tf_op jit(solution)/shard_map/ppermute | solution.py:137
  208.6 14.6 %collective-permute-start.25 = (bf16[208,256]{1,0:T(8,128)(2,1)S(1)}, bf16[208,256]{1,0:T(8,128)(2,1)S(1)}, u32[]{:S(2)}, u32[]{:S(2)}) collective-permute-start(bf16[208,256]{1,0:T(8,128)(2,1)S(1)} %fusion.4), channel_id=1, source_target_pairs={{0,1},{1,0},{2,3},{3,2},{4,5},{5,4},{6,7},{7,6},{8,9},{9,8},{10,11... | collective-permute-start | bytes 319496 | tf_op jit(solution)/shard_map/ppermute | solution.py:137
  235.1 11.8 %all-to-all-start.5 = ((f32[4,2,2048]{2,1,0:T(2,128)}), f32[4,2,2048]{2,1,0:T(2,128)S(1)}, u32[]{:S(2)}, u32[]{:S(2)}) async-start(f32[4,2,2048]{2,1,0:T(2,128)} %broadcast_in_dim.58), calls=%async_computation.5 | async-start | bytes 131072 | tf_op jit(solution)/shard_map/all_to_all | solution.py:97
  257.0 11.4 %collective-permute-start.30 = (bf16[832,256]{1,0:T(8,128)(2,1)S(1)}, bf16[832,256]{1,0:T(8,128)(2,1)S(1)}, u32[]{:S(2)}, u32[]{:S(2)}) collective-permute-start(bf16[832,256]{1,0:T(8,128)(2,1)S(1)} %bitcast.101), channel_id=1, source_target_pairs={{0,8},{4,12},{8,0},{12,4},{16,24},{20,28},{24,16},{28,20},{1,9},{5... | collective-permute-start | bytes 1277960 | tf_op jit(solution)/shard_map/ppermute | solution.py:149
  257.6 11.2 %collective-permute-start.31 = (bf16[832,256]{1,0:T(8,128)(2,1)S(1)}, bf16[832,256]{1,0:T(8,128)(2,1)S(1)}, u32[]{:S(2)}, u32[]{:S(2)}) collective-permute-start(bf16[832,256]{1,0:T(8,128)(2,1)S(1)} %bitcast.102), channel_id=1, source_target_pairs={{0,16},{4,20},{8,24},{12,28},{16,0},{20,4},{24,8},{28,12},{1,17},{... | collective-permute-start | bytes 1277960 | tf_op jit(solution)/shard_map/ppermute | solution.py:149
  269.9 20.2 %collective-permute-start.32 = (bf16[832,256]{1,0:T(8,128)(2,1)}, bf16[832,256]{1,0:T(8,128)(2,1)}, u32[]{:S(2)}, u32[]{:S(2)}) collective-permute-start(bf16[832,256]{1,0:T(8,128)(2,1)} %broadcast_select_fusion.2), channel_id=1, source_target_pairs={{0,16},{4,12},{8,24},{12,4},{16,0},{20,28},{24,8},{28,20},{1,17},{... | collective-permute-start | bytes 1277960 | tf_op jit(solution)/shard_map/ppermute | solution.py:154
  307.1 43.0 %all-to-all-start.9 = ((bf16[4,392,512]{2,1,0:T(8,128)(2,1)}), bf16[4,392,512]{2,1,0:T(8,128)(2,1)}, u32[]{:S(2)}, u32[]{:S(2)}) async-start(bf16[4,392,512]{2,1,0:T(8,128)(2,1)} %get-tuple-element.250), calls=%async_computation.9 | async-start | bytes 3211264 | tf_op jit(solution)/shard_map/all_to_all | solution.py:133
  311.9 2.3 collective-permute-start.34
  312.1 2.8 collective-permute-start.35
  312.5 3.1 collective-permute-start.36
  385.3 11.4 %collective-permute-start.37 = (bf16[4,4,512,256]{3,2,1,0:T(8,128)(2,1)}, bf16[4,4,512,256]{3,2,1,0:T(8,128)(2,1)S(1)}, u32[]{:S(2)}, u32[]{:S(2)}) collective-permute-start(bf16[4,4,512,256]{3,2,1,0:T(8,128)(2,1)} %get-tuple-element.256), channel_id=1, source_target_pairs={{0,4},{4,0},{8,12},{12,8},{16,20},{20,16},{24,28},{28,24},{1,5},{5... | collective-permute-start | bytes 12582920 | tf_op jit(solution)/shard_map/ppermute | solution.py:177
  401.0 14.9 %collective-permute-start.38 = (bf16[4,512,256]{2,1,0:T(8,128)(2,1)S(1)}, bf16[4,512,256]{2,1,0:T(8,128)(2,1)S(1)}, u32[]{:S(2)}, u32[]{:S(2)}) collective-permute-start(bf16[4,512,256]{2,1,0:T(8,128)(2,1)S(1)} %twin_sums.6), channel_id=1, source_target_pairs={{0,16},{4,12},{8,24},{12,4},{16,0},{20,28},{24,8},{28,20},{1,17},{... | collective-permute-start | bytes 3145736 | tf_op jit(solution)/shard_map/ppermute | solution.py:171
  433.0 41.4 %all-to-all-start.14 = ((bf16[4,392,512]{2,1,0:T(8,128)(2,1)}), bf16[4,392,512]{2,1,0:T(8,128)(2,1)}, u32[]{:S(2)}, u32[]{:S(2)}) async-start(bf16[4,392,512]{2,1,0:T(8,128)(2,1)} %copy-done.32), calls=%async_computation.14 | async-start | bytes 3211264 | tf_op jit(solution)/shard_map/all_to_all | solution.py:133
  443.2 25.5 %collective-permute-start.39 = (bf16[4,512,256]{2,1,0:T(8,128)(2,1)S(1)}, bf16[4,512,256]{2,1,0:T(8,128)(2,1)S(1)}, u32[]{:S(2)}, u32[]{:S(2)}) collective-permute-start(bf16[4,512,256]{2,1,0:T(8,128)(2,1)S(1)} %get-tuple-element.272), channel_id=1, source_target_pairs={{0,8},{4,12},{8,0},{12,4},{16,24},{20,28},{24,16},{28,20},{1,9},{5... | collective-permute-start | bytes 3145736 | tf_op jit(solution)/shard_map/ppermute | solution.py:181
  443.9 25.9 %collective-permute-start.40 = (bf16[4,512,256]{2,1,0:T(8,128)(2,1)S(1)}, bf16[4,512,256]{2,1,0:T(8,128)(2,1)S(1)}, u32[]{:S(2)}, u32[]{:S(2)}) collective-permute-start(bf16[4,512,256]{2,1,0:T(8,128)(2,1)S(1)} %get-tuple-element.273), channel_id=1, source_target_pairs={{0,16},{4,20},{8,24},{12,28},{16,0},{20,4},{24,8},{28,12},{1,17},{... | collective-permute-start | bytes 3145736 | tf_op jit(solution)/shard_map/ppermute | solution.py:181
  474.4 9.9 %collective-permute-start.44 = (bf16[4,1,504,256]{3,2,1,0:T(8,128)(2,1)}, bf16[4,1,504,256]{3,2,1,0:T(8,128)(2,1)S(1)}, u32[]{:S(2)}, u32[]{:S(2)}) collective-permute-start(bf16[4,1,504,256]{3,2,1,0:T(8,128)(2,1)} %copy-done.105), channel_id=1, source_target_pairs={{0,4},{4,0},{8,12},{12,8},{16,20},{20,16},{24,28},{28,24},{1,5},{5... | collective-permute-start | bytes 3096584 | tf_op jit(solution)/shard_map/ppermute | solution.py:177
  480.0 18.2 %collective-permute-start.41 = (bf16[512,256]{1,0:T(8,128)(2,1)}, bf16[512,256]{1,0:T(8,128)(2,1)}, u32[]{:S(2)}, u32[]{:S(2)}) collective-permute-start(bf16[512,256]{1,0:T(8,128)(2,1)} %get-tuple-element.282), channel_id=1, source_target_pairs={{0,1},{1,0},{2,3},{3,2},{4,5},{5,4},{6,7},{7,6},{8,9},{9,8},{10,11... | collective-permute-start | bytes 786440 | tf_op jit(solution)/shard_map/ppermute | solution.py:185
  480.0 21.6 %collective-permute-start.42 = (bf16[512,256]{1,0:T(8,128)(2,1)}, bf16[512,256]{1,0:T(8,128)(2,1)}, u32[]{:S(2)}, u32[]{:S(2)}) collective-permute-start(bf16[512,256]{1,0:T(8,128)(2,1)} %get-tuple-element.283), channel_id=1, source_target_pairs={{0,2},{1,3},{2,0},{3,1},{4,6},{5,7},{6,4},{7,5},{8,10},{9,11},{10,... | collective-permute-start | bytes 786440 | tf_op jit(solution)/shard_map/ppermute | solution.py:185
  482.0 19.6 %collective-permute-start.43 = (bf16[512,256]{1,0:T(8,128)(2,1)}, bf16[512,256]{1,0:T(8,128)(2,1)}, u32[]{:S(2)}, u32[]{:S(2)}) collective-permute-start(bf16[512,256]{1,0:T(8,128)(2,1)} %get-tuple-element.284), channel_id=1, source_target_pairs={{0,3},{1,2},{2,1},{3,0},{4,7},{5,6},{6,5},{7,4},{8,11},{9,10},{10,... | collective-permute-start | bytes 786440 | tf_op jit(solution)/shard_map/ppermute | solution.py:185
  486.1 10.9 %collective-permute-start.45 = (bf16[1,504,256]{2,1,0:T(8,128)(2,1)}, bf16[1,504,256]{2,1,0:T(8,128)(2,1)}, u32[]{:S(2)}, u32[]{:S(2)}) collective-permute-start(bf16[1,504,256]{2,1,0:T(8,128)(2,1)} %twin_sums.9), channel_id=1, source_target_pairs={{0,16},{4,12},{8,24},{12,4},{16,0},{20,28},{24,8},{28,20},{1,17},{... | collective-permute-start | bytes 774152 | tf_op jit(solution)/shard_map/ppermute | solution.py:171
  502.2 12.8 %all-to-all-start.16 = ((f32[4,2,2048]{2,1,0:T(2,128)}), f32[4,2,2048]{2,1,0:T(2,128)S(1)}, u32[]{:S(2)}, u32[]{:S(2)}) async-start(f32[4,2,2048]{2,1,0:T(2,128)} %broadcast_in_dim.67), calls=%async_computation.16 | async-start | bytes 131072 | tf_op jit(solution)/shard_map/all_to_all | solution.py:97
  509.3 11.4 %collective-permute-start.46 = (bf16[1,504,256]{2,1,0:T(8,128)(2,1)S(1)}, bf16[1,504,256]{2,1,0:T(8,128)(2,1)S(1)}, u32[]{:S(2)}, u32[]{:S(2)}) collective-permute-start(bf16[1,504,256]{2,1,0:T(8,128)(2,1)S(1)} %get-tuple-element.292), channel_id=1, source_target_pairs={{0,8},{4,12},{8,0},{12,4},{16,24},{20,28},{24,16},{28,20},{1,9},{5... | collective-permute-start | bytes 774152 | tf_op jit(solution)/shard_map/ppermute | solution.py:181
  510.0 10.7 %collective-permute-start.47 = (bf16[1,504,256]{2,1,0:T(8,128)(2,1)S(1)}, bf16[1,504,256]{2,1,0:T(8,128)(2,1)S(1)}, u32[]{:S(2)}, u32[]{:S(2)}) collective-permute-start(bf16[1,504,256]{2,1,0:T(8,128)(2,1)S(1)} %get-tuple-element.293), channel_id=1, source_target_pairs={{0,16},{4,20},{8,24},{12,28},{16,0},{20,4},{24,8},{28,12},{1,17},{... | collective-permute-start | bytes 774152 | tf_op jit(solution)/shard_map/ppermute | solution.py:181
  527.5 22.9 %collective-permute-start.48 = (bf16[4,4,512,256]{3,2,1,0:T(8,128)(2,1)}, bf16[4,4,512,256]{3,2,1,0:T(8,128)(2,1)}, u32[]{:S(2)}, u32[]{:S(2)}) collective-permute-start(bf16[4,4,512,256]{3,2,1,0:T(8,128)(2,1)} %get-tuple-element.300), channel_id=1, source_target_pairs={{0,4},{4,0},{8,12},{12,8},{16,20},{20,16},{24,28},{28,24},{1,5},{5... | collective-permute-start | bytes 12582920 | tf_op jit(solution)/shard_map/ppermute | solution.py:177
  528.7 37.8 %all-to-all-start.17 = ((bf16[32,2,5120]{2,1,0:T(2,128)(2,1)}), bf16[32,2,5120]{2,1,0:T(2,128)(2,1)S(1)}, u32[]{:S(2)}, u32[]{:S(2)}) async-start(bf16[32,2,5120]{2,1,0:T(2,128)(2,1)} %broadcast_in_dim.68), calls=%async_computation.17 | async-start | bytes 1310720 | tf_op jit(solution)/shard_map/all_to_all | solution.py:112
  531.6 18.7 %collective-permute-start.49 = (bf16[504,256]{1,0:T(8,128)(2,1)S(1)}, bf16[504,256]{1,0:T(8,128)(2,1)S(1)}, u32[]{:S(2)}, u32[]{:S(2)}) collective-permute-start(bf16[504,256]{1,0:T(8,128)(2,1)S(1)} %convert_element_type.65), channel_id=1, source_target_pairs={{0,1},{1,0},{2,3},{3,2},{4,5},{5,4},{6,7},{7,6},{8,9},{9,8},{10,11... | collective-permute-start | bytes 774152 | tf_op jit(solution)/shard_map/ppermute | solution.py:1687
  550.4 15.4 %collective-permute-start.50 = (bf16[504,256]{1,0:T(8,128)(2,1)S(1)}, bf16[504,256]{1,0:T(8,128)(2,1)S(1)}, u32[]{:S(2)}, u32[]{:S(2)}) collective-permute-start(bf16[504,256]{1,0:T(8,128)(2,1)S(1)} %convert_add_fusion), channel_id=1, source_target_pairs={{0,2},{1,3},{2,0},{3,1},{4,6},{5,7},{6,4},{7,5},{8,10},{9,11},{10,... | collective-permute-start | bytes 774152 | tf_op jit(solution)/shard_map/ppermute | solution.py:1693
  566.5 49.3 %all-to-all-start.18 = ((bf16[4,392,512]{2,1,0:T(8,128)(2,1)}), bf16[4,392,512]{2,1,0:T(8,128)(2,1)S(1)}, u32[]{:S(2)}, u32[]{:S(2)}) async-start(bf16[4,392,512]{2,1,0:T(8,128)(2,1)} %mix_back.3), calls=%async_computation.18 | async-start | bytes 3211264 | tf_op jit(solution)/shard_map/all_to_all | solution.py:133
  574.4 14.9 %collective-permute-start.51 = (bf16[4,512,256]{2,1,0:T(8,128)(2,1)S(1)}, bf16[4,512,256]{2,1,0:T(8,128)(2,1)S(1)}, u32[]{:S(2)}, u32[]{:S(2)}) collective-permute-start(bf16[4,512,256]{2,1,0:T(8,128)(2,1)S(1)} %twin_sums.11), channel_id=1, source_target_pairs={{0,16},{4,12},{8,24},{12,4},{16,0},{20,28},{24,8},{28,20},{1,17},{... | collective-permute-start | bytes 3145736 | tf_op jit(solution)/shard_map/ppermute | solution.py:171
  590.0 23.6 %collective-permute-start.52 = (bf16[4,512,256]{2,1,0:T(8,128)(2,1)S(1)}, bf16[4,512,256]{2,1,0:T(8,128)(2,1)S(1)}, u32[]{:S(2)}, u32[]{:S(2)}) collective-permute-start(bf16[4,512,256]{2,1,0:T(8,128)(2,1)S(1)} %get-tuple-element.315), channel_id=1, source_target_pairs={{0,8},{4,12},{8,0},{12,4},{16,24},{20,28},{24,16},{28,20},{1,9},{5... | collective-permute-start | bytes 3145736 | tf_op jit(solution)/shard_map/ppermute | solution.py:181
  591.6 23.3 %collective-permute-start.53 = (bf16[4,512,256]{2,1,0:T(8,128)(2,1)S(1)}, bf16[4,512,256]{2,1,0:T(8,128)(2,1)S(1)}, u32[]{:S(2)}, u32[]{:S(2)}) collective-permute-start(bf16[4,512,256]{2,1,0:T(8,128)(2,1)S(1)} %get-tuple-element.316), channel_id=1, source_target_pairs={{0,16},{4,20},{8,24},{12,28},{16,0},{20,4},{24,8},{28,12},{1,17},{... | collective-permute-start | bytes 3145736 | tf_op jit(solution)/shard_map/ppermute | solution.py:181
  618.7 16.6 %collective-permute-start.54 = (bf16[512,256]{1,0:T(8,128)(2,1)S(1)}, bf16[512,256]{1,0:T(8,128)(2,1)S(1)}, u32[]{:S(2)}, u32[]{:S(2)}) collective-permute-start(bf16[512,256]{1,0:T(8,128)(2,1)S(1)} %get-tuple-element.334), channel_id=1, source_target_pairs={{0,1},{1,0},{2,3},{3,2},{4,5},{5,4},{6,7},{7,6},{8,9},{9,8},{10,11... | collective-permute-start | bytes 786440 | tf_op jit(solution)/shard_map/ppermute | solution.py:185
  620.4 20.0 %collective-permute-start.55 = (bf16[512,256]{1,0:T(8,128)(2,1)S(1)}, bf16[512,256]{1,0:T(8,128)(2,1)S(1)}, u32[]{:S(2)}, u32[]{:S(2)}) collective-permute-start(bf16[512,256]{1,0:T(8,128)(2,1)S(1)} %get-tuple-element.335), channel_id=1, source_target_pairs={{0,2},{1,3},{2,0},{3,1},{4,6},{5,7},{6,4},{7,5},{8,10},{9,11},{10,... | collective-permute-start | bytes 786440 | tf_op jit(solution)/shard_map/ppermute | solution.py:185
  622.9 17.6 %collective-permute-start.56 = (bf16[512,256]{1,0:T(8,128)(2,1)S(1)}, bf16[512,256]{1,0:T(8,128)(2,1)S(1)}, u32[]{:S(2)}, u32[]{:S(2)}) collective-permute-start(bf16[512,256]{1,0:T(8,128)(2,1)S(1)} %get-tuple-element.336), channel_id=1, source_target_pairs={{0,3},{1,2},{2,1},{3,0},{4,7},{5,6},{6,5},{7,4},{8,11},{9,10},{10,... | collective-permute-start | bytes 786440 | tf_op jit(solution)/shard_map/ppermute | solution.py:185
  (123 other events, 800.4 us)
where the time goes:
time: 683 us; the launch traced here: 678 us
  Pallas kernels  197 us (29%)
  waiting for transfers between devices  177 us (26%)
  starting transfers between devices  109 us (16%)
  blocking collectives  101 us (15%)
  local copies, waits for them, and re-layouts  76 us (11%)
  other arithmetic  15.6 us (2%)
    all_to_all x10, blocking collectives, spread(): lax.all_to_all(jnp.broadcast_to(v[None], (n,) + v.shape), axis, split_axi...  89.4 us
    unnamed x241, local copies, waits for them, and re-layouts  65.1 us
    ppermute x9, waiting for transfers between devices, parts_mp(): lax.ppermute(v, 'mp', flips('mp', k))  38.6 us
    all_to_all x4, waiting for transfers between devices, exchange(): return lax.all_to_all(blocks, 'mp', split_axis=0, concat_axis=0, tiled=True)  32.4 us
    all_to_all x5, starting transfers between devices, spread(): lax.all_to_all(jnp.broadcast_to(v[None], (n,) + v.shape), axis, split_axi...  32.4 us
    all_to_all x5, waiting for transfers between devices, spread(): lax.all_to_all(jnp.broadcast_to(v[None], (n,) + v.shape), axis, split_axi...  32.2 us
    pallas_call x1, Pallas kernels, head(): pl.pallas_call(functools.partial(head_kernel, width), in_specs=[SCALAR, p...  24.3 us
    pallas_call x2, Pallas kernels, mix_back(): pl.pallas_call(functools.partial(mix_back_kernel, len(more)), in_specs=[S...  24.2 us
  transfers between devices with their start and end apart: 67, of which 30 were waited for; matrix products, arithmetic and copies ran while one was open for 3% of the time, Pallas kernels for 22%

commit v1 on v0

--- a/solution.py
+++ b/solution.py
@@ -28,7 +28,7 @@
 SE_PART = 63
 SE_LANES = 64
 PITCH = 16
-VMEM_BYTES = 48 * 1024 * 1024
+VMEM_BYTES = 60 * 1024 * 1024
 f32 = jnp.float32
 bf16 = jnp.bfloat16
 NN = (((1,), (0,)), ((), ()))
@@ -97,6 +97,15 @@
     return lax.all_to_all(
         jnp.broadcast_to(v[None], (n,) + v.shape), axis, split_axis=0, concat_axis=0, tiled=True
     )
+
+
+def sum_axis(v, axis):
+    n = lax.axis_size(axis)
+    bit = 1
+    while bit < n:
+        v = v + lax.ppermute(v, axis, flips(axis, bit))
+        bit *= 2
+    return v
 
 
 def total(v):
@@ -167,10 +176,7 @@
 
 
 def scatter_corner(kept, got):
-    (last,) = twin_sums(kept, got, (3,))
-    corner = lax.ppermute(last, "dp", diagonal(8))
-    own, across, up = twin_sums(kept, got, (0, 1, 2))
-    return (own, across, up), corner
+    return lax.ppermute(twin_sum(kept, got), "dp", diagonal(8))
 
 
 def from_twin(sent):
@@ -212,10 +218,12 @@
     return full.reshape(rows, n, -1).transpose(1, 0, 2)
 
 
-def out_channels(blocks, channels, dtype):
-    if quick_mesh():
-        blocks = join_rows(blocks, dtype)
+def natural_channels(blocks, channels, dtype):
     return blocks.astype(dtype).reshape(-1, channels).T
+
+
+def out_channels(parts, channels, dtype, me):
+    return natural_channels(join_rows(parts, dtype, me), channels, dtype)
 
 
 def shard_square(w):
@@ -253,7 +261,6 @@
 
 
 SE_ROWS = 256
-SE_OFFSET = QUADS * LANES
 HEAD_ROWS = 208
 PROTO_ROWS = 96
 QUEUE_ROWS = 32
@@ -333,21 +340,24 @@
     return pl.ds(pl.multiple_of(index * 256, 256), 256)
 
 
-def join_rows_kernel(blocks_ref, out_ref):
-    for j in range(QUADS):
-        v = blocks_ref[j].astype(f32)
+def join_rows_kernel(me_ref, *refs):
+    out_ref = refs[-1]
+    for k, part in enumerate(refs[:-1]):
+        v = part[...].astype(f32)
         v = jnp.concatenate([v[:, :HALF], v[:, HALF + GAP :]], 1)
-        out_ref[j] = v.astype(out_ref.dtype)
-
-
-def join_rows(blocks, dtype):
+        out_ref[me_ref[0] ^ k] = v.astype(out_ref.dtype)
+
+
+def join_rows(parts, dtype, me):
+    rows = parts[0].shape[0]
     return pl.pallas_call(
         join_rows_kernel,
-        out_shape=jax.ShapeDtypeStruct(blocks.shape[:2] + (QUAD,), dtype),
+        in_specs=[SCALAR] + [pl.BlockSpec(memory_space=pltpu.VMEM)] * len(parts),
+        out_shape=jax.ShapeDtypeStruct((len(parts), rows, QUAD), dtype),
         compiler_params=params(),
         cost_estimate=BRIEF,
         name="join_rows",
-    )(blocks)
+    )(me, *parts)
 
 
 def piece_list(w):
@@ -397,15 +407,18 @@
 
     for b in range(8):
         copy(b).start()
-    for b in range(8):
-        index = me_ref[0] ^ b
+    for b in range(0, 8, 2):
         copy(b).wait()
-        acc = dot(g_ref[...], hold_ref[b])
-        if rest:
-            acc = acc + refs[8][:, half_block(index)]
-            out_ref[index // 2, :, half_block(index % 2)] = acc.astype(bf16)
-        else:
-            out_ref[:, half_block(index)] = acc
+        copy(b + 1).wait()
+        pair = dot(g_ref[...], jnp.concatenate([hold_ref[b], hold_ref[b + 1]], 1))
+        for i in range(2):
+            index = me_ref[0] ^ (b + i)
+            acc = pair[:, 256 * i : 256 * (i + 1)]
+            if rest:
+                acc = acc + refs[8][:, half_block(index)]
+                out_ref[index // 2, :, half_block(index % 2)] = acc.astype(bf16)
+            else:
+                out_ref[:, half_block(index)] = acc
 
 
 def mix_back(g, w, rest=None):
@@ -431,103 +444,155 @@
     )(index_scalar("dp"), g, *piece_list(w), *more)
 
 
-def weight_grad_kernel(me_ref, x_ref, g_ref, kept_ref, sent_ref):
-    turned = g_ref[...].T
-    for odd, out_ref in ((1, sent_ref), (0, kept_ref)):
-        wanted = jnp.concatenate(
-            [half_of(x_ref, me_ref[0] ^ (2 * i + odd)) for i in range(4)], 1
-        )
-        result = dot(turned, wanted)
-        for i in range(4):
-            out_ref[i, 0] = result[:, 256 * i : 256 * (i + 1)].astype(bf16)
-
-
-def weight_grad(x, g):
-    rows, width = g.shape
-    return pl.pallas_call(
-        weight_grad_kernel,
+def piece_grads(me_ref, x_ref, g, odd, out_ref):
+    wanted = jnp.concatenate([half_of(x_ref, me_ref[0] ^ (2 * i + odd)) for i in range(4)], 1)
+    result = dot(g.T, wanted)
+    for i in range(4):
+        out_ref[i, 0] = result[:, 256 * i : 256 * (i + 1)].astype(bf16)
+
+
+def sent_grads_kernel(
+    k, sloped, count, me_ref, x_ref, g_ref, a_ref, sums_ref, norms_ref, grad_sums_ref, grad_ref, out_ref
+):
+    grad, values = g_ref[...].astype(f32), a_ref[...]
+    if sloped:
+        _, _, scale, shift = affine(sums_ref[...], norms_ref[...], k, count)
+        grad = grad * swish_slope(values * scale + shift)
+    grad = norm_back(
+        grad, values, sums_ref[...], norms_ref[...], k, grad_sums_ref[...], count
+    ).astype(bf16)
+    grad_ref[...] = grad
+    piece_grads(me_ref, x_ref, grad, 1, out_ref)
+
+
+PIECES = jax.ShapeDtypeStruct((4, QUADS, LANES, 256), bf16)
+
+
+def pieces_spec():
+    return pl.BlockSpec((4, 1, LANES, 256), lambda m: (0, m, 0, 0))
+
+
+def sent_grads(x, g, a, sums, norms, k, grad_sums, count, sloped):
+    rows, width = a.shape
+    return pl.pallas_call(
+        functools.partial(sent_grads_kernel, k, sloped, count),
         grid=(QUADS,),
         in_specs=[
-            SCALAR,
-            pl.BlockSpec(x.shape, lambda m: (0, 0, 0)),
-            pl.BlockSpec((rows, LANES), lambda m: (0, m)),
-        ],
-        out_specs=[pl.BlockSpec((4, 1, LANES, 256), lambda m: (0, m, 0, 0))] * 2,
-        out_shape=[jax.ShapeDtypeStruct((4, QUADS, LANES, 256), bf16)] * 2,
-        compiler_params=params(),
-        cost_estimate=BRIEF,
-        name="weight_grad",
+            SCALAR, pl.BlockSpec(x.shape, lambda m: (0, 0, 0)), quad_spec(rows), quad_spec(rows),
+            quad_spec(2), quad_spec(6), quad_spec(2),
+        ],
+        out_specs=[quad_spec(rows), pieces_spec()],
+        out_shape=[jax.ShapeDtypeStruct((rows, width), bf16), PIECES],
+        compiler_params=params(),
+        cost_estimate=BRIEF,
+        name="sent_grads",
+    )(index_scalar("dp"), x, g, a, sums, norms, grad_sums)
+
+
+def kept_grads_kernel(me_ref, x_ref, g_ref, out_ref):
+    piece_grads(me_ref, x_ref, g_ref[...], 0, out_ref)
+
+
+def kept_grads(x, g):
+    rows, width = g.shape
+    return pl.pallas_call(
+        kept_grads_kernel,
+        grid=(QUADS,),
+        in_specs=[SCALAR, pl.BlockSpec(x.shape, lambda m: (0, 0, 0)), quad_spec(rows)],
+        out_specs=pieces_spec(),
+        out_shape=PIECES,
+        compiler_params=params(),
+        cost_estimate=BRIEF,
+        name="kept_grads",
     )(index_scalar("dp"), x, g)
 
 
-def twin_sums_kernel(count, *refs):
-    for i in range(count):
-        refs[2 * count + i][...] = (
-            refs[i][...].astype(f32) + refs[count + i][...].astype(f32)
-        ).astype(bf16)
-
-
-def twin_sums(kept, got, picks):
-    shape = kept.shape[1:]
-    specs = [
-        pl.BlockSpec((None, 1) + shape[1:], lambda m, i=i: (i, m, 0, 0)) for i in picks
-    ]
-    return pl.pallas_call(
-        functools.partial(twin_sums_kernel, len(picks)),
-        grid=shape[:1],
-        in_specs=specs * 2,
-        out_specs=[pl.BlockSpec((1,) + shape[1:], lambda m: (m, 0, 0))] * len(picks),
-        out_shape=[jax.ShapeDtypeStruct(shape, bf16)] * len(picks),
-        compiler_params=params(),
-        cost_estimate=BRIEF,
-        name="twin_sums",
-    )(*([kept] * len(picks) + [got] * len(picks)))
-
-
-def corner_sums_kernel(me_ref, across_ref, up_ref, corner_ref, across_out, up_out):
+def entry_spec(shape, i, steps):
+    return pl.BlockSpec((None, shape[1] // steps) + shape[2:], lambda m, i=i: (i, m, 0, 0))
+
+
+def twin_sum_kernel(a_ref, b_ref, out_ref):
+    out_ref[...] = (a_ref[...].astype(f32) + b_ref[...].astype(f32)).astype(bf16)
+
+
+def twin_sum(kept, got):
+    shape = kept.shape
+    steps = min(2, shape[1])
+    return pl.pallas_call(
+        twin_sum_kernel,
+        grid=(steps,),
+        in_specs=[entry_spec(shape, 3, steps)] * 2,
+        out_specs=pl.BlockSpec((shape[1] // steps,) + shape[2:], lambda m: (m, 0, 0)),
+        out_shape=jax.ShapeDtypeStruct(shape[1:], bf16),
+        compiler_params=params(),
+        cost_estimate=BRIEF,
+        name="twin_sum",
+    )(kept, got)
+
+
+def corner_sums_kernel(me_ref, a1_ref, b1_ref, a2_ref, b2_ref, corner_ref, across_ref, up_ref):
     even = me_ref[0] % 2 == 0
     corner = corner_ref[...].astype(f32)
-    across_out[...] = (across_ref[...].astype(f32) + jnp.where(even, corner, 0.0)).astype(bf16)
-    up_out[...] = (up_ref[...].astype(f32) + jnp.where(even, 0.0, corner)).astype(bf16)
-
-
-def corner_sums(across, up, corner):
-    block = pl.BlockSpec((1,) + across.shape[1:], lambda m: (m, 0, 0))
+    across = a1_ref[...].astype(f32) + b1_ref[...].astype(f32)
+    across_ref[...] = (across + jnp.where(even, corner, 0.0)).astype(bf16)
+    up = a2_ref[...].astype(f32) + b2_ref[...].astype(f32)
+    up_ref[...] = (up + jnp.where(even, 0.0, corner)).astype(bf16)
+
+
+def corner_sums(kept, got, corner):
+    shape = kept.shape
+    steps = min(2, shape[1])
+    block = pl.BlockSpec((shape[1] // steps,) + shape[2:], lambda m: (m, 0, 0))
     return pl.pallas_call(
         corner_sums_kernel,
-        grid=across.shape[:1],
-        in_specs=[SCALAR, block, block, block],
+        grid=(steps,),
+        in_specs=[SCALAR] + [entry_spec(shape, i, steps) for i in (1, 1, 2, 2)] + [block],
         out_specs=[block, block],
-        out_shape=[jax.ShapeDtypeStruct(across.shape, bf16)] * 2,
+        out_shape=[jax.ShapeDtypeStruct(shape[1:], bf16)] * 2,
         compiler_params=params(),
         cost_estimate=BRIEF,
         name="corner_sums",
-    )(index_scalar("dp"), across, up, corner)
-
-
-def side_sums_kernel(me_ref, own_ref, across_ref, up_ref, out_ref, *parts):
-    for k in range(len(parts) + 1):
-        j = me_ref[0] ^ k
-        value = (
-            own_ref[j].astype(f32) + across_ref[j].astype(f32) + up_ref[j].astype(f32)
-        )
-        if k:
-            parts[k - 1][...] = value.astype(bf16)
-        else:
-            out_ref[...] = value
-
-
-def side_sums(own, across, up):
-    n, *shape = own.shape
+    )(index_scalar("dp"), kept, got, kept, got, corner)
+
+
+def side_sums_kernel(me_ref, a_ref, b_ref, across_ref, up_ref, out_ref, *parts):
+    value = (
+        a_ref[...].astype(f32)
+        + b_ref[...].astype(f32)
+        + across_ref[...].astype(f32)
+        + up_ref[...].astype(f32)
+    )
+
+    @pl.when(pl.program_id(0) == 0)
+    def _():
+        out_ref[...] = value
+
+    for k, part in enumerate(parts):
+
+        @pl.when(pl.program_id(0) == k + 1)
+        def _(part=part):
+            part[...] = value.astype(bf16)
+
+
+def side_sums(kept, got, across, up):
+    _, n, *shape = kept.shape
     me = index_scalar("mp") if n > 1 else jnp.zeros((1,), jnp.int32)
+    entry = pl.BlockSpec((None, None, *shape), lambda k, me: (0, me[0] ^ k, 0, 0))
+    block = pl.BlockSpec((None, *shape), lambda k, me: (me[0] ^ k, 0, 0))
+    spec = pltpu.PrefetchScalarGridSpec(
+        num_scalar_prefetch=1,
+        grid=(n,),
+        in_specs=[entry, entry, block, block],
+        out_specs=[pl.BlockSpec(tuple(shape), lambda k, me: (0, 0))] * n,
+    )
     return pl.pallas_call(
         side_sums_kernel,
-        in_specs=[SCALAR] + [pl.BlockSpec(memory_space=pltpu.VMEM)] * 3,
+        grid_spec=spec,
         out_shape=[jax.ShapeDtypeStruct(shape, f32)] + [jax.ShapeDtypeStruct(shape, bf16)] * (n - 1),
         compiler_params=params(),
         cost_estimate=BRIEF,
         name="side_sums",
-    )(me, own, across, up)
+    )(me, kept, got, across, up)
 
 
 def own_square_kernel(me_ref, own_ref, *refs):
@@ -576,35 +641,62 @@
     )
 
 
-def value_kernel(crops, count, x_ref, a_ref, sums_ref, norms_ref, y_ref, summary_ref, work_ref):
+def turned_quad(rows):
+    return pl.BlockSpec((rows, LANES), lambda k, me, *_: (0, me[0] ^ k))
+
+
+def turned_block(rows):
+    return pl.BlockSpec((None, rows, LANES), lambda k, me, *_: (me[0] ^ k, 0, 0))
+
+
+def whole_part(rows):
+    return pl.BlockSpec((rows, LANES), lambda k, *_: (0, 0))
+
+
+def value_kernel(crops, count, me_ref, x_ref, a_ref, sums_ref, norms_ref, *refs):
+    parts, summary_ref, work_ref = refs[:-2], refs[-2], refs[-1]
     _, _, scale, shift = affine(sums_ref[...], norms_ref[...], 2, count)
     work_ref[...] = swish(x_ref[...].astype(f32) + a_ref[...] * scale + shift)
-    y_ref[...] = work_ref[...].astype(bf16)
+    for k, part in enumerate(parts):
+
+        @pl.when(pl.program_id(0) == k)
+        def _(part=part):
+            part[...] = work_ref[...].astype(bf16)
+
     summary_ref[...] = (crop_totals(work_ref, crops) / PIXELS).astype(bf16)
 
 
 def block_value(x, a, sums, norms, count):
     rows, width = a.shape
     crops = rows // PIXELS
+    spec = pltpu.PrefetchScalarGridSpec(
+        num_scalar_prefetch=1,
+        grid=(QUADS,),
+        in_specs=[turned_block(rows), turned_quad(rows), turned_quad(2), turned_quad(6)],
+        out_specs=[whole_part(rows)] * QUADS + [turned_quad(crops)],
+        scratch_shapes=[pltpu.VMEM((rows, LANES), f32)],
+    )
     return pl.pallas_call(
         functools.partial(value_kernel, crops, count),
-        grid=(QUADS,),
-        in_specs=[block_spec(rows), quad_spec(rows), quad_spec(2), quad_spec(6)],
-        out_specs=[block_spec(rows), quad_spec(crops)],
-        out_shape=[
-            jax.ShapeDtypeStruct((QUADS, rows, LANES), bf16),
-            jax.ShapeDtypeStruct((crops, width), bf16),
-        ],
-        scratch_shapes=[pltpu.VMEM((rows, LANES), f32)],
+        grid_spec=spec,
+        out_shape=[jax.ShapeDtypeStruct((rows, LANES), bf16)] * QUADS
+        + [jax.ShapeDtypeStruct((crops, width), bf16)],
         compiler_params=params(),
         cost_estimate=BRIEF,
         name="value",
-    )(x, a, sums, norms)
+    )(index_scalar("mp"), x, a, sums, norms)
 
 
 def value_back_kernel(
-    crops, count, first_ref, x_ref, a_ref, sums_ref, norms_ref, dy_ref, do_ref, out_ref, stats_ref
+    crops, count, me_ref, first_ref, x_ref, a_ref, sums_ref, norms_ref, do_ref, *refs
 ):
+    parts, (out_ref, stats_ref, work_ref) = refs[:-3], refs[-3:]
+    for k, part in enumerate(parts):
+
+        @pl.when(pl.program_id(0) == k)
+        def _(part=part):
+            work_ref[...] = part[...].astype(f32)
+
     mean, inverse, scale, shift = affine(sums_ref[...], norms_ref[...], 2, count)
     values = a_ref[...]
     row = lax.broadcasted_iota(jnp.int32, (do_ref.shape[0], 1), 0)
@@ -616,58 +708,40 @@
         0,
     )
     slope = swish_slope(x_ref[...].astype(f32) + values * scale + shift)
-    grad = (dy_ref[...].astype(f32) + rows_of_crops(own / PIXELS, values.shape[0])) * slope
+    grad = (work_ref[...] + rows_of_crops(own / PIXELS, values.shape[0])) * slope
     out_ref[...] = grad
     column_sums(stats_ref, grad, grad * ((values - mean) * inverse))
 
 
-def value_back(first, x, a, sums, norms, dy, do, count):
+def value_back(first, x, a, sums, norms, dy_parts, do, count):
     rows, width = a.shape
-    return pl.pallas_call(
-        functools.partial(value_back_kernel, rows // PIXELS, count),
+    spec = pltpu.PrefetchScalarGridSpec(
+        num_scalar_prefetch=2,
         grid=(QUADS,),
         in_specs=[
-            SCALAR, block_spec(rows), quad_spec(rows), quad_spec(2), quad_spec(6),
-            block_spec(rows), quad_spec(do.shape[0]),
-        ],
-        out_specs=[quad_spec(rows), quad_spec(2)],
+            turned_block(rows), turned_quad(rows), turned_quad(2), turned_quad(6),
+            turned_quad(do.shape[0]),
+        ]
+        + [whole_part(rows)] * QUADS,
+        out_specs=[turned_quad(rows), turned_quad(2)],
+        scratch_shapes=[pltpu.VMEM((rows, LANES), f32)],
+    )
+    return pl.pallas_call(
+        functools.partial(value_back_kernel, rows // PIXELS, count),
+        grid_spec=spec,
         out_shape=[
             jax.ShapeDtypeStruct((rows, width), f32), jax.ShapeDtypeStruct((2, width), f32),
         ],
         compiler_params=params(),
         cost_estimate=BRIEF,
         name="value_back",
-    )(first, x, a, sums, norms, dy, do)
+    )(index_scalar("mp"), first, x, a, sums, norms, do, *dy_parts)
 
 
 def norm_back(grad, values, sums, norms, k, grad_sums, count):
     mean, inverse, scale, _ = affine(sums, norms, k, count)
     centred = (values - mean) * inverse
     return scale * (grad - (grad_sums[0:1] + centred * grad_sums[1:2]) / count)
-
-
-def norm_back_kernel(k, sloped, count, g_ref, a_ref, sums_ref, norms_ref, grad_sums_ref, out_ref):
-    grad, values = g_ref[...].astype(f32), a_ref[...]
-    if sloped:
-        _, _, scale, shift = affine(sums_ref[...], norms_ref[...], k, count)
-        grad = grad * swish_slope(values * scale + shift)
-    out_ref[...] = norm_back(
-        grad, values, sums_ref[...], norms_ref[...], k, grad_sums_ref[...], count
-    ).astype(bf16)
-
-
-def norm_backward(g, a, sums, norms, k, grad_sums, count, sloped):
-    rows, width = a.shape
-    return pl.pallas_call(
-        functools.partial(norm_back_kernel, k, sloped, count),
-        grid=(QUADS,),
-        in_specs=[quad_spec(rows), quad_spec(rows), quad_spec(2), quad_spec(6), quad_spec(2)],
-        out_specs=quad_spec(rows),
-        out_shape=jax.ShapeDtypeStruct((rows, width), bf16),
-        compiler_params=params(),
-        cost_estimate=BRIEF,
-        name="norm_backward",
-    )(g, a, sums, norms, grad_sums)
 
 
 def lane_mask(low, high, rows=GROUP):
@@ -977,7 +1051,7 @@
 
 def gate_kernel(crops, count, me_ref, a_ref, sums_ref, norms_ref, *refs):
     h_ref, pooled_ref, squeezed_ref, act_ref, gate_ref, f2_ref, se_ref, sems = refs[8:]
-    copies = fetch_pieces(me_ref, refs[:8], se_ref, sems, SE_OFFSET)
+    copies = fetch_pieces(me_ref, refs[:8], se_ref, sems, 0)
     rows = a_ref.shape[0]
     _, _, scale, shift = affine(sums_ref[...], norms_ref[...], 1, count)
     f2_ref[...] = swish(a_ref[...].astype(f32) * scale + shift)
@@ -1029,7 +1103,7 @@
     crops, count, me_ref, dh_ref, a_ref, sums_ref, norms_ref, gate_ref, squeezed_ref, *refs
 ):
     q_ref, stats_ref, excite_grad_ref, squeeze_grad_ref, work_ref, se_ref, sems = refs[8:]
-    copies = fetch_pieces(me_ref, refs[:8], se_ref, sems, SE_OFFSET)
+    copies = fetch_pieces(me_ref, refs[:8], se_ref, sems, 0)
     rows = a_ref.shape[0]
     for m in range(QUADS):
         lanes = pl.ds(m * LANES, LANES)
@@ -1106,7 +1180,6 @@
     for copy in copies:
         copy.wait()
     parts = 2 * QUADS * QUADS
-    blocks = parts * QUEUE_ROWS // crops
     for i in range(parts):
         d, m = i // QUADS, i % QUADS
         low = 64
@@ -1128,25 +1201,40 @@
     first = jnp.where(there, jnp.exp(scores / EPS_SINK), 0.0)
     plan_ref[pl.ds(0, crops), :] = first
 
+    size = 2 * crops
+
+    def partial_sums(value):
+        return jnp.sum(value.reshape(-1, 8, value.shape[1]), 0)
+
+    def rows_at(i):
+        return pl.ds(pl.multiple_of(crops + i * size, crops), size)
+
     def fill(i, column):
-        rows = queue_ref[pl.ds(pl.multiple_of(i * crops, crops), crops), :]
+        rows = queue_ref[pl.ds(pl.multiple_of(i * size, size), size), :]
         value = jnp.exp(dot(rows, protos, NT) / EPS_SINK)
-        plan_ref[pl.ds(pl.multiple_of((i + 1) * crops, crops), crops), :] = value
-        return column + jnp.sum(value, 0, keepdims=True)
-
-    column = lax.fori_loop(0, blocks, fill, jnp.sum(first, 0, keepdims=True))
-    inverse = jnp.where(there, 1.0 / column, 0.0)
+        plan_ref[rows_at(i), :] = value
+        return column + partial_sums(value)
+
+    steps = parts * QUEUE_ROWS // size
+    column = lax.fori_loop(0, steps, fill, partial_sums(first))
+    column = jnp.sum(column, 0, keepdims=True)
+    large = jnp.where(column > 1e37, 2.0**-8, 1.0)
+    inverse = jnp.where(there, 1.0 / (column * large), 0.0)
     for sweep in range(SINK - 1):
 
-        def pass_rows(i, column, inverse=inverse):
-            place = pl.ds(pl.multiple_of(i * crops, crops), crops)
-            value = plan_ref[place, :] * inverse
+        def balanced(place, inverse=inverse, sweep=sweep):
+            value = plan_ref[place, :]
+            if sweep == 0:
+                value = value * large
+            value = value * inverse
             value = value * (1.0 / jnp.sum(value, 1, keepdims=True))
             plan_ref[place, :] = value
-            return column + jnp.sum(value, 0, keepdims=True)
-
-        column = lax.fori_loop(0, blocks + 1, pass_rows, jnp.zeros_like(column))
-        inverse = jnp.where(there, 1.0 / column, 0.0)
+            return partial_sums(value)
+
+        column = lax.fori_loop(
+            0, steps, lambda i, column: column + balanced(rows_at(i)), balanced(pl.ds(0, crops))
+        )
+        inverse = jnp.where(there, 1.0 / jnp.sum(column, 0, keepdims=True), 0.0)
     value = plan_ref[pl.ds(0, crops), :] * inverse
     value = value / jnp.sum(value, 1, keepdims=True)
     pairs = jnp.concatenate(
@@ -1350,7 +1438,7 @@
 
 
 def squares_kernel(
-    n_dp, n_mp, weights_ref, norms_ref, small_ref, reduce_ref, expand_ref, kernel_ref,
+    n_dp, n_mp, weights_ref, norms_ref, small_ref, expand_ref, kernel_ref,
     g1_ref, g2_ref, g3_ref, out_ref,
 ):
     lane = lax.broadcasted_iota(jnp.int32, (1, 128), 1)
@@ -1363,7 +1451,7 @@
         portions = portions + at(i, 1.0 / n_dp)
     weights = weights_ref[...] * portions
     small = small_ref[...]
-    grads = at(0, reduce_ref[...]) + at(1, kernel_ref[...] / n_mp) + at(4, expand_ref[...])
+    grads = at(1, kernel_ref[...] / n_mp) + at(4, expand_ref[...])
     for i, k in enumerate((2, 3, 5, 6)):
         grads = grads + at(k, small[:, i : i + 1] / n_dp)
     everywhere = 1.0 / (n_dp * n_mp)
@@ -1376,6 +1464,12 @@
     out_ref[1:2, :] = grads
 
 
+def first_gradient():
+    lane = lax.broadcasted_iota(jnp.int32, (2, 128), 1)
+    row = lax.broadcasted_iota(jnp.int32, (2, 128), 0)
+    return (lane == 0) & (row == 1)
+
+
 def squares(n_dp, n_mp, *values):
     return pl.pallas_call(
         functools.partial(squares_kernel, n_dp, n_mp),
@@ -1413,53 +1507,39 @@
     )(*[v for item in items for v in item])
 
 
-def lars_kernel(squares_ref, weight_ref, gradient_ref, momentum_ref, *refs):
-    norm_squares = squares_ref[...]
-    n = len(refs) // 3
-    refs[2 * n][...] = step(
-        weight_ref[...], gradient_ref[...], momentum_ref[...], norm_squares, 0
-    )
-    for i in range(n):
-        refs[2 * n + 1 + i][...] = (
-            refs[2 * i + 1][...] + rate_of(norm_squares, i + 1) * refs[2 * i][...]
-        )
-
-
-def lars(norm_squares, weight, gradient, momentum, prepared):
-    shapes = [weight.shape] + [v.shape for v in prepared[::2]]
-    return pl.pallas_call(
-        lars_kernel,
-        out_shape=[jax.ShapeDtypeStruct(shape, f32) for shape in shapes],
-        compiler_params=params(),
-        cost_estimate=BRIEF,
-        name="lars",
-    )(norm_squares, weight, gradient, momentum, *prepared)
-
-
-def lars_norms_kernel(
-    m_ref, squares_ref, gains_ref, biases_ref, m_gains_ref, m_biases_ref, g1_ref, g2_ref, g3_ref,
-    gains_out, biases_out,
+def lars_kernel(
+    m_ref, squares_ref, weight_ref, gradient_ref, momentum_ref,
+    gains_ref, biases_ref, m_gains_ref, m_biases_ref, g1_ref, g2_ref, g3_ref, *refs
 ):
     norm_squares = squares_ref[...]
+    n = (len(refs) - 3) // 3
+    out = refs[2 * n :]
+    out[0][...] = step(weight_ref[...], gradient_ref[...], momentum_ref[...], norm_squares, 0)
+    for i in range(n):
+        out[1 + i][...] = refs[2 * i + 1][...] + rate_of(norm_squares, i + 1) * refs[2 * i][...]
     lanes = pl.ds(pl.multiple_of(m_ref[0] * LANES, LANES), LANES)
     for k, ref in enumerate((g1_ref, g2_ref, g3_ref)):
         own = narrow_lanes(ref[:, lanes])
         row = slice(k, k + 1)
-        gains_out[row, :] = step(gains_ref[row, :], own[1:2], m_gains_ref[row, :], norm_squares, 7 + k)
-        biases_out[row, :] = step(
+        out[n + 1][row, :] = step(
+            gains_ref[row, :], own[1:2], m_gains_ref[row, :], norm_squares, 7 + k
+        )
+        out[n + 2][row, :] = step(
             biases_ref[row, :], own[0:1], m_biases_ref[row, :], norm_squares, 10 + k
         )
 
 
-def lars_norms(norm_squares, *values):
-    return pl.pallas_call(
-        lars_norms_kernel,
-        in_specs=[SCALAR] + [pl.BlockSpec(memory_space=pltpu.VMEM)] * 8,
-        out_shape=[jax.ShapeDtypeStruct(values[0].shape, f32)] * 2,
-        compiler_params=params(),
-        cost_estimate=BRIEF,
-        name="lars_norms",
-    )(index_scalar("mp"), norm_squares, *values)
+def lars(norm_squares, weight, gradient, momentum, norm_values, prepared):
+    shapes = [weight.shape] + [v.shape for v in prepared[::2]] + [norm_values[0].shape] * 2
+    values = [norm_squares, weight, gradient, momentum, *norm_values, *prepared]
+    return pl.pallas_call(
+        lars_kernel,
+        in_specs=[SCALAR] + [pl.BlockSpec(memory_space=pltpu.VMEM)] * len(values),
+        out_shape=[jax.ShapeDtypeStruct(shape, f32) for shape in shapes],
+        compiler_params=params(),
+        cost_estimate=BRIEF,
+        name="lars",
+    )(index_scalar("mp"), *values)
 
 
 def plain_finish(
@@ -1554,34 +1634,28 @@
     norms = spread(jnp.concatenate([bn_gains, bn_biases], 0), "mp")
     norms = spread_channels(norms.transpose(1, 0, 2).reshape(norms.shape[1], -1))
     if quick:
-        reduce_quads = gather_mp(shard_square(w_reduce)).reshape(-1, 256)
-        rest = jnp.concatenate([shard_square(w_expand), shard_excitation(w_squeeze, w_excite)], 0)
-        reduce_quads, rest, norms, *kernel_low = tie(reduce_quads, rest, norms, *kernel_low)
-        across, up = gather_sides(reduce_quads)
-        rest_parts = parts_mp(rest)
+        low = gather_mp(shard_square(w_reduce)).reshape(-1, 256)
+        expand_low = shard_square(w_expand)
+        se_low = shard_excitation(w_squeeze, w_excite)
+        low, x_blocks, norms, expand_low, se_low, *kernel_low = tie(
+            low, x_blocks, norms, expand_low, se_low, *kernel_low
+        )
+        across, up = gather_sides(low)
+        x_blocks = exchange(x_blocks)
         windows = dense_windows(kernel_low)
-        across, up, windows, x_blocks = tie(across, up, windows, x_blocks)
+        across, up, windows = tie(across, up, windows)
         corner = gather_corner(across, up)
-        x_blocks, corner, *rest_parts = tie(x_blocks, corner, *rest_parts)
-        x_blocks = exchange(x_blocks)
-        rest = in_order(rest_parts, m_index)
-        rest = jnp.concatenate(
-            [rest[:, :LANES].reshape(-1, 256), rest[:, LANES:].reshape(-1, 256)], 0
-        )
-        rest_across, rest_up = gather_sides(rest)
-        reduce_pieces = gather_twins(reduce_quads, across, up, corner)
+        x_blocks, se_low = tie(x_blocks, se_low)
+        se_low = spread(se_low, "mp").reshape(-1, 256)
+        reduce_pieces = gather_twins(low, across, up, corner)
         head_values = tie(w_project, prototypes, queue_rows, pairing, corner)
         bundle = shard_head(*head_values[:4])
     else:
         x_blocks = exchange(x_blocks)
-        y_grad_blocks = exchange(y_grad_blocks)
+        y_grad_parts = list(quad_blocks(exchange(y_grad_blocks)))
         reduce_pieces = gather_square(w_reduce)
-        rest_pieces = gather_excitation(w_squeeze, w_excite)
+        se_pieces = list(gather_excitation(w_squeeze, w_excite).reshape(8, -1, 256))
         expand_pieces = gather_square(w_expand)
-        rest_pieces = jnp.concatenate(
-            [expand_pieces.reshape(8, -1, 256), rest_pieces.reshape(8, -1, 256)], 1
-        )
-        rest_pieces = [rest_pieces[b] for b in range(8)]
         project_low, protos_low, queue_low, pairs = gather_head(
             w_project, prototypes, queue_rows, pairing
         )
@@ -1591,39 +1665,62 @@
 
     reduced, sums1 = mix(x, reduce_pieces)
     if quick:
-        sums1, rest_across, rest_up = tie(sums1, rest_across, rest_up)
-        rest_corner = gather_corner(rest_across, rest_up)
-    sums1 = total(sums1)
-    if quick:
-        sums1, bundle, rest_corner = tie(sums1, bundle, rest_corner)
-        bundle = gather_mp(bundle).reshape(-1, 256)
+        sums1 = sum_axis(sums1, "dp")
+        sums1, expand_low, se_low = tie(sums1, expand_low, se_low)
+        expand_low = spread(expand_low, "mp").reshape(-1, 256)
+        se_across, se_up = gather_sides(se_low)
+        sums1 = sum_axis(sums1, "mp")
+        sums1, expand_low, se_across, se_up = tie(sums1, expand_low, se_across, se_up)
+        se_corner = gather_corner(se_across, se_up)
+        across, up = gather_sides(expand_low)
+        y_grad_parts = [
+            lax.dynamic_index_in_dim(y_grad_blocks, m_index ^ k, 0, keepdims=False) for k in range(QUADS)
+        ]
+        sums1, bundle, y_grad_parts[1] = tie(sums1, bundle, y_grad_parts[1])
+        y_grad_parts[1] = lax.ppermute(y_grad_parts[1], "mp", flips("mp", 1))
+        bundle = spread(bundle, "mp").reshape(-1, 256)
+    else:
+        sums1 = total(sums1)
     grouped, sums2 = conv(reduced, sums1, norms, windows, count)
     if quick:
-        sums2, bundle = tie(sums2, bundle)
-    sums2 = total(sums2)
+        sums2, bundle, across, up, se_corner, y_grad_parts[1] = tie(
+            sums2, bundle, across, up, se_corner, y_grad_parts[1]
+        )
+        se_pieces = gather_twins(se_low, se_across, se_up, se_corner)
+        corner = gather_corner(across, up)
+        sums2 = jnp.sum(spread(sums2, "dp"), 0)
+        sums2, corner = tie(sums2, corner)
+        expand_pieces = gather_twins(expand_low, across, up, corner)
+        sums2 = jnp.sum(spread(sums2, "mp"), 0)
+    else:
+        sums2 = total(sums2)
     if quick:
-        weight_squares = weight_sums(weights[:7])
-        sums2, weight_squares = tie(sums2, weight_squares)
-        rest_pieces = expand_pieces = gather_twins(rest, rest_across, rest_up, rest_corner)
-    gated, pooled, squeezed, squeeze_act, gates = gate(grouped, sums2, norms, rest_pieces, count)
-    if quick:
-        gated, bundle = tie(gated, bundle)
-        across, up = gather_sides(bundle)
+        sums2, y_grad_parts[2] = tie(sums2, y_grad_parts[2])
+        y_grad_parts[2] = lax.ppermute(y_grad_parts[2], "mp", flips("mp", 2))
+    gated, pooled, squeezed, squeeze_act, gates = gate(grouped, sums2, norms, se_pieces, count)
     expanded, sums3 = mix(gated, expand_pieces)
     if quick:
+        sums3, bundle = tie(sums3, bundle)
+        sums3 = jnp.sum(spread(sums3, "dp"), 0)
+        sums3, bundle, y_grad_parts[2] = tie(sums3, bundle, y_grad_parts[2])
+        across, up = gather_sides(bundle)
+        sums3 = jnp.sum(spread(sums3, "mp"), 0)
         sums3, across, up = tie(sums3, across, up)
         corner = gather_corner(across, up)
-    sums3 = total(sums3)
+    else:
+        sums3 = total(sums3)
+    *y_parts, summary = block_value(x, expanded, sums3, norms, count)
     if quick:
-        sums3, corner = tie(sums3, corner)
+        summary, corner = tie(summary, corner)
         bundle = gather_twins(bundle, across, up, corner)
-    y_blocks, summary = block_value(x, expanded, sums3, norms, count)
     summary = gather_all(summary)
+    if quick:
+        summary, y_grad_parts[3], y_parts[1] = tie(summary, y_grad_parts[3], y_parts[1])
+        y_grad_parts[3] = lax.ppermute(y_grad_parts[3], "mp", flips("mp", 3))
+        y_parts[1] = lax.ppermute(y_parts[1], "mp", flips("mp", 1))
 
     first_crop = ((lax.axis_index("dp") * n_mp + m_index) * crops).astype(jnp.int32)[None]
     if quick:
-        summary, y_grad_blocks = tie(summary, y_grad_blocks)
-        y_grad_blocks = exchange(y_grad_blocks)
         loss, unit, score_grad, embed_grad, summary_grad, summary = head(
             summary, bundle, prototypes.shape[1]
         )
@@ -1634,69 +1731,84 @@
         )
 
     joined_grad, grad_sums3 = value_back(
-        first_crop, x, expanded, sums3, norms, quad_blocks(y_grad_blocks), summary_grad, count
-    )
+        first_crop, x, expanded, sums3, norms, y_grad_parts, summary_grad, count
+    )
+    if quick:
+        grad_sums3, y_parts[1] = tie(grad_sums3, y_parts[1])
     grad_sums3 = total(grad_sums3)
-    expanded_grad = norm_backward(joined_grad, expanded, sums3, norms, 2, grad_sums3, count, False)
-    expand_kept, expand_sent = weight_grad(gated, expanded_grad)
+    if quick:
+        grad_sums3, y_parts[2], y_parts[3] = tie(grad_sums3, y_parts[2], y_parts[3])
+        y_parts[2] = lax.ppermute(y_parts[2], "mp", flips("mp", 2))
+    expanded_grad, expand_sent = sent_grads(
+        gated, joined_grad, expanded, sums3, norms, 2, grad_sums3, count, False
+    )
     if quick:
         expand_got = from_twin(expand_sent)
+    expand_kept = kept_grads(gated, expanded_grad)
     gated_grad = mix_back(expanded_grad, expand_pieces)
     if quick:
         gated_grad, expand_got = tie(gated_grad, expand_got)
-        expand_sums, expand_corner = scatter_corner(expand_kept, expand_got)
+        last = twin_sum(expand_kept, expand_got)
+        last, gated_grad, y_parts[2] = tie(last, gated_grad, y_parts[2])
+        expand_corner = lax.ppermute(last, "dp", diagonal(8))
     act2_grad, grad_sums2, excite_grad, squeeze_grad = gate_back(
-        gated_grad, grouped, sums2, norms, gates, squeezed, rest_pieces, count
+        gated_grad, grouped, sums2, norms, gates, squeezed, se_pieces, count
     )
     small = jnp.concatenate([pooled, squeeze_act, squeeze_grad, excite_grad], 1)
     if quick:
         grad_sums2, expand_corner = tie(grad_sums2, expand_corner)
     grad_sums2 = total(grad_sums2)
-    grad_sums2, y_blocks = tie(grad_sums2, y_blocks)
-    y_blocks = exchange(out_blocks(y_blocks))
+    grad_sums2, small = tie(grad_sums2, small)
+    small = gather_all(small)
     if quick:
-        expand_own, across, up = expand_sums
-        across, up = corner_sums(across, up, expand_corner)
+        grad_sums2, y_parts[3] = tie(grad_sums2, y_parts[3])
+        y_parts[3] = lax.ppermute(y_parts[3], "mp", flips("mp", 3))
+        across, up = corner_sums(expand_kept, expand_got, expand_corner)
         across, up = scatter_sides(across, up)
     act1_grad, kernel_kept, kernel_sent, grad_sums1 = conv_back(
         act2_grad, grouped, sums2, grad_sums2, reduced, sums1, norms, windows, count
     )
     if quick:
-        grad_sums1, across, up, kernel_kept, kernel_sent, y_blocks = tie(
-            grad_sums1, across, up, kernel_kept, kernel_sent, y_blocks
-        )
-        expand_own, *expand_parts = side_sums(expand_own, across, up)
+        grad_sums1, across, up, kernel_kept, kernel_sent, small, y_parts[3] = tie(
+            grad_sums1, across, up, kernel_kept, kernel_sent, small, y_parts[3]
+        )
+        expand_own, *expand_parts = side_sums(expand_kept, expand_got, across, up)
         expand_parts = scatter_mp(expand_own, expand_parts)
-        kernel_sums, kernel_corner = scatter_corner(kernel_kept, from_twin(kernel_sent))
-        kernel_own, across, up = kernel_sums
-        kernel_across, kernel_up = corner_sums(across, up, kernel_corner)
+        kernel_got = from_twin(kernel_sent)
+        kernel_across, kernel_up = corner_sums(
+            kernel_kept, kernel_got, scatter_corner(kernel_kept, kernel_got)
+        )
         grad_sums1 = jnp.sum(spread(grad_sums1, "dp"), 0)
         grad_sums1, expand_parts, kernel_across, kernel_up = tie(
             grad_sums1, expand_parts, kernel_across, kernel_up
         )
         kernel_across, kernel_up = scatter_sides(kernel_across, kernel_up)
         grad_sums1 = jnp.sum(spread(grad_sums1, "mp"), 0)
+        grad_sums1, kernel_across, kernel_up = tie(grad_sums1, kernel_across, kernel_up)
+        kernel_sum = side_sums(kernel_kept, kernel_got, kernel_across, kernel_up)[0].astype(bf16)
+        kernel_got = lax.ppermute(kernel_sum, "mp", flips("mp", 2))
     else:
         grad_sums1 = total(grad_sums1)
-    reduced_grad = norm_backward(act1_grad, reduced, sums1, norms, 0, grad_sums1, count, True)
+    reduced_grad, reduce_sent = sent_grads(
+        x, act1_grad, reduced, sums1, norms, 0, grad_sums1, count, True
+    )
     if quick:
-        reduced_grad, kernel_across, kernel_up, small = tie(
-            reduced_grad, kernel_across, kernel_up, small
-        )
-        kernel_sum = side_sums(kernel_own, kernel_across, kernel_up)[0].astype(bf16)
-        kernel_sum = kernel_sum + lax.ppermute(kernel_sum, "mp", flips("mp", 1))
-    small = gather_all(small)
-    reduce_kept, reduce_sent = weight_grad(x, reduced_grad)
+        reduced_grad, reduce_sent, kernel_got = tie(reduced_grad, reduce_sent, kernel_got)
+        reduce_got = from_twin(reduce_sent)
+        kernel_sum = kernel_sum + kernel_got
+        kernel_got = lax.ppermute(kernel_sum, "mp", flips("mp", 1))
+    reduce_kept = kept_grads(x, reduced_grad)
     if quick:
-        reduce_got = from_twin(reduce_sent)
-        reduce_got, kernel_sum = tie(reduce_got, kernel_sum)
-        kernel_sum = kernel_sum + lax.ppermute(kernel_sum, "mp", flips("mp", 2))
+        reduced_grad, reduce_got, reduce_kept, kernel_got = tie(
+            reduced_grad, reduce_got, reduce_kept, kernel_got
+        )
+        kernel_sum = kernel_sum + kernel_got
+        corner = scatter_corner(reduce_kept, reduce_got)
     x_grad = out_blocks(mix_back(reduced_grad, reduce_pieces, joined_grad))
     if quick:
-        x_grad, reduce_got, kernel_sum, small = tie(x_grad, reduce_got, kernel_sum, small)
-        (own, across, up), corner = scatter_corner(reduce_kept, reduce_got)
+        x_grad, corner = tie(x_grad, corner)
         x_grad = exchange(x_grad)
-        across, up = corner_sums(across, up, corner)
+        across, up = corner_sums(reduce_kept, reduce_got, corner)
         across, up, small, kernel_sum = tie(across, up, small, kernel_sum)
         across, up = scatter_sides(across, up)
         squeeze_part, excite_part, project_part, protos_part, small_squares = small_grads(
@@ -1704,13 +1816,13 @@
         )
         expand_grad, expand_square = own_square(expand_parts)
         kernel_grad, kernel_square = own_kernel(kernel_sum)
-        across, up, x_grad, small_squares, expand_square, kernel_square = tie(
-            across, up, x_grad, small_squares, expand_square, kernel_square
-        )
-        own, *parts = side_sums(own, across, up)
+        across, up, small_squares, expand_square, kernel_square = tie(
+            across, up, small_squares, expand_square, kernel_square
+        )
+        own, *parts = side_sums(reduce_kept, reduce_got, across, up)
         parts = scatter_mp(own, parts)
-        input_grad = out_channels(x_grad, channels_here, f32)
-        block_output = out_channels(y_blocks, channels_here, bf16)
+        input_grad = out_channels(list(x_grad), channels_here, f32, jnp.zeros((1,), jnp.int32))
+        block_output = out_channels(y_parts, channels_here, bf16, index_scalar("mp"))
         prepared = lars_prepare(
             [
                 (w_group.T, kernel_grad, m_group.T),
@@ -1721,29 +1833,32 @@
                 (prototypes.T, protos_part, m_protos.T),
             ]
         )
-        parts, input_grad, block_output, *prepared = tie(
-            parts, input_grad, block_output, *prepared
+        weight_squares = weight_sums(weights[:7])
+        shares = squares(
+            n_dp, n_mp, weight_squares, norms, small_squares, expand_square, kernel_square,
+            grad_sums1, grad_sums2, grad_sums3,
+        )
+        parts, input_grad, block_output, shares, *prepared = tie(
+            parts, input_grad, block_output, shares, *prepared
         )
         reduce_grad, reduce_square = own_square(parts)
-        norm_squares = total(
-            squares(
-                n_dp, n_mp, weight_squares, norms, small_squares, reduce_square, expand_square,
-                kernel_square, grad_sums1, grad_sums2, grad_sums3,
-            )
-        )
-        mom_reduce, mom_group, mom_squeeze, mom_excite, mom_expand, mom_project, mom_protos = lars(
-            norm_squares, w_reduce.T, reduce_grad, m_reduce.T, prepared
-        )
-        mom_gains, mom_biases = lars_norms(
-            norm_squares, bn_gains, bn_biases, m_gains, m_biases, grad_sums1, grad_sums2, grad_sums3
+        norm_squares = total(jnp.where(first_gradient(), reduce_square, shares))
+        (
+            mom_reduce, mom_group, mom_squeeze, mom_excite, mom_expand, mom_project, mom_protos,
+            mom_gains, mom_biases,
+        ) = lars(
+            norm_squares, w_reduce.T, reduce_grad, m_reduce.T,
+            [bn_gains, bn_biases, m_gains, m_biases, grad_sums1, grad_sums2, grad_sums3], prepared,
         )
         stepped = [
             mom_reduce.T, mom_group.T, mom_squeeze, mom_excite, mom_expand.T, mom_project.T,
             mom_protos.T, mom_gains, mom_biases,
         ]
     else:
-        input_grad = out_channels(exchange(x_grad), channels_here, f32)
-        block_output = out_channels(y_blocks, channels_here, bf16)
+        input_grad = natural_channels(exchange(x_grad), channels_here, f32)
+        block_output = natural_channels(
+            exchange(out_blocks(jnp.stack(y_parts))), channels_here, bf16
+        )
         big_grads = (
             scatter_square(reduce_kept, reduce_sent),
             scatter_kernel(kernel_kept[:, 0], kernel_sent[:, 0]),

time: 683 us -> 594 us (0.87)
  waiting for transfers between devices: 177 us -> 117 us
  local copies, waits for them, and re-layouts: 76 us -> 31.2 us
  Pallas kernels: 197 us -> 220 us
  blocking collectives: 101 us -> 89.9 us
  starting transfers between devices: 109 us -> 102 us
    unnamed x241 -> x115, local copies, waits for them, and re-layouts: 65.1 us -> 10.6 us
    ppermute x9 -> x3, waiting for transfers between devices: 38.6 us -> 0.01 us  [parts_mp(): lax.ppermute(v, 'mp', flips('mp', k))]
    all_to_all x4 -> x2, waiting for transfers between devices: 32.4 us -> 1.41 us  [exchange(): return lax.all_to_all(blocks, 'mp', split_axis=0, concat_axis=0, tiled=True)]
    pallas_call x21 -> x17, Pallas kernels: 52 us -> 74.4 us  [the longest x2 16.6 us: sent_grads(): pl.pallas_call(functools.partial(sent_grads_kernel, k, sloped, count), gr...]
    ppermute x4 -> x5, waiting for transfers between devices: 0.01 us -> 20.3 us  [gather_corner(): return lax.ppermute(jnp.where(even, across, up), 'dp', diagonal(8))]
    ppermute x5 -> x16, starting transfers between devices: 7.15 us -> 20.5 us  [the longest x5 8.24 us: sum_axis(): v = v + lax.ppermute(v, axis, flips(axis, bit))]
    all_to_all x4 -> x2, starting transfers between devices: 20.2 us -> 7.52 us  [exchange(): return lax.all_to_all(blocks, 'mp', split_axis=0, concat_axis=0, tiled=True)]
    all_to_all x5 -> x6, waiting for transfers between devices: 32.2 us -> 19.7 us  [spread(): lax.all_to_all(jnp.broadcast_to(v[None], (n,) + v.shape), axis, split_axi...]
  transfers between devices with their start and end apart: 67 -> 79, of which waited for: 30 -> 26; matrix products, arithmetic and copies ran while one was open for 3% -> 5% of each run, Pallas kernels for 22% -> 34%
where the time goes in v1:
time: 594 us; the launch traced here: 584 us
  Pallas kernels  220 us (37%)
  waiting for transfers between devices  117 us (20%)
  starting transfers between devices  102 us (17%)
  blocking collectives  89.9 us (15%)
  local copies, waits for them, and re-layouts  31.2 us (5%)
  other arithmetic  21 us (4%)
    all_to_all x10, blocking collectives, spread(): lax.all_to_all(jnp.broadcast_to(v[None], (n,) + v.shape), axis, split_axi...  89.9 us
    all_to_all x6, starting transfers between devices, spread(): lax.all_to_all(jnp.broadcast_to(v[None], (n,) + v.shape), axis, split_axi...  25 us
    pallas_call x1, Pallas kernels, conv_back(): pl.pallas_call(functools.partial(conv_back_kernel, crops, count), grid_sp...  22.8 us
    ppermute x5, waiting for transfers between devices, sum_axis(): v = v + lax.ppermute(v, axis, flips(axis, bit))  20.5 us
    ppermute x5, waiting for transfers between devices, gather_corner(): return lax.ppermute(jnp.where(even, across, up), 'dp', diagonal(8))  20.3 us
    all_to_all x6, waiting for transfers between devices, spread(): lax.all_to_all(jnp.broadcast_to(v[None], (n,) + v.shape), axis, split_axi...  19.7 us
    pallas_call x1, Pallas kernels, head(): pl.pallas_call(functools.partial(head_kernel, width), in_specs=[SCALAR, p...  18.6 us
    pallas_call x2, Pallas kernels, mix_back(): pl.pallas_call(functools.partial(mix_back_kernel, len(more)), in_specs=[S...  18.1 us
  transfers between devices with their start and end apart: 79, of which 26 were waited for; matrix products, arithmetic and copies ran while one was open for 5% of the time, Pallas kernels for 34%

profile of v1, /device:TPU:0, one launch (start us, length us, event | category | flops | bytes accessed | tf_op | source)
XLA Modules:
  0.0 584.2 jit_solution(9744511877043828616)
XLA Ops:
  4.2 5.0 collective-permute-start
  14.0 4.9 all-to-all-start
  28.3 4.9 all-to-all-done
  40.1 3.7 all-to-all-start.1
  43.8 7.1 %dense_windows.1.w_ref = bf16[4,3,9,256,256]{4,3,2,1,0:T(8,128)(2,1)} custom-call(s32[1]{0:T(128)} %bitcast.1.me_ref, bf16[504,256]{1,0:T(8,128)(2,1)} %copy-done.19, bf16[504,256]{1,0:T(8,128)(2,1)} %copy-done.37, bf16[504,256]{1,0:T(8,128)(2,1)} %copy-done.20, bf16[504,256]{1,0:T(8,128)(2,1)} %copy-done.39, ...), custom_call_target="tpu_custom_call" | custom-call | flops 1 | bytes 1 | tf_op jit(solution)/shard_map/dense_windows/pallas_call | solution.py:788
  50.9 11.8 %collective-permute-done.11.refs_2_ = bf16[2048,256]{1,0:T(8,128)(2,1)} collective-permute-done((bf16[2048,256]{1,0:T(8,128)(2,1)S(1)}, bf16[2048,256]{1,0:T(8,128)(2,1)}, u32[]{:S(2)}, u32[]{:S(2)}) %collective-permute-start.11) | collective-permute-done | bytes 1048608 | tf_op jit(solution)/shard_map/ppermute | solution.py:158
  67.3 12.9 %collective-permute-done.15.refs_6_ = bf16[2048,256]{1,0:T(8,128)(2,1)} collective-permute-done((bf16[2048,256]{1,0:T(8,128)(2,1)S(1)}, bf16[2048,256]{1,0:T(8,128)(2,1)}, u32[]{:S(2)}, u32[]{:S(2)}) %collective-permute-start.15) | collective-permute-done | bytes 1048608 | tf_op jit(solution)/shard_map/ppermute | solution.py:163
  82.7 4.1 all-to-all-start.2
  86.9 8.4 %mix.2 = (f32[392,2048]{1,0:T(8,128)}, f32[2,2048]{1,0:T(2,128)}) custom-call(s32[1]{0:T(128)} %bitcast.1.me_ref, bf16[4,392,512]{2,1,0:T(8,128)(2,1)} %copy-done, bf16[2048,256]{1,0:T(8,128)(2,1)} %bitcast.84, bf16[2048,256]{1,0:T(8,128)(2,1)} %collective-permute-done.10.refs_1_, bf16[2048,256]{1,0:T(8,128)(2,1)} %collective-permute-done.11.refs_2_, ...), custom_call_target="tpu_custom_call" | custom-call | flops 1 | bytes 1 | tf_op jit(solution)/shard_map/mix/pallas_call | solution.py:382
  98.1 3.2 collective-permute-done.18
  101.9 3.2 collective-permute-done.19
  106.3 5.0 all-to-all-start.3
  118.0 8.7 %collective-permute-done.20 = f32[2,2048]{1,0:T(2,128)S(1)} collective-permute-done((f32[2,2048]{1,0:T(2,128)S(1)}, f32[2,2048]{1,0:T(2,128)S(1)}, u32[]{:S(2)}, u32[]{:S(2)}) %collective-permute-start.20) | collective-permute-done | bytes 16416 | tf_op jit(solution)/shard_map/ppermute | solution.py:106
  126.7 4.9 collective-permute-start.21
  131.7 4.0 collective-permute-done.21
  140.1 4.3 all-to-all-start.4
  148.2 12.3 %conv.1 = (bf16[392,2048]{1,0:T(8,128)(2,1)}, f32[2,2048]{1,0:T(2,128)}) custom-call(f32[392,2048]{1,0:T(8,128)} %get-tuple-element.234.a_ref, f32[2,2048]{1,0:T(2,128)} %add.102.sums_ref, f32[6,2048]{1,0:T(8,128)} %bitcast.94, bf16[4,3,9,256,256]{4,3,2,1,0:T(8,128)(2,1)} %dense_windows.1.w_ref), custom_call_target="tpu_custom_call" | custom-call | flops 1 | bytes 1 | tf_op jit(solution)/shard_map/conv/pallas_call | solution.py:867
  161.5 5.0 collective-permute-done.26.refs_6_
  170.3 3.4 all-to-all-start.5
  174.2 9.9 %all-to-all-done.5 = f32[8,2,2048]{2,1,0:T(2,128)S(1)} async-done(((f32[8,2,2048]{2,1,0:T(2,128)}), f32[8,2,2048]{2,1,0:T(2,128)S(1)}, u32[]{:S(2)}, u32[]{:S(2)}) %all-to-all-start.5) | async-done | bytes 131104 | tf_op jit(solution)/shard_map/all_to_all | solution.py:97
  185.3 8.1 %all_to_all.100 = f32[4,2,2048]{2,1,0:T(2,128)S(1)} all-to-all(f32[4,2,2048]{2,1,0:T(2,128)S(1)} %broadcast_in_dim.67), channel_id=1, replica_groups=mesh['dp'=8,'mp'=4] {'mp'}, dimensions={0} | all-to-all | bytes 131072 | tf_op jit(solution)/shard_map/all_to_all | solution.py:97
  194.8 6.1 %gate.1 = (bf16[4,392,512]{2,1,0:T(8,128)(2,1)}, bf16[2,2048]{1,0:T(2,128)(2,1)}, f32[2,512]{1,0:T(2,128)}, bf16[2,512]{1,0:T(2,128)(2,1)}, f32[2,2048]{1,0:T(2,128)}) custom-call(s32[1]{0:T(128)} %bitcast.1.me_ref, bf16[392,2048]{1,0:T(8,128)(2,1)} %get-tuple-element.249.a_ref.a2_ref, f32[2,2048]{1,0:T(2,128)} %reduce_sum.109.sums_ref.sums2_ref, ...), custom_call_target="tpu_custom_call" | custom-call | flops 1 | bytes 1 | tf_op jit(solution)/shard_map/gate/pallas_call | solution.py:1084
  201.0 8.5 %mix.3 = (f32[392,2048]{1,0:T(8,128)}, f32[2,2048]{1,0:T(2,128)}) custom-call(s32[1]{0:T(128)} %bitcast.1.me_ref, bf16[4,392,512]{2,1,0:T(8,128)(2,1)} %get-tuple-element.262.x_ref, bf16[2048,256]{1,0:T(8,128)(2,1)} %bitcast.89, bf16[2048,256]{1,0:T(8,128)(2,1)} %collective-permute-done.33.refs_1_, bf16[2048,256]{1,0:T(8,128)(2,1)} %copy-done.4, ...), custom_call_target="tpu_custom_call" | custom-call | flops 1 | bytes 1 | tf_op jit(solution)/shard_map/mix/pallas_call | solution.py:382
  210.2 8.1 %all_to_all.101 = f32[8,2,2048]{2,1,0:T(2,128)S(1)} all-to-all(f32[8,2,2048]{2,1,0:T(2,128)S(1)} %broadcast_in_dim.69), channel_id=1, replica_groups=mesh['dp'=8,'mp'=4] {'dp'}, dimensions={0} | all-to-all | bytes 262144 | tf_op jit(solution)/shard_map/all_to_all | solution.py:97
  219.6 9.4 %all_to_all.102 = f32[4,2,2048]{2,1,0:T(2,128)S(1)} all-to-all(f32[4,2,2048]{2,1,0:T(2,128)S(1)} %broadcast_in_dim.70), channel_id=1, replica_groups=mesh['dp'=8,'mp'=4] {'mp'}, dimensions={0} | all-to-all | bytes 131072 | tf_op jit(solution)/shard_map/all_to_all | solution.py:97
  231.2 5.1 value.1
  240.2 3.7 all-to-all-start.9
  245.0 9.1 %all-to-all-done.9.summary_ref = bf16[32,2,2048]{2,1,0:T(2,128)(2,1)S(1)} async-done(((bf16[32,2,2048]{2,1,0:T(2,128)(2,1)}), bf16[32,2,2048]{2,1,0:T(2,128)(2,1)S(1)}, u32[]{:S(2)}, u32[]{:S(2)}) %all-to-all-start.9) | async-done | bytes 262176 | tf_op jit(solution)/shard_map/all_to_all | solution.py:121
  257.7 18.6 %head.1 = (f32[1,1]{1,0:T(1,128)}, bf16[64,256]{1,0:T(8,128)(2,1)}, bf16[3072,64]{1,0:T(8,128)(2,1)}, bf16[64,256]{1,0:T(8,128)(2,1)}, f32[64,2048]{1,0:T(8,128)}, /*index=5*/bf16[64,2048]{1,0:T(8,128)(2,1)}) custom-call(s32[1]{0:T(128)} %bitcast.1.me_ref, bf16[32,2,2048]{2,1,0:T(2,128)(2,1)} %copy-done.15, bf16[832,256]{1,0:T(8,128)(2,1)} %bitcast.26.refs_0_, ...), custom_call_target="tpu_custom_call" | custom-call | flops 1 | bytes 1 | tf_op jit(solution)/shard_map/head/pallas_call | solution.py:1266
  276.3 6.7 %value_back.1 = (f32[392,2048]{1,0:T(8,128)}, f32[2,2048]{1,0:T(2,128)}) custom-call(s32[1]{0:T(128)} %bitcast.me_ref.m_ref, s32[1]{0:T(128)} %bitcast.28.first_ref, bf16[4,392,512]{2,1,0:T(8,128)(2,1)} %copy-done, f32[392,2048]{1,0:T(8,128)} %get-tuple-element.264.a_ref, f32[2,2048]{1,0:T(2,128)} %reduce_sum.111.sums_ref, f32[6,2048]{1,0:T(8,128)} %bitcast.97, ...), custom_call_target="tpu_custom_call" | custom-call | flops 1 | bytes 1 | tf_op jit(solution)/shard_map/value_back/pallas_call | solution.py:729
  283.7 7.9 %all_to_all.103 = f32[8,2,2048]{2,1,0:T(2,128)S(1)} all-to-all(f32[8,2,2048]{2,1,0:T(2,128)S(1)} %broadcast_in_dim.72), channel_id=1, replica_groups=mesh['dp'=8,'mp'=4] {'dp'}, dimensions={0} | all-to-all | bytes 262144 | tf_op jit(solution)/shard_map/all_to_all | solution.py:97
  291.7 9.7 %all_to_all.104 = f32[4,2,2048]{2,1,0:T(2,128)S(1)} all-to-all(f32[4,2,2048]{2,1,0:T(2,128)S(1)} %broadcast_in_dim.73), channel_id=1, replica_groups=mesh['dp'=8,'mp'=4] {'mp'}, dimensions={0} | all-to-all | bytes 131072 | tf_op jit(solution)/shard_map/all_to_all | solution.py:97
  302.1 8.1 %sent_grads.2 = (bf16[392,2048]{1,0:T(8,128)(2,1)}, bf16[4,4,512,256]{3,2,1,0:T(8,128)(2,1)}) custom-call(s32[1]{0:T(128)} %bitcast.1.me_ref, bf16[4,392,512]{2,1,0:T(8,128)(2,1)} %get-tuple-element.262.x_ref, f32[392,2048]{1,0:T(8,128)} %get-tuple-element.284.g_ref.refs_8_, f32[392,2048]{1,0:T(8,128)} %get-tuple-element.264.a_ref, ...), custom_call_target="tpu_custom_call" | custom-call | flops 1 | bytes 1 | tf_op jit(solution)/shard_map/sent_grads/pallas_call | solution.py:477
  311.0 6.1 %kept_grads.2.a_ref.a1_ref.a2_ref = bf16[4,4,512,256]{3,2,1,0:T(8,128)(2,1)} custom-call(s32[1]{0:T(128)} %bitcast.1.me_ref, bf16[4,392,512]{2,1,0:T(8,128)(2,1)} %get-tuple-element.262.x_ref, bf16[392,2048]{1,0:T(8,128)(2,1)} %get-tuple-element.291.g_ref), custom_call_target="tpu_custom_call" | custom-call | flops 1 | bytes 1 | tf_op jit(solution)/shard_map/kept_grads/pallas_call | solution.py:498
  317.2 8.8 %mix_back.2.dh_ref = f32[392,2048]{1,0:T(8,128)} custom-call(s32[1]{0:T(128)} %bitcast.1.me_ref, bf16[392,2048]{1,0:T(8,128)(2,1)} %get-tuple-element.291.g_ref, bf16[2048,256]{1,0:T(8,128)(2,1)} %bitcast.90, bf16[2048,256]{1,0:T(8,128)(2,1)} %collective-permute-done.33.refs_1_, bf16[2048,256]{1,0:T(8,128)(2,1)} %copy-done.4, ...), custom_call_target="tpu_custom_call" | custom-call | flops 1 | bytes 1 | tf_op jit(solution)/shard_map/mix_back/pallas_call | solution.py:430
  328.5 2.9 collective-permute-done.48.refs_2_
  332.0 10.8 %gate_back.1 = (f32[392,2048]{1,0:T(8,128)}, f32[2,2048]{1,0:T(2,128)}, bf16[2,2048]{1,0:T(2,128)(2,1)}, bf16[2,512]{1,0:T(2,128)(2,1)}) custom-call(s32[1]{0:T(128)} %bitcast.1.me_ref, f32[392,2048]{1,0:T(8,128)} %mix_back.2.dh_ref, bf16[392,2048]{1,0:T(8,128)(2,1)} %get-tuple-element.249.a_ref.a2_ref, f32[2,2048]{1,0:T(2,128)} %reduce_sum.109.sums_ref.sums2_ref, ...), custom_call_target="tpu_custom_call" | custom-call | flops 1 | bytes 1 | tf_op jit(solution)/shard_map/gate_back/pallas_call | solution.py:1150
  342.8 3.7 collective-permute-done.49.corner_ref
  347.2 7.9 %all_to_all.105 = f32[8,2,2048]{2,1,0:T(2,128)S(1)} all-to-all(f32[8,2,2048]{2,1,0:T(2,128)S(1)} %broadcast_in_dim.74), channel_id=1, replica_groups=mesh['dp'=8,'mp'=4] {'dp'}, dimensions={0} | all-to-all | bytes 262144 | tf_op jit(solution)/shard_map/all_to_all | solution.py:97
  355.8 3.3 all-to-all-start.13
  359.9 5.0 all-to-all-done.13
  369.4 3.7 corner_sums.3
  376.4 3.5 collective-permute-start.52
  379.9 22.8 %conv_back.1 = (bf16[392,2048]{1,0:T(8,128)(2,1)}, bf16[4,1,504,256]{3,2,1,0:T(8,128)(2,1)}, bf16[4,1,504,256]{3,2,1,0:T(8,128)(2,1)}, f32[2,2048]{1,0:T(2,128)}) custom-call(s32[1]{0:T(128)} %bitcast.1.me_ref, f32[392,2048]{1,0:T(8,128)} %get-tuple-element.299.g_ref, bf16[392,2048]{1,0:T(8,128)(2,1)} %get-tuple-element.249.a_ref.a2_ref, ...), custom_call_target="tpu_custom_call" | custom-call | flops 1 | bytes 1 | tf_op jit(solution)/shard_map/conv_back/pallas_call | solution.py:990
  404.8 4.3 side_sums.3
  418.2 8.1 %all_to_all.106 = f32[8,2,2048]{2,1,0:T(2,128)S(1)} all-to-all(f32[8,2,2048]{2,1,0:T(2,128)S(1)} %broadcast_in_dim.77), channel_id=1, replica_groups=mesh['dp'=8,'mp'=4] {'dp'}, dimensions={0} | all-to-all | bytes 262144 | tf_op jit(solution)/shard_map/all_to_all | solution.py:97
  429.4 3.6 collective-permute-done.54.refs_1_
  436.1 11.4 %all_to_all.107 = f32[4,2,2048]{2,1,0:T(2,128)S(1)} all-to-all(f32[4,2,2048]{2,1,0:T(2,128)S(1)} %broadcast_in_dim.78), channel_id=1, replica_groups=mesh['dp'=8,'mp'=4] {'mp'}, dimensions={0} | all-to-all | bytes 131072 | tf_op jit(solution)/shard_map/all_to_all | solution.py:97
  453.7 8.5 %sent_grads.3 = (bf16[392,2048]{1,0:T(8,128)(2,1)}, bf16[4,4,512,256]{3,2,1,0:T(8,128)(2,1)}) custom-call(s32[1]{0:T(128)} %bitcast.1.me_ref, bf16[4,392,512]{2,1,0:T(8,128)(2,1)} %copy-done, bf16[392,2048]{1,0:T(8,128)(2,1)} %get-tuple-element.310.g_ref, f32[392,2048]{1,0:T(8,128)} %get-tuple-element.234.a_ref, f32[2,2048]{1,0:T(2,128)} %add.102.sums_ref, ...), custom_call_target="tpu_custom_call" | custom-call | flops 1 | bytes 1 | tf_op jit(solution)/shard_map/sent_grads/pallas_call | solution.py:477
  464.4 6.2 %kept_grads.3.a_ref.a1_ref.a2_ref = bf16[4,4,512,256]{3,2,1,0:T(8,128)(2,1)} custom-call(s32[1]{0:T(128)} %bitcast.1.me_ref, bf16[4,392,512]{2,1,0:T(8,128)(2,1)} %copy-done, bf16[392,2048]{1,0:T(8,128)(2,1)} %get-tuple-element.343.g_ref), custom_call_target="tpu_custom_call" | custom-call | flops 1 | bytes 1 | tf_op jit(solution)/shard_map/kept_grads/pallas_call | solution.py:498
  476.0 9.3 %mix_back.3 = bf16[4,392,512]{2,1,0:T(8,128)(2,1)} custom-call(s32[1]{0:T(128)} %bitcast.1.me_ref, bf16[392,2048]{1,0:T(8,128)(2,1)} %get-tuple-element.343.g_ref, bf16[2048,256]{1,0:T(8,128)(2,1)} %bitcast.85, bf16[2048,256]{1,0:T(8,128)(2,1)} %collective-permute-done.10.refs_1_, bf16[2048,256]{1,0:T(8,128)(2,1)} %collective-permute-done.11.refs_2_, ...), custom_call_target="tpu_custom_call" | custom-call | flops 1 | bytes 1 | tf_op jit(solution)/shard_map/mix_back/pallas_call | solution.py:430
  485.3 5.2 collective-permute-done.63.corner_ref
  491.5 3.8 all-to-all-start.17
  496.0 3.7 corner_sums.5
  500.6 3.6 weight_sums.1.weights_ref
  504.2 2.8 join_rows.3
  511.7 4.6 small_grads.1
  516.3 8.5 %lars_prepare.1 = (f32[504,252]{1,0:T(8,128)}, f32[504,252]{1,0:T(8,128)}, f32[2016,126]{1,0:T(8,128)}, f32[2016,126]{1,0:T(8,128)}, f32[504,504]{1,0:T(8,128)},...) custom-call(f32[504,252]{1,0:T(8,128)} %bitcast.106, ...), custom_call_target="tpu_custom_call" | custom-call | flops 1 | bytes 1 | tf_op jit(solution)/shard_map/lars_prepare/pallas_call | solution.py:1501
  525.8 4.3 side_sums.5
  538.5 3.4 join_rows.2
  542.1 11.2 %collective-permute-done.67.refs_1_ = bf16[512,256]{1,0:T(8,128)(2,1)S(1)} collective-permute-done((bf16[512,256]{1,0:T(8,128)(2,1)}, bf16[512,256]{1,0:T(8,128)(2,1)S(1)}, u32[]{:S(2)}, u32[]{:S(2)}) %collective-permute-start.67) | collective-permute-done | bytes 262176 | tf_op jit(solution)/shard_map/ppermute | solution.py:191
  557.4 8.4 %all_to_all.108 = f32[8,2,128]{2,1,0:T(2,128)S(1)} all-to-all(f32[8,2,128]{2,1,0:T(2,128)S(1)} %broadcast_in_dim.81), channel_id=1, replica_groups=mesh['dp'=8,'mp'=4] {'dp'}, dimensions={0} | all-to-all | bytes 16384 | tf_op jit(solution)/shard_map/all_to_all | solution.py:97
  565.8 10.8 %all_to_all.109 = f32[4,2,128]{2,1,0:T(2,128)S(1)} all-to-all(f32[4,2,128]{2,1,0:T(2,128)S(1)} %broadcast_in_dim.82), channel_id=1, replica_groups=mesh['dp'=8,'mp'=4] {'mp'}, dimensions={0} | all-to-all | bytes 8192 | tf_op jit(solution)/shard_map/all_to_all | solution.py:97
  577.2 6.8 %lars.1 = (f32[504,252]{1,0:T(8,128)}, f32[504,252]{1,0:T(8,128)}, f32[2016,126]{1,0:T(8,128)}, f32[504,504]{1,0:T(8,128)}, f32[504,252]{1,0:T(8,128)}, /*index=...) custom-call(s32[1]{0:T(128)} %bitcast.me_ref.m_ref, f32[2,128]{1,0:T(2,128)} %copy-done.50, ...), custom_call_target="tpu_custom_call" | custom-call | flops 1 | bytes 1 | tf_op jit(solution)/shard_map/lars/pallas_call | solution.py:1535
  (347 shorter events, 139.4 us)
Async XLA Ops:
  4.2 29.8 %collective-permute-start = (bf16[512,256]{1,0:T(8,128)(2,1)}, bf16[512,256]{1,0:T(8,128)(2,1)}, u32[]{:S(2)}, u32[]{:S(2)}) collective-permute-start(bf16[512,256]{1,0:T(8,128)(2,1)} %fusion), channel_id=1, source_target_pairs={{0,3},{1,2},{2,1},{3,0},{4,7},{5,6},{6,5},{7,4},{8,11},{9,10},{10,... | collective-permute-start | bytes 786440 | tf_op jit(solution)/shard_map/ppermute | solution.py:146
  9.2 24.7 %collective-permute-start.1 = (bf16[512,256]{1,0:T(8,128)(2,1)}, bf16[512,256]{1,0:T(8,128)(2,1)}, u32[]{:S(2)}, u32[]{:S(2)}) collective-permute-start(bf16[512,256]{1,0:T(8,128)(2,1)} %fusion), channel_id=1, source_target_pairs={{0,2},{1,3},{2,0},{3,1},{4,6},{5,7},{6,4},{7,5},{8,10},{9,11},{10,... | collective-permute-start | bytes 786440 | tf_op jit(solution)/shard_map/ppermute | solution.py:146
  9.2 25.3 %collective-permute-start.2 = (bf16[512,256]{1,0:T(8,128)(2,1)}, bf16[512,256]{1,0:T(8,128)(2,1)}, u32[]{:S(2)}, u32[]{:S(2)}) collective-permute-start(bf16[512,256]{1,0:T(8,128)(2,1)} %fusion), channel_id=1, source_target_pairs={{0,1},{1,0},{2,3},{3,2},{4,5},{5,4},{6,7},{7,6},{8,9},{9,8},{10,11... | collective-permute-start | bytes 786440 | tf_op jit(solution)/shard_map/ppermute | solution.py:146
  10.0 17.5 %collective-permute-start.4 = (bf16[504,256]{1,0:T(8,128)(2,1)S(1)}, bf16[504,256]{1,0:T(8,128)(2,1)S(1)}, u32[]{:S(2)}, u32[]{:S(2)}) collective-permute-start(bf16[504,256]{1,0:T(8,128)(2,1)S(1)} %fusion.2.refs_0_), channel_id=1, source_target_pairs={{0,8},{4,12},{8,0},{12,4},{16,24},{20,28},{24,16},{28,20},{1,9},{5... | collective-permute-start | bytes 774152 | tf_op jit(solution)/shard_map/ppermute | solution.py:158
  11.8 15.8 %collective-permute-start.6 = (bf16[504,256]{1,0:T(8,128)(2,1)S(1)}, bf16[504,256]{1,0:T(8,128)(2,1)}, u32[]{:S(2)}, u32[]{:S(2)}) collective-permute-start(bf16[504,256]{1,0:T(8,128)(2,1)S(1)} %fusion.2.refs_0_), channel_id=1, source_target_pairs={{0,16},{4,20},{8,24},{12,28},{16,0},{20,4},{24,8},{28,12},{1,17},{... | collective-permute-start | bytes 774152 | tf_op jit(solution)/shard_map/ppermute | solution.py:158
  14.0 19.2 %all-to-all-start = ((f32[4,6,504]{2,1,0:T(8,128)}), f32[4,6,504]{2,1,0:T(8,128)S(1)}, u32[]{:S(2)}, u32[]{:S(2)}) async-start(f32[4,6,504]{2,1,0:T(8,128)} %broadcast_in_dim.59), calls=%async_computation | async-start | bytes 131072 | tf_op jit(solution)/shard_map/all_to_all | solution.py:97
  37.1 25.6 %collective-permute-start.11 = (bf16[2048,256]{1,0:T(8,128)(2,1)S(1)}, bf16[2048,256]{1,0:T(8,128)(2,1)}, u32[]{:S(2)}, u32[]{:S(2)}) collective-permute-start(bf16[2048,256]{1,0:T(8,128)(2,1)S(1)} %bitcast.81), channel_id=1, source_target_pairs={{0,8},{4,12},{8,0},{12,4},{16,24},{20,28},{24,16},{28,20},{1,9},{5... | collective-permute-start | bytes 3145736 | tf_op jit(solution)/shard_map/ppermute | solution.py:158
  38.6 25.3 %collective-permute-start.12 = (bf16[2048,256]{1,0:T(8,128)(2,1)S(1)}, bf16[2048,256]{1,0:T(8,128)(2,1)}, u32[]{:S(2)}, u32[]{:S(2)}) collective-permute-start(bf16[2048,256]{1,0:T(8,128)(2,1)S(1)} %bitcast.82), channel_id=1, source_target_pairs={{0,16},{4,20},{8,24},{12,28},{16,0},{20,4},{24,8},{28,12},{1,17},{... | collective-permute-start | bytes 3145736 | tf_op jit(solution)/shard_map/ppermute | solution.py:158
  40.1 41.5 %all-to-all-start.1 = ((bf16[4,392,512]{2,1,0:T(8,128)(2,1)}), bf16[4,392,512]{2,1,0:T(8,128)(2,1)S(1)}, u32[]{:S(2)}, u32[]{:S(2)}) async-start(bf16[4,392,512]{2,1,0:T(8,128)(2,1)} %get-tuple-element.220), calls=%async_computation.1 | async-start | bytes 3211264 | tf_op jit(solution)/shard_map/all_to_all | solution.py:142
  65.2 15.0 %collective-permute-start.15 = (bf16[2048,256]{1,0:T(8,128)(2,1)S(1)}, bf16[2048,256]{1,0:T(8,128)(2,1)}, u32[]{:S(2)}, u32[]{:S(2)}) collective-permute-start(bf16[2048,256]{1,0:T(8,128)(2,1)S(1)} %broadcast_select_fusion.1), channel_id=1, source_target_pairs={{0,16},{4,12},{8,24},{12,4},{16,0},{20,28},{24,8},{28,20},{1,17},{... | collective-permute-start | bytes 3145736 | tf_op jit(solution)/shard_map/ppermute | solution.py:163
  66.8 20.0 %collective-permute-start.10 = (bf16[2048,256]{1,0:T(8,128)(2,1)S(1)}, bf16[2048,256]{1,0:T(8,128)(2,1)}, u32[]{:S(2)}, u32[]{:S(2)}) collective-permute-start(bf16[2048,256]{1,0:T(8,128)(2,1)S(1)} %bitcast.83), channel_id=1, source_target_pairs={{0,4},{4,0},{8,12},{12,8},{16,20},{20,16},{24,28},{28,24},{1,5},{5... | collective-permute-start | bytes 3145736 | tf_op jit(solution)/shard_map/ppermute | solution.py:169
  66.8 20.0 %collective-permute-start.13 = (bf16[2048,256]{1,0:T(8,128)(2,1)}, bf16[2048,256]{1,0:T(8,128)(2,1)}, u32[]{:S(2)}, u32[]{:S(2)}) collective-permute-start(bf16[2048,256]{1,0:T(8,128)(2,1)} %collective-permute-done.11.refs_2_), channel_id=1, source_target_pairs={{0,4},{4,0},{8,12},{12,8},{16,20},{20,16},{24,28},{28,24},{1,5},{5... | collective-permute-start | bytes 3145736 | tf_op jit(solution)/shard_map/ppermute | solution.py:169
  67.3 19.5 %collective-permute-start.14 = (bf16[2048,256]{1,0:T(8,128)(2,1)}, bf16[2048,256]{1,0:T(8,128)(2,1)}, u32[]{:S(2)}, u32[]{:S(2)}) collective-permute-start(bf16[2048,256]{1,0:T(8,128)(2,1)} %collective-permute-done.12.refs_4_), channel_id=1, source_target_pairs={{0,4},{4,0},{8,12},{12,8},{16,20},{20,16},{24,28},{28,24},{1,5},{5... | collective-permute-start | bytes 3145736 | tf_op jit(solution)/shard_map/ppermute | solution.py:169
  82.7 22.5 %all-to-all-start.2 = ((bf16[4,256,256]{2,1,0:T(8,128)(2,1)}), bf16[4,256,256]{2,1,0:T(8,128)(2,1)}, u32[]{:S(2)}, u32[]{:S(2)}) async-start(bf16[4,256,256]{2,1,0:T(8,128)(2,1)} %broadcast_in_dim.62), calls=%async_computation.2 | async-start | bytes 1048576 | tf_op jit(solution)/shard_map/all_to_all | solution.py:97
  106.3 30.1 %all-to-all-start.3 = ((bf16[4,512,256]{2,1,0:T(8,128)(2,1)}), bf16[4,512,256]{2,1,0:T(8,128)(2,1)S(1)}, u32[]{:S(2)}, u32[]{:S(2)}) async-start(bf16[4,512,256]{2,1,0:T(8,128)(2,1)} %broadcast_in_dim.63), calls=%async_computation.3 | async-start | bytes 2097152 | tf_op jit(solution)/shard_map/all_to_all | solution.py:97
  112.8 23.5 %collective-permute-start.22 = (bf16[1024,256]{1,0:T(8,128)(2,1)}, bf16[1024,256]{1,0:T(8,128)(2,1)}, u32[]{:S(2)}, u32[]{:S(2)}) collective-permute-start(bf16[1024,256]{1,0:T(8,128)(2,1)} %bitcast.16.refs_0_), channel_id=1, source_target_pairs={{0,8},{4,12},{8,0},{12,4},{16,24},{20,28},{24,16},{28,20},{1,9},{5... | collective-permute-start | bytes 1572872 | tf_op jit(solution)/shard_map/ppermute | solution.py:158
  113.4 23.0 %collective-permute-start.23 = (bf16[1024,256]{1,0:T(8,128)(2,1)}, bf16[1024,256]{1,0:T(8,128)(2,1)}, u32[]{:S(2)}, u32[]{:S(2)}) collective-permute-start(bf16[1024,256]{1,0:T(8,128)(2,1)} %bitcast.16.refs_0_), channel_id=1, source_target_pairs={{0,16},{4,20},{8,24},{12,28},{16,0},{20,4},{24,8},{28,12},{1,17},{... | collective-permute-start | bytes 1572872 | tf_op jit(solution)/shard_map/ppermute | solution.py:158
  115.0 11.7 %collective-permute-start.20 = (f32[2,2048]{1,0:T(2,128)S(1)}, f32[2,2048]{1,0:T(2,128)S(1)}, u32[]{:S(2)}, u32[]{:S(2)}) collective-permute-start(f32[2,2048]{1,0:T(2,128)S(1)} %add.100), channel_id=1, source_target_pairs={{0,1},{1,0},{2,3},{3,2},{4,5},{5,4},{6,7},{7,6},{8,9},{9,8},{10,11... | collective-permute-start | bytes 49160 | tf_op jit(solution)/shard_map/ppermute | solution.py:106
  136.4 30.2 %collective-permute-start.24 = (bf16[2048,256]{1,0:T(8,128)(2,1)S(1)}, bf16[2048,256]{1,0:T(8,128)(2,1)S(1)}, u32[]{:S(2)}, u32[]{:S(2)}) collective-permute-start(bf16[2048,256]{1,0:T(8,128)(2,1)S(1)} %bitcast.86), channel_id=1, source_target_pairs={{0,8},{4,12},{8,0},{12,4},{16,24},{20,28},{24,16},{28,20},{1,9},{5... | collective-permute-start | bytes 3145736 | tf_op jit(solution)/shard_map/ppermute | solution.py:158
  137.0 29.6 %collective-permute-start.25 = (bf16[2048,256]{1,0:T(8,128)(2,1)S(1)}, bf16[2048,256]{1,0:T(8,128)(2,1)S(1)}, u32[]{:S(2)}, u32[]{:S(2)}) collective-permute-start(bf16[2048,256]{1,0:T(8,128)(2,1)S(1)} %bitcast.87), channel_id=1, source_target_pairs={{0,16},{4,20},{8,24},{12,28},{16,0},{20,4},{24,8},{28,12},{1,17},{... | collective-permute-start | bytes 3145736 | tf_op jit(solution)/shard_map/ppermute | solution.py:158
  140.1 26.4 %all-to-all-start.4 = ((bf16[4,208,256]{2,1,0:T(8,128)(2,1)}), bf16[4,208,256]{2,1,0:T(8,128)(2,1)}, u32[]{:S(2)}, u32[]{:S(2)}) async-start(bf16[4,208,256]{2,1,0:T(8,128)(2,1)} %broadcast_in_dim.65), calls=%async_computation.4 | async-start | bytes 851968 | tf_op jit(solution)/shard_map/all_to_all | solution.py:97
  145.5 21.0 %collective-permute-start.26 = (bf16[1024,256]{1,0:T(8,128)(2,1)S(1)}, bf16[1024,256]{1,0:T(8,128)(2,1)}, u32[]{:S(2)}, u32[]{:S(2)}) collective-permute-start(bf16[1024,256]{1,0:T(8,128)(2,1)S(1)} %broadcast_select_fusion.2), channel_id=1, source_target_pairs={{0,16},{4,12},{8,24},{12,4},{16,0},{20,28},{24,8},{28,20},{1,17},{... | collective-permute-start | bytes 1572872 | tf_op jit(solution)/shard_map/ppermute | solution.py:163
  146.2 15.3 %collective-permute-start.27 = (bf16[392,512]{1,0:T(8,128)(2,1)}, bf16[392,512]{1,0:T(8,128)(2,1)S(1)}, u32[]{:S(2)}, u32[]{:S(2)}) collective-permute-start(bf16[392,512]{1,0:T(8,128)(2,1)} %get-tuple-element.255), channel_id=1, source_target_pairs={{0,1},{1,0},{2,3},{3,2},{4,5},{5,4},{6,7},{7,6},{8,9},{9,8},{10,11... | collective-permute-start | bytes 1204232 | tf_op jit(solution)/shard_map/ppermute | solution.py:1680
  167.7 16.5 %collective-permute-start.28 = (bf16[2048,256]{1,0:T(8,128)(2,1)}, bf16[2048,256]{1,0:T(8,128)(2,1)}, u32[]{:S(2)}, u32[]{:S(2)}) collective-permute-start(bf16[2048,256]{1,0:T(8,128)(2,1)} %broadcast_select_fusion), channel_id=1, source_target_pairs={{0,16},{4,12},{8,24},{12,4},{16,0},{20,28},{24,8},{28,20},{1,17},{... | collective-permute-start | bytes 3145736 | tf_op jit(solution)/shard_map/ppermute | solution.py:163
  169.1 15.2 %collective-permute-start.29 = (bf16[1024,256]{1,0:T(8,128)(2,1)}, bf16[1024,256]{1,0:T(8,128)(2,1)}, u32[]{:S(2)}, u32[]{:S(2)}) collective-permute-start(bf16[1024,256]{1,0:T(8,128)(2,1)} %bitcast.16.refs_0_), channel_id=1, source_target_pairs={{0,4},{4,0},{8,12},{12,8},{16,20},{20,16},{24,28},{28,24},{1,5},{5... | collective-permute-start | bytes 1572872 | tf_op jit(solution)/shard_map/ppermute | solution.py:169
  169.1 15.7 %collective-permute-start.30 = (bf16[1024,256]{1,0:T(8,128)(2,1)}, bf16[1024,256]{1,0:T(8,128)(2,1)}, u32[]{:S(2)}, u32[]{:S(2)}) collective-permute-start(bf16[1024,256]{1,0:T(8,128)(2,1)} %collective-permute-done.22.refs_2_), channel_id=1, source_target_pairs={{0,4},{4,0},{8,12},{12,8},{16,20},{20,16},{24,28},{28,24},{1,5},{5... | collective-permute-start | bytes 1572872 | tf_op jit(solution)/shard_map/ppermute | solution.py:169
  169.6 15.2 %collective-permute-start.31 = (bf16[1024,256]{1,0:T(8,128)(2,1)}, bf16[1024,256]{1,0:T(8,128)(2,1)}, u32[]{:S(2)}, u32[]{:S(2)}) collective-permute-start(bf16[1024,256]{1,0:T(8,128)(2,1)} %collective-permute-done.23.refs_4_), channel_id=1, source_target_pairs={{0,4},{4,0},{8,12},{12,8},{16,20},{20,16},{24,28},{28,24},{1,5},{5... | collective-permute-start | bytes 1572872 | tf_op jit(solution)/shard_map/ppermute | solution.py:169
  170.3 13.8 %all-to-all-start.5 = ((f32[8,2,2048]{2,1,0:T(2,128)}), f32[8,2,2048]{2,1,0:T(2,128)S(1)}, u32[]{:S(2)}, u32[]{:S(2)}) async-start(f32[8,2,2048]{2,1,0:T(2,128)} %broadcast_in_dim.66), calls=%async_computation.5 | async-start | bytes 262144 | tf_op jit(solution)/shard_map/all_to_all | solution.py:97
  173.7 27.2 %collective-permute-start.33 = (bf16[2048,256]{1,0:T(8,128)(2,1)S(1)}, bf16[2048,256]{1,0:T(8,128)(2,1)}, u32[]{:S(2)}, u32[]{:S(2)}) collective-permute-start(bf16[2048,256]{1,0:T(8,128)(2,1)S(1)} %bitcast.88), channel_id=1, source_target_pairs={{0,4},{4,0},{8,12},{12,8},{16,20},{20,16},{24,28},{28,24},{1,5},{5... | collective-permute-start | bytes 3145736 | tf_op jit(solution)/shard_map/ppermute | solution.py:169
  184.2 16.7 %collective-permute-start.34 = (bf16[2048,256]{1,0:T(8,128)(2,1)S(1)}, bf16[2048,256]{1,0:T(8,128)(2,1)}, u32[]{:S(2)}, u32[]{:S(2)}) collective-permute-start(bf16[2048,256]{1,0:T(8,128)(2,1)S(1)} %collective-permute-done.24.refs_2_), channel_id=1, source_target_pairs={{0,4},{4,0},{8,12},{12,8},{16,20},{20,16},{24,28},{28,24},{1,5},{5... | collective-permute-start | bytes 3145736 | tf_op jit(solution)/shard_map/ppermute | solution.py:169
  184.3 16.6 %collective-permute-start.35 = (bf16[2048,256]{1,0:T(8,128)(2,1)S(1)}, bf16[2048,256]{1,0:T(8,128)(2,1)}, u32[]{:S(2)}, u32[]{:S(2)}) collective-permute-start(bf16[2048,256]{1,0:T(8,128)(2,1)S(1)} %collective-permute-done.25.refs_4_), channel_id=1, source_target_pairs={{0,4},{4,0},{8,12},{12,8},{16,20},{20,16},{24,28},{28,24},{1,5},{5... | collective-permute-start | bytes 3145736 | tf_op jit(solution)/shard_map/ppermute | solution.py:169
  184.8 16.2 %collective-permute-start.36 = (bf16[2048,256]{1,0:T(8,128)(2,1)}, bf16[2048,256]{1,0:T(8,128)(2,1)}, u32[]{:S(2)}, u32[]{:S(2)}) collective-permute-start(bf16[2048,256]{1,0:T(8,128)(2,1)} %collective-permute-done.28.refs_6_), channel_id=1, source_target_pairs={{0,4},{4,0},{8,12},{12,8},{16,20},{20,16},{24,28},{28,24},{1,5},{5... | collective-permute-start | bytes 3145736 | tf_op jit(solution)/shard_map/ppermute | solution.py:169
  194.1 24.3 %collective-permute-start.37 = (bf16[392,512]{1,0:T(8,128)(2,1)}, bf16[392,512]{1,0:T(8,128)(2,1)S(1)}, u32[]{:S(2)}, u32[]{:S(2)}) collective-permute-start(bf16[392,512]{1,0:T(8,128)(2,1)} %get-tuple-element.269), channel_id=1, source_target_pairs={{0,2},{1,3},{2,0},{3,1},{4,6},{5,7},{6,4},{7,5},{8,10},{9,11},{10,... | collective-permute-start | bytes 1204232 | tf_op jit(solution)/shard_map/ppermute | solution.py:1699
  218.4 11.6 %collective-permute-start.38 = (bf16[832,256]{1,0:T(8,128)(2,1)}, bf16[832,256]{1,0:T(8,128)(2,1)S(1)}, u32[]{:S(2)}, u32[]{:S(2)}) collective-permute-start(bf16[832,256]{1,0:T(8,128)(2,1)} %bitcast.26.refs_0_), channel_id=1, source_target_pairs={{0,8},{4,12},{8,0},{12,4},{16,24},{20,28},{24,16},{28,20},{1,9},{5... | collective-permute-start | bytes 1277960 | tf_op jit(solution)/shard_map/ppermute | solution.py:158
  219.0 11.4 %collective-permute-start.39 = (bf16[832,256]{1,0:T(8,128)(2,1)}, bf16[832,256]{1,0:T(8,128)(2,1)S(1)}, u32[]{:S(2)}, u32[]{:S(2)}) collective-permute-start(bf16[832,256]{1,0:T(8,128)(2,1)} %bitcast.26.refs_0_), channel_id=1, source_target_pairs={{0,16},{4,20},{8,24},{12,28},{16,0},{20,4},{24,8},{28,12},{1,17},{... | collective-permute-start | bytes 1277960 | tf_op jit(solution)/shard_map/ppermute | solution.py:158
  240.2 13.9 %all-to-all-start.9 = ((bf16[32,2,2048]{2,1,0:T(2,128)(2,1)}), bf16[32,2,2048]{2,1,0:T(2,128)(2,1)S(1)}, u32[]{:S(2)}, u32[]{:S(2)}) async-start(bf16[32,2,2048]{2,1,0:T(2,128)(2,1)} %broadcast_in_dim.71), calls=%async_computation.9 | async-start | bytes 524288 | tf_op jit(solution)/shard_map/all_to_all | solution.py:121
  243.9 12.0 %collective-permute-start.41 = (bf16[832,256]{1,0:T(8,128)(2,1)}, bf16[832,256]{1,0:T(8,128)(2,1)S(1)}, u32[]{:S(2)}, u32[]{:S(2)}) collective-permute-start(bf16[832,256]{1,0:T(8,128)(2,1)} %bitcast.26.refs_0_), channel_id=1, source_target_pairs={{0,4},{4,0},{8,12},{12,8},{16,20},{20,16},{24,28},{28,24},{1,5},{5... | collective-permute-start | bytes 1277960 | tf_op jit(solution)/shard_map/ppermute | solution.py:169
  244.2 11.7 %collective-permute-start.42 = (bf16[832,256]{1,0:T(8,128)(2,1)S(1)}, bf16[832,256]{1,0:T(8,128)(2,1)S(1)}, u32[]{:S(2)}, u32[]{:S(2)}) collective-permute-start(bf16[832,256]{1,0:T(8,128)(2,1)S(1)} %collective-permute-done.38.refs_2_), channel_id=1, source_target_pairs={{0,4},{4,0},{8,12},{12,8},{16,20},{20,16},{24,28},{28,24},{1,5},{5... | collective-permute-start | bytes 1277960 | tf_op jit(solution)/shard_map/ppermute | solution.py:169
  244.5 11.4 %collective-permute-start.43 = (bf16[832,256]{1,0:T(8,128)(2,1)S(1)}, bf16[832,256]{1,0:T(8,128)(2,1)S(1)}, u32[]{:S(2)}, u32[]{:S(2)}) collective-permute-start(bf16[832,256]{1,0:T(8,128)(2,1)S(1)} %collective-permute-done.39.refs_4_), channel_id=1, source_target_pairs={{0,4},{4,0},{8,12},{12,8},{16,20},{20,16},{24,28},{28,24},{1,5},{5... | collective-permute-start | bytes 1277960 | tf_op jit(solution)/shard_map/ppermute | solution.py:169
  244.7 11.2 %collective-permute-start.44 = (bf16[832,256]{1,0:T(8,128)(2,1)S(1)}, bf16[832,256]{1,0:T(8,128)(2,1)S(1)}, u32[]{:S(2)}, u32[]{:S(2)}) collective-permute-start(bf16[832,256]{1,0:T(8,128)(2,1)S(1)} %collective-permute-done.40.refs_6_), channel_id=1, source_target_pairs={{0,4},{4,0},{8,12},{12,8},{16,20},{20,16},{24,28},{28,24},{1,5},{5... | collective-permute-start | bytes 1277960 | tf_op jit(solution)/shard_map/ppermute | solution.py:169
  254.1 22.2 %collective-permute-start.45 = (bf16[392,512]{1,0:T(8,128)(2,1)}, bf16[392,512]{1,0:T(8,128)(2,1)}, u32[]{:S(2)}, u32[]{:S(2)}) collective-permute-start(bf16[392,512]{1,0:T(8,128)(2,1)} %get-tuple-element.283), channel_id=1, source_target_pairs={{0,3},{1,2},{2,1},{3,0},{4,7},{5,6},{6,5},{7,4},{8,11},{9,10},{10,... | collective-permute-start | bytes 1204232 | tf_op jit(solution)/shard_map/ppermute | solution.py:1719
  255.9 27.1 %collective-permute-start.46 = (bf16[392,512]{1,0:T(8,128)(2,1)}, bf16[392,512]{1,0:T(8,128)(2,1)}, u32[]{:S(2)}, u32[]{:S(2)}) collective-permute-start(bf16[392,512]{1,0:T(8,128)(2,1)} %get-tuple-element.286), channel_id=1, source_target_pairs={{0,1},{1,0},{2,3},{3,2},{4,5},{5,4},{6,7},{7,6},{8,9},{9,8},{10,11... | collective-permute-start | bytes 1204232 | tf_op jit(solution)/shard_map/ppermute | solution.py:1720
  310.2 15.8 %collective-permute-start.47 = (bf16[4,4,512,256]{3,2,1,0:T(8,128)(2,1)}, bf16[4,4,512,256]{3,2,1,0:T(8,128)(2,1)}, u32[]{:S(2)}, u32[]{:S(2)}) collective-permute-start(bf16[4,4,512,256]{3,2,1,0:T(8,128)(2,1)} %get-tuple-element.292), channel_id=1, source_target_pairs={{0,4},{4,0},{8,12},{12,8},{16,20},{20,16},{24,28},{28,24},{1,5},{5... | collective-permute-start | bytes 12582920 | tf_op jit(solution)/shard_map/ppermute | solution.py:183
  310.2 21.2 %collective-permute-start.48 = (bf16[392,512]{1,0:T(8,128)(2,1)S(1)}, bf16[392,512]{1,0:T(8,128)(2,1)S(1)}, u32[]{:S(2)}, u32[]{:S(2)}) collective-permute-start(bf16[392,512]{1,0:T(8,128)(2,1)S(1)} %copy-done.56), channel_id=1, source_target_pairs={{0,2},{1,3},{2,0},{3,1},{4,6},{5,7},{6,4},{7,5},{8,10},{9,11},{10,... | collective-permute-start | bytes 1204232 | tf_op jit(solution)/shard_map/ppermute | solution.py:1741
  331.4 15.0 %collective-permute-start.49 = (bf16[4,512,256]{2,1,0:T(8,128)(2,1)}, bf16[4,512,256]{2,1,0:T(8,128)(2,1)S(1)}, u32[]{:S(2)}, u32[]{:S(2)}) collective-permute-start(bf16[4,512,256]{2,1,0:T(8,128)(2,1)} %twin_sum.3), channel_id=1, source_target_pairs={{0,16},{4,12},{8,24},{12,4},{16,0},{20,28},{24,8},{28,20},{1,17},{... | collective-permute-start | bytes 3145736 | tf_op jit(solution)/shard_map/ppermute | solution.py:1753
  366.6 36.8 %all-to-all-start.14 = ((bf16[32,2,5120]{2,1,0:T(2,128)(2,1)}), bf16[32,2,5120]{2,1,0:T(2,128)(2,1)S(1)}, u32[]{:S(2)}, u32[]{:S(2)}) async-start(bf16[32,2,5120]{2,1,0:T(2,128)(2,1)} %broadcast_in_dim.76), calls=%async_computation.14 | async-start | bytes 1310720 | tf_op jit(solution)/shard_map/all_to_all | solution.py:121
  373.2 29.5 %collective-permute-start.50 = (bf16[4,512,256]{2,1,0:T(8,128)(2,1)}, bf16[4,512,256]{2,1,0:T(8,128)(2,1)S(1)}, u32[]{:S(2)}, u32[]{:S(2)}) collective-permute-start(bf16[4,512,256]{2,1,0:T(8,128)(2,1)} %get-tuple-element.313), channel_id=1, source_target_pairs={{0,8},{4,12},{8,0},{12,4},{16,24},{20,28},{24,16},{28,20},{1,9},{5... | collective-permute-start | bytes 3145736 | tf_op jit(solution)/shard_map/ppermute | solution.py:187
  374.9 28.5 %collective-permute-start.51 = (bf16[4,512,256]{2,1,0:T(8,128)(2,1)}, bf16[4,512,256]{2,1,0:T(8,128)(2,1)S(1)}, u32[]{:S(2)}, u32[]{:S(2)}) collective-permute-start(bf16[4,512,256]{2,1,0:T(8,128)(2,1)} %get-tuple-element.314), channel_id=1, source_target_pairs={{0,16},{4,20},{8,24},{12,28},{16,0},{20,4},{24,8},{28,12},{1,17},{... | collective-permute-start | bytes 3145736 | tf_op jit(solution)/shard_map/ppermute | solution.py:187
  376.4 26.2 %collective-permute-start.52 = (bf16[392,512]{1,0:T(8,128)(2,1)}, bf16[392,512]{1,0:T(8,128)(2,1)S(1)}, u32[]{:S(2)}, u32[]{:S(2)}) collective-permute-start(bf16[392,512]{1,0:T(8,128)(2,1)} %get-tuple-element.318), channel_id=1, source_target_pairs={{0,3},{1,2},{2,1},{3,0},{4,7},{5,6},{6,5},{7,4},{8,11},{9,10},{10,... | collective-permute-start | bytes 1204232 | tf_op jit(solution)/shard_map/ppermute | solution.py:1765
  403.5 10.4 %collective-permute-start.56 = (bf16[4,1,504,256]{3,2,1,0:T(8,128)(2,1)}, bf16[4,1,504,256]{3,2,1,0:T(8,128)(2,1)S(1)}, u32[]{:S(2)}, u32[]{:S(2)}) collective-permute-start(bf16[4,1,504,256]{3,2,1,0:T(8,128)(2,1)} %get-tuple-element.327), channel_id=1, source_target_pairs={{0,4},{4,0},{8,12},{12,8},{16,20},{20,16},{24,28},{28,24},{1,5},{5... | collective-permute-start | bytes 3096584 | tf_op jit(solution)/shard_map/ppermute | solution.py:183
  409.1 20.3 %collective-permute-start.53 = (bf16[512,256]{1,0:T(8,128)(2,1)}, bf16[512,256]{1,0:T(8,128)(2,1)S(1)}, u32[]{:S(2)}, u32[]{:S(2)}) collective-permute-start(bf16[512,256]{1,0:T(8,128)(2,1)} %get-tuple-element.323), channel_id=1, source_target_pairs={{0,1},{1,0},{2,3},{3,2},{4,5},{5,4},{6,7},{7,6},{8,9},{9,8},{10,11... | collective-permute-start | bytes 786440 | tf_op jit(solution)/shard_map/ppermute | solution.py:191
  411.5 21.6 %collective-permute-start.54 = (bf16[512,256]{1,0:T(8,128)(2,1)}, bf16[512,256]{1,0:T(8,128)(2,1)S(1)}, u32[]{:S(2)}, u32[]{:S(2)}) collective-permute-start(bf16[512,256]{1,0:T(8,128)(2,1)} %get-tuple-element.324), channel_id=1, source_target_pairs={{0,2},{1,3},{2,0},{3,1},{4,6},{5,7},{6,4},{7,5},{8,10},{9,11},{10,... | collective-permute-start | bytes 786440 | tf_op jit(solution)/shard_map/ppermute | solution.py:191
  412.0 21.1 %collective-permute-start.55 = (bf16[512,256]{1,0:T(8,128)(2,1)}, bf16[512,256]{1,0:T(8,128)(2,1)S(1)}, u32[]{:S(2)}, u32[]{:S(2)}) collective-permute-start(bf16[512,256]{1,0:T(8,128)(2,1)} %get-tuple-element.325), channel_id=1, source_target_pairs={{0,3},{1,2},{2,1},{3,0},{4,7},{5,6},{6,5},{7,4},{8,11},{9,10},{10,... | collective-permute-start | bytes 786440 | tf_op jit(solution)/shard_map/ppermute | solution.py:191
  416.7 9.7 %collective-permute-start.57 = (bf16[1,504,256]{2,1,0:T(8,128)(2,1)}, bf16[1,504,256]{2,1,0:T(8,128)(2,1)S(1)}, u32[]{:S(2)}, u32[]{:S(2)}) collective-permute-start(bf16[1,504,256]{2,1,0:T(8,128)(2,1)} %twin_sum.4), channel_id=1, source_target_pairs={{0,16},{4,12},{8,24},{12,4},{16,0},{20,28},{24,8},{28,20},{1,17},{... | collective-permute-start | bytes 774152 | tf_op jit(solution)/shard_map/ppermute | solution.py:179
  433.1 15.1 %collective-permute-start.58 = (bf16[1,504,256]{2,1,0:T(8,128)(2,1)}, bf16[1,504,256]{2,1,0:T(8,128)(2,1)S(1)}, u32[]{:S(2)}, u32[]{:S(2)}) collective-permute-start(bf16[1,504,256]{2,1,0:T(8,128)(2,1)} %get-tuple-element.331), channel_id=1, source_target_pairs={{0,8},{4,12},{8,0},{12,4},{16,24},{20,28},{24,16},{28,20},{1,9},{5... | collective-permute-start | bytes 774152 | tf_op jit(solution)/shard_map/ppermute | solution.py:187
  434.6 13.6 %collective-permute-start.59 = (bf16[1,504,256]{2,1,0:T(8,128)(2,1)}, bf16[1,504,256]{2,1,0:T(8,128)(2,1)S(1)}, u32[]{:S(2)}, u32[]{:S(2)}) collective-permute-start(bf16[1,504,256]{2,1,0:T(8,128)(2,1)} %get-tuple-element.332), channel_id=1, source_target_pairs={{0,16},{4,20},{8,24},{12,28},{16,0},{20,4},{24,8},{28,12},{1,17},{... | collective-permute-start | bytes 774152 | tf_op jit(solution)/shard_map/ppermute | solution.py:187
  452.9 11.3 %collective-permute-start.60 = (bf16[504,256]{1,0:T(8,128)(2,1)S(1)}, bf16[504,256]{1,0:T(8,128)(2,1)S(1)}, u32[]{:S(2)}, u32[]{:S(2)}) collective-permute-start(bf16[504,256]{1,0:T(8,128)(2,1)S(1)} %convert_element_type.65), channel_id=1, source_target_pairs={{0,2},{1,3},{2,0},{3,1},{4,6},{5,7},{6,4},{7,5},{8,10},{9,11},{10,... | collective-permute-start | bytes 774152 | tf_op jit(solution)/shard_map/ppermute | solution.py:1789
  475.5 15.0 %collective-permute-start.63 = (bf16[4,512,256]{2,1,0:T(8,128)(2,1)}, bf16[4,512,256]{2,1,0:T(8,128)(2,1)S(1)}, u32[]{:S(2)}, u32[]{:S(2)}) collective-permute-start(bf16[4,512,256]{2,1,0:T(8,128)(2,1)} %twin_sum.5), channel_id=1, source_target_pairs={{0,16},{4,12},{8,24},{12,4},{16,0},{20,28},{24,8},{28,20},{1,17},{... | collective-permute-start | bytes 3145736 | tf_op jit(solution)/shard_map/ppermute | solution.py:179
  491.5 45.9 %all-to-all-start.17 = ((bf16[4,392,512]{2,1,0:T(8,128)(2,1)}), bf16[4,392,512]{2,1,0:T(8,128)(2,1)S(1)}, u32[]{:S(2)}, u32[]{:S(2)}) async-start(bf16[4,392,512]{2,1,0:T(8,128)(2,1)} %mix_back.3), calls=%async_computation.17 | async-start | bytes 3211264 | tf_op jit(solution)/shard_map/all_to_all | solution.py:142
  499.7 25.1 %collective-permute-start.64 = (bf16[4,512,256]{2,1,0:T(8,128)(2,1)}, bf16[4,512,256]{2,1,0:T(8,128)(2,1)S(1)}, u32[]{:S(2)}, u32[]{:S(2)}) collective-permute-start(bf16[4,512,256]{2,1,0:T(8,128)(2,1)} %get-tuple-element.349), channel_id=1, source_target_pairs={{0,8},{4,12},{8,0},{12,4},{16,24},{20,28},{24,16},{28,20},{1,9},{5... | collective-permute-start | bytes 3145736 | tf_op jit(solution)/shard_map/ppermute | solution.py:187
  500.2 24.6 %collective-permute-start.65 = (bf16[4,512,256]{2,1,0:T(8,128)(2,1)}, bf16[4,512,256]{2,1,0:T(8,128)(2,1)}, u32[]{:S(2)}, u32[]{:S(2)}) collective-permute-start(bf16[4,512,256]{2,1,0:T(8,128)(2,1)} %get-tuple-element.350), channel_id=1, source_target_pairs={{0,16},{4,20},{8,24},{12,28},{16,0},{20,4},{24,8},{28,12},{1,17},{... | collective-permute-start | bytes 3145736 | tf_op jit(solution)/shard_map/ppermute | solution.py:187
  530.1 12.0 %collective-permute-start.66 = (bf16[512,256]{1,0:T(8,128)(2,1)}, bf16[512,256]{1,0:T(8,128)(2,1)S(1)}, u32[]{:S(2)}, u32[]{:S(2)}) collective-permute-start(bf16[512,256]{1,0:T(8,128)(2,1)} %get-tuple-element.367), channel_id=1, source_target_pairs={{0,1},{1,0},{2,3},{3,2},{4,5},{5,4},{6,7},{7,6},{8,9},{9,8},{10,11... | collective-permute-start | bytes 786440 | tf_op jit(solution)/shard_map/ppermute | solution.py:191
  532.1 21.2 %collective-permute-start.67 = (bf16[512,256]{1,0:T(8,128)(2,1)}, bf16[512,256]{1,0:T(8,128)(2,1)S(1)}, u32[]{:S(2)}, u32[]{:S(2)}) collective-permute-start(bf16[512,256]{1,0:T(8,128)(2,1)} %get-tuple-element.368), channel_id=1, source_target_pairs={{0,2},{1,3},{2,0},{3,1},{4,6},{5,7},{6,4},{7,5},{8,10},{9,11},{10,... | collective-permute-start | bytes 786440 | tf_op jit(solution)/shard_map/ppermute | solution.py:191
  534.5 18.8 %collective-permute-start.68 = (bf16[512,256]{1,0:T(8,128)(2,1)}, bf16[512,256]{1,0:T(8,128)(2,1)S(1)}, u32[]{:S(2)}, u32[]{:S(2)}) collective-permute-start(bf16[512,256]{1,0:T(8,128)(2,1)} %get-tuple-element.369), channel_id=1, source_target_pairs={{0,3},{1,2},{2,1},{3,0},{4,7},{5,6},{6,5},{7,4},{8,11},{9,10},{10,... | collective-permute-start | bytes 786440 | tf_op jit(solution)/shard_map/ppermute | solution.py:191
  (72 other events, 619.4 us)

commit v2 on v1

--- a/solution.py
+++ b/solution.py
@@ -237,8 +237,7 @@
     return full.reshape(QUADS, LANES, 2 * QUADS, 256).transpose(2, 0, 1, 3)
 
 
-def scatter_square(kept, sent):
-    g = jnp.stack([kept, sent], 1).reshape((8,) + kept.shape[1:])
+def scatter_square(g):
     full = g.transpose(1, 2, 0, 3).reshape(QUADS * LANES, 2 * QUADS * 256)
     full = pack_channels(pack_channels(full).T)
     part = lax.psum_scatter(full, "dp", scatter_dimension=0, tiled=True)
@@ -253,8 +252,7 @@
     return spread_channels(full.T).reshape(-1, 2 * QUADS, 256).transpose(1, 0, 2)
 
 
-def scatter_kernel(kept, sent):
-    g = jnp.stack([kept, sent], 1).reshape((8,) + kept.shape[1:])
+def scatter_kernel(g):
     full = pack_channels(g.transpose(1, 0, 2).reshape(g.shape[1], -1)).T
     part = lax.psum_scatter(full, "dp", scatter_dimension=0, tiled=True).astype(f32)
     return lax.psum(part, "mp")
@@ -489,6 +487,42 @@
     )(index_scalar("dp"), x, g, a, sums, norms, grad_sums)
 
 
+def all_grads_kernel(
+    k, count, x_ref, g_ref, a_ref, sums_ref, norms_ref, grad_sums_ref, grad_ref, out_ref
+):
+    grad = norm_back(
+        g_ref[...], a_ref[...], sums_ref[...], norms_ref[...], k, grad_sums_ref[...], count
+    ).astype(bf16)
+    grad_ref[...] = grad
+    turned = grad.T
+    for q in range(QUADS):
+        result = dot(turned, x_ref[q])
+        for i in range(2):
+            out_ref[2 * q + i, 0] = result[:, 256 * i : 256 * (i + 1)].astype(bf16)
+
+
+def all_grads(x, g, a, sums, norms, k, grad_sums, count):
+    rows, width = a.shape
+    return pl.pallas_call(
+        functools.partial(all_grads_kernel, k, count),
+        grid=(QUADS,),
+        in_specs=[
+            pl.BlockSpec(x.shape, lambda m: (0, 0, 0)), quad_spec(rows), quad_spec(rows),
+            quad_spec(2), quad_spec(6), quad_spec(2),
+        ],
+        out_specs=[
+            quad_spec(rows), pl.BlockSpec((8, 1, LANES, 256), lambda m: (0, m, 0, 0)),
+        ],
+        out_shape=[
+            jax.ShapeDtypeStruct((rows, width), bf16),
+            jax.ShapeDtypeStruct((8, QUADS, LANES, 256), bf16),
+        ],
+        compiler_params=params(),
+        cost_estimate=BRIEF,
+        name="all_grads",
+    )(x, g, a, sums, norms, grad_sums)
+
+
 def kept_grads_kernel(me_ref, x_ref, g_ref, out_ref):
     piece_grads(me_ref, x_ref, g_ref[...], 0, out_ref)
 
@@ -555,56 +589,96 @@
     )(index_scalar("dp"), kept, got, kept, got, corner)
 
 
-def side_sums_kernel(me_ref, a_ref, b_ref, across_ref, up_ref, out_ref, *parts):
+def side_sums_kernel(me_ref, a_ref, b_ref, across_ref, up_ref, more_ref, out_ref, *parts):
     value = (
         a_ref[...].astype(f32)
         + b_ref[...].astype(f32)
         + across_ref[...].astype(f32)
         + up_ref[...].astype(f32)
     )
+    rows = value.shape[0]
 
     @pl.when(pl.program_id(0) == 0)
     def _():
-        out_ref[...] = value
+        out_ref[:rows, :] = value
+        out_ref[rows:, :] = more_ref[...].astype(f32)
 
     for k, part in enumerate(parts):
 
         @pl.when(pl.program_id(0) == k + 1)
         def _(part=part):
-            part[...] = value.astype(bf16)
-
-
-def side_sums(kept, got, across, up):
+            part[:rows, :] = value.astype(bf16)
+            part[rows:, :] = more_ref[...]
+
+
+def side_sums(kept, got, across, up, more):
     _, n, *shape = kept.shape
-    me = index_scalar("mp") if n > 1 else jnp.zeros((1,), jnp.int32)
+    rows = shape[0] + more.shape[1]
     entry = pl.BlockSpec((None, None, *shape), lambda k, me: (0, me[0] ^ k, 0, 0))
     block = pl.BlockSpec((None, *shape), lambda k, me: (me[0] ^ k, 0, 0))
     spec = pltpu.PrefetchScalarGridSpec(
         num_scalar_prefetch=1,
         grid=(n,),
-        in_specs=[entry, entry, block, block],
-        out_specs=[pl.BlockSpec(tuple(shape), lambda k, me: (0, 0))] * n,
+        in_specs=[
+            entry, entry, block, block,
+            pl.BlockSpec((None,) + more.shape[1:], lambda k, me: (me[0] ^ k, 0, 0)),
+        ],
+        out_specs=[pl.BlockSpec((rows, 256), lambda k, me: (0, 0))] * n,
     )
     return pl.pallas_call(
         side_sums_kernel,
         grid_spec=spec,
-        out_shape=[jax.ShapeDtypeStruct(shape, f32)] + [jax.ShapeDtypeStruct(shape, bf16)] * (n - 1),
+        out_shape=[jax.ShapeDtypeStruct((rows, 256), f32)]
+        + [jax.ShapeDtypeStruct((rows, 256), bf16)] * (n - 1),
         compiler_params=params(),
         cost_estimate=BRIEF,
         name="side_sums",
-    )(me, kept, got, across, up)
-
-
-def own_square_kernel(me_ref, own_ref, *refs):
-    out_ref, square_ref = refs[-2:]
-    value = own_ref[...]
-    for part in refs[:-2]:
-        value = value + part[...].astype(f32)
+    )(index_scalar("mp"), kept, got, across, up, more)
+
+
+def without_padding(value, odd):
     row = lax.broadcasted_iota(jnp.int32, (QUAD, 1), 0)
     value = jnp.where(row < HALF, value[:QUAD], value[GAP:])
-    value = jnp.where(me_ref[0] % 2 == 1, value[:, 256 - HALF :], value[:, :HALF])
+    return jnp.where(odd, value[:, 256 - HALF :], value[:, :HALF])
+
+
+def own_plain_kernel(me_ref, own_ref, out_ref, square_ref):
+    value = without_padding(own_ref[...].astype(f32), me_ref[0] % 2 == 1)
     out_ref[...] = value
-    square_ref[...] = jnp.sum(jnp.sum(value * value, 1, keepdims=True), 0, keepdims=True)
+    square_ref[...] = square_sum(value)
+
+
+def own_plain(v):
+    return pl.pallas_call(
+        own_plain_kernel,
+        in_specs=[SCALAR, pl.BlockSpec(memory_space=pltpu.VMEM)],
+        out_shape=[
+            jax.ShapeDtypeStruct((QUAD, HALF), f32), jax.ShapeDtypeStruct((1, 1), f32),
+        ],
+        compiler_params=params(),
+        cost_estimate=BRIEF,
+        name="own_plain",
+    )(index_scalar("dp"), v)
+
+
+def gradient_lane(i):
+    lane = lax.broadcasted_iota(jnp.int32, (2, 128), 1)
+    row = lax.broadcasted_iota(jnp.int32, (2, 128), 0)
+    return (lane == i) & (row == 1)
+
+
+def own_square_kernel(me_ref, own_ref, *refs):
+    out_ref, more_ref, squares_ref = refs[-3:]
+    value = own_ref[...]
+    for part in refs[:-3]:
+        value = value + part[...].astype(f32)
+    more = value[LANES:]
+    value = without_padding(value[:LANES], me_ref[0] % 2 == 1)
+    out_ref[...] = value
+    more_ref[...] = more.astype(bf16)
+    squares_ref[...] = jnp.where(gradient_lane(0), square_sum(value), 0.0) + jnp.where(
+        gradient_lane(1), square_sum(more), 0.0
+    )
 
 
 def own_square(parts):
@@ -612,7 +686,9 @@
         own_square_kernel,
         in_specs=[SCALAR] + [pl.BlockSpec(memory_space=pltpu.VMEM)] * len(parts),
         out_shape=[
-            jax.ShapeDtypeStruct((QUAD, HALF), f32), jax.ShapeDtypeStruct((1, 1), f32),
+            jax.ShapeDtypeStruct((QUAD, HALF), f32),
+            jax.ShapeDtypeStruct((parts[0].shape[0] - LANES, 256), bf16),
+            jax.ShapeDtypeStruct((2, 128), f32),
         ],
         compiler_params=params(),
         cost_estimate=BRIEF,
@@ -892,8 +968,8 @@
 
 
 def conv_back_kernel(
-    crops, count, me_ref, g_ref, a2_ref, sums2_ref, grad_sums_ref, a_ref, sums_ref, norms_ref, w_ref,
-    out_ref, kept_ref, sent_ref, stats_ref,
+    crops, count, g_ref, a2_ref, sums2_ref, grad_sums_ref, a_ref, sums_ref, norms_ref, w_ref,
+    out_ref, grads_ref, stats_ref,
     pad_ref, moved_ref, pad_x_ref, moved_x_ref, wide_ref, act_ref, hold_ref,
 ):
     @pl.when(pl.program_id(0) == 0)
@@ -954,29 +1030,26 @@
         nothing = jnp.zeros((GROUP, 128), f32)
         even = even + jnp.concatenate([nothing, across[:, :128]], 1)
         odd = odd + jnp.concatenate([across[:, 128:], nothing], 1)
-        twin = me_ref[0] % 2 == 1
-        hold_ref[0, pl.ds(GROUP * tap, GROUP), :] = jnp.where(twin, odd, even)
-        hold_ref[1, pl.ds(GROUP * tap, GROUP), :] = jnp.where(twin, even, odd)
-    kept_ref[0, 0] = hold_ref[0].astype(bf16)
-    sent_ref[0, 0] = hold_ref[1].astype(bf16)
+        hold_ref[0, pl.ds(GROUP * tap, GROUP), :] = even
+        hold_ref[1, pl.ds(GROUP * tap, GROUP), :] = odd
+    grads_ref[:, : 9 * GROUP, :] = hold_ref[...].astype(bf16)
+    grads_ref[:, 9 * GROUP :, :] = jnp.zeros((2, LANES - 9 * GROUP, 256), bf16)
 
 
 def conv_back(g, a2, sums2, grad_sums, a, sums, norms, windows, count):
     rows, width = a.shape
     crops = rows // PIXELS
-    piece = pl.BlockSpec((1, 1, 9 * GROUP, 256), lambda q, me: (q ^ (me[0] // 2), 0, 0, 0))
-
-    def quad(n):
-        return pl.BlockSpec((n, LANES), lambda q, me: (0, q))
-
-    spec = pltpu.PrefetchScalarGridSpec(
-        num_scalar_prefetch=1,
+    return pl.pallas_call(
+        functools.partial(conv_back_kernel, crops, count),
         grid=(QUADS,),
         in_specs=[
-            quad(rows), quad(rows), quad(2), quad(2), quad(rows), quad(2), quad(6),
-            pl.BlockSpec((1, 3, 9, 256, 256), lambda q, me: (q, 0, 0, 0, 0)),
-        ],
-        out_specs=[quad(rows), piece, piece, quad(2)],
+            quad_spec(rows), quad_spec(rows), quad_spec(2), quad_spec(2), quad_spec(rows),
+            quad_spec(2), quad_spec(6),
+            pl.BlockSpec((1, 3, 9, 256, 256), lambda q: (q, 0, 0, 0, 0)),
+        ],
+        out_specs=[
+            quad_spec(rows), pl.BlockSpec((2, LANES, 256), lambda q: (q, 0, 0)), quad_spec(2),
+        ],
         scratch_shapes=[
             pltpu.VMEM((2 * PITCH + 256 * crops, LANES), f32),
             pltpu.VMEM((3, 256 * crops, LANES), bf16),
@@ -986,20 +1059,15 @@
             pltpu.VMEM((rows, LANES), f32),
             pltpu.VMEM((2, 9 * GROUP, 256), f32),
         ],
-    )
-    return pl.pallas_call(
-        functools.partial(conv_back_kernel, crops, count),
-        grid_spec=spec,
         out_shape=[
             jax.ShapeDtypeStruct((rows, width), bf16),
-            jax.ShapeDtypeStruct((QUADS, 1, 9 * GROUP, 256), bf16),
-            jax.ShapeDtypeStruct((QUADS, 1, 9 * GROUP, 256), bf16),
+            jax.ShapeDtypeStruct((8, LANES, 256), bf16),
             jax.ShapeDtypeStruct((2, width), f32),
         ],
         compiler_params=params(),
         cost_estimate=BRIEF,
         name="conv_back",
-    )(index_scalar("dp"), g, a2, sums2, grad_sums, a, sums, norms, windows)
+    )(g, a2, sums2, grad_sums, a, sums, norms, windows)
 
 
 def squeeze_weight(se_ref, d):
@@ -1399,20 +1467,16 @@
     )(index_scalar("mp"), small, summary, embed_grad, score_grad, unit)
 
 
-def own_kernel_kernel(me_ref, v_ref, out_ref, square_ref):
+def own_kernel_kernel(me_ref, v_ref, out_ref):
     value = v_ref[: 9 * GROUP].astype(f32)
-    value = jnp.where(me_ref[0] % 2 == 1, value[:, 256 - HALF :], value[:, :HALF])
-    out_ref[...] = value
-    square_ref[...] = square_sum(value)
+    out_ref[...] = jnp.where(me_ref[0] % 2 == 1, value[:, 256 - HALF :], value[:, :HALF])
 
 
 def own_kernel(v):
     return pl.pallas_call(
         own_kernel_kernel,
         in_specs=[SCALAR, pl.BlockSpec(memory_space=pltpu.VMEM)],
-        out_shape=[
-            jax.ShapeDtypeStruct((9 * GROUP, HALF), f32), jax.ShapeDtypeStruct((1, 1), f32),
-        ],
+        out_shape=jax.ShapeDtypeStruct((9 * GROUP, HALF), f32),
         compiler_params=params(),
         cost_estimate=BRIEF,
         name="own_kernel",
@@ -1438,8 +1502,7 @@
 
 
 def squares_kernel(
-    n_dp, n_mp, weights_ref, norms_ref, small_ref, expand_ref, kernel_ref,
-    g1_ref, g2_ref, g3_ref, out_ref,
+    n_dp, n_mp, weights_ref, norms_ref, small_ref, expand_ref, g1_ref, g2_ref, g3_ref, out_ref,
 ):
     lane = lax.broadcasted_iota(jnp.int32, (1, 128), 1)
 
@@ -1451,7 +1514,7 @@
         portions = portions + at(i, 1.0 / n_dp)
     weights = weights_ref[...] * portions
     small = small_ref[...]
-    grads = at(1, kernel_ref[...] / n_mp) + at(4, expand_ref[...])
+    grads = at(4, expand_ref[...])
     for i, k in enumerate((2, 3, 5, 6)):
         grads = grads + at(k, small[:, i : i + 1] / n_dp)
     everywhere = 1.0 / (n_dp * n_mp)
@@ -1464,12 +1527,6 @@
     out_ref[1:2, :] = grads
 
 
-def first_gradient():
-    lane = lax.broadcasted_iota(jnp.int32, (2, 128), 1)
-    row = lax.broadcasted_iota(jnp.int32, (2, 128), 0)
-    return (lane == 0) & (row == 1)
-
-
 def squares(n_dp, n_mp, *values):
     return pl.pallas_call(
         functools.partial(squares_kernel, n_dp, n_mp),
@@ -1508,15 +1565,18 @@
 
 
 def lars_kernel(
-    m_ref, squares_ref, weight_ref, gradient_ref, momentum_ref,
-    gains_ref, biases_ref, m_gains_ref, m_biases_ref, g1_ref, g2_ref, g3_ref, *refs
+    first, m_ref, squares_ref, gains_ref, biases_ref, m_gains_ref, m_biases_ref, g1_ref, g2_ref, g3_ref, *refs
 ):
     norm_squares = squares_ref[...]
-    n = (len(refs) - 3) // 3
-    out = refs[2 * n :]
-    out[0][...] = step(weight_ref[...], gradient_ref[...], momentum_ref[...], norm_squares, 0)
+    n = (len(refs) - 4 * first - 2) // 3
+    prepared, out = refs[3 * first : 3 * first + 2 * n], refs[3 * first + 2 * n :]
+    for i in range(first):
+        weight, gradient, momentum = (refs[3 * i + j] for j in range(3))
+        out[i][...] = step(weight[...], gradient[...], momentum[...], norm_squares, i)
     for i in range(n):
-        out[1 + i][...] = refs[2 * i + 1][...] + rate_of(norm_squares, i + 1) * refs[2 * i][...]
+        rate = rate_of(norm_squares, first + i)
+        out[first + i][...] = prepared[2 * i + 1][...] + rate * prepared[2 * i][...]
+    n = n + first - 1
     lanes = pl.ds(pl.multiple_of(m_ref[0] * LANES, LANES), LANES)
     for k, ref in enumerate((g1_ref, g2_ref, g3_ref)):
         own = narrow_lanes(ref[:, lanes])
@@ -1529,11 +1589,12 @@
         )
 
 
-def lars(norm_squares, weight, gradient, momentum, norm_values, prepared):
-    shapes = [weight.shape] + [v.shape for v in prepared[::2]] + [norm_values[0].shape] * 2
-    values = [norm_squares, weight, gradient, momentum, *norm_values, *prepared]
-    return pl.pallas_call(
-        lars_kernel,
+def lars(norm_squares, items, norm_values, prepared):
+    shapes = [w.shape for w, _, _ in items] + [v.shape for v in prepared[::2]]
+    shapes += [norm_values[0].shape] * 2
+    values = [norm_squares, *norm_values, *[v for item in items for v in item], *prepared]
+    return pl.pallas_call(
+        functools.partial(lars_kernel, len(items)),
         in_specs=[SCALAR] + [pl.BlockSpec(memory_space=pltpu.VMEM)] * len(values),
         out_shape=[jax.ShapeDtypeStruct(shape, f32) for shape in shapes],
         compiler_params=params(),
@@ -1666,43 +1727,47 @@
     reduced, sums1 = mix(x, reduce_pieces)
     if quick:
         sums1 = sum_axis(sums1, "dp")
-        sums1, expand_low, se_low = tie(sums1, expand_low, se_low)
-        expand_low = spread(expand_low, "mp").reshape(-1, 256)
+        sums1, se_low = tie(sums1, se_low)
         se_across, se_up = gather_sides(se_low)
         sums1 = sum_axis(sums1, "mp")
         sums1, expand_low, se_across, se_up = tie(sums1, expand_low, se_across, se_up)
+        expand_low = spread(expand_low, "mp").reshape(-1, 256)
         se_corner = gather_corner(se_across, se_up)
-        across, up = gather_sides(expand_low)
         y_grad_parts = [
             lax.dynamic_index_in_dim(y_grad_blocks, m_index ^ k, 0, keepdims=False) for k in range(QUADS)
         ]
-        sums1, bundle, y_grad_parts[1] = tie(sums1, bundle, y_grad_parts[1])
-        y_grad_parts[1] = lax.ppermute(y_grad_parts[1], "mp", flips("mp", 1))
-        bundle = spread(bundle, "mp").reshape(-1, 256)
     else:
         sums1 = total(sums1)
     grouped, sums2 = conv(reduced, sums1, norms, windows, count)
     if quick:
-        sums2, bundle, across, up, se_corner, y_grad_parts[1] = tie(
-            sums2, bundle, across, up, se_corner, y_grad_parts[1]
-        )
+        sums2, se_corner = tie(sums2, se_corner)
         se_pieces = gather_twins(se_low, se_across, se_up, se_corner)
-        corner = gather_corner(across, up)
-        sums2 = jnp.sum(spread(sums2, "dp"), 0)
-        sums2, corner = tie(sums2, corner)
-        expand_pieces = gather_twins(expand_low, across, up, corner)
-        sums2 = jnp.sum(spread(sums2, "mp"), 0)
+        sums2 = sum_axis(sums2, "dp")
+        sums2, expand_low = tie(sums2, expand_low)
+        across, up = gather_sides(expand_low)
+        sums2 = sum_axis(sums2, "mp")
     else:
         sums2 = total(sums2)
     if quick:
-        sums2, y_grad_parts[2] = tie(sums2, y_grad_parts[2])
+        sums2, bundle, y_grad_parts[1], y_grad_parts[2] = tie(
+            sums2, bundle, y_grad_parts[1], y_grad_parts[2]
+        )
+        bundle = spread(bundle, "mp").reshape(-1, 256)
+        y_grad_parts[1] = lax.ppermute(y_grad_parts[1], "mp", flips("mp", 1))
         y_grad_parts[2] = lax.ppermute(y_grad_parts[2], "mp", flips("mp", 2))
     gated, pooled, squeezed, squeeze_act, gates = gate(grouped, sums2, norms, se_pieces, count)
+    if quick:
+        gated, across, up = tie(gated, across, up)
+        corner = gather_corner(across, up)
+        corner, bundle = tie(corner, bundle)
+        expand_pieces = gather_twins(expand_low, across, up, corner)
     expanded, sums3 = mix(gated, expand_pieces)
     if quick:
         sums3, bundle = tie(sums3, bundle)
         sums3 = jnp.sum(spread(sums3, "dp"), 0)
-        sums3, bundle, y_grad_parts[2] = tie(sums3, bundle, y_grad_parts[2])
+        sums3, bundle, y_grad_parts[1], y_grad_parts[2] = tie(
+            sums3, bundle, y_grad_parts[1], y_grad_parts[2]
+        )
         across, up = gather_sides(bundle)
         sums3 = jnp.sum(spread(sums3, "mp"), 0)
         sums3, across, up = tie(sums3, across, up)
@@ -1739,93 +1804,68 @@
     if quick:
         grad_sums3, y_parts[2], y_parts[3] = tie(grad_sums3, y_parts[2], y_parts[3])
         y_parts[2] = lax.ppermute(y_parts[2], "mp", flips("mp", 2))
-    expanded_grad, expand_sent = sent_grads(
-        gated, joined_grad, expanded, sums3, norms, 2, grad_sums3, count, False
+    expanded_grad, expand_all = all_grads(
+        gated, joined_grad, expanded, sums3, norms, 2, grad_sums3, count
     )
     if quick:
-        expand_got = from_twin(expand_sent)
-    expand_kept = kept_grads(gated, expanded_grad)
+        expand_part = lax.psum_scatter(expand_all, "dp", scatter_dimension=0, tiled=False)
     gated_grad = mix_back(expanded_grad, expand_pieces)
-    if quick:
-        gated_grad, expand_got = tie(gated_grad, expand_got)
-        last = twin_sum(expand_kept, expand_got)
-        last, gated_grad, y_parts[2] = tie(last, gated_grad, y_parts[2])
-        expand_corner = lax.ppermute(last, "dp", diagonal(8))
     act2_grad, grad_sums2, excite_grad, squeeze_grad = gate_back(
         gated_grad, grouped, sums2, norms, gates, squeezed, se_pieces, count
     )
     small = jnp.concatenate([pooled, squeeze_act, squeeze_grad, excite_grad], 1)
     if quick:
-        grad_sums2, expand_corner = tie(grad_sums2, expand_corner)
+        grad_sums2, y_parts[2] = tie(grad_sums2, y_parts[2])
     grad_sums2 = total(grad_sums2)
-    grad_sums2, small = tie(grad_sums2, small)
+    if quick:
+        grad_sums2, small = tie(grad_sums2, small)
     small = gather_all(small)
+    act1_grad, kernel_all, grad_sums1 = conv_back(
+        act2_grad, grouped, sums2, grad_sums2, reduced, sums1, norms, windows, count
+    )
     if quick:
-        grad_sums2, y_parts[3] = tie(grad_sums2, y_parts[3])
+        grad_sums1, kernel_all, small, expand_part = tie(
+            grad_sums1, kernel_all, small, expand_part
+        )
+        expand_part = lax.psum_scatter(expand_part, "mp", scatter_dimension=0, tiled=False)
+    grad_sums1 = total(grad_sums1)
+    if quick:
+        grad_sums1, y_parts[3] = tie(grad_sums1, y_parts[3])
         y_parts[3] = lax.ppermute(y_parts[3], "mp", flips("mp", 3))
-        across, up = corner_sums(expand_kept, expand_got, expand_corner)
-        across, up = scatter_sides(across, up)
-    act1_grad, kernel_kept, kernel_sent, grad_sums1 = conv_back(
-        act2_grad, grouped, sums2, grad_sums2, reduced, sums1, norms, windows, count
-    )
-    if quick:
-        grad_sums1, across, up, kernel_kept, kernel_sent, small, y_parts[3] = tie(
-            grad_sums1, across, up, kernel_kept, kernel_sent, small, y_parts[3]
-        )
-        expand_own, *expand_parts = side_sums(expand_kept, expand_got, across, up)
-        expand_parts = scatter_mp(expand_own, expand_parts)
-        kernel_got = from_twin(kernel_sent)
-        kernel_across, kernel_up = corner_sums(
-            kernel_kept, kernel_got, scatter_corner(kernel_kept, kernel_got)
-        )
-        grad_sums1 = jnp.sum(spread(grad_sums1, "dp"), 0)
-        grad_sums1, expand_parts, kernel_across, kernel_up = tie(
-            grad_sums1, expand_parts, kernel_across, kernel_up
-        )
-        kernel_across, kernel_up = scatter_sides(kernel_across, kernel_up)
-        grad_sums1 = jnp.sum(spread(grad_sums1, "mp"), 0)
-        grad_sums1, kernel_across, kernel_up = tie(grad_sums1, kernel_across, kernel_up)
-        kernel_sum = side_sums(kernel_kept, kernel_got, kernel_across, kernel_up)[0].astype(bf16)
-        kernel_got = lax.ppermute(kernel_sum, "mp", flips("mp", 2))
-    else:
-        grad_sums1 = total(grad_sums1)
     reduced_grad, reduce_sent = sent_grads(
         x, act1_grad, reduced, sums1, norms, 0, grad_sums1, count, True
     )
     if quick:
-        reduced_grad, reduce_sent, kernel_got = tie(reduced_grad, reduce_sent, kernel_got)
+        reduced_grad, reduce_sent, expand_part, kernel_all = tie(
+            reduced_grad, reduce_sent, expand_part, kernel_all
+        )
+        kernel_sum = lax.psum_scatter(kernel_all, "dp", scatter_dimension=0, tiled=False)
         reduce_got = from_twin(reduce_sent)
-        kernel_sum = kernel_sum + kernel_got
-        kernel_got = lax.ppermute(kernel_sum, "mp", flips("mp", 1))
     reduce_kept = kept_grads(x, reduced_grad)
     if quick:
-        reduced_grad, reduce_got, reduce_kept, kernel_got = tie(
-            reduced_grad, reduce_got, reduce_kept, kernel_got
-        )
-        kernel_sum = kernel_sum + kernel_got
+        reduced_grad, reduce_got, reduce_kept = tie(reduced_grad, reduce_got, reduce_kept)
         corner = scatter_corner(reduce_kept, reduce_got)
     x_grad = out_blocks(mix_back(reduced_grad, reduce_pieces, joined_grad))
     if quick:
-        x_grad, corner = tie(x_grad, corner)
+        x_grad, corner, y_parts[3] = tie(x_grad, corner, y_parts[3])
         x_grad = exchange(x_grad)
         across, up = corner_sums(reduce_kept, reduce_got, corner)
-        across, up, small, kernel_sum = tie(across, up, small, kernel_sum)
+        across, up, small = tie(across, up, small)
         across, up = scatter_sides(across, up)
         squeeze_part, excite_part, project_part, protos_part, small_squares = small_grads(
             small, summary, embed_grad, score_grad, unit, prototypes.shape[1]
         )
-        expand_grad, expand_square = own_square(expand_parts)
-        kernel_grad, kernel_square = own_kernel(kernel_sum)
-        across, up, small_squares, expand_square, kernel_square = tie(
-            across, up, small_squares, expand_square, kernel_square
-        )
-        own, *parts = side_sums(reduce_kept, reduce_got, across, up)
+        expand_grad, expand_square = own_plain(expand_part)
+        across, up, small_squares, expand_square, kernel_sum = tie(
+            across, up, small_squares, expand_square, kernel_sum
+        )
+        kernel_sum = kernel_sum.reshape(QUADS, LANES // QUADS, 256)
+        own, *parts = side_sums(reduce_kept, reduce_got, across, up, kernel_sum)
         parts = scatter_mp(own, parts)
         input_grad = out_channels(list(x_grad), channels_here, f32, jnp.zeros((1,), jnp.int32))
         block_output = out_channels(y_parts, channels_here, bf16, index_scalar("mp"))
         prepared = lars_prepare(
             [
-                (w_group.T, kernel_grad, m_group.T),
                 (w_squeeze, squeeze_part, m_squeeze),
                 (w_excite, excite_part, m_excite),
                 (w_expand.T, expand_grad, m_expand.T),
@@ -1835,19 +1875,24 @@
         )
         weight_squares = weight_sums(weights[:7])
         shares = squares(
-            n_dp, n_mp, weight_squares, norms, small_squares, expand_square, kernel_square,
+            n_dp, n_mp, weight_squares, norms, small_squares, expand_square,
             grad_sums1, grad_sums2, grad_sums3,
         )
         parts, input_grad, block_output, shares, *prepared = tie(
             parts, input_grad, block_output, shares, *prepared
         )
-        reduce_grad, reduce_square = own_square(parts)
-        norm_squares = total(jnp.where(first_gradient(), reduce_square, shares))
+        reduce_grad, kernel_sum, big_squares = own_square(parts)
+        kernel_sum = parts_mp(kernel_sum)
+        norm_squares = jnp.sum(spread(shares + big_squares, "dp"), 0)
+        norm_squares, *kernel_sum = tie(norm_squares, *kernel_sum)
+        kernel_grad = own_kernel(in_order(kernel_sum, m_index).reshape(LANES, 256))
+        norm_squares = jnp.sum(spread(norm_squares, "mp"), 0)
         (
             mom_reduce, mom_group, mom_squeeze, mom_excite, mom_expand, mom_project, mom_protos,
             mom_gains, mom_biases,
         ) = lars(
-            norm_squares, w_reduce.T, reduce_grad, m_reduce.T,
+            norm_squares,
+            [(w_reduce.T, reduce_grad, m_reduce.T), (w_group.T, kernel_grad, m_group.T)],
             [bn_gains, bn_biases, m_gains, m_biases, grad_sums1, grad_sums2, grad_sums3], prepared,
         )
         stepped = [
@@ -1860,9 +1905,9 @@
             exchange(out_blocks(jnp.stack(y_parts))), channels_here, bf16
         )
         big_grads = (
-            scatter_square(reduce_kept, reduce_sent),
-            scatter_kernel(kernel_kept[:, 0], kernel_sent[:, 0]),
-            scatter_square(expand_kept, expand_sent),
+            scatter_square(jnp.stack([reduce_kept, reduce_sent], 1).reshape(expand_all.shape)),
+            scatter_kernel(kernel_all[:, : 9 * GROUP]),
+            scatter_square(expand_all),
         )
         stepped, norm_squares = plain_finish(
             small, summary, unit, score_grad, embed_grad, (grad_sums1, grad_sums2, grad_sums3),

time: 594 us -> 565 us (0.951)
  Pallas kernels: 220 us -> 199 us
  blocking collectives: 89.9 us -> 72.5 us
  between operations: 1.97 us -> 15.2 us
  starting transfers between devices: 102 us -> 108 us
    all_to_all x10 -> x8, blocking collectives: 89.9 us -> 72.5 us  [spread(): lax.all_to_all(jnp.broadcast_to(v[None], (n,) + v.shape), axis, split_axi...]
    ppermute x6 -> x3, waiting for transfers between devices: 15 us -> 2.22 us  [scatter_mp(): lax.ppermute(v, 'mp', flips('mp', k + 1))]
    pallas_call x2 -> x4, Pallas kernels: 29.5 us -> 41.8 us  [the longest x1 22.7 us: conv_back(): pl.pallas_call(functools.partial(conv_back_kernel, crops, count), grid=(Q...]
    ppermute x3 -> x1, waiting for transfers between devices: 0.01 us -> 12 us  [scatter_sides(): lax.ppermute(across, 'dp', flips('dp', 2))]
    pallas_call x2 -> x1, Pallas kernels: 16.6 us -> 8.48 us  [sent_grads(): pl.pallas_call(functools.partial(sent_grads_kernel, k, sloped, count), gr...]
    ppermute x3 -> x0, waiting for transfers between devices: 8.13 us -> none  [the longest x1 3.67 us: body(): expand_corner = lax.ppermute(last, 'dp', diagonal(8))]
    reduce_scatter x0 -> x3, waiting for transfers between devices: none -> 7.39 us  [the longest x1 5.33 us: body(): lax.psum_scatter(kernel_all, 'dp', scatter_dimension=0, tiled=False)]
    ppermute x3 -> x6, starting transfers between devices: 5.62 us -> 12.2 us  [parts_mp(): lax.ppermute(v, 'mp', flips('mp', k))]
  transfers between devices with their start and end apart: 79 -> 77, of which waited for: 26 -> 36; matrix products, arithmetic and copies ran while one was open for 5% -> 6% of each run, Pallas kernels for 34% -> 32%
where the time goes in v2:
time: 565 us; the launch traced here: 556 us
  Pallas kernels  199 us (35%)
  waiting for transfers between devices  113 us (20%)
  starting transfers between devices  108 us (19%)
  blocking collectives  72.5 us (13%)
  local copies, waits for them, and re-layouts  26.7 us (5%)
  other arithmetic  20.4 us (4%)
  between operations  15.2 us (3%)
    all_to_all x8, blocking collectives, spread(): lax.all_to_all(jnp.broadcast_to(v[None], (n,) + v.shape), axis, split_axi...  72.5 us
    all_to_all x6, starting transfers between devices, spread(): lax.all_to_all(jnp.broadcast_to(v[None], (n,) + v.shape), axis, split_axi...  26.1 us
    pallas_call x1, Pallas kernels, conv_back(): pl.pallas_call(functools.partial(conv_back_kernel, crops, count), grid=(Q...  22.7 us
    all_to_all x6, waiting for transfers between devices, spread(): lax.all_to_all(jnp.broadcast_to(v[None], (n,) + v.shape), axis, split_axi...  20.6 us
    ppermute x10, waiting for transfers between devices, sum_axis(): v = v + lax.ppermute(v, axis, flips(axis, bit))  19.5 us
    pallas_call x2, Pallas kernels, mix_back(): pl.pallas_call(functools.partial(mix_back_kernel, len(more)), in_specs=[S...  19.1 us
    pallas_call x1, Pallas kernels, head(): pl.pallas_call(functools.partial(head_kernel, width), in_specs=[SCALAR, p...  18.6 us
    ppermute x5, waiting for transfers between devices, gather_sides(): lax.ppermute(v, 'dp', flips('dp', 2))  17.2 us
  transfers between devices with their start and end apart: 77, of which 36 were waited for; matrix products, arithmetic and copies ran while one was open for 6% of the time, Pallas kernels for 32%

profile of v2, /device:TPU:0, one launch (start us, length us, event | category | flops | bytes accessed | tf_op | source)
XLA Modules:
  0.0 555.6 jit_solution(7015975199370403927)
XLA Ops:
  10.7 5.0 collective-permute-start
  20.5 4.9 all-to-all-start
  28.1 2.4 fusion.9
  31.3 2.8 pad_maximum_fusion.1
  34.8 4.8 all-to-all-done
  46.6 3.7 all-to-all-start.1
  50.3 7.1 %dense_windows.1.w_ref = bf16[4,3,9,256,256]{4,3,2,1,0:T(8,128)(2,1)} custom-call(s32[1]{0:T(128)} %bitcast.1.me_ref, bf16[504,256]{1,0:T(8,128)(2,1)} %copy-done.17, bf16[504,256]{1,0:T(8,128)(2,1)} %copy-done.31, bf16[504,256]{1,0:T(8,128)(2,1)} %copy-done.18, bf16[504,256]{1,0:T(8,128)(2,1)} %copy-done.33, ...), custom_call_target="tpu_custom_call" | custom-call | flops 1 | bytes 1 | tf_op jit(solution)/shard_map/dense_windows/pallas_call | solution.py:864
  57.4 11.7 %collective-permute-done.11.refs_2_ = bf16[2048,256]{1,0:T(8,128)(2,1)} collective-permute-done((bf16[2048,256]{1,0:T(8,128)(2,1)S(1)}, bf16[2048,256]{1,0:T(8,128)(2,1)}, u32[]{:S(2)}, u32[]{:S(2)}) %collective-permute-start.11) | collective-permute-done | bytes 1048608 | tf_op jit(solution)/shard_map/ppermute | solution.py:158
  73.8 12.9 %collective-permute-done.15.refs_6_ = bf16[2048,256]{1,0:T(8,128)(2,1)} collective-permute-done((bf16[2048,256]{1,0:T(8,128)(2,1)S(1)}, bf16[2048,256]{1,0:T(8,128)(2,1)}, u32[]{:S(2)}, u32[]{:S(2)}) %collective-permute-start.15) | collective-permute-done | bytes 1048608 | tf_op jit(solution)/shard_map/ppermute | solution.py:163
  89.2 4.1 all-to-all-start.2
  93.4 8.4 %mix.2 = (f32[392,2048]{1,0:T(8,128)}, f32[2,2048]{1,0:T(2,128)}) custom-call(s32[1]{0:T(128)} %bitcast.1.me_ref, bf16[4,392,512]{2,1,0:T(8,128)(2,1)} %copy-done, bf16[2048,256]{1,0:T(8,128)(2,1)} %bitcast.96, bf16[2048,256]{1,0:T(8,128)(2,1)} %collective-permute-done.10.refs_1_, bf16[2048,256]{1,0:T(8,128)(2,1)} %collective-permute-done.11.refs_2_, ...), custom_call_target="tpu_custom_call" | custom-call | flops 1 | bytes 1 | tf_op jit(solution)/shard_map/mix/pallas_call | solution.py:380
  104.6 3.2 collective-permute-done.18
  108.4 3.2 collective-permute-done.19
  117.5 2.9 collective-permute-start.21
  125.4 5.0 all-to-all-start.3
  132.1 12.5 %conv.1 = (bf16[392,2048]{1,0:T(8,128)(2,1)}, f32[2,2048]{1,0:T(2,128)}) custom-call(f32[392,2048]{1,0:T(8,128)} %get-tuple-element.207.a_ref, f32[2,2048]{1,0:T(2,128)} %add.120.sums_ref, f32[6,2048]{1,0:T(8,128)} %bitcast.106, bf16[4,3,9,256,256]{4,3,2,1,0:T(8,128)(2,1)} %dense_windows.1.w_ref), custom_call_target="tpu_custom_call" | custom-call | flops 1 | bytes 1 | tf_op jit(solution)/shard_map/conv/pallas_call | solution.py:943
  151.2 3.2 collective-permute-done.27
  160.6 3.0 collective-permute-start.29
  167.7 6.1 %gate.1 = (bf16[4,392,512]{2,1,0:T(8,128)(2,1)}, bf16[2,2048]{1,0:T(2,128)(2,1)}, f32[2,512]{1,0:T(2,128)}, bf16[2,512]{1,0:T(2,128)(2,1)}, f32[2,2048]{1,0:T(2,128)}) custom-call(s32[1]{0:T(128)} %bitcast.1.me_ref, bf16[392,2048]{1,0:T(8,128)(2,1)} %get-tuple-element.216.a_ref.a2_ref, f32[2,2048]{1,0:T(2,128)} %add.125.sums_ref.sums2_ref, ...), custom_call_target="tpu_custom_call" | custom-call | flops 1 | bytes 1 | tf_op jit(solution)/shard_map/gate/pallas_call | solution.py:1152
  173.8 4.2 collective-permute-done.34.refs_2_
  181.7 4.8 all-to-all-start.4
  187.1 8.7 %all-to-all-done.4 = bf16[4,208,256]{2,1,0:T(8,128)(2,1)} async-done(((bf16[4,208,256]{2,1,0:T(8,128)(2,1)}), bf16[4,208,256]{2,1,0:T(8,128)(2,1)}, u32[]{:S(2)}, u32[]{:S(2)}) %all-to-all-start.4) | async-done | bytes 426016 | tf_op jit(solution)/shard_map/all_to_all | solution.py:97
  196.4 2.4 collective-permute-start.42
  198.9 8.5 %mix.3 = (f32[392,2048]{1,0:T(8,128)}, f32[2,2048]{1,0:T(2,128)}) custom-call(s32[1]{0:T(128)} %bitcast.1.me_ref, bf16[4,392,512]{2,1,0:T(8,128)(2,1)} %get-tuple-element.231.x_ref, bf16[2048,256]{1,0:T(8,128)(2,1)} %bitcast.101, bf16[2048,256]{1,0:T(8,128)(2,1)} %collective-permute-done.36.refs_1_, bf16[2048,256]{1,0:T(8,128)(2,1)} %copy-done.3, ...), custom_call_target="tpu_custom_call" | custom-call | flops 1 | bytes 1 | tf_op jit(solution)/shard_map/mix/pallas_call | solution.py:380
  208.1 8.1 %all_to_all.90 = f32[8,2,2048]{2,1,0:T(2,128)S(1)} all-to-all(f32[8,2,2048]{2,1,0:T(2,128)S(1)} %broadcast_in_dim.56), channel_id=1, replica_groups=mesh['dp'=8,'mp'=4] {'dp'}, dimensions={0} | all-to-all | bytes 262144 | tf_op jit(solution)/shard_map/all_to_all | solution.py:97
  219.7 9.2 %all_to_all.91 = f32[4,2,2048]{2,1,0:T(2,128)S(1)} all-to-all(f32[4,2,2048]{2,1,0:T(2,128)S(1)} %broadcast_in_dim.57), channel_id=1, replica_groups=mesh['dp'=8,'mp'=4] {'mp'}, dimensions={0} | all-to-all | bytes 131072 | tf_op jit(solution)/shard_map/all_to_all | solution.py:97
  230.8 5.1 value.1
  239.3 4.0 all-to-all-start.7
  245.0 8.5 %all-to-all-done.7.summary_ref = bf16[32,2,2048]{2,1,0:T(2,128)(2,1)S(1)} async-done(((bf16[32,2,2048]{2,1,0:T(2,128)(2,1)}), bf16[32,2,2048]{2,1,0:T(2,128)(2,1)S(1)}, u32[]{:S(2)}, u32[]{:S(2)}) %all-to-all-start.7) | async-done | bytes 262176 | tf_op jit(solution)/shard_map/all_to_all | solution.py:121
  257.1 18.6 %head.1 = (f32[1,1]{1,0:T(1,128)}, bf16[64,256]{1,0:T(8,128)(2,1)}, bf16[3072,64]{1,0:T(8,128)(2,1)}, bf16[64,256]{1,0:T(8,128)(2,1)}, f32[64,2048]{1,0:T(8,128)}, /*index=5*/bf16[64,2048]{1,0:T(8,128)(2,1)}) custom-call(s32[1]{0:T(128)} %bitcast.1.me_ref, bf16[32,2,2048]{2,1,0:T(2,128)(2,1)} %copy-done.15, bf16[832,256]{1,0:T(8,128)(2,1)} %bitcast.28.refs_0_, ...), custom_call_target="tpu_custom_call" | custom-call | flops 1 | bytes 1 | tf_op jit(solution)/shard_map/head/pallas_call | solution.py:1334
  275.7 6.7 %value_back.1 = (f32[392,2048]{1,0:T(8,128)}, f32[2,2048]{1,0:T(2,128)}) custom-call(s32[1]{0:T(128)} %bitcast.me_ref.m_ref, s32[1]{0:T(128)} %bitcast.27.first_ref, bf16[4,392,512]{2,1,0:T(8,128)(2,1)} %copy-done, f32[392,2048]{1,0:T(8,128)} %get-tuple-element.236.a_ref, f32[2,2048]{1,0:T(2,128)} %reduce_sum.91.sums_ref, f32[6,2048]{1,0:T(8,128)} %bitcast.109, ...), custom_call_target="tpu_custom_call" | custom-call | flops 1 | bytes 1 | tf_op jit(solution)/shard_map/value_back/pallas_call | solution.py:805
  283.2 7.9 %all_to_all.92 = f32[8,2,2048]{2,1,0:T(2,128)S(1)} all-to-all(f32[8,2,2048]{2,1,0:T(2,128)S(1)} %broadcast_in_dim.59), channel_id=1, replica_groups=mesh['dp'=8,'mp'=4] {'dp'}, dimensions={0} | all-to-all | bytes 262144 | tf_op jit(solution)/shard_map/all_to_all | solution.py:97
  291.2 9.4 %all_to_all.93 = f32[4,2,2048]{2,1,0:T(2,128)S(1)} all-to-all(f32[4,2,2048]{2,1,0:T(2,128)S(1)} %broadcast_in_dim.60), channel_id=1, replica_groups=mesh['dp'=8,'mp'=4] {'mp'}, dimensions={0} | all-to-all | bytes 131072 | tf_op jit(solution)/shard_map/all_to_all | solution.py:97
  301.3 10.0 %all_grads.1 = (bf16[392,2048]{1,0:T(8,128)(2,1)}, bf16[8,4,512,256]{3,2,1,0:T(8,128)(2,1)}) custom-call(bf16[4,392,512]{2,1,0:T(8,128)(2,1)} %get-tuple-element.231.x_ref, f32[392,2048]{1,0:T(8,128)} %get-tuple-element.257.g_ref.refs_8_, f32[392,2048]{1,0:T(8,128)} %get-tuple-element.236.a_ref, f32[2,2048]{1,0:T(2,128)} %reduce_sum.91.sums_ref, ...), custom_call_target="tpu_custom_call" | custom-call | flops 1 | bytes 1 | tf_op jit(solution)/shard_map/all_grads/pallas_call | solution.py:506
  313.0 9.6 %mix_back.2.dh_ref = f32[392,2048]{1,0:T(8,128)} custom-call(s32[1]{0:T(128)} %bitcast.1.me_ref, bf16[392,2048]{1,0:T(8,128)(2,1)} %get-tuple-element.264.g_ref, bf16[2048,256]{1,0:T(8,128)(2,1)} %bitcast.102, bf16[2048,256]{1,0:T(8,128)(2,1)} %collective-permute-done.36.refs_1_, bf16[2048,256]{1,0:T(8,128)(2,1)} %copy-done.3, ...), custom_call_target="tpu_custom_call" | custom-call | flops 1 | bytes 1 | tf_op jit(solution)/shard_map/mix_back/pallas_call | solution.py:428
  322.6 11.0 %gate_back.1 = (f32[392,2048]{1,0:T(8,128)}, f32[2,2048]{1,0:T(2,128)}, bf16[2,2048]{1,0:T(2,128)(2,1)}, bf16[2,512]{1,0:T(2,128)(2,1)}) custom-call(s32[1]{0:T(128)} %bitcast.1.me_ref, f32[392,2048]{1,0:T(8,128)} %mix_back.2.dh_ref, bf16[392,2048]{1,0:T(8,128)(2,1)} %get-tuple-element.216.a_ref.a2_ref, f32[2,2048]{1,0:T(2,128)} %add.125.sums_ref.sums2_ref, ...), custom_call_target="tpu_custom_call" | custom-call | flops 1 | bytes 1 | tf_op jit(solution)/shard_map/gate_back/pallas_call | solution.py:1218
  334.5 9.6 %all_to_all.94 = f32[8,2,2048]{2,1,0:T(2,128)S(1)} all-to-all(f32[8,2,2048]{2,1,0:T(2,128)S(1)} %broadcast_in_dim.61), channel_id=1, replica_groups=mesh['dp'=8,'mp'=4] {'dp'}, dimensions={0} | all-to-all | bytes 262144 | tf_op jit(solution)/shard_map/all_to_all | solution.py:97
  344.8 3.9 all-to-all-start.11
  349.5 5.0 all-to-all-done.11
  356.3 2.6 all-to-all-start.12
  359.2 22.7 %conv_back.1 = (bf16[392,2048]{1,0:T(8,128)(2,1)}, bf16[8,512,256]{2,1,0:T(8,128)(2,1)}, f32[2,2048]{1,0:T(2,128)}) custom-call(f32[392,2048]{1,0:T(8,128)} %get-tuple-element.267.g_ref, bf16[392,2048]{1,0:T(8,128)(2,1)} %get-tuple-element.216.a_ref.a2_ref, f32[2,2048]{1,0:T(2,128)} %add.125.sums_ref.sums2_ref, f32[2,2048]{1,0:T(2,128)} %reduce_sum.95.grad_sums_ref.g2_ref, ...), custom_call_target="tpu_custom_call" | custom-call | flops 1 | bytes 1 | tf_op jit(solution)/shard_map/conv_back/pallas_call | solution.py:1042
  384.2 8.2 %all_to_all.95 = f32[8,2,2048]{2,1,0:T(2,128)S(1)} all-to-all(f32[8,2,2048]{2,1,0:T(2,128)S(1)} %broadcast_in_dim.64), channel_id=1, replica_groups=mesh['dp'=8,'mp'=4] {'dp'}, dimensions={0} | all-to-all | bytes 262144 | tf_op jit(solution)/shard_map/all_to_all | solution.py:97
  392.4 11.6 %all_to_all.96 = f32[4,2,2048]{2,1,0:T(2,128)S(1)} all-to-all(f32[4,2,2048]{2,1,0:T(2,128)S(1)} %broadcast_in_dim.65), channel_id=1, replica_groups=mesh['dp'=8,'mp'=4] {'mp'}, dimensions={0} | all-to-all | bytes 131072 | tf_op jit(solution)/shard_map/all_to_all | solution.py:97
  404.6 8.5 %sent_grads.1 = (bf16[392,2048]{1,0:T(8,128)(2,1)}, bf16[4,4,512,256]{3,2,1,0:T(8,128)(2,1)}) custom-call(s32[1]{0:T(128)} %bitcast.1.me_ref, bf16[4,392,512]{2,1,0:T(8,128)(2,1)} %copy-done, bf16[392,2048]{1,0:T(8,128)(2,1)} %get-tuple-element.276.g_ref, f32[392,2048]{1,0:T(8,128)} %get-tuple-element.207.a_ref, f32[2,2048]{1,0:T(2,128)} %add.120.sums_ref, ...), custom_call_target="tpu_custom_call" | custom-call | flops 1 | bytes 1 | tf_op jit(solution)/shard_map/sent_grads/pallas_call | solution.py:475
  413.7 6.2 %kept_grads.1.a_ref.a1_ref.a2_ref = bf16[4,4,512,256]{3,2,1,0:T(8,128)(2,1)} custom-call(s32[1]{0:T(128)} %bitcast.1.me_ref, bf16[4,392,512]{2,1,0:T(8,128)(2,1)} %copy-done, bf16[392,2048]{1,0:T(8,128)(2,1)} %get-tuple-element.292.g_ref), custom_call_target="tpu_custom_call" | custom-call | flops 1 | bytes 1 | tf_op jit(solution)/shard_map/kept_grads/pallas_call | solution.py:532
  421.2 2.4 twin_sum.1
  426.3 9.5 %mix_back.3 = bf16[4,392,512]{2,1,0:T(8,128)(2,1)} custom-call(s32[1]{0:T(128)} %bitcast.1.me_ref, bf16[392,2048]{1,0:T(8,128)(2,1)} %get-tuple-element.292.g_ref, bf16[2048,256]{1,0:T(8,128)(2,1)} %bitcast.97, bf16[2048,256]{1,0:T(8,128)(2,1)} %collective-permute-done.10.refs_1_, bf16[2048,256]{1,0:T(8,128)(2,1)} %collective-permute-done.11.refs_2_, ...), custom_call_target="tpu_custom_call" | custom-call | flops 1 | bytes 1 | tf_op jit(solution)/shard_map/mix_back/pallas_call | solution.py:428
  435.8 2.4 collective-permute-done.55.refs_3_
  439.6 8.9 %all-to-all-start.15 = ((bf16[4,392,512]{2,1,0:T(8,128)(2,1)}), bf16[4,392,512]{2,1,0:T(8,128)(2,1)S(1)}, u32[]{:S(2)}, u32[]{:S(2)}) async-start(bf16[4,392,512]{2,1,0:T(8,128)(2,1)} %mix_back.3), calls=%async_computation.18 | async-start | bytes 3211264 | tf_op jit(solution)/shard_map/all_to_all | solution.py:142
  448.6 3.8 corner_sums.1
  457.2 4.7 small_grads.1
  461.9 5.3 reduce-scatter.8.cloned.1.call-done
  467.2 12.0 %collective-permute-done.56.across_ref = bf16[4,512,256]{2,1,0:T(8,128)(2,1)S(1)} collective-permute-done((bf16[4,512,256]{2,1,0:T(8,128)(2,1)}, bf16[4,512,256]{2,1,0:T(8,128)(2,1)S(1)}, u32[]{:S(2)}, u32[]{:S(2)}) %collective-permute-start.56) | collective-permute-done | bytes 1048608 | tf_op jit(solution)/shard_map/ppermute | solution.py:187
  480.3 4.5 side_sums.1
  489.2 3.6 weight_sums.1.weights_ref
  492.8 2.8 join_rows.3
  495.6 7.7 %lars_prepare.1 = (f32[2016,126]{1,0:T(8,128)}, f32[2016,126]{1,0:T(8,128)}, f32[504,504]{1,0:T(8,128)}, f32[504,504]{1,0:T(8,128)}, f32[504,252]{1,0:T(8,128)},...) custom-call(f32[2016,126]{1,0:T(8,128)} %refs_0_.1, ...), custom_call_target="tpu_custom_call" | custom-call | flops 1 | bytes 1 | tf_op jit(solution)/shard_map/lars_prepare/pallas_call | solution.py:1558
  506.6 3.4 join_rows.2
  510.0 2.2 collective-permute-done.59.refs_1_
  513.1 2.6 own_square.1
  515.7 4.2 collective-permute-start.61
  523.0 8.5 %all_to_all.97 = f32[8,2,128]{2,1,0:T(2,128)S(1)} all-to-all(f32[8,2,128]{2,1,0:T(2,128)S(1)} %broadcast_in_dim.66), channel_id=1, replica_groups=mesh['dp'=8,'mp'=4] {'dp'}, dimensions={0} | all-to-all | bytes 16384 | tf_op jit(solution)/shard_map/all_to_all | solution.py:97
  532.1 3.4 all-to-all-start.17
  541.6 7.0 %lars.1 = (f32[504,252]{1,0:T(8,128)}, f32[504,252]{1,0:T(8,128)}, f32[2016,126]{1,0:T(8,128)}, f32[504,504]{1,0:T(8,128)}, f32[504,252]{1,0:T(8,128)}, /*index=...) custom-call(s32[1]{0:T(128)} %bitcast.me_ref.m_ref, f32[2,128]{1,0:T(2,128)} %copy-done.39, ...), custom_call_target="tpu_custom_call" | custom-call | flops 1 | bytes 1 | tf_op jit(solution)/shard_map/lars/pallas_call | solution.py:1596
  (315 shorter events, 119.2 us)
Async XLA Ops:
  10.7 29.8 %collective-permute-start = (bf16[512,256]{1,0:T(8,128)(2,1)}, bf16[512,256]{1,0:T(8,128)(2,1)}, u32[]{:S(2)}, u32[]{:S(2)}) collective-permute-start(bf16[512,256]{1,0:T(8,128)(2,1)} %fusion), channel_id=1, source_target_pairs={{0,3},{1,2},{2,1},{3,0},{4,7},{5,6},{6,5},{7,4},{8,11},{9,10},{10,... | collective-permute-start | bytes 786440 | tf_op jit(solution)/shard_map/ppermute | solution.py:146
  15.7 24.7 %collective-permute-start.1 = (bf16[512,256]{1,0:T(8,128)(2,1)}, bf16[512,256]{1,0:T(8,128)(2,1)}, u32[]{:S(2)}, u32[]{:S(2)}) collective-permute-start(bf16[512,256]{1,0:T(8,128)(2,1)} %fusion), channel_id=1, source_target_pairs={{0,2},{1,3},{2,0},{3,1},{4,6},{5,7},{6,4},{7,5},{8,10},{9,11},{10,... | collective-permute-start | bytes 786440 | tf_op jit(solution)/shard_map/ppermute | solution.py:146
  15.8 25.3 %collective-permute-start.2 = (bf16[512,256]{1,0:T(8,128)(2,1)}, bf16[512,256]{1,0:T(8,128)(2,1)}, u32[]{:S(2)}, u32[]{:S(2)}) collective-permute-start(bf16[512,256]{1,0:T(8,128)(2,1)} %fusion), channel_id=1, source_target_pairs={{0,1},{1,0},{2,3},{3,2},{4,5},{5,4},{6,7},{7,6},{8,9},{9,8},{10,11... | collective-permute-start | bytes 786440 | tf_op jit(solution)/shard_map/ppermute | solution.py:146
  16.6 17.5 %collective-permute-start.4 = (bf16[504,256]{1,0:T(8,128)(2,1)S(1)}, bf16[504,256]{1,0:T(8,128)(2,1)S(1)}, u32[]{:S(2)}, u32[]{:S(2)}) collective-permute-start(bf16[504,256]{1,0:T(8,128)(2,1)S(1)} %fusion.2.refs_0_), channel_id=1, source_target_pairs={{0,8},{4,12},{8,0},{12,4},{16,24},{20,28},{24,16},{28,20},{1,9},{5... | collective-permute-start | bytes 774152 | tf_op jit(solution)/shard_map/ppermute | solution.py:158
  18.3 15.9 %collective-permute-start.6 = (bf16[504,256]{1,0:T(8,128)(2,1)S(1)}, bf16[504,256]{1,0:T(8,128)(2,1)}, u32[]{:S(2)}, u32[]{:S(2)}) collective-permute-start(bf16[504,256]{1,0:T(8,128)(2,1)S(1)} %fusion.2.refs_0_), channel_id=1, source_target_pairs={{0,16},{4,20},{8,24},{12,28},{16,0},{20,4},{24,8},{28,12},{1,17},{... | collective-permute-start | bytes 774152 | tf_op jit(solution)/shard_map/ppermute | solution.py:158
  20.5 19.2 %all-to-all-start = ((f32[4,6,504]{2,1,0:T(8,128)}), f32[4,6,504]{2,1,0:T(8,128)S(1)}, u32[]{:S(2)}, u32[]{:S(2)}) async-start(f32[4,6,504]{2,1,0:T(8,128)} %broadcast_in_dim.48), calls=%async_computation | async-start | bytes 131072 | tf_op jit(solution)/shard_map/all_to_all | solution.py:97
  34.1 8.7 %collective-permute-start.3 = (bf16[504,256]{1,0:T(8,128)(2,1)S(1)}, bf16[504,256]{1,0:T(8,128)(2,1)S(1)}, u32[]{:S(2)}, u32[]{:S(2)}) collective-permute-start(bf16[504,256]{1,0:T(8,128)(2,1)S(1)} %fusion.2.refs_0_), channel_id=1, source_target_pairs={{0,4},{4,0},{8,12},{12,8},{16,20},{20,16},{24,28},{28,24},{1,5},{5... | collective-permute-start | bytes 774152 | tf_op jit(solution)/shard_map/ppermute | solution.py:169
  34.3 6.7 %collective-permute-start.8 = (bf16[504,256]{1,0:T(8,128)(2,1)S(1)}, bf16[504,256]{1,0:T(8,128)(2,1)S(1)}, u32[]{:S(2)}, u32[]{:S(2)}) collective-permute-start(bf16[504,256]{1,0:T(8,128)(2,1)S(1)} %broadcast_select_fusion.4), channel_id=1, source_target_pairs={{0,16},{4,12},{8,24},{12,4},{16,0},{20,28},{24,8},{28,20},{1,17},{... | collective-permute-start | bytes 774152 | tf_op jit(solution)/shard_map/ppermute | solution.py:163
  43.6 25.6 %collective-permute-start.11 = (bf16[2048,256]{1,0:T(8,128)(2,1)S(1)}, bf16[2048,256]{1,0:T(8,128)(2,1)}, u32[]{:S(2)}, u32[]{:S(2)}) collective-permute-start(bf16[2048,256]{1,0:T(8,128)(2,1)S(1)} %bitcast.93), channel_id=1, source_target_pairs={{0,8},{4,12},{8,0},{12,4},{16,24},{20,28},{24,16},{28,20},{1,9},{5... | collective-permute-start | bytes 3145736 | tf_op jit(solution)/shard_map/ppermute | solution.py:158
  45.1 25.3 %collective-permute-start.12 = (bf16[2048,256]{1,0:T(8,128)(2,1)S(1)}, bf16[2048,256]{1,0:T(8,128)(2,1)}, u32[]{:S(2)}, u32[]{:S(2)}) collective-permute-start(bf16[2048,256]{1,0:T(8,128)(2,1)S(1)} %bitcast.94), channel_id=1, source_target_pairs={{0,16},{4,20},{8,24},{12,28},{16,0},{20,4},{24,8},{28,12},{1,17},{... | collective-permute-start | bytes 3145736 | tf_op jit(solution)/shard_map/ppermute | solution.py:158
  46.6 41.5 %all-to-all-start.1 = ((bf16[4,392,512]{2,1,0:T(8,128)(2,1)}), bf16[4,392,512]{2,1,0:T(8,128)(2,1)S(1)}, u32[]{:S(2)}, u32[]{:S(2)}) async-start(bf16[4,392,512]{2,1,0:T(8,128)(2,1)} %get-tuple-element.193), calls=%async_computation.1 | async-start | bytes 3211264 | tf_op jit(solution)/shard_map/all_to_all | solution.py:142
  71.7 15.0 %collective-permute-start.15 = (bf16[2048,256]{1,0:T(8,128)(2,1)S(1)}, bf16[2048,256]{1,0:T(8,128)(2,1)}, u32[]{:S(2)}, u32[]{:S(2)}) collective-permute-start(bf16[2048,256]{1,0:T(8,128)(2,1)S(1)} %broadcast_select_fusion.1), channel_id=1, source_target_pairs={{0,16},{4,12},{8,24},{12,4},{16,0},{20,28},{24,8},{28,20},{1,17},{... | collective-permute-start | bytes 3145736 | tf_op jit(solution)/shard_map/ppermute | solution.py:163
  73.3 20.0 %collective-permute-start.10 = (bf16[2048,256]{1,0:T(8,128)(2,1)S(1)}, bf16[2048,256]{1,0:T(8,128)(2,1)}, u32[]{:S(2)}, u32[]{:S(2)}) collective-permute-start(bf16[2048,256]{1,0:T(8,128)(2,1)S(1)} %bitcast.95), channel_id=1, source_target_pairs={{0,4},{4,0},{8,12},{12,8},{16,20},{20,16},{24,28},{28,24},{1,5},{5... | collective-permute-start | bytes 3145736 | tf_op jit(solution)/shard_map/ppermute | solution.py:169
  73.3 20.0 %collective-permute-start.13 = (bf16[2048,256]{1,0:T(8,128)(2,1)}, bf16[2048,256]{1,0:T(8,128)(2,1)}, u32[]{:S(2)}, u32[]{:S(2)}) collective-permute-start(bf16[2048,256]{1,0:T(8,128)(2,1)} %collective-permute-done.11.refs_2_), channel_id=1, source_target_pairs={{0,4},{4,0},{8,12},{12,8},{16,20},{20,16},{24,28},{28,24},{1,5},{5... | collective-permute-start | bytes 3145736 | tf_op jit(solution)/shard_map/ppermute | solution.py:169
  73.8 19.5 %collective-permute-start.14 = (bf16[2048,256]{1,0:T(8,128)(2,1)}, bf16[2048,256]{1,0:T(8,128)(2,1)}, u32[]{:S(2)}, u32[]{:S(2)}) collective-permute-start(bf16[2048,256]{1,0:T(8,128)(2,1)} %collective-permute-done.12.refs_4_), channel_id=1, source_target_pairs={{0,4},{4,0},{8,12},{12,8},{16,20},{20,16},{24,28},{28,24},{1,5},{5... | collective-permute-start | bytes 3145736 | tf_op jit(solution)/shard_map/ppermute | solution.py:169
  86.7 6.7 %collective-permute-start.16 = (bf16[2048,256]{1,0:T(8,128)(2,1)}, bf16[2048,256]{1,0:T(8,128)(2,1)}, u32[]{:S(2)}, u32[]{:S(2)}) collective-permute-start(bf16[2048,256]{1,0:T(8,128)(2,1)} %collective-permute-done.15.refs_6_), channel_id=1, source_target_pairs={{0,4},{4,0},{8,12},{12,8},{16,20},{20,16},{24,28},{28,24},{1,5},{5... | collective-permute-start | bytes 3145736 | tf_op jit(solution)/shard_map/ppermute | solution.py:169
  89.2 22.5 %all-to-all-start.2 = ((bf16[4,256,256]{2,1,0:T(8,128)(2,1)}), bf16[4,256,256]{2,1,0:T(8,128)(2,1)}, u32[]{:S(2)}, u32[]{:S(2)}) async-start(bf16[4,256,256]{2,1,0:T(8,128)(2,1)} %broadcast_in_dim.51), calls=%async_computation.2 | async-start | bytes 1048576 | tf_op jit(solution)/shard_map/all_to_all | solution.py:97
  104.0 3.8 collective-permute-start.18
  111.7 12.4 %collective-permute-start.22 = (bf16[1024,256]{1,0:T(8,128)(2,1)}, bf16[1024,256]{1,0:T(8,128)(2,1)S(1)}, u32[]{:S(2)}, u32[]{:S(2)}) collective-permute-start(bf16[1024,256]{1,0:T(8,128)(2,1)} %bitcast.16.refs_0_), channel_id=1, source_target_pairs={{0,8},{4,12},{8,0},{12,4},{16,24},{20,28},{24,16},{28,20},{1,9},{5... | collective-permute-start | bytes 1572872 | tf_op jit(solution)/shard_map/ppermute | solution.py:158
  112.3 12.0 %collective-permute-start.23 = (bf16[1024,256]{1,0:T(8,128)(2,1)}, bf16[1024,256]{1,0:T(8,128)(2,1)S(1)}, u32[]{:S(2)}, u32[]{:S(2)}) collective-permute-start(bf16[1024,256]{1,0:T(8,128)(2,1)} %bitcast.16.refs_0_), channel_id=1, source_target_pairs={{0,16},{4,20},{8,24},{12,28},{16,0},{20,4},{24,8},{28,12},{1,17},{... | collective-permute-start | bytes 1572872 | tf_op jit(solution)/shard_map/ppermute | solution.py:158
  117.5 4.7 collective-permute-start.21
  125.4 29.0 %all-to-all-start.3 = ((bf16[4,512,256]{2,1,0:T(8,128)(2,1)}), bf16[4,512,256]{2,1,0:T(8,128)(2,1)S(1)}, u32[]{:S(2)}, u32[]{:S(2)}) async-start(bf16[4,512,256]{2,1,0:T(8,128)(2,1)} %broadcast_in_dim.52), calls=%async_computation.3 | async-start | bytes 2097152 | tf_op jit(solution)/shard_map/all_to_all | solution.py:97
  130.6 14.0 %collective-permute-start.24 = (bf16[1024,256]{1,0:T(8,128)(2,1)S(1)}, bf16[1024,256]{1,0:T(8,128)(2,1)}, u32[]{:S(2)}, u32[]{:S(2)}) collective-permute-start(bf16[1024,256]{1,0:T(8,128)(2,1)S(1)} %broadcast_select_fusion.2), channel_id=1, source_target_pairs={{0,16},{4,12},{8,24},{12,4},{16,0},{20,28},{24,8},{28,20},{1,17},{... | collective-permute-start | bytes 1572872 | tf_op jit(solution)/shard_map/ppermute | solution.py:163
  151.2 12.7 %collective-permute-start.30 = (bf16[1024,256]{1,0:T(8,128)(2,1)}, bf16[1024,256]{1,0:T(8,128)(2,1)}, u32[]{:S(2)}, u32[]{:S(2)}) collective-permute-start(bf16[1024,256]{1,0:T(8,128)(2,1)} %bitcast.16.refs_0_), channel_id=1, source_target_pairs={{0,4},{4,0},{8,12},{12,8},{16,20},{20,16},{24,28},{28,24},{1,5},{5... | collective-permute-start | bytes 1572872 | tf_op jit(solution)/shard_map/ppermute | solution.py:169
  154.4 23.6 %collective-permute-start.34 = (bf16[2048,256]{1,0:T(8,128)(2,1)S(1)}, bf16[2048,256]{1,0:T(8,128)(2,1)S(1)}, u32[]{:S(2)}, u32[]{:S(2)}) collective-permute-start(bf16[2048,256]{1,0:T(8,128)(2,1)S(1)} %bitcast.98), channel_id=1, source_target_pairs={{0,8},{4,12},{8,0},{12,4},{16,24},{20,28},{24,16},{28,20},{1,9},{5... | collective-permute-start | bytes 3145736 | tf_op jit(solution)/shard_map/ppermute | solution.py:158
  155.0 23.1 %collective-permute-start.35 = (bf16[2048,256]{1,0:T(8,128)(2,1)S(1)}, bf16[2048,256]{1,0:T(8,128)(2,1)S(1)}, u32[]{:S(2)}, u32[]{:S(2)}) collective-permute-start(bf16[2048,256]{1,0:T(8,128)(2,1)S(1)} %bitcast.99), channel_id=1, source_target_pairs={{0,16},{4,20},{8,24},{12,28},{16,0},{20,4},{24,8},{28,12},{1,17},{... | collective-permute-start | bytes 3145736 | tf_op jit(solution)/shard_map/ppermute | solution.py:158
  156.8 3.8 collective-permute-start.28
  160.6 4.7 collective-permute-start.29
  179.4 16.5 %collective-permute-start.39 = (bf16[2048,256]{1,0:T(8,128)(2,1)}, bf16[2048,256]{1,0:T(8,128)(2,1)}, u32[]{:S(2)}, u32[]{:S(2)}) collective-permute-start(bf16[2048,256]{1,0:T(8,128)(2,1)} %broadcast_select_fusion), channel_id=1, source_target_pairs={{0,16},{4,12},{8,24},{12,4},{16,0},{20,28},{24,8},{28,20},{1,17},{... | collective-permute-start | bytes 3145736 | tf_op jit(solution)/shard_map/ppermute | solution.py:163
  181.7 14.1 %all-to-all-start.4 = ((bf16[4,208,256]{2,1,0:T(8,128)(2,1)}), bf16[4,208,256]{2,1,0:T(8,128)(2,1)}, u32[]{:S(2)}, u32[]{:S(2)}) async-start(bf16[4,208,256]{2,1,0:T(8,128)(2,1)} %broadcast_in_dim.55), calls=%async_computation.4 | async-start | bytes 851968 | tf_op jit(solution)/shard_map/all_to_all | solution.py:97
  186.5 9.9 %collective-permute-start.36 = (bf16[2048,256]{1,0:T(8,128)(2,1)S(1)}, bf16[2048,256]{1,0:T(8,128)(2,1)}, u32[]{:S(2)}, u32[]{:S(2)}) collective-permute-start(bf16[2048,256]{1,0:T(8,128)(2,1)S(1)} %bitcast.100), channel_id=1, source_target_pairs={{0,4},{4,0},{8,12},{12,8},{16,20},{20,16},{24,28},{28,24},{1,5},{5... | collective-permute-start | bytes 3145736 | tf_op jit(solution)/shard_map/ppermute | solution.py:169
  186.6 12.2 %collective-permute-start.37 = (bf16[2048,256]{1,0:T(8,128)(2,1)S(1)}, bf16[2048,256]{1,0:T(8,128)(2,1)}, u32[]{:S(2)}, u32[]{:S(2)}) collective-permute-start(bf16[2048,256]{1,0:T(8,128)(2,1)S(1)} %collective-permute-done.34.refs_2_), channel_id=1, source_target_pairs={{0,4},{4,0},{8,12},{12,8},{16,20},{20,16},{24,28},{28,24},{1,5},{5... | collective-permute-start | bytes 3145736 | tf_op jit(solution)/shard_map/ppermute | solution.py:169
  187.1 11.7 %collective-permute-start.38 = (bf16[2048,256]{1,0:T(8,128)(2,1)S(1)}, bf16[2048,256]{1,0:T(8,128)(2,1)}, u32[]{:S(2)}, u32[]{:S(2)}) collective-permute-start(bf16[2048,256]{1,0:T(8,128)(2,1)S(1)} %collective-permute-done.35.refs_4_), channel_id=1, source_target_pairs={{0,4},{4,0},{8,12},{12,8},{16,20},{20,16},{24,28},{28,24},{1,5},{5... | collective-permute-start | bytes 3145736 | tf_op jit(solution)/shard_map/ppermute | solution.py:169
  195.9 20.3 %collective-permute-start.41 = (bf16[392,512]{1,0:T(8,128)(2,1)}, bf16[392,512]{1,0:T(8,128)(2,1)S(1)}, u32[]{:S(2)}, u32[]{:S(2)}) collective-permute-start(bf16[392,512]{1,0:T(8,128)(2,1)} %get-tuple-element.241), channel_id=1, source_target_pairs={{0,1},{1,0},{2,3},{3,2},{4,5},{5,4},{6,7},{7,6},{8,9},{9,8},{10,11... | collective-permute-start | bytes 1204232 | tf_op jit(solution)/shard_map/ppermute | solution.py:1756
  196.4 21.3 %collective-permute-start.42 = (bf16[392,512]{1,0:T(8,128)(2,1)}, bf16[392,512]{1,0:T(8,128)(2,1)}, u32[]{:S(2)}, u32[]{:S(2)}) collective-permute-start(bf16[392,512]{1,0:T(8,128)(2,1)} %get-tuple-element.242), channel_id=1, source_target_pairs={{0,2},{1,3},{2,0},{3,1},{4,6},{5,7},{6,4},{7,5},{8,10},{9,11},{10,... | collective-permute-start | bytes 1204232 | tf_op jit(solution)/shard_map/ppermute | solution.py:1757
  217.7 11.8 %collective-permute-start.43 = (bf16[832,256]{1,0:T(8,128)(2,1)}, bf16[832,256]{1,0:T(8,128)(2,1)S(1)}, u32[]{:S(2)}, u32[]{:S(2)}) collective-permute-start(bf16[832,256]{1,0:T(8,128)(2,1)} %bitcast.28.refs_0_), channel_id=1, source_target_pairs={{0,8},{4,12},{8,0},{12,4},{16,24},{20,28},{24,16},{28,20},{1,9},{5... | collective-permute-start | bytes 1277960 | tf_op jit(solution)/shard_map/ppermute | solution.py:158
  218.8 10.8 %collective-permute-start.44 = (bf16[832,256]{1,0:T(8,128)(2,1)}, bf16[832,256]{1,0:T(8,128)(2,1)S(1)}, u32[]{:S(2)}, u32[]{:S(2)}) collective-permute-start(bf16[832,256]{1,0:T(8,128)(2,1)} %bitcast.28.refs_0_), channel_id=1, source_target_pairs={{0,16},{4,20},{8,24},{12,28},{16,0},{20,4},{24,8},{28,12},{1,17},{... | collective-permute-start | bytes 1277960 | tf_op jit(solution)/shard_map/ppermute | solution.py:158
  229.6 8.2 %collective-permute-start.45 = (bf16[832,256]{1,0:T(8,128)(2,1)S(1)}, bf16[832,256]{1,0:T(8,128)(2,1)S(1)}, u32[]{:S(2)}, u32[]{:S(2)}) collective-permute-start(bf16[832,256]{1,0:T(8,128)(2,1)S(1)} %broadcast_select_fusion.3), channel_id=1, source_target_pairs={{0,16},{4,12},{8,24},{12,4},{16,0},{20,28},{24,8},{28,20},{1,17},{... | collective-permute-start | bytes 1277960 | tf_op jit(solution)/shard_map/ppermute | solution.py:163
  239.3 14.2 %all-to-all-start.7 = ((bf16[32,2,2048]{2,1,0:T(2,128)(2,1)}), bf16[32,2,2048]{2,1,0:T(2,128)(2,1)S(1)}, u32[]{:S(2)}, u32[]{:S(2)}) async-start(bf16[32,2,2048]{2,1,0:T(2,128)(2,1)} %broadcast_in_dim.58), calls=%async_computation.7 | async-start | bytes 524288 | tf_op jit(solution)/shard_map/all_to_all | solution.py:121
  243.3 140.0 %reduce-scatter.4.cloned.1.call-start = ((), (), s32[]{:S(2)}) async-start(), calls=%async_computation.21 | async-start | bytes 9437184 | tf_op jit(solution)/shard_map/reduce_scatter | solution.py:1811
  243.9 11.4 %collective-permute-start.46 = (bf16[832,256]{1,0:T(8,128)(2,1)}, bf16[832,256]{1,0:T(8,128)(2,1)S(1)}, u32[]{:S(2)}, u32[]{:S(2)}) collective-permute-start(bf16[832,256]{1,0:T(8,128)(2,1)} %bitcast.28.refs_0_), channel_id=1, source_target_pairs={{0,4},{4,0},{8,12},{12,8},{16,20},{20,16},{24,28},{28,24},{1,5},{5... | collective-permute-start | bytes 1277960 | tf_op jit(solution)/shard_map/ppermute | solution.py:169
  244.2 11.1 %collective-permute-start.47 = (bf16[832,256]{1,0:T(8,128)(2,1)S(1)}, bf16[832,256]{1,0:T(8,128)(2,1)S(1)}, u32[]{:S(2)}, u32[]{:S(2)}) collective-permute-start(bf16[832,256]{1,0:T(8,128)(2,1)S(1)} %collective-permute-done.43.refs_2_), channel_id=1, source_target_pairs={{0,4},{4,0},{8,12},{12,8},{16,20},{20,16},{24,28},{28,24},{1,5},{5... | collective-permute-start | bytes 1277960 | tf_op jit(solution)/shard_map/ppermute | solution.py:169
  244.5 10.8 %collective-permute-start.48 = (bf16[832,256]{1,0:T(8,128)(2,1)S(1)}, bf16[832,256]{1,0:T(8,128)(2,1)S(1)}, u32[]{:S(2)}, u32[]{:S(2)}) collective-permute-start(bf16[832,256]{1,0:T(8,128)(2,1)S(1)} %collective-permute-done.44.refs_4_), channel_id=1, source_target_pairs={{0,4},{4,0},{8,12},{12,8},{16,20},{20,16},{24,28},{28,24},{1,5},{5... | collective-permute-start | bytes 1277960 | tf_op jit(solution)/shard_map/ppermute | solution.py:169
  244.7 10.6 %collective-permute-start.49 = (bf16[832,256]{1,0:T(8,128)(2,1)S(1)}, bf16[832,256]{1,0:T(8,128)(2,1)S(1)}, u32[]{:S(2)}, u32[]{:S(2)}) collective-permute-start(bf16[832,256]{1,0:T(8,128)(2,1)S(1)} %collective-permute-done.45.refs_6_), channel_id=1, source_target_pairs={{0,4},{4,0},{8,12},{12,8},{16,20},{20,16},{24,28},{28,24},{1,5},{5... | collective-permute-start | bytes 1277960 | tf_op jit(solution)/shard_map/ppermute | solution.py:169
  253.5 22.2 %collective-permute-start.50 = (bf16[392,512]{1,0:T(8,128)(2,1)}, bf16[392,512]{1,0:T(8,128)(2,1)}, u32[]{:S(2)}, u32[]{:S(2)}) collective-permute-start(bf16[392,512]{1,0:T(8,128)(2,1)} %get-tuple-element.256), channel_id=1, source_target_pairs={{0,3},{1,2},{2,1},{3,0},{4,7},{5,6},{6,5},{7,4},{8,11},{9,10},{10,... | collective-permute-start | bytes 1204232 | tf_op jit(solution)/shard_map/ppermute | solution.py:1784
  255.3 27.2 %collective-permute-start.51 = (bf16[392,512]{1,0:T(8,128)(2,1)}, bf16[392,512]{1,0:T(8,128)(2,1)}, u32[]{:S(2)}, u32[]{:S(2)}) collective-permute-start(bf16[392,512]{1,0:T(8,128)(2,1)} %get-tuple-element.259), channel_id=1, source_target_pairs={{0,1},{1,0},{2,3},{3,2},{4,5},{5,4},{6,7},{7,6},{8,9},{9,8},{10,11... | collective-permute-start | bytes 1204232 | tf_op jit(solution)/shard_map/ppermute | solution.py:1785
  312.2 21.4 %collective-permute-start.52 = (bf16[392,512]{1,0:T(8,128)(2,1)S(1)}, bf16[392,512]{1,0:T(8,128)(2,1)S(1)}, u32[]{:S(2)}, u32[]{:S(2)}) collective-permute-start(bf16[392,512]{1,0:T(8,128)(2,1)S(1)} %copy-done.46), channel_id=1, source_target_pairs={{0,2},{1,3},{2,0},{3,1},{4,6},{5,7},{6,4},{7,5},{8,10},{9,11},{10,... | collective-permute-start | bytes 1204232 | tf_op jit(solution)/shard_map/ppermute | solution.py:1806
  344.8 9.7 %all-to-all-start.11 = ((f32[4,2,2048]{2,1,0:T(2,128)}), f32[4,2,2048]{2,1,0:T(2,128)S(1)}, u32[]{:S(2)}, u32[]{:S(2)}) async-start(f32[4,2,2048]{2,1,0:T(2,128)} %broadcast_in_dim.62), calls=%async_computation.11 | async-start | bytes 131072 | tf_op jit(solution)/shard_map/all_to_all | solution.py:97
  356.3 25.6 %all-to-all-start.12 = ((bf16[32,2,5120]{2,1,0:T(2,128)(2,1)}), bf16[32,2,5120]{2,1,0:T(2,128)(2,1)S(1)}, u32[]{:S(2)}, u32[]{:S(2)}) async-start(bf16[32,2,5120]{2,1,0:T(2,128)(2,1)} %broadcast_in_dim.63), calls=%async_computation.12 | async-start | bytes 1310720 | tf_op jit(solution)/shard_map/all_to_all | solution.py:121
  358.9 54.8 %reduce-scatter.6.cloned.1.call-start = ((), (), s32[]{:S(2)}) async-start(), calls=%async_computation.22 | async-start | bytes 1310720 | tf_op jit(solution)/shard_map/reduce_scatter | solution.py:1830
  383.4 83.9 %reduce-scatter.8.cloned.1.call-start = ((), (), s32[]{:S(2)}) async-start(), calls=%async_computation.23 | async-start | bytes 2359296 | tf_op jit(solution)/shard_map/reduce_scatter | solution.py:1842
  413.7 7.5 %collective-permute-start.53 = (bf16[4,4,512,256]{3,2,1,0:T(8,128)(2,1)}, bf16[4,4,512,256]{3,2,1,0:T(8,128)(2,1)}, u32[]{:S(2)}, u32[]{:S(2)}) collective-permute-start(bf16[4,4,512,256]{3,2,1,0:T(8,128)(2,1)} %get-tuple-element.289), channel_id=1, source_target_pairs={{0,4},{4,0},{8,12},{12,8},{16,20},{20,16},{24,28},{28,24},{1,5},{5... | collective-permute-start | bytes 12582920 | tf_op jit(solution)/shard_map/ppermute | solution.py:183
  423.7 15.0 %collective-permute-start.54 = (bf16[4,512,256]{2,1,0:T(8,128)(2,1)}, bf16[4,512,256]{2,1,0:T(8,128)(2,1)S(1)}, u32[]{:S(2)}, u32[]{:S(2)}) collective-permute-start(bf16[4,512,256]{2,1,0:T(8,128)(2,1)} %twin_sum.1), channel_id=1, source_target_pairs={{0,16},{4,12},{8,24},{12,4},{16,0},{20,28},{24,8},{28,20},{1,17},{... | collective-permute-start | bytes 3145736 | tf_op jit(solution)/shard_map/ppermute | solution.py:179
  425.2 13.0 %collective-permute-start.55 = (bf16[392,512]{1,0:T(8,128)(2,1)S(1)}, bf16[392,512]{1,0:T(8,128)(2,1)S(1)}, u32[]{:S(2)}, u32[]{:S(2)}) collective-permute-start(bf16[392,512]{1,0:T(8,128)(2,1)S(1)} %copy-done.45), channel_id=1, source_target_pairs={{0,3},{1,2},{2,1},{3,0},{4,7},{5,6},{6,5},{7,4},{8,11},{9,10},{10,... | collective-permute-start | bytes 1204232 | tf_op jit(solution)/shard_map/ppermute | solution.py:1834
  439.6 65.8 %all-to-all-start.15 = ((bf16[4,392,512]{2,1,0:T(8,128)(2,1)}), bf16[4,392,512]{2,1,0:T(8,128)(2,1)S(1)}, u32[]{:S(2)}, u32[]{:S(2)}) async-start(bf16[4,392,512]{2,1,0:T(8,128)(2,1)} %mix_back.3), calls=%async_computation.18 | async-start | bytes 3211264 | tf_op jit(solution)/shard_map/all_to_all | solution.py:142
  452.4 26.8 %collective-permute-start.56 = (bf16[4,512,256]{2,1,0:T(8,128)(2,1)}, bf16[4,512,256]{2,1,0:T(8,128)(2,1)S(1)}, u32[]{:S(2)}, u32[]{:S(2)}) collective-permute-start(bf16[4,512,256]{2,1,0:T(8,128)(2,1)} %get-tuple-element.298), channel_id=1, source_target_pairs={{0,8},{4,12},{8,0},{12,4},{16,24},{20,28},{24,16},{28,20},{1,9},{5... | collective-permute-start | bytes 3145736 | tf_op jit(solution)/shard_map/ppermute | solution.py:187
  453.6 26.7 %collective-permute-start.57 = (bf16[4,512,256]{2,1,0:T(8,128)(2,1)}, bf16[4,512,256]{2,1,0:T(8,128)(2,1)}, u32[]{:S(2)}, u32[]{:S(2)}) collective-permute-start(bf16[4,512,256]{2,1,0:T(8,128)(2,1)} %get-tuple-element.299), channel_id=1, source_target_pairs={{0,16},{4,20},{8,24},{12,28},{16,0},{20,4},{24,8},{28,12},{1,17},{... | collective-permute-start | bytes 3145736 | tf_op jit(solution)/shard_map/ppermute | solution.py:187
  484.8 25.2 %collective-permute-start.58 = (bf16[640,256]{1,0:T(8,128)(2,1)}, bf16[640,256]{1,0:T(8,128)(2,1)S(1)}, u32[]{:S(2)}, u32[]{:S(2)}) collective-permute-start(bf16[640,256]{1,0:T(8,128)(2,1)} %get-tuple-element.313), channel_id=1, source_target_pairs={{0,1},{1,0},{2,3},{3,2},{4,5},{5,4},{6,7},{7,6},{8,9},{9,8},{10,11... | collective-permute-start | bytes 983048 | tf_op jit(solution)/shard_map/ppermute | solution.py:191
  486.7 25.6 %collective-permute-start.59 = (bf16[640,256]{1,0:T(8,128)(2,1)}, bf16[640,256]{1,0:T(8,128)(2,1)S(1)}, u32[]{:S(2)}, u32[]{:S(2)}) collective-permute-start(bf16[640,256]{1,0:T(8,128)(2,1)} %get-tuple-element.314), channel_id=1, source_target_pairs={{0,2},{1,3},{2,0},{3,1},{4,6},{5,7},{6,4},{7,5},{8,10},{9,11},{10,... | collective-permute-start | bytes 983048 | tf_op jit(solution)/shard_map/ppermute | solution.py:191
  488.9 23.4 %collective-permute-start.60 = (bf16[640,256]{1,0:T(8,128)(2,1)}, bf16[640,256]{1,0:T(8,128)(2,1)S(1)}, u32[]{:S(2)}, u32[]{:S(2)}) collective-permute-start(bf16[640,256]{1,0:T(8,128)(2,1)} %get-tuple-element.315), channel_id=1, source_target_pairs={{0,3},{1,2},{2,1},{3,0},{4,7},{5,6},{6,5},{7,4},{8,11},{9,10},{10,... | collective-permute-start | bytes 983048 | tf_op jit(solution)/shard_map/ppermute | solution.py:191
  515.7 15.7 %collective-permute-start.61 = (bf16[128,256]{1,0:T(8,128)(2,1)}, bf16[128,256]{1,0:T(8,128)(2,1)S(1)}, u32[]{:S(2)}, u32[]{:S(2)}) collective-permute-start(bf16[128,256]{1,0:T(8,128)(2,1)} %get-tuple-element.353), channel_id=1, source_target_pairs={{0,1},{1,0},{2,3},{3,2},{4,5},{5,4},{6,7},{7,6},{8,9},{9,8},{10,11... | collective-permute-start | bytes 196616 | tf_op jit(solution)/shard_map/ppermute | solution.py:146
  519.9 11.6 %collective-permute-start.62 = (bf16[128,256]{1,0:T(8,128)(2,1)}, bf16[128,256]{1,0:T(8,128)(2,1)S(1)}, u32[]{:S(2)}, u32[]{:S(2)}) collective-permute-start(bf16[128,256]{1,0:T(8,128)(2,1)} %get-tuple-element.353), channel_id=1, source_target_pairs={{0,2},{1,3},{2,0},{3,1},{4,6},{5,7},{6,4},{7,5},{8,10},{9,11},{10,... | collective-permute-start | bytes 196616 | tf_op jit(solution)/shard_map/ppermute | solution.py:146
  520.5 10.9 %collective-permute-start.63 = (bf16[128,256]{1,0:T(8,128)(2,1)}, bf16[128,256]{1,0:T(8,128)(2,1)S(1)}, u32[]{:S(2)}, u32[]{:S(2)}) collective-permute-start(bf16[128,256]{1,0:T(8,128)(2,1)} %get-tuple-element.353), channel_id=1, source_target_pairs={{0,3},{1,2},{2,1},{3,0},{4,7},{5,6},{6,5},{7,4},{8,11},{9,10},{10,... | collective-permute-start | bytes 196616 | tf_op jit(solution)/shard_map/ppermute | solution.py:146
  532.1 8.9 %all-to-all-start.17 = ((f32[4,2,128]{2,1,0:T(2,128)}), f32[4,2,128]{2,1,0:T(2,128)S(1)}, u32[]{:S(2)}, u32[]{:S(2)}) async-start(f32[4,2,128]{2,1,0:T(2,128)} %broadcast_in_dim.67), calls=%async_computation.20 | async-start | bytes 8192 | tf_op jit(solution)/shard_map/all_to_all | solution.py:97
  (60 other events, 508.9 us)
Sparse Core Ops, SparseCore 0:
  311.4 71.9 reduce-scatter.3
  385.7 27.9 reduce-scatter.5
  425.3 41.8 reduce-scatter.7

commit v3 on v2

--- a/solution.py
+++ b/solution.py
@@ -1269,7 +1269,7 @@
     first = jnp.where(there, jnp.exp(scores / EPS_SINK), 0.0)
     plan_ref[pl.ds(0, crops), :] = first
 
-    size = 2 * crops
+    size, large_size = 4 * crops, 8 * crops
 
     def partial_sums(value):
         return jnp.sum(value.reshape(-1, 8, value.shape[1]), 0)
@@ -1278,13 +1278,15 @@
         return pl.ds(pl.multiple_of(crops + i * size, crops), size)
 
     def fill(i, column):
-        rows = queue_ref[pl.ds(pl.multiple_of(i * size, size), size), :]
-        value = jnp.exp(dot(rows, protos, NT) / EPS_SINK)
-        plan_ref[rows_at(i), :] = value
+        place = pl.multiple_of(i * large_size, large_size)
+        value = jnp.exp(dot(queue_ref[pl.ds(place, large_size), :], protos, NT) / EPS_SINK)
+        plan_ref[pl.ds(pl.multiple_of(place + crops, crops), large_size), :] = value
         return column + partial_sums(value)
 
     steps = parts * QUEUE_ROWS // size
-    column = lax.fori_loop(0, steps, fill, partial_sums(first))
+    column = lax.fori_loop(
+        0, parts * QUEUE_ROWS // large_size, fill, partial_sums(first)
+    )
     column = jnp.sum(column, 0, keepdims=True)
     large = jnp.where(column > 1e37, 2.0**-8, 1.0)
     inverse = jnp.where(there, 1.0 / (column * large), 0.0)
@@ -1760,24 +1762,24 @@
         gated, across, up = tie(gated, across, up)
         corner = gather_corner(across, up)
         corner, bundle = tie(corner, bundle)
+        head_sides = gather_sides(bundle)
         expand_pieces = gather_twins(expand_low, across, up, corner)
     expanded, sums3 = mix(gated, expand_pieces)
     if quick:
-        sums3, bundle = tie(sums3, bundle)
+        sums3, *head_sides = tie(sums3, *head_sides)
         sums3 = jnp.sum(spread(sums3, "dp"), 0)
-        sums3, bundle, y_grad_parts[1], y_grad_parts[2] = tie(
-            sums3, bundle, y_grad_parts[1], y_grad_parts[2]
-        )
-        across, up = gather_sides(bundle)
+        sums3, y_grad_parts[1], y_grad_parts[2], *head_sides = tie(
+            sums3, y_grad_parts[1], y_grad_parts[2], *head_sides
+        )
+        head_corner = gather_corner(*head_sides)
         sums3 = jnp.sum(spread(sums3, "mp"), 0)
-        sums3, across, up = tie(sums3, across, up)
-        corner = gather_corner(across, up)
+        sums3, head_corner = tie(sums3, head_corner)
+        bundle = gather_twins(bundle, *head_sides, head_corner)
     else:
         sums3 = total(sums3)
     *y_parts, summary = block_value(x, expanded, sums3, norms, count)
     if quick:
-        summary, corner = tie(summary, corner)
-        bundle = gather_twins(bundle, across, up, corner)
+        summary, *bundle = tie(summary, *bundle)
     summary = gather_all(summary)
     if quick:
         summary, y_grad_parts[3], y_parts[1] = tie(summary, y_grad_parts[3], y_parts[1])

time: 565 us -> 560 us (level)
  waiting for transfers between devices: 113 us -> 107 us
    all_to_all x0 -> x1, blocking collectives: none -> 13 us  [gather_all(): lax.all_to_all(jnp.broadcast_to(v[None], (n,) + v.shape), ('dp', 'mp'), s...]
    all_to_all x2 -> x1, waiting for transfers between devices: 8.53 us -> 0.01 us  [gather_all(): lax.all_to_all(jnp.broadcast_to(v[None], (n,) + v.shape), ('dp', 'mp'), s...]
    all_to_all x8 -> x7, blocking collectives: 72.5 us -> 64.7 us  [spread(): lax.all_to_all(jnp.broadcast_to(v[None], (n,) + v.shape), axis, split_axi...]
    all_to_all x6 -> x7, waiting for transfers between devices: 20.6 us -> 25.7 us  [spread(): lax.all_to_all(jnp.broadcast_to(v[None], (n,) + v.shape), axis, split_axi...]
    all_to_all x6 -> x7, starting transfers between devices: 26.1 us -> 29.8 us  [spread(): lax.all_to_all(jnp.broadcast_to(v[None], (n,) + v.shape), axis, split_axi...]
  transfers between devices with their start and end apart: 77 -> 77, of which waited for: 36 -> 34; matrix products, arithmetic and copies ran while one was open for 6% -> 6% of each run, Pallas kernels for 32% -> 32%
where the time goes in v3:
time: 560 us; the launch traced here: 551 us
  Pallas kernels  197 us (35%)
  starting transfers between devices  107 us (19%)
  waiting for transfers between devices  107 us (19%)
  blocking collectives  77.6 us (14%)
  local copies, waits for them, and re-layouts  25.8 us (5%)
  other arithmetic  21.7 us (4%)
  between operations  15.2 us (3%)
    all_to_all x7, blocking collectives, spread(): lax.all_to_all(jnp.broadcast_to(v[None], (n,) + v.shape), axis, split_axi...  64.7 us
    all_to_all x7, starting transfers between devices, spread(): lax.all_to_all(jnp.broadcast_to(v[None], (n,) + v.shape), axis, split_axi...  29.8 us
    all_to_all x7, waiting for transfers between devices, spread(): lax.all_to_all(jnp.broadcast_to(v[None], (n,) + v.shape), axis, split_axi...  25.7 us
    pallas_call x1, Pallas kernels, conv_back(): pl.pallas_call(functools.partial(conv_back_kernel, crops, count), grid=(Q...  22.7 us
    ppermute x10, waiting for transfers between devices, sum_axis(): v = v + lax.ppermute(v, axis, flips(axis, bit))  19.5 us
    pallas_call x2, Pallas kernels, mix_back(): pl.pallas_call(functools.partial(mix_back_kernel, len(more)), in_specs=[S...  19 us
    ppermute x5, waiting for transfers between devices, gather_sides(): lax.ppermute(v, 'dp', flips('dp', 2))  17.2 us
    pallas_call x2, Pallas kernels, mix(): pl.pallas_call(mix_kernel, grid=(QUADS,), in_specs=[SCALAR, pl.BlockSpec(...  16.9 us
  transfers between devices with their start and end apart: 77, of which 34 were waited for; matrix products, arithmetic and copies ran while one was open for 6% of the time, Pallas kernels for 32%

profile of v3, /device:TPU:0, one launch (start us, length us, event | category | flops | bytes accessed | tf_op | source)
XLA Modules:
  0.0 550.6 jit_solution(12522876432105804748)
XLA Ops:
  10.7 5.0 collective-permute-start
  20.5 4.9 all-to-all-start
  28.1 2.4 fusion.9
  31.3 2.8 pad_maximum_fusion.1
  34.8 4.8 all-to-all-done
  46.6 3.7 all-to-all-start.1
  50.3 7.2 %dense_windows.1.w_ref = bf16[4,3,9,256,256]{4,3,2,1,0:T(8,128)(2,1)} custom-call(s32[1]{0:T(128)} %bitcast.1.me_ref, bf16[504,256]{1,0:T(8,128)(2,1)} %copy-done.15, bf16[504,256]{1,0:T(8,128)(2,1)} %copy-done.32, bf16[504,256]{1,0:T(8,128)(2,1)} %copy-done.16, bf16[504,256]{1,0:T(8,128)(2,1)} %copy-done.34, ...), custom_call_target="tpu_custom_call" | custom-call | flops 1 | bytes 1 | tf_op jit(solution)/shard_map/dense_windows/pallas_call | solution.py:864
  57.5 11.7 %collective-permute-done.11.refs_2_ = bf16[2048,256]{1,0:T(8,128)(2,1)} collective-permute-done((bf16[2048,256]{1,0:T(8,128)(2,1)S(1)}, bf16[2048,256]{1,0:T(8,128)(2,1)}, u32[]{:S(2)}, u32[]{:S(2)}) %collective-permute-start.11) | collective-permute-done | bytes 1048608 | tf_op jit(solution)/shard_map/ppermute | solution.py:158
  73.8 12.9 %collective-permute-done.15.refs_6_ = bf16[2048,256]{1,0:T(8,128)(2,1)} collective-permute-done((bf16[2048,256]{1,0:T(8,128)(2,1)S(1)}, bf16[2048,256]{1,0:T(8,128)(2,1)}, u32[]{:S(2)}, u32[]{:S(2)}) %collective-permute-start.15) | collective-permute-done | bytes 1048608 | tf_op jit(solution)/shard_map/ppermute | solution.py:163
  89.2 4.1 all-to-all-start.2
  93.4 8.4 %mix.2 = (f32[392,2048]{1,0:T(8,128)}, f32[2,2048]{1,0:T(2,128)}) custom-call(s32[1]{0:T(128)} %bitcast.1.me_ref, bf16[4,392,512]{2,1,0:T(8,128)(2,1)} %copy-done, bf16[2048,256]{1,0:T(8,128)(2,1)} %bitcast.96, bf16[2048,256]{1,0:T(8,128)(2,1)} %collective-permute-done.10.refs_1_, bf16[2048,256]{1,0:T(8,128)(2,1)} %collective-permute-done.11.refs_2_, ...), custom_call_target="tpu_custom_call" | custom-call | flops 1 | bytes 1 | tf_op jit(solution)/shard_map/mix/pallas_call | solution.py:380
  104.6 3.2 collective-permute-done.18
  108.4 3.2 collective-permute-done.19
  117.5 2.9 collective-permute-start.21
  125.4 5.0 all-to-all-start.3
  132.0 12.5 %conv.1 = (bf16[392,2048]{1,0:T(8,128)(2,1)}, f32[2,2048]{1,0:T(2,128)}) custom-call(f32[392,2048]{1,0:T(8,128)} %get-tuple-element.215.a_ref, f32[2,2048]{1,0:T(2,128)} %add.120.sums_ref, f32[6,2048]{1,0:T(8,128)} %bitcast.106, bf16[4,3,9,256,256]{4,3,2,1,0:T(8,128)(2,1)} %dense_windows.1.w_ref), custom_call_target="tpu_custom_call" | custom-call | flops 1 | bytes 1 | tf_op jit(solution)/shard_map/conv/pallas_call | solution.py:943
  151.2 3.2 collective-permute-done.27
  160.5 3.0 collective-permute-start.29
  167.6 6.1 %gate.1 = (bf16[4,392,512]{2,1,0:T(8,128)(2,1)}, bf16[2,2048]{1,0:T(2,128)(2,1)}, f32[2,512]{1,0:T(2,128)}, bf16[2,512]{1,0:T(2,128)(2,1)}, f32[2,2048]{1,0:T(2,128)}) custom-call(s32[1]{0:T(128)} %bitcast.1.me_ref, bf16[392,2048]{1,0:T(8,128)(2,1)} %get-tuple-element.224.a_ref.a2_ref, f32[2,2048]{1,0:T(2,128)} %add.125.sums_ref.sums2_ref, ...), custom_call_target="tpu_custom_call" | custom-call | flops 1 | bytes 1 | tf_op jit(solution)/shard_map/gate/pallas_call | solution.py:1152
  173.7 4.2 collective-permute-done.34.refs_2_
  181.8 4.8 all-to-all-start.4
  187.2 8.7 %all-to-all-done.4 = bf16[4,208,256]{2,1,0:T(8,128)(2,1)} async-done(((bf16[4,208,256]{2,1,0:T(8,128)(2,1)}), bf16[4,208,256]{2,1,0:T(8,128)(2,1)}, u32[]{:S(2)}, u32[]{:S(2)}) %all-to-all-start.4) | async-done | bytes 426016 | tf_op jit(solution)/shard_map/all_to_all | solution.py:97
  198.5 2.4 collective-permute-start.44
  200.8 8.4 %mix.3 = (f32[392,2048]{1,0:T(8,128)}, f32[2,2048]{1,0:T(2,128)}) custom-call(s32[1]{0:T(128)} %bitcast.1.me_ref, bf16[4,392,512]{2,1,0:T(8,128)(2,1)} %get-tuple-element.239.x_ref, bf16[2048,256]{1,0:T(8,128)(2,1)} %bitcast.101, bf16[2048,256]{1,0:T(8,128)(2,1)} %collective-permute-done.36.refs_1_, bf16[2048,256]{1,0:T(8,128)(2,1)} %copy-done.3, ...), custom_call_target="tpu_custom_call" | custom-call | flops 1 | bytes 1 | tf_op jit(solution)/shard_map/mix/pallas_call | solution.py:380
  210.1 8.1 %all_to_all.90 = f32[8,2,2048]{2,1,0:T(2,128)S(1)} all-to-all(f32[8,2,2048]{2,1,0:T(2,128)S(1)} %broadcast_in_dim.56), channel_id=1, replica_groups=mesh['dp'=8,'mp'=4] {'dp'}, dimensions={0} | all-to-all | bytes 262144 | tf_op jit(solution)/shard_map/all_to_all | solution.py:97
  222.1 3.7 all-to-all-start.6
  226.4 5.2 all-to-all-done.6
  232.2 5.2 value.1
  238.4 13.0 %all_to_all.91.summary_ref = bf16[32,2,2048]{2,1,0:T(2,128)(2,1)} all-to-all(bf16[32,2,2048]{2,1,0:T(2,128)(2,1)S(1)} %broadcast_in_dim.58), channel_id=1, replica_groups=mesh['dp'=8,'mp'=4] {'dp','mp'}, dimensions={0} | all-to-all | bytes 524288 | tf_op jit(solution)/shard_map/all_to_all | solution.py:121
  253.1 15.7 %head.1 = (f32[1,1]{1,0:T(1,128)}, bf16[64,256]{1,0:T(8,128)(2,1)}, bf16[3072,64]{1,0:T(8,128)(2,1)}, bf16[64,256]{1,0:T(8,128)(2,1)}, f32[64,2048]{1,0:T(8,128)}, /*index=5*/bf16[64,2048]{1,0:T(8,128)(2,1)}) custom-call(s32[1]{0:T(128)} %bitcast.1.me_ref, bf16[32,2,2048]{2,1,0:T(2,128)(2,1)} %all_to_all.91.summary_ref, bf16[832,256]{1,0:T(8,128)(2,1)} %bitcast.28.refs_0_, ...), custom_call_target="tpu_custom_call" | custom-call | flops 1 | bytes 1 | tf_op jit(solution)/shard_map/head/pallas_call | solution.py:1336
  269.6 6.7 %value_back.1 = (f32[392,2048]{1,0:T(8,128)}, f32[2,2048]{1,0:T(2,128)}) custom-call(s32[1]{0:T(128)} %bitcast.me_ref.m_ref, s32[1]{0:T(128)} %bitcast.27.first_ref, bf16[4,392,512]{2,1,0:T(8,128)(2,1)} %copy-done, f32[392,2048]{1,0:T(8,128)} %get-tuple-element.244.a_ref, f32[2,2048]{1,0:T(2,128)} %reduce_sum.91.sums_ref, f32[6,2048]{1,0:T(8,128)} %bitcast.109, ...), custom_call_target="tpu_custom_call" | custom-call | flops 1 | bytes 1 | tf_op jit(solution)/shard_map/value_back/pallas_call | solution.py:805
  277.1 7.9 %all_to_all.92 = f32[8,2,2048]{2,1,0:T(2,128)S(1)} all-to-all(f32[8,2,2048]{2,1,0:T(2,128)S(1)} %broadcast_in_dim.59), channel_id=1, replica_groups=mesh['dp'=8,'mp'=4] {'dp'}, dimensions={0} | all-to-all | bytes 262144 | tf_op jit(solution)/shard_map/all_to_all | solution.py:97
  285.1 10.6 %all_to_all.93 = f32[4,2,2048]{2,1,0:T(2,128)S(1)} all-to-all(f32[4,2,2048]{2,1,0:T(2,128)S(1)} %broadcast_in_dim.60), channel_id=1, replica_groups=mesh['dp'=8,'mp'=4] {'mp'}, dimensions={0} | all-to-all | bytes 131072 | tf_op jit(solution)/shard_map/all_to_all | solution.py:97
  296.3 10.0 %all_grads.1 = (bf16[392,2048]{1,0:T(8,128)(2,1)}, bf16[8,4,512,256]{3,2,1,0:T(8,128)(2,1)}) custom-call(bf16[4,392,512]{2,1,0:T(8,128)(2,1)} %get-tuple-element.239.x_ref, f32[392,2048]{1,0:T(8,128)} %get-tuple-element.273.g_ref.refs_8_, f32[392,2048]{1,0:T(8,128)} %get-tuple-element.244.a_ref, f32[2,2048]{1,0:T(2,128)} %reduce_sum.91.sums_ref, ...), custom_call_target="tpu_custom_call" | custom-call | flops 1 | bytes 1 | tf_op jit(solution)/shard_map/all_grads/pallas_call | solution.py:506
  308.1 9.5 %mix_back.2.dh_ref = f32[392,2048]{1,0:T(8,128)} custom-call(s32[1]{0:T(128)} %bitcast.1.me_ref, bf16[392,2048]{1,0:T(8,128)(2,1)} %get-tuple-element.280.g_ref, bf16[2048,256]{1,0:T(8,128)(2,1)} %bitcast.102, bf16[2048,256]{1,0:T(8,128)(2,1)} %collective-permute-done.36.refs_1_, bf16[2048,256]{1,0:T(8,128)(2,1)} %copy-done.3, ...), custom_call_target="tpu_custom_call" | custom-call | flops 1 | bytes 1 | tf_op jit(solution)/shard_map/mix_back/pallas_call | solution.py:428
  317.6 11.0 %gate_back.1 = (f32[392,2048]{1,0:T(8,128)}, f32[2,2048]{1,0:T(2,128)}, bf16[2,2048]{1,0:T(2,128)(2,1)}, bf16[2,512]{1,0:T(2,128)(2,1)}) custom-call(s32[1]{0:T(128)} %bitcast.1.me_ref, f32[392,2048]{1,0:T(8,128)} %mix_back.2.dh_ref, bf16[392,2048]{1,0:T(8,128)(2,1)} %get-tuple-element.224.a_ref.a2_ref, f32[2,2048]{1,0:T(2,128)} %add.125.sums_ref.sums2_ref, ...), custom_call_target="tpu_custom_call" | custom-call | flops 1 | bytes 1 | tf_op jit(solution)/shard_map/gate_back/pallas_call | solution.py:1218
  329.5 9.6 %all_to_all.94 = f32[8,2,2048]{2,1,0:T(2,128)S(1)} all-to-all(f32[8,2,2048]{2,1,0:T(2,128)S(1)} %broadcast_in_dim.61), channel_id=1, replica_groups=mesh['dp'=8,'mp'=4] {'dp'}, dimensions={0} | all-to-all | bytes 262144 | tf_op jit(solution)/shard_map/all_to_all | solution.py:97
  339.8 4.0 all-to-all-start.11
  344.5 5.0 all-to-all-done.11
  351.3 2.6 all-to-all-start.12
  354.2 22.7 %conv_back.1 = (bf16[392,2048]{1,0:T(8,128)(2,1)}, bf16[8,512,256]{2,1,0:T(8,128)(2,1)}, f32[2,2048]{1,0:T(2,128)}) custom-call(f32[392,2048]{1,0:T(8,128)} %get-tuple-element.283.g_ref, bf16[392,2048]{1,0:T(8,128)(2,1)} %get-tuple-element.224.a_ref.a2_ref, f32[2,2048]{1,0:T(2,128)} %add.125.sums_ref.sums2_ref, f32[2,2048]{1,0:T(2,128)} %reduce_sum.95.grad_sums_ref.g2_ref, ...), custom_call_target="tpu_custom_call" | custom-call | flops 1 | bytes 1 | tf_op jit(solution)/shard_map/conv_back/pallas_call | solution.py:1042
  379.2 8.2 %all_to_all.95 = f32[8,2,2048]{2,1,0:T(2,128)S(1)} all-to-all(f32[8,2,2048]{2,1,0:T(2,128)S(1)} %broadcast_in_dim.64), channel_id=1, replica_groups=mesh['dp'=8,'mp'=4] {'dp'}, dimensions={0} | all-to-all | bytes 262144 | tf_op jit(solution)/shard_map/all_to_all | solution.py:97
  387.5 11.6 %all_to_all.96 = f32[4,2,2048]{2,1,0:T(2,128)S(1)} all-to-all(f32[4,2,2048]{2,1,0:T(2,128)S(1)} %broadcast_in_dim.65), channel_id=1, replica_groups=mesh['dp'=8,'mp'=4] {'mp'}, dimensions={0} | all-to-all | bytes 131072 | tf_op jit(solution)/shard_map/all_to_all | solution.py:97
  399.7 8.5 %sent_grads.1 = (bf16[392,2048]{1,0:T(8,128)(2,1)}, bf16[4,4,512,256]{3,2,1,0:T(8,128)(2,1)}) custom-call(s32[1]{0:T(128)} %bitcast.1.me_ref, bf16[4,392,512]{2,1,0:T(8,128)(2,1)} %copy-done, bf16[392,2048]{1,0:T(8,128)(2,1)} %get-tuple-element.292.g_ref, f32[392,2048]{1,0:T(8,128)} %get-tuple-element.215.a_ref, f32[2,2048]{1,0:T(2,128)} %add.120.sums_ref, ...), custom_call_target="tpu_custom_call" | custom-call | flops 1 | bytes 1 | tf_op jit(solution)/shard_map/sent_grads/pallas_call | solution.py:475
  408.8 6.2 %kept_grads.1.a_ref.a1_ref.a2_ref = bf16[4,4,512,256]{3,2,1,0:T(8,128)(2,1)} custom-call(s32[1]{0:T(128)} %bitcast.1.me_ref, bf16[4,392,512]{2,1,0:T(8,128)(2,1)} %copy-done, bf16[392,2048]{1,0:T(8,128)(2,1)} %get-tuple-element.308.g_ref), custom_call_target="tpu_custom_call" | custom-call | flops 1 | bytes 1 | tf_op jit(solution)/shard_map/kept_grads/pallas_call | solution.py:532
  416.3 2.4 twin_sum.1
  421.4 9.5 %mix_back.3 = bf16[4,392,512]{2,1,0:T(8,128)(2,1)} custom-call(s32[1]{0:T(128)} %bitcast.1.me_ref, bf16[392,2048]{1,0:T(8,128)(2,1)} %get-tuple-element.308.g_ref, bf16[2048,256]{1,0:T(8,128)(2,1)} %bitcast.97, bf16[2048,256]{1,0:T(8,128)(2,1)} %collective-permute-done.10.refs_1_, bf16[2048,256]{1,0:T(8,128)(2,1)} %collective-permute-done.11.refs_2_, ...), custom_call_target="tpu_custom_call" | custom-call | flops 1 | bytes 1 | tf_op jit(solution)/shard_map/mix_back/pallas_call | solution.py:428
  430.9 2.4 collective-permute-done.55.refs_3_
  434.7 8.9 %all-to-all-start.15 = ((bf16[4,392,512]{2,1,0:T(8,128)(2,1)}), bf16[4,392,512]{2,1,0:T(8,128)(2,1)S(1)}, u32[]{:S(2)}, u32[]{:S(2)}) async-start(bf16[4,392,512]{2,1,0:T(8,128)(2,1)} %mix_back.3), calls=%async_computation.18 | async-start | bytes 3211264 | tf_op jit(solution)/shard_map/all_to_all | solution.py:142
  443.6 3.8 corner_sums.1
  452.2 4.8 small_grads.1
  457.0 5.3 reduce-scatter.8.cloned.1.call-done
  462.3 12.0 %collective-permute-done.56.across_ref = bf16[4,512,256]{2,1,0:T(8,128)(2,1)S(1)} collective-permute-done((bf16[4,512,256]{2,1,0:T(8,128)(2,1)}, bf16[4,512,256]{2,1,0:T(8,128)(2,1)S(1)}, u32[]{:S(2)}, u32[]{:S(2)}) %collective-permute-start.56) | collective-permute-done | bytes 1048608 | tf_op jit(solution)/shard_map/ppermute | solution.py:187
  475.3 4.5 side_sums.1
  484.2 3.6 weight_sums.1.weights_ref
  487.8 2.8 join_rows.3
  490.6 7.7 %lars_prepare.1 = (f32[2016,126]{1,0:T(8,128)}, f32[2016,126]{1,0:T(8,128)}, f32[504,504]{1,0:T(8,128)}, f32[504,504]{1,0:T(8,128)}, f32[504,252]{1,0:T(8,128)},...) custom-call(f32[2016,126]{1,0:T(8,128)} %refs_0_.1, ...), custom_call_target="tpu_custom_call" | custom-call | flops 1 | bytes 1 | tf_op jit(solution)/shard_map/lars_prepare/pallas_call | solution.py:1560
  498.3 2.3 squares.1
  501.7 3.4 join_rows.2
  508.1 2.6 own_square.1
  510.8 4.0 collective-permute-start.61
  517.9 8.6 %all_to_all.97 = f32[8,2,128]{2,1,0:T(2,128)S(1)} all-to-all(f32[8,2,128]{2,1,0:T(2,128)S(1)} %broadcast_in_dim.66), channel_id=1, replica_groups=mesh['dp'=8,'mp'=4] {'dp'}, dimensions={0} | all-to-all | bytes 16384 | tf_op jit(solution)/shard_map/all_to_all | solution.py:97
  527.1 3.3 all-to-all-start.17
  536.6 7.0 %lars.1 = (f32[504,252]{1,0:T(8,128)}, f32[504,252]{1,0:T(8,128)}, f32[2016,126]{1,0:T(8,128)}, f32[504,504]{1,0:T(8,128)}, f32[504,252]{1,0:T(8,128)}, /*index=...) custom-call(s32[1]{0:T(128)} %bitcast.me_ref.m_ref, f32[2,128]{1,0:T(2,128)} %copy-done.40, ...), custom_call_target="tpu_custom_call" | custom-call | flops 1 | bytes 1 | tf_op jit(solution)/shard_map/lars/pallas_call | solution.py:1598
  (317 shorter events, 115.9 us)
Async XLA Ops:
  10.7 29.8 %collective-permute-start = (bf16[512,256]{1,0:T(8,128)(2,1)}, bf16[512,256]{1,0:T(8,128)(2,1)}, u32[]{:S(2)}, u32[]{:S(2)}) collective-permute-start(bf16[512,256]{1,0:T(8,128)(2,1)} %fusion), channel_id=1, source_target_pairs={{0,3},{1,2},{2,1},{3,0},{4,7},{5,6},{6,5},{7,4},{8,11},{9,10},{10,... | collective-permute-start | bytes 786440 | tf_op jit(solution)/shard_map/ppermute | solution.py:146
  15.7 24.7 %collective-permute-start.1 = (bf16[512,256]{1,0:T(8,128)(2,1)}, bf16[512,256]{1,0:T(8,128)(2,1)}, u32[]{:S(2)}, u32[]{:S(2)}) collective-permute-start(bf16[512,256]{1,0:T(8,128)(2,1)} %fusion), channel_id=1, source_target_pairs={{0,2},{1,3},{2,0},{3,1},{4,6},{5,7},{6,4},{7,5},{8,10},{9,11},{10,... | collective-permute-start | bytes 786440 | tf_op jit(solution)/shard_map/ppermute | solution.py:146
  15.8 25.3 %collective-permute-start.2 = (bf16[512,256]{1,0:T(8,128)(2,1)}, bf16[512,256]{1,0:T(8,128)(2,1)}, u32[]{:S(2)}, u32[]{:S(2)}) collective-permute-start(bf16[512,256]{1,0:T(8,128)(2,1)} %fusion), channel_id=1, source_target_pairs={{0,1},{1,0},{2,3},{3,2},{4,5},{5,4},{6,7},{7,6},{8,9},{9,8},{10,11... | collective-permute-start | bytes 786440 | tf_op jit(solution)/shard_map/ppermute | solution.py:146
  16.6 17.6 %collective-permute-start.4 = (bf16[504,256]{1,0:T(8,128)(2,1)S(1)}, bf16[504,256]{1,0:T(8,128)(2,1)S(1)}, u32[]{:S(2)}, u32[]{:S(2)}) collective-permute-start(bf16[504,256]{1,0:T(8,128)(2,1)S(1)} %fusion.2.refs_0_), channel_id=1, source_target_pairs={{0,8},{4,12},{8,0},{12,4},{16,24},{20,28},{24,16},{28,20},{1,9},{5... | collective-permute-start | bytes 774152 | tf_op jit(solution)/shard_map/ppermute | solution.py:158
  18.3 15.9 %collective-permute-start.6 = (bf16[504,256]{1,0:T(8,128)(2,1)S(1)}, bf16[504,256]{1,0:T(8,128)(2,1)}, u32[]{:S(2)}, u32[]{:S(2)}) collective-permute-start(bf16[504,256]{1,0:T(8,128)(2,1)S(1)} %fusion.2.refs_0_), channel_id=1, source_target_pairs={{0,16},{4,20},{8,24},{12,28},{16,0},{20,4},{24,8},{28,12},{1,17},{... | collective-permute-start | bytes 774152 | tf_op jit(solution)/shard_map/ppermute | solution.py:158
  20.5 19.2 %all-to-all-start = ((f32[4,6,504]{2,1,0:T(8,128)}), f32[4,6,504]{2,1,0:T(8,128)S(1)}, u32[]{:S(2)}, u32[]{:S(2)}) async-start(f32[4,6,504]{2,1,0:T(8,128)} %broadcast_in_dim.48), calls=%async_computation | async-start | bytes 131072 | tf_op jit(solution)/shard_map/all_to_all | solution.py:97
  34.1 8.7 %collective-permute-start.3 = (bf16[504,256]{1,0:T(8,128)(2,1)S(1)}, bf16[504,256]{1,0:T(8,128)(2,1)S(1)}, u32[]{:S(2)}, u32[]{:S(2)}) collective-permute-start(bf16[504,256]{1,0:T(8,128)(2,1)S(1)} %fusion.2.refs_0_), channel_id=1, source_target_pairs={{0,4},{4,0},{8,12},{12,8},{16,20},{20,16},{24,28},{28,24},{1,5},{5... | collective-permute-start | bytes 774152 | tf_op jit(solution)/shard_map/ppermute | solution.py:169
  34.3 6.7 %collective-permute-start.8 = (bf16[504,256]{1,0:T(8,128)(2,1)S(1)}, bf16[504,256]{1,0:T(8,128)(2,1)S(1)}, u32[]{:S(2)}, u32[]{:S(2)}) collective-permute-start(bf16[504,256]{1,0:T(8,128)(2,1)S(1)} %broadcast_select_fusion.4), channel_id=1, source_target_pairs={{0,16},{4,12},{8,24},{12,4},{16,0},{20,28},{24,8},{28,20},{1,17},{... | collective-permute-start | bytes 774152 | tf_op jit(solution)/shard_map/ppermute | solution.py:163
  43.6 25.6 %collective-permute-start.11 = (bf16[2048,256]{1,0:T(8,128)(2,1)S(1)}, bf16[2048,256]{1,0:T(8,128)(2,1)}, u32[]{:S(2)}, u32[]{:S(2)}) collective-permute-start(bf16[2048,256]{1,0:T(8,128)(2,1)S(1)} %bitcast.93), channel_id=1, source_target_pairs={{0,8},{4,12},{8,0},{12,4},{16,24},{20,28},{24,16},{28,20},{1,9},{5... | collective-permute-start | bytes 3145736 | tf_op jit(solution)/shard_map/ppermute | solution.py:158
  45.1 25.3 %collective-permute-start.12 = (bf16[2048,256]{1,0:T(8,128)(2,1)S(1)}, bf16[2048,256]{1,0:T(8,128)(2,1)}, u32[]{:S(2)}, u32[]{:S(2)}) collective-permute-start(bf16[2048,256]{1,0:T(8,128)(2,1)S(1)} %bitcast.94), channel_id=1, source_target_pairs={{0,16},{4,20},{8,24},{12,28},{16,0},{20,4},{24,8},{28,12},{1,17},{... | collective-permute-start | bytes 3145736 | tf_op jit(solution)/shard_map/ppermute | solution.py:158
  46.6 41.5 %all-to-all-start.1 = ((bf16[4,392,512]{2,1,0:T(8,128)(2,1)}), bf16[4,392,512]{2,1,0:T(8,128)(2,1)S(1)}, u32[]{:S(2)}, u32[]{:S(2)}) async-start(bf16[4,392,512]{2,1,0:T(8,128)(2,1)} %get-tuple-element.201), calls=%async_computation.1 | async-start | bytes 3211264 | tf_op jit(solution)/shard_map/all_to_all | solution.py:142
  71.7 15.0 %collective-permute-start.15 = (bf16[2048,256]{1,0:T(8,128)(2,1)S(1)}, bf16[2048,256]{1,0:T(8,128)(2,1)}, u32[]{:S(2)}, u32[]{:S(2)}) collective-permute-start(bf16[2048,256]{1,0:T(8,128)(2,1)S(1)} %broadcast_select_fusion.1), channel_id=1, source_target_pairs={{0,16},{4,12},{8,24},{12,4},{16,0},{20,28},{24,8},{28,20},{1,17},{... | collective-permute-start | bytes 3145736 | tf_op jit(solution)/shard_map/ppermute | solution.py:163
  73.3 20.0 %collective-permute-start.10 = (bf16[2048,256]{1,0:T(8,128)(2,1)S(1)}, bf16[2048,256]{1,0:T(8,128)(2,1)}, u32[]{:S(2)}, u32[]{:S(2)}) collective-permute-start(bf16[2048,256]{1,0:T(8,128)(2,1)S(1)} %bitcast.95), channel_id=1, source_target_pairs={{0,4},{4,0},{8,12},{12,8},{16,20},{20,16},{24,28},{28,24},{1,5},{5... | collective-permute-start | bytes 3145736 | tf_op jit(solution)/shard_map/ppermute | solution.py:169
  73.3 20.0 %collective-permute-start.13 = (bf16[2048,256]{1,0:T(8,128)(2,1)}, bf16[2048,256]{1,0:T(8,128)(2,1)}, u32[]{:S(2)}, u32[]{:S(2)}) collective-permute-start(bf16[2048,256]{1,0:T(8,128)(2,1)} %collective-permute-done.11.refs_2_), channel_id=1, source_target_pairs={{0,4},{4,0},{8,12},{12,8},{16,20},{20,16},{24,28},{28,24},{1,5},{5... | collective-permute-start | bytes 3145736 | tf_op jit(solution)/shard_map/ppermute | solution.py:169
  73.8 19.5 %collective-permute-start.14 = (bf16[2048,256]{1,0:T(8,128)(2,1)}, bf16[2048,256]{1,0:T(8,128)(2,1)}, u32[]{:S(2)}, u32[]{:S(2)}) collective-permute-start(bf16[2048,256]{1,0:T(8,128)(2,1)} %collective-permute-done.12.refs_4_), channel_id=1, source_target_pairs={{0,4},{4,0},{8,12},{12,8},{16,20},{20,16},{24,28},{28,24},{1,5},{5... | collective-permute-start | bytes 3145736 | tf_op jit(solution)/shard_map/ppermute | solution.py:169
  86.7 6.7 %collective-permute-start.16 = (bf16[2048,256]{1,0:T(8,128)(2,1)}, bf16[2048,256]{1,0:T(8,128)(2,1)}, u32[]{:S(2)}, u32[]{:S(2)}) collective-permute-start(bf16[2048,256]{1,0:T(8,128)(2,1)} %collective-permute-done.15.refs_6_), channel_id=1, source_target_pairs={{0,4},{4,0},{8,12},{12,8},{16,20},{20,16},{24,28},{28,24},{1,5},{5... | collective-permute-start | bytes 3145736 | tf_op jit(solution)/shard_map/ppermute | solution.py:169
  89.2 22.5 %all-to-all-start.2 = ((bf16[4,256,256]{2,1,0:T(8,128)(2,1)}), bf16[4,256,256]{2,1,0:T(8,128)(2,1)}, u32[]{:S(2)}, u32[]{:S(2)}) async-start(bf16[4,256,256]{2,1,0:T(8,128)(2,1)} %broadcast_in_dim.51), calls=%async_computation.2 | async-start | bytes 1048576 | tf_op jit(solution)/shard_map/all_to_all | solution.py:97
  111.7 12.4 %collective-permute-start.22 = (bf16[1024,256]{1,0:T(8,128)(2,1)}, bf16[1024,256]{1,0:T(8,128)(2,1)S(1)}, u32[]{:S(2)}, u32[]{:S(2)}) collective-permute-start(bf16[1024,256]{1,0:T(8,128)(2,1)} %bitcast.16.refs_0_), channel_id=1, source_target_pairs={{0,8},{4,12},{8,0},{12,4},{16,24},{20,28},{24,16},{28,20},{1,9},{5... | collective-permute-start | bytes 1572872 | tf_op jit(solution)/shard_map/ppermute | solution.py:158
  112.3 12.0 %collective-permute-start.23 = (bf16[1024,256]{1,0:T(8,128)(2,1)}, bf16[1024,256]{1,0:T(8,128)(2,1)S(1)}, u32[]{:S(2)}, u32[]{:S(2)}) collective-permute-start(bf16[1024,256]{1,0:T(8,128)(2,1)} %bitcast.16.refs_0_), channel_id=1, source_target_pairs={{0,16},{4,20},{8,24},{12,28},{16,0},{20,4},{24,8},{28,12},{1,17},{... | collective-permute-start | bytes 1572872 | tf_op jit(solution)/shard_map/ppermute | solution.py:158
  117.5 4.7 collective-permute-start.21
  125.4 28.9 %all-to-all-start.3 = ((bf16[4,512,256]{2,1,0:T(8,128)(2,1)}), bf16[4,512,256]{2,1,0:T(8,128)(2,1)S(1)}, u32[]{:S(2)}, u32[]{:S(2)}) async-start(bf16[4,512,256]{2,1,0:T(8,128)(2,1)} %broadcast_in_dim.52), calls=%async_computation.3 | async-start | bytes 2097152 | tf_op jit(solution)/shard_map/all_to_all | solution.py:97
  130.5 14.0 %collective-permute-start.24 = (bf16[1024,256]{1,0:T(8,128)(2,1)S(1)}, bf16[1024,256]{1,0:T(8,128)(2,1)}, u32[]{:S(2)}, u32[]{:S(2)}) collective-permute-start(bf16[1024,256]{1,0:T(8,128)(2,1)S(1)} %broadcast_select_fusion.2), channel_id=1, source_target_pairs={{0,16},{4,12},{8,24},{12,4},{16,0},{20,28},{24,8},{28,20},{1,17},{... | collective-permute-start | bytes 1572872 | tf_op jit(solution)/shard_map/ppermute | solution.py:163
  151.2 12.7 %collective-permute-start.30 = (bf16[1024,256]{1,0:T(8,128)(2,1)}, bf16[1024,256]{1,0:T(8,128)(2,1)}, u32[]{:S(2)}, u32[]{:S(2)}) collective-permute-start(bf16[1024,256]{1,0:T(8,128)(2,1)} %bitcast.16.refs_0_), channel_id=1, source_target_pairs={{0,4},{4,0},{8,12},{12,8},{16,20},{20,16},{24,28},{28,24},{1,5},{5... | collective-permute-start | bytes 1572872 | tf_op jit(solution)/shard_map/ppermute | solution.py:169
  154.4 23.6 %collective-permute-start.34 = (bf16[2048,256]{1,0:T(8,128)(2,1)S(1)}, bf16[2048,256]{1,0:T(8,128)(2,1)S(1)}, u32[]{:S(2)}, u32[]{:S(2)}) collective-permute-start(bf16[2048,256]{1,0:T(8,128)(2,1)S(1)} %bitcast.98), channel_id=1, source_target_pairs={{0,8},{4,12},{8,0},{12,4},{16,24},{20,28},{24,16},{28,20},{1,9},{5... | collective-permute-start | bytes 3145736 | tf_op jit(solution)/shard_map/ppermute | solution.py:158
  155.0 23.1 %collective-permute-start.35 = (bf16[2048,256]{1,0:T(8,128)(2,1)S(1)}, bf16[2048,256]{1,0:T(8,128)(2,1)S(1)}, u32[]{:S(2)}, u32[]{:S(2)}) collective-permute-start(bf16[2048,256]{1,0:T(8,128)(2,1)S(1)} %bitcast.99), channel_id=1, source_target_pairs={{0,16},{4,20},{8,24},{12,28},{16,0},{20,4},{24,8},{28,12},{1,17},{... | collective-permute-start | bytes 3145736 | tf_op jit(solution)/shard_map/ppermute | solution.py:158
  156.7 3.8 collective-permute-start.28
  160.5 4.7 collective-permute-start.29
  179.4 16.6 %collective-permute-start.39 = (bf16[2048,256]{1,0:T(8,128)(2,1)}, bf16[2048,256]{1,0:T(8,128)(2,1)}, u32[]{:S(2)}, u32[]{:S(2)}) collective-permute-start(bf16[2048,256]{1,0:T(8,128)(2,1)} %broadcast_select_fusion), channel_id=1, source_target_pairs={{0,16},{4,12},{8,24},{12,4},{16,0},{20,28},{24,8},{28,20},{1,17},{... | collective-permute-start | bytes 3145736 | tf_op jit(solution)/shard_map/ppermute | solution.py:163
  181.8 14.1 %all-to-all-start.4 = ((bf16[4,208,256]{2,1,0:T(8,128)(2,1)}), bf16[4,208,256]{2,1,0:T(8,128)(2,1)}, u32[]{:S(2)}, u32[]{:S(2)}) async-start(bf16[4,208,256]{2,1,0:T(8,128)(2,1)} %broadcast_in_dim.55), calls=%async_computation.4 | async-start | bytes 851968 | tf_op jit(solution)/shard_map/all_to_all | solution.py:97
  186.6 10.2 %collective-permute-start.36 = (bf16[2048,256]{1,0:T(8,128)(2,1)S(1)}, bf16[2048,256]{1,0:T(8,128)(2,1)}, u32[]{:S(2)}, u32[]{:S(2)}) collective-permute-start(bf16[2048,256]{1,0:T(8,128)(2,1)S(1)} %bitcast.100), channel_id=1, source_target_pairs={{0,4},{4,0},{8,12},{12,8},{16,20},{20,16},{24,28},{28,24},{1,5},{5... | collective-permute-start | bytes 3145736 | tf_op jit(solution)/shard_map/ppermute | solution.py:169
  186.6 11.4 %collective-permute-start.37 = (bf16[2048,256]{1,0:T(8,128)(2,1)S(1)}, bf16[2048,256]{1,0:T(8,128)(2,1)}, u32[]{:S(2)}, u32[]{:S(2)}) collective-permute-start(bf16[2048,256]{1,0:T(8,128)(2,1)S(1)} %collective-permute-done.34.refs_2_), channel_id=1, source_target_pairs={{0,4},{4,0},{8,12},{12,8},{16,20},{20,16},{24,28},{28,24},{1,5},{5... | collective-permute-start | bytes 3145736 | tf_op jit(solution)/shard_map/ppermute | solution.py:169
  187.1 11.4 %collective-permute-start.38 = (bf16[2048,256]{1,0:T(8,128)(2,1)S(1)}, bf16[2048,256]{1,0:T(8,128)(2,1)}, u32[]{:S(2)}, u32[]{:S(2)}) collective-permute-start(bf16[2048,256]{1,0:T(8,128)(2,1)S(1)} %collective-permute-done.35.refs_4_), channel_id=1, source_target_pairs={{0,4},{4,0},{8,12},{12,8},{16,20},{20,16},{24,28},{28,24},{1,5},{5... | collective-permute-start | bytes 3145736 | tf_op jit(solution)/shard_map/ppermute | solution.py:169
  195.9 4.9 collective-permute-start.40
  195.9 13.4 %collective-permute-start.41 = (bf16[832,256]{1,0:T(8,128)(2,1)}, bf16[832,256]{1,0:T(8,128)(2,1)}, u32[]{:S(2)}, u32[]{:S(2)}) collective-permute-start(bf16[832,256]{1,0:T(8,128)(2,1)} %bitcast.28.refs_0_), channel_id=1, source_target_pairs={{0,8},{4,12},{8,0},{12,4},{16,24},{20,28},{24,16},{28,20},{1,9},{5... | collective-permute-start | bytes 1277960 | tf_op jit(solution)/shard_map/ppermute | solution.py:158
  196.8 12.5 %collective-permute-start.42 = (bf16[832,256]{1,0:T(8,128)(2,1)}, bf16[832,256]{1,0:T(8,128)(2,1)S(1)}, u32[]{:S(2)}, u32[]{:S(2)}) collective-permute-start(bf16[832,256]{1,0:T(8,128)(2,1)} %bitcast.28.refs_0_), channel_id=1, source_target_pairs={{0,16},{4,20},{8,24},{12,28},{16,0},{20,4},{24,8},{28,12},{1,17},{... | collective-permute-start | bytes 1277960 | tf_op jit(solution)/shard_map/ppermute | solution.py:158
  197.9 20.3 %collective-permute-start.43 = (bf16[392,512]{1,0:T(8,128)(2,1)}, bf16[392,512]{1,0:T(8,128)(2,1)S(1)}, u32[]{:S(2)}, u32[]{:S(2)}) collective-permute-start(bf16[392,512]{1,0:T(8,128)(2,1)} %get-tuple-element.248), channel_id=1, source_target_pairs={{0,1},{1,0},{2,3},{3,2},{4,5},{5,4},{6,7},{7,6},{8,9},{9,8},{10,11... | collective-permute-start | bytes 1204232 | tf_op jit(solution)/shard_map/ppermute | solution.py:1758
  198.5 20.6 %collective-permute-start.44 = (bf16[392,512]{1,0:T(8,128)(2,1)}, bf16[392,512]{1,0:T(8,128)(2,1)S(1)}, u32[]{:S(2)}, u32[]{:S(2)}) collective-permute-start(bf16[392,512]{1,0:T(8,128)(2,1)} %get-tuple-element.249), channel_id=1, source_target_pairs={{0,2},{1,3},{2,0},{3,1},{4,6},{5,7},{6,4},{7,5},{8,10},{9,11},{10,... | collective-permute-start | bytes 1204232 | tf_op jit(solution)/shard_map/ppermute | solution.py:1759
  220.3 11.9 %collective-permute-start.45 = (bf16[832,256]{1,0:T(8,128)(2,1)S(1)}, bf16[832,256]{1,0:T(8,128)(2,1)S(1)}, u32[]{:S(2)}, u32[]{:S(2)}) collective-permute-start(bf16[832,256]{1,0:T(8,128)(2,1)S(1)} %broadcast_select_fusion.3), channel_id=1, source_target_pairs={{0,16},{4,12},{8,24},{12,4},{16,0},{20,28},{24,8},{28,20},{1,17},{... | collective-permute-start | bytes 1277960 | tf_op jit(solution)/shard_map/ppermute | solution.py:163
  222.1 9.4 %all-to-all-start.6 = ((f32[4,2,2048]{2,1,0:T(2,128)}), f32[4,2,2048]{2,1,0:T(2,128)S(1)}, u32[]{:S(2)}, u32[]{:S(2)}) async-start(f32[4,2,2048]{2,1,0:T(2,128)} %broadcast_in_dim.57), calls=%async_computation.6 | async-start | bytes 131072 | tf_op jit(solution)/shard_map/all_to_all | solution.py:97
  225.8 152.6 %reduce-scatter.4.cloned.1.call-start = ((), (), s32[]{:S(2)}) async-start(), calls=%async_computation.21 | async-start | bytes 9437184 | tf_op jit(solution)/shard_map/reduce_scatter | solution.py:1813
  225.8 11.6 %collective-permute-start.46 = (bf16[832,256]{1,0:T(8,128)(2,1)}, bf16[832,256]{1,0:T(8,128)(2,1)S(1)}, u32[]{:S(2)}, u32[]{:S(2)}) collective-permute-start(bf16[832,256]{1,0:T(8,128)(2,1)} %bitcast.28.refs_0_), channel_id=1, source_target_pairs={{0,4},{4,0},{8,12},{12,8},{16,20},{20,16},{24,28},{28,24},{1,5},{5... | collective-permute-start | bytes 1277960 | tf_op jit(solution)/shard_map/ppermute | solution.py:169
  225.8 11.6 %collective-permute-start.47 = (bf16[832,256]{1,0:T(8,128)(2,1)}, bf16[832,256]{1,0:T(8,128)(2,1)S(1)}, u32[]{:S(2)}, u32[]{:S(2)}) collective-permute-start(bf16[832,256]{1,0:T(8,128)(2,1)} %collective-permute-done.41.refs_2_), channel_id=1, source_target_pairs={{0,4},{4,0},{8,12},{12,8},{16,20},{20,16},{24,28},{28,24},{1,5},{5... | collective-permute-start | bytes 1277960 | tf_op jit(solution)/shard_map/ppermute | solution.py:169
  226.3 11.2 %collective-permute-start.48 = (bf16[832,256]{1,0:T(8,128)(2,1)S(1)}, bf16[832,256]{1,0:T(8,128)(2,1)S(1)}, u32[]{:S(2)}, u32[]{:S(2)}) collective-permute-start(bf16[832,256]{1,0:T(8,128)(2,1)S(1)} %collective-permute-done.42.refs_4_), channel_id=1, source_target_pairs={{0,4},{4,0},{8,12},{12,8},{16,20},{20,16},{24,28},{28,24},{1,5},{5... | collective-permute-start | bytes 1277960 | tf_op jit(solution)/shard_map/ppermute | solution.py:169
  232.2 5.3 collective-permute-start.49
  251.4 17.5 %collective-permute-start.50 = (bf16[392,512]{1,0:T(8,128)(2,1)}, bf16[392,512]{1,0:T(8,128)(2,1)S(1)}, u32[]{:S(2)}, u32[]{:S(2)}) collective-permute-start(bf16[392,512]{1,0:T(8,128)(2,1)} %get-tuple-element.272), channel_id=1, source_target_pairs={{0,3},{1,2},{2,1},{3,0},{4,7},{5,6},{6,5},{7,4},{8,11},{9,10},{10,... | collective-permute-start | bytes 1204232 | tf_op jit(solution)/shard_map/ppermute | solution.py:1786
  253.1 23.2 %collective-permute-start.51 = (bf16[392,512]{1,0:T(8,128)(2,1)}, bf16[392,512]{1,0:T(8,128)(2,1)S(1)}, u32[]{:S(2)}, u32[]{:S(2)}) collective-permute-start(bf16[392,512]{1,0:T(8,128)(2,1)} %get-tuple-element.275), channel_id=1, source_target_pairs={{0,1},{1,0},{2,3},{3,2},{4,5},{5,4},{6,7},{7,6},{8,9},{9,8},{10,11... | collective-permute-start | bytes 1204232 | tf_op jit(solution)/shard_map/ppermute | solution.py:1787
  307.3 21.3 %collective-permute-start.52 = (bf16[392,512]{1,0:T(8,128)(2,1)S(1)}, bf16[392,512]{1,0:T(8,128)(2,1)S(1)}, u32[]{:S(2)}, u32[]{:S(2)}) collective-permute-start(bf16[392,512]{1,0:T(8,128)(2,1)S(1)} %copy-done.47), channel_id=1, source_target_pairs={{0,2},{1,3},{2,0},{3,1},{4,6},{5,7},{6,4},{7,5},{8,10},{9,11},{10,... | collective-permute-start | bytes 1204232 | tf_op jit(solution)/shard_map/ppermute | solution.py:1808
  339.8 9.7 %all-to-all-start.11 = ((f32[4,2,2048]{2,1,0:T(2,128)}), f32[4,2,2048]{2,1,0:T(2,128)S(1)}, u32[]{:S(2)}, u32[]{:S(2)}) async-start(f32[4,2,2048]{2,1,0:T(2,128)} %broadcast_in_dim.62), calls=%async_computation.11 | async-start | bytes 131072 | tf_op jit(solution)/shard_map/all_to_all | solution.py:97
  351.3 25.6 %all-to-all-start.12 = ((bf16[32,2,5120]{2,1,0:T(2,128)(2,1)}), bf16[32,2,5120]{2,1,0:T(2,128)(2,1)S(1)}, u32[]{:S(2)}, u32[]{:S(2)}) async-start(bf16[32,2,5120]{2,1,0:T(2,128)(2,1)} %broadcast_in_dim.63), calls=%async_computation.12 | async-start | bytes 1310720 | tf_op jit(solution)/shard_map/all_to_all | solution.py:121
  353.9 54.8 %reduce-scatter.6.cloned.1.call-start = ((), (), s32[]{:S(2)}) async-start(), calls=%async_computation.22 | async-start | bytes 1310720 | tf_op jit(solution)/shard_map/reduce_scatter | solution.py:1832
  378.4 83.9 %reduce-scatter.8.cloned.1.call-start = ((), (), s32[]{:S(2)}) async-start(), calls=%async_computation.23 | async-start | bytes 2359296 | tf_op jit(solution)/shard_map/reduce_scatter | solution.py:1844
  408.8 7.5 %collective-permute-start.53 = (bf16[4,4,512,256]{3,2,1,0:T(8,128)(2,1)}, bf16[4,4,512,256]{3,2,1,0:T(8,128)(2,1)}, u32[]{:S(2)}, u32[]{:S(2)}) collective-permute-start(bf16[4,4,512,256]{3,2,1,0:T(8,128)(2,1)} %get-tuple-element.305), channel_id=1, source_target_pairs={{0,4},{4,0},{8,12},{12,8},{16,20},{20,16},{24,28},{28,24},{1,5},{5... | collective-permute-start | bytes 12582920 | tf_op jit(solution)/shard_map/ppermute | solution.py:183
  418.7 15.0 %collective-permute-start.54 = (bf16[4,512,256]{2,1,0:T(8,128)(2,1)}, bf16[4,512,256]{2,1,0:T(8,128)(2,1)S(1)}, u32[]{:S(2)}, u32[]{:S(2)}) collective-permute-start(bf16[4,512,256]{2,1,0:T(8,128)(2,1)} %twin_sum.1), channel_id=1, source_target_pairs={{0,16},{4,12},{8,24},{12,4},{16,0},{20,28},{24,8},{28,20},{1,17},{... | collective-permute-start | bytes 3145736 | tf_op jit(solution)/shard_map/ppermute | solution.py:179
  420.2 13.0 %collective-permute-start.55 = (bf16[392,512]{1,0:T(8,128)(2,1)S(1)}, bf16[392,512]{1,0:T(8,128)(2,1)S(1)}, u32[]{:S(2)}, u32[]{:S(2)}) collective-permute-start(bf16[392,512]{1,0:T(8,128)(2,1)S(1)} %copy-done.46), channel_id=1, source_target_pairs={{0,3},{1,2},{2,1},{3,0},{4,7},{5,6},{6,5},{7,4},{8,11},{9,10},{10,... | collective-permute-start | bytes 1204232 | tf_op jit(solution)/shard_map/ppermute | solution.py:1836
  434.7 65.8 %all-to-all-start.15 = ((bf16[4,392,512]{2,1,0:T(8,128)(2,1)}), bf16[4,392,512]{2,1,0:T(8,128)(2,1)S(1)}, u32[]{:S(2)}, u32[]{:S(2)}) async-start(bf16[4,392,512]{2,1,0:T(8,128)(2,1)} %mix_back.3), calls=%async_computation.18 | async-start | bytes 3211264 | tf_op jit(solution)/shard_map/all_to_all | solution.py:142
  447.4 26.9 %collective-permute-start.56 = (bf16[4,512,256]{2,1,0:T(8,128)(2,1)}, bf16[4,512,256]{2,1,0:T(8,128)(2,1)S(1)}, u32[]{:S(2)}, u32[]{:S(2)}) collective-permute-start(bf16[4,512,256]{2,1,0:T(8,128)(2,1)} %get-tuple-element.314), channel_id=1, source_target_pairs={{0,8},{4,12},{8,0},{12,4},{16,24},{20,28},{24,16},{28,20},{1,9},{5... | collective-permute-start | bytes 3145736 | tf_op jit(solution)/shard_map/ppermute | solution.py:187
  448.6 26.7 %collective-permute-start.57 = (bf16[4,512,256]{2,1,0:T(8,128)(2,1)}, bf16[4,512,256]{2,1,0:T(8,128)(2,1)}, u32[]{:S(2)}, u32[]{:S(2)}) collective-permute-start(bf16[4,512,256]{2,1,0:T(8,128)(2,1)} %get-tuple-element.315), channel_id=1, source_target_pairs={{0,16},{4,20},{8,24},{12,28},{16,0},{20,4},{24,8},{28,12},{1,17},{... | collective-permute-start | bytes 3145736 | tf_op jit(solution)/shard_map/ppermute | solution.py:187
  479.8 25.3 %collective-permute-start.58 = (bf16[640,256]{1,0:T(8,128)(2,1)}, bf16[640,256]{1,0:T(8,128)(2,1)S(1)}, u32[]{:S(2)}, u32[]{:S(2)}) collective-permute-start(bf16[640,256]{1,0:T(8,128)(2,1)} %get-tuple-element.329), channel_id=1, source_target_pairs={{0,1},{1,0},{2,3},{3,2},{4,5},{5,4},{6,7},{7,6},{8,9},{9,8},{10,11... | collective-permute-start | bytes 983048 | tf_op jit(solution)/shard_map/ppermute | solution.py:191
  481.7 25.6 %collective-permute-start.59 = (bf16[640,256]{1,0:T(8,128)(2,1)}, bf16[640,256]{1,0:T(8,128)(2,1)S(1)}, u32[]{:S(2)}, u32[]{:S(2)}) collective-permute-start(bf16[640,256]{1,0:T(8,128)(2,1)} %get-tuple-element.330), channel_id=1, source_target_pairs={{0,2},{1,3},{2,0},{3,1},{4,6},{5,7},{6,4},{7,5},{8,10},{9,11},{10,... | collective-permute-start | bytes 983048 | tf_op jit(solution)/shard_map/ppermute | solution.py:191
  483.9 23.4 %collective-permute-start.60 = (bf16[640,256]{1,0:T(8,128)(2,1)}, bf16[640,256]{1,0:T(8,128)(2,1)S(1)}, u32[]{:S(2)}, u32[]{:S(2)}) collective-permute-start(bf16[640,256]{1,0:T(8,128)(2,1)} %get-tuple-element.331), channel_id=1, source_target_pairs={{0,3},{1,2},{2,1},{3,0},{4,7},{5,6},{6,5},{7,4},{8,11},{9,10},{10,... | collective-permute-start | bytes 983048 | tf_op jit(solution)/shard_map/ppermute | solution.py:191
  510.8 15.7 %collective-permute-start.61 = (bf16[128,256]{1,0:T(8,128)(2,1)}, bf16[128,256]{1,0:T(8,128)(2,1)S(1)}, u32[]{:S(2)}, u32[]{:S(2)}) collective-permute-start(bf16[128,256]{1,0:T(8,128)(2,1)} %get-tuple-element.369), channel_id=1, source_target_pairs={{0,1},{1,0},{2,3},{3,2},{4,5},{5,4},{6,7},{7,6},{8,9},{9,8},{10,11... | collective-permute-start | bytes 196616 | tf_op jit(solution)/shard_map/ppermute | solution.py:146
  514.8 11.7 %collective-permute-start.62 = (bf16[128,256]{1,0:T(8,128)(2,1)}, bf16[128,256]{1,0:T(8,128)(2,1)S(1)}, u32[]{:S(2)}, u32[]{:S(2)}) collective-permute-start(bf16[128,256]{1,0:T(8,128)(2,1)} %get-tuple-element.369), channel_id=1, source_target_pairs={{0,2},{1,3},{2,0},{3,1},{4,6},{5,7},{6,4},{7,5},{8,10},{9,11},{10,... | collective-permute-start | bytes 196616 | tf_op jit(solution)/shard_map/ppermute | solution.py:146
  515.6 10.9 %collective-permute-start.63 = (bf16[128,256]{1,0:T(8,128)(2,1)}, bf16[128,256]{1,0:T(8,128)(2,1)S(1)}, u32[]{:S(2)}, u32[]{:S(2)}) collective-permute-start(bf16[128,256]{1,0:T(8,128)(2,1)} %get-tuple-element.369), channel_id=1, source_target_pairs={{0,3},{1,2},{2,1},{3,0},{4,7},{5,6},{6,5},{7,4},{8,11},{9,10},{10,... | collective-permute-start | bytes 196616 | tf_op jit(solution)/shard_map/ppermute | solution.py:146
  527.1 8.9 %all-to-all-start.17 = ((f32[4,2,128]{2,1,0:T(2,128)}), f32[4,2,128]{2,1,0:T(2,128)S(1)}, u32[]{:S(2)}, u32[]{:S(2)}) async-start(f32[4,2,128]{2,1,0:T(2,128)} %broadcast_in_dim.67), calls=%async_computation.20 | async-start | bytes 8192 | tf_op jit(solution)/shard_map/all_to_all | solution.py:97
  (61 other events, 601.7 us)
Sparse Core Ops, SparseCore 0:
  306.5 71.8 reduce-scatter.3
  380.8 27.9 reduce-scatter.5
  420.3 41.8 reduce-scatter.7

commit v4 on v3

--- a/solution.py
+++ b/solution.py
@@ -1168,12 +1168,27 @@
 
 
 def gate_back_kernel(
-    crops, count, me_ref, dh_ref, a_ref, sums_ref, norms_ref, gate_ref, squeezed_ref, *refs
+    crops, count, me_ref, dh_from, a_ref, sums_ref, norms_ref, gate_ref, squeezed_ref, *refs
 ):
-    q_ref, stats_ref, excite_grad_ref, squeeze_grad_ref, work_ref, se_ref, sems = refs[8:]
+    (
+        q_to, stats_ref, excite_grad_ref, squeeze_grad_ref,
+        work_ref, dh_ref, q_ref, in_sems, out_sems, se_ref, sems,
+    ) = refs[8:]
+
+    def into(m):
+        lanes = pl.ds(m * LANES, LANES)
+        return pltpu.make_async_copy(dh_from.at[:, lanes], dh_ref.at[:, lanes], in_sems.at[m])
+
+    def out_of(m):
+        lanes = pl.ds(m * LANES, LANES)
+        return pltpu.make_async_copy(q_ref.at[:, lanes], q_to.at[:, lanes], out_sems.at[m])
+
+    for m in range(QUADS):
+        into(m).start()
     copies = fetch_pieces(me_ref, refs[:8], se_ref, sems, 0)
     rows = a_ref.shape[0]
     for m in range(QUADS):
+        into(m).wait()
         lanes = pl.ds(m * LANES, LANES)
         _, _, scale, shift = affine(sums_ref[:, lanes], norms_ref[:, lanes], 1, count)
         normed = a_ref[:, lanes].astype(f32) * scale + shift
@@ -1210,6 +1225,10 @@
         centred = (values - mean) * inverse
         stats_ref[0:1, lanes] = jnp.sum(q, 0, keepdims=True)
         stats_ref[1:2, lanes] = jnp.sum(q * centred, 0, keepdims=True)
+        if d % 2:
+            out_of(d // 2).start()
+    for m in range(QUADS):
+        out_of(m).wait()
 
 
 def gate_back(dh, a, sums, norms, gates, squeezed, se, count):
@@ -1217,15 +1236,19 @@
     crops = rows // PIXELS
     return pl.pallas_call(
         functools.partial(gate_back_kernel, crops, count),
-        in_specs=[SCALAR] + [pl.BlockSpec(memory_space=pltpu.VMEM)] * 6
+        in_specs=[SCALAR, pl.BlockSpec(memory_space=pl.ANY)]
+        + [pl.BlockSpec(memory_space=pltpu.VMEM)] * 5
         + [pl.BlockSpec(memory_space=pl.ANY)] * 8,
+        out_specs=[pl.BlockSpec(memory_space=pl.ANY)] + [pl.BlockSpec(memory_space=pltpu.VMEM)] * 3,
         out_shape=[
             jax.ShapeDtypeStruct((rows, width), f32),
             jax.ShapeDtypeStruct((2, width), f32),
             jax.ShapeDtypeStruct((crops, width), bf16),
             jax.ShapeDtypeStruct((crops, 512), bf16),
         ],
-        scratch_shapes=[pltpu.VMEM((rows, width), f32)] + fetch_scratch(SE_ROWS),
+        scratch_shapes=[pltpu.VMEM((rows, width), f32)] * 3
+        + [pltpu.SemaphoreType.DMA((QUADS,))] * 2
+        + fetch_scratch(SE_ROWS),
         compiler_params=params(),
         cost_estimate=BRIEF,
         name="gate_back",
@@ -1567,42 +1590,67 @@
 
 
 def lars_kernel(
-    first, m_ref, squares_ref, gains_ref, biases_ref, m_gains_ref, m_biases_ref, g1_ref, g2_ref, g3_ref, *refs
+    first, n, m_ref, squares_ref, gains_ref, biases_ref, m_gains_ref, m_biases_ref,
+    g1_ref, g2_ref, g3_ref, *refs
 ):
+    size = 3 * first + 2 * n
+    sources, refs = refs[:size], refs[size:]
+    targets, refs = refs[: first + n], refs[first + n :]
+    gains_out, biases_out, refs = refs[0], refs[1], refs[2:]
+    held, out, (in_sems, out_sems) = refs[:size], refs[size : size + first + n], refs[-2:]
+
+    def into(i):
+        return pltpu.make_async_copy(sources[i], held[i], in_sems.at[i])
+
+    def out_of(i):
+        return pltpu.make_async_copy(out[i], targets[i], out_sems.at[i])
+
+    for i in range(size):
+        into(i).start()
     norm_squares = squares_ref[...]
-    n = (len(refs) - 4 * first - 2) // 3
-    prepared, out = refs[3 * first : 3 * first + 2 * n], refs[3 * first + 2 * n :]
-    for i in range(first):
-        weight, gradient, momentum = (refs[3 * i + j] for j in range(3))
-        out[i][...] = step(weight[...], gradient[...], momentum[...], norm_squares, i)
-    for i in range(n):
-        rate = rate_of(norm_squares, first + i)
-        out[first + i][...] = prepared[2 * i + 1][...] + rate * prepared[2 * i][...]
-    n = n + first - 1
     lanes = pl.ds(pl.multiple_of(m_ref[0] * LANES, LANES), LANES)
     for k, ref in enumerate((g1_ref, g2_ref, g3_ref)):
         own = narrow_lanes(ref[:, lanes])
         row = slice(k, k + 1)
-        out[n + 1][row, :] = step(
+        gains_out[row, :] = step(
             gains_ref[row, :], own[1:2], m_gains_ref[row, :], norm_squares, 7 + k
         )
-        out[n + 2][row, :] = step(
+        biases_out[row, :] = step(
             biases_ref[row, :], own[0:1], m_biases_ref[row, :], norm_squares, 10 + k
         )
+    for i in range(first):
+        for j in range(3):
+            into(3 * i + j).wait()
+        weight, gradient, momentum = (held[3 * i + j][...] for j in range(3))
+        out[i][...] = step(weight, gradient, momentum, norm_squares, i)
+        out_of(i).start()
+    for i in range(n):
+        at = 3 * first + 2 * i
+        into(at).wait()
+        into(at + 1).wait()
+        out[first + i][...] = held[at + 1][...] + rate_of(norm_squares, first + i) * held[at][...]
+        out_of(first + i).start()
+    for i in range(first + n):
+        out_of(i).wait()
 
 
 def lars(norm_squares, items, norm_values, prepared):
     shapes = [w.shape for w, _, _ in items] + [v.shape for v in prepared[::2]]
-    shapes += [norm_values[0].shape] * 2
-    values = [norm_squares, *norm_values, *[v for item in items for v in item], *prepared]
-    return pl.pallas_call(
-        functools.partial(lars_kernel, len(items)),
-        in_specs=[SCALAR] + [pl.BlockSpec(memory_space=pltpu.VMEM)] * len(values),
-        out_shape=[jax.ShapeDtypeStruct(shape, f32) for shape in shapes],
+    moved = [v for item in items for v in item] + list(prepared)
+    fixed = [norm_squares, *norm_values]
+    anywhere, vmem = pl.BlockSpec(memory_space=pl.ANY), pl.BlockSpec(memory_space=pltpu.VMEM)
+    return pl.pallas_call(
+        functools.partial(lars_kernel, len(items), len(prepared) // 2),
+        in_specs=[SCALAR] + [vmem] * len(fixed) + [anywhere] * len(moved),
+        out_specs=[anywhere] * len(shapes) + [vmem] * 2,
+        out_shape=[jax.ShapeDtypeStruct(shape, f32) for shape in shapes + [norm_values[0].shape] * 2],
+        scratch_shapes=[pltpu.VMEM(v.shape, f32) for v in moved]
+        + [pltpu.VMEM(shape, f32) for shape in shapes]
+        + [pltpu.SemaphoreType.DMA((len(moved),)), pltpu.SemaphoreType.DMA((len(shapes),))],
         compiler_params=params(),
         cost_estimate=BRIEF,
         name="lars",
-    )(index_scalar("mp"), *values)
+    )(index_scalar("mp"), *fixed, *moved)
 
 
 def plain_finish(

time: 560 us -> 561 us (level)
  no operation moved by 1% of the time
where the time goes in v4:
time: 561 us; the launch traced here: 552 us
  Pallas kernels  198 us (35%)
  starting transfers between devices  106 us (19%)
  waiting for transfers between devices  106 us (19%)
  blocking collectives  77.9 us (14%)
  local copies, waits for them, and re-layouts  25.8 us (5%)
  other arithmetic  21.7 us (4%)
  between operations  15.2 us (3%)
    all_to_all x7, blocking collectives, spread(): lax.all_to_all(jnp.broadcast_to(v[None], (n,) + v.shape), axis, split_axi...  64.9 us
    all_to_all x7, starting transfers between devices, spread(): lax.all_to_all(jnp.broadcast_to(v[None], (n,) + v.shape), axis, split_axi...  29.4 us
    all_to_all x7, waiting for transfers between devices, spread(): lax.all_to_all(jnp.broadcast_to(v[None], (n,) + v.shape), axis, split_axi...  25.7 us
    pallas_call x1, Pallas kernels, conv_back(): pl.pallas_call(functools.partial(conv_back_kernel, crops, count), grid=(Q...  22.7 us
    ppermute x10, waiting for transfers between devices, sum_axis(): v = v + lax.ppermute(v, axis, flips(axis, bit))  19.5 us
    pallas_call x2, Pallas kernels, mix_back(): pl.pallas_call(functools.partial(mix_back_kernel, len(more)), in_specs=[S...  19 us
    ppermute x5, waiting for transfers between devices, gather_sides(): lax.ppermute(v, 'dp', flips('dp', 2))  17.2 us
    pallas_call x2, Pallas kernels, mix(): pl.pallas_call(mix_kernel, grid=(QUADS,), in_specs=[SCALAR, pl.BlockSpec(...  16.9 us
  transfers between devices with their start and end apart: 77, of which 34 were waited for; matrix products, arithmetic and copies ran while one was open for 6% of the time, Pallas kernels for 32%

profile of v4, /device:TPU:0, one launch (start us, length us, event | category | flops | bytes accessed | tf_op | source)
XLA Modules:
  0.0 551.6 jit_solution(16090074136876723424)
XLA Ops:
  10.7 5.0 collective-permute-start
  20.5 4.9 all-to-all-start
  28.1 2.4 fusion.9
  31.3 2.8 pad_maximum_fusion.1
  34.8 4.8 all-to-all-done
  46.6 3.7 all-to-all-start.1
  50.3 7.2 %dense_windows.1.w_ref = bf16[4,3,9,256,256]{4,3,2,1,0:T(8,128)(2,1)} custom-call(s32[1]{0:T(128)} %bitcast.1.me_ref, bf16[504,256]{1,0:T(8,128)(2,1)} %copy-done.15, bf16[504,256]{1,0:T(8,128)(2,1)} %copy-done.32, bf16[504,256]{1,0:T(8,128)(2,1)} %copy-done.16, bf16[504,256]{1,0:T(8,128)(2,1)} %copy-done.34, ...), custom_call_target="tpu_custom_call" | custom-call | flops 1 | bytes 1 | tf_op jit(solution)/shard_map/dense_windows/pallas_call | solution.py:864
  57.5 11.7 %collective-permute-done.11.refs_2_ = bf16[2048,256]{1,0:T(8,128)(2,1)} collective-permute-done((bf16[2048,256]{1,0:T(8,128)(2,1)S(1)}, bf16[2048,256]{1,0:T(8,128)(2,1)}, u32[]{:S(2)}, u32[]{:S(2)}) %collective-permute-start.11) | collective-permute-done | bytes 1048608 | tf_op jit(solution)/shard_map/ppermute | solution.py:158
  73.8 12.9 %collective-permute-done.15.refs_6_ = bf16[2048,256]{1,0:T(8,128)(2,1)} collective-permute-done((bf16[2048,256]{1,0:T(8,128)(2,1)S(1)}, bf16[2048,256]{1,0:T(8,128)(2,1)}, u32[]{:S(2)}, u32[]{:S(2)}) %collective-permute-start.15) | collective-permute-done | bytes 1048608 | tf_op jit(solution)/shard_map/ppermute | solution.py:163
  89.2 4.1 all-to-all-start.2
  93.4 8.4 %mix.2 = (f32[392,2048]{1,0:T(8,128)}, f32[2,2048]{1,0:T(2,128)}) custom-call(s32[1]{0:T(128)} %bitcast.1.me_ref, bf16[4,392,512]{2,1,0:T(8,128)(2,1)} %copy-done, bf16[2048,256]{1,0:T(8,128)(2,1)} %bitcast.96, bf16[2048,256]{1,0:T(8,128)(2,1)} %collective-permute-done.10.refs_1_, bf16[2048,256]{1,0:T(8,128)(2,1)} %collective-permute-done.11.refs_2_, ...), custom_call_target="tpu_custom_call" | custom-call | flops 1 | bytes 1 | tf_op jit(solution)/shard_map/mix/pallas_call | solution.py:380
  104.6 3.2 collective-permute-done.18
  108.4 3.2 collective-permute-done.19
  117.5 2.9 collective-permute-start.21
  125.4 5.0 all-to-all-start.3
  132.0 12.5 %conv.1 = (bf16[392,2048]{1,0:T(8,128)(2,1)}, f32[2,2048]{1,0:T(2,128)}) custom-call(f32[392,2048]{1,0:T(8,128)} %get-tuple-element.215.a_ref, f32[2,2048]{1,0:T(2,128)} %add.120.sums_ref, f32[6,2048]{1,0:T(8,128)} %bitcast.106, bf16[4,3,9,256,256]{4,3,2,1,0:T(8,128)(2,1)} %dense_windows.1.w_ref), custom_call_target="tpu_custom_call" | custom-call | flops 1 | bytes 1 | tf_op jit(solution)/shard_map/conv/pallas_call | solution.py:943
  151.2 3.2 collective-permute-done.27
  160.5 3.0 collective-permute-start.29
  167.6 6.1 %gate.1 = (bf16[4,392,512]{2,1,0:T(8,128)(2,1)}, bf16[2,2048]{1,0:T(2,128)(2,1)}, f32[2,512]{1,0:T(2,128)}, bf16[2,512]{1,0:T(2,128)(2,1)}, f32[2,2048]{1,0:T(2,128)}) custom-call(s32[1]{0:T(128)} %bitcast.1.me_ref, bf16[392,2048]{1,0:T(8,128)(2,1)} %get-tuple-element.224.a_ref.a2_ref, f32[2,2048]{1,0:T(2,128)} %add.125.sums_ref.sums2_ref, ...), custom_call_target="tpu_custom_call" | custom-call | flops 1 | bytes 1 | tf_op jit(solution)/shard_map/gate/pallas_call | solution.py:1152
  173.7 4.2 collective-permute-done.34.refs_2_
  181.8 4.8 all-to-all-start.4
  187.2 8.7 %all-to-all-done.4 = bf16[4,208,256]{2,1,0:T(8,128)(2,1)} async-done(((bf16[4,208,256]{2,1,0:T(8,128)(2,1)}), bf16[4,208,256]{2,1,0:T(8,128)(2,1)}, u32[]{:S(2)}, u32[]{:S(2)}) %all-to-all-start.4) | async-done | bytes 426016 | tf_op jit(solution)/shard_map/all_to_all | solution.py:97
  198.5 2.4 collective-permute-start.44
  200.8 8.4 %mix.3 = (f32[392,2048]{1,0:T(8,128)}, f32[2,2048]{1,0:T(2,128)}) custom-call(s32[1]{0:T(128)} %bitcast.1.me_ref, bf16[4,392,512]{2,1,0:T(8,128)(2,1)} %get-tuple-element.239.x_ref, bf16[2048,256]{1,0:T(8,128)(2,1)} %bitcast.101, bf16[2048,256]{1,0:T(8,128)(2,1)} %collective-permute-done.36.refs_1_, bf16[2048,256]{1,0:T(8,128)(2,1)} %copy-done.3, ...), custom_call_target="tpu_custom_call" | custom-call | flops 1 | bytes 1 | tf_op jit(solution)/shard_map/mix/pallas_call | solution.py:380
  210.1 8.1 %all_to_all.90 = f32[8,2,2048]{2,1,0:T(2,128)S(1)} all-to-all(f32[8,2,2048]{2,1,0:T(2,128)S(1)} %broadcast_in_dim.56), channel_id=1, replica_groups=mesh['dp'=8,'mp'=4] {'dp'}, dimensions={0} | all-to-all | bytes 262144 | tf_op jit(solution)/shard_map/all_to_all | solution.py:97
  222.1 3.7 all-to-all-start.6
  226.4 5.2 all-to-all-done.6
  232.2 5.2 value.1
  238.4 13.0 %all_to_all.91.summary_ref = bf16[32,2,2048]{2,1,0:T(2,128)(2,1)} all-to-all(bf16[32,2,2048]{2,1,0:T(2,128)(2,1)S(1)} %broadcast_in_dim.58), channel_id=1, replica_groups=mesh['dp'=8,'mp'=4] {'dp','mp'}, dimensions={0} | all-to-all | bytes 524288 | tf_op jit(solution)/shard_map/all_to_all | solution.py:121
  253.1 15.7 %head.1 = (f32[1,1]{1,0:T(1,128)}, bf16[64,256]{1,0:T(8,128)(2,1)}, bf16[3072,64]{1,0:T(8,128)(2,1)}, bf16[64,256]{1,0:T(8,128)(2,1)}, f32[64,2048]{1,0:T(8,128)}, /*index=5*/bf16[64,2048]{1,0:T(8,128)(2,1)}) custom-call(s32[1]{0:T(128)} %bitcast.1.me_ref, bf16[32,2,2048]{2,1,0:T(2,128)(2,1)} %all_to_all.91.summary_ref, bf16[832,256]{1,0:T(8,128)(2,1)} %bitcast.28.refs_0_, ...), custom_call_target="tpu_custom_call" | custom-call | flops 1 | bytes 1 | tf_op jit(solution)/shard_map/head/pallas_call | solution.py:1359
  269.6 6.7 %value_back.1 = (f32[392,2048]{1,0:T(8,128)}, f32[2,2048]{1,0:T(2,128)}) custom-call(s32[1]{0:T(128)} %bitcast.me_ref.m_ref, s32[1]{0:T(128)} %bitcast.27.first_ref, bf16[4,392,512]{2,1,0:T(8,128)(2,1)} %copy-done, f32[392,2048]{1,0:T(8,128)} %get-tuple-element.244.a_ref, f32[2,2048]{1,0:T(2,128)} %reduce_sum.91.sums_ref, f32[6,2048]{1,0:T(8,128)} %bitcast.109, ...), custom_call_target="tpu_custom_call" | custom-call | flops 1 | bytes 1 | tf_op jit(solution)/shard_map/value_back/pallas_call | solution.py:805
  277.1 7.9 %all_to_all.92 = f32[8,2,2048]{2,1,0:T(2,128)S(1)} all-to-all(f32[8,2,2048]{2,1,0:T(2,128)S(1)} %broadcast_in_dim.59), channel_id=1, replica_groups=mesh['dp'=8,'mp'=4] {'dp'}, dimensions={0} | all-to-all | bytes 262144 | tf_op jit(solution)/shard_map/all_to_all | solution.py:97
  285.1 10.6 %all_to_all.93 = f32[4,2,2048]{2,1,0:T(2,128)S(1)} all-to-all(f32[4,2,2048]{2,1,0:T(2,128)S(1)} %broadcast_in_dim.60), channel_id=1, replica_groups=mesh['dp'=8,'mp'=4] {'mp'}, dimensions={0} | all-to-all | bytes 131072 | tf_op jit(solution)/shard_map/all_to_all | solution.py:97
  296.3 10.0 %all_grads.1 = (bf16[392,2048]{1,0:T(8,128)(2,1)}, bf16[8,4,512,256]{3,2,1,0:T(8,128)(2,1)}) custom-call(bf16[4,392,512]{2,1,0:T(8,128)(2,1)} %get-tuple-element.239.x_ref, f32[392,2048]{1,0:T(8,128)} %get-tuple-element.273.g_ref.refs_8_, f32[392,2048]{1,0:T(8,128)} %get-tuple-element.244.a_ref, f32[2,2048]{1,0:T(2,128)} %reduce_sum.91.sums_ref, ...), custom_call_target="tpu_custom_call" | custom-call | flops 1 | bytes 1 | tf_op jit(solution)/shard_map/all_grads/pallas_call | solution.py:506
  308.1 9.5 %mix_back.2.dh_from = f32[392,2048]{1,0:T(8,128)} custom-call(s32[1]{0:T(128)} %bitcast.1.me_ref, bf16[392,2048]{1,0:T(8,128)(2,1)} %get-tuple-element.280.g_ref, bf16[2048,256]{1,0:T(8,128)(2,1)} %bitcast.102, bf16[2048,256]{1,0:T(8,128)(2,1)} %collective-permute-done.36.refs_1_, bf16[2048,256]{1,0:T(8,128)(2,1)} %copy-done.3, ...), custom_call_target="tpu_custom_call" | custom-call | flops 1 | bytes 1 | tf_op jit(solution)/shard_map/mix_back/pallas_call | solution.py:428
  317.6 11.7 %gate_back.1 = (f32[392,2048]{1,0:T(8,128)}, f32[2,2048]{1,0:T(2,128)}, bf16[2,2048]{1,0:T(2,128)(2,1)}, bf16[2,512]{1,0:T(2,128)(2,1)}) custom-call(s32[1]{0:T(128)} %bitcast.1.me_ref, f32[392,2048]{1,0:T(8,128)} %mix_back.2.dh_from, bf16[392,2048]{1,0:T(8,128)(2,1)} %get-tuple-element.224.a_ref.a2_ref, f32[2,2048]{1,0:T(2,128)} %add.125.sums_ref.sums2_ref, ...), custom_call_target="tpu_custom_call" | custom-call | flops 1 | bytes 1 | tf_op jit(solution)/shard_map/gate_back/pallas_call | solution.py:1237
  330.1 9.7 %all_to_all.94 = f32[8,2,2048]{2,1,0:T(2,128)S(1)} all-to-all(f32[8,2,2048]{2,1,0:T(2,128)S(1)} %broadcast_in_dim.61), channel_id=1, replica_groups=mesh['dp'=8,'mp'=4] {'dp'}, dimensions={0} | all-to-all | bytes 262144 | tf_op jit(solution)/shard_map/all_to_all | solution.py:97
  340.4 3.7 all-to-all-start.11
  344.9 5.0 all-to-all-done.11
  351.7 2.6 all-to-all-start.12
  354.6 22.7 %conv_back.1 = (bf16[392,2048]{1,0:T(8,128)(2,1)}, bf16[8,512,256]{2,1,0:T(8,128)(2,1)}, f32[2,2048]{1,0:T(2,128)}) custom-call(f32[392,2048]{1,0:T(8,128)} %get-tuple-element.283.g_ref, bf16[392,2048]{1,0:T(8,128)(2,1)} %get-tuple-element.224.a_ref.a2_ref, f32[2,2048]{1,0:T(2,128)} %add.125.sums_ref.sums2_ref, f32[2,2048]{1,0:T(2,128)} %reduce_sum.95.grad_sums_ref.g2_ref, ...), custom_call_target="tpu_custom_call" | custom-call | flops 1 | bytes 1 | tf_op jit(solution)/shard_map/conv_back/pallas_call | solution.py:1042
  379.3 8.2 %all_to_all.95 = f32[8,2,2048]{2,1,0:T(2,128)S(1)} all-to-all(f32[8,2,2048]{2,1,0:T(2,128)S(1)} %broadcast_in_dim.64), channel_id=1, replica_groups=mesh['dp'=8,'mp'=4] {'dp'}, dimensions={0} | all-to-all | bytes 262144 | tf_op jit(solution)/shard_map/all_to_all | solution.py:97
  387.6 11.8 %all_to_all.96 = f32[4,2,2048]{2,1,0:T(2,128)S(1)} all-to-all(f32[4,2,2048]{2,1,0:T(2,128)S(1)} %broadcast_in_dim.65), channel_id=1, replica_groups=mesh['dp'=8,'mp'=4] {'mp'}, dimensions={0} | all-to-all | bytes 131072 | tf_op jit(solution)/shard_map/all_to_all | solution.py:97
  400.0 8.5 %sent_grads.1 = (bf16[392,2048]{1,0:T(8,128)(2,1)}, bf16[4,4,512,256]{3,2,1,0:T(8,128)(2,1)}) custom-call(s32[1]{0:T(128)} %bitcast.1.me_ref, bf16[4,392,512]{2,1,0:T(8,128)(2,1)} %copy-done, bf16[392,2048]{1,0:T(8,128)(2,1)} %get-tuple-element.292.g_ref, f32[392,2048]{1,0:T(8,128)} %get-tuple-element.215.a_ref, f32[2,2048]{1,0:T(2,128)} %add.120.sums_ref, ...), custom_call_target="tpu_custom_call" | custom-call | flops 1 | bytes 1 | tf_op jit(solution)/shard_map/sent_grads/pallas_call | solution.py:475
  408.8 6.2 %kept_grads.1.a_ref.a1_ref.a2_ref = bf16[4,4,512,256]{3,2,1,0:T(8,128)(2,1)} custom-call(s32[1]{0:T(128)} %bitcast.1.me_ref, bf16[4,392,512]{2,1,0:T(8,128)(2,1)} %copy-done, bf16[392,2048]{1,0:T(8,128)(2,1)} %get-tuple-element.308.g_ref), custom_call_target="tpu_custom_call" | custom-call | flops 1 | bytes 1 | tf_op jit(solution)/shard_map/kept_grads/pallas_call | solution.py:532
  416.3 2.4 twin_sum.1
  421.4 9.5 %mix_back.3 = bf16[4,392,512]{2,1,0:T(8,128)(2,1)} custom-call(s32[1]{0:T(128)} %bitcast.1.me_ref, bf16[392,2048]{1,0:T(8,128)(2,1)} %get-tuple-element.308.g_ref, bf16[2048,256]{1,0:T(8,128)(2,1)} %bitcast.97, bf16[2048,256]{1,0:T(8,128)(2,1)} %collective-permute-done.10.refs_1_, bf16[2048,256]{1,0:T(8,128)(2,1)} %collective-permute-done.11.refs_2_, ...), custom_call_target="tpu_custom_call" | custom-call | flops 1 | bytes 1 | tf_op jit(solution)/shard_map/mix_back/pallas_call | solution.py:428
  430.9 2.4 collective-permute-done.55.refs_3_
  434.7 8.9 %all-to-all-start.15 = ((bf16[4,392,512]{2,1,0:T(8,128)(2,1)}), bf16[4,392,512]{2,1,0:T(8,128)(2,1)S(1)}, u32[]{:S(2)}, u32[]{:S(2)}) async-start(bf16[4,392,512]{2,1,0:T(8,128)(2,1)} %mix_back.3), calls=%async_computation.18 | async-start | bytes 3211264 | tf_op jit(solution)/shard_map/all_to_all | solution.py:142
  443.6 3.8 corner_sums.1
  452.2 4.8 small_grads.1
  457.0 5.3 reduce-scatter.8.cloned.1.call-done
  462.3 12.0 %collective-permute-done.56.across_ref = bf16[4,512,256]{2,1,0:T(8,128)(2,1)S(1)} collective-permute-done((bf16[4,512,256]{2,1,0:T(8,128)(2,1)}, bf16[4,512,256]{2,1,0:T(8,128)(2,1)S(1)}, u32[]{:S(2)}, u32[]{:S(2)}) %collective-permute-start.56) | collective-permute-done | bytes 1048608 | tf_op jit(solution)/shard_map/ppermute | solution.py:187
  475.3 4.5 side_sums.1
  484.2 3.6 weight_sums.1.weights_ref
  487.8 2.8 join_rows.3
  490.6 7.7 %lars_prepare.1 = (f32[2016,126]{1,0:T(8,128)}, f32[2016,126]{1,0:T(8,128)}, f32[504,504]{1,0:T(8,128)}, f32[504,504]{1,0:T(8,128)}, f32[504,252]{1,0:T(8,128)},...) custom-call(f32[2016,126]{1,0:T(8,128)} %refs_0_.1, ...), custom_call_target="tpu_custom_call" | custom-call | flops 1 | bytes 1 | tf_op jit(solution)/shard_map/lars_prepare/pallas_call | solution.py:1583
  498.3 2.3 squares.1
  501.7 3.4 join_rows.2
  508.2 2.6 own_square.1
  510.8 4.0 collective-permute-start.61
  517.9 8.6 %all_to_all.97 = f32[8,2,128]{2,1,0:T(2,128)S(1)} all-to-all(f32[8,2,128]{2,1,0:T(2,128)S(1)} %broadcast_in_dim.66), channel_id=1, replica_groups=mesh['dp'=8,'mp'=4] {'dp'}, dimensions={0} | all-to-all | bytes 16384 | tf_op jit(solution)/shard_map/all_to_all | solution.py:97
  527.2 3.3 all-to-all-start.17
  536.6 8.0 %lars.1 = (f32[504,252]{1,0:T(8,128)}, f32[504,252]{1,0:T(8,128)}, f32[2016,126]{1,0:T(8,128)}, f32[504,504]{1,0:T(8,128)}, f32[504,252]{1,0:T(8,128)}, /*index=...) custom-call(s32[1]{0:T(128)} %bitcast.me_ref.m_ref, f32[2,128]{1,0:T(2,128)} %copy-done.40, ...), custom_call_target="tpu_custom_call" | custom-call | flops 1 | bytes 1 | tf_op jit(solution)/shard_map/lars/pallas_call | solution.py:1642
  (317 shorter events, 115.3 us)
Async XLA Ops:
  10.7 29.8 %collective-permute-start = (bf16[512,256]{1,0:T(8,128)(2,1)}, bf16[512,256]{1,0:T(8,128)(2,1)}, u32[]{:S(2)}, u32[]{:S(2)}) collective-permute-start(bf16[512,256]{1,0:T(8,128)(2,1)} %fusion), channel_id=1, source_target_pairs={{0,3},{1,2},{2,1},{3,0},{4,7},{5,6},{6,5},{7,4},{8,11},{9,10},{10,... | collective-permute-start | bytes 786440 | tf_op jit(solution)/shard_map/ppermute | solution.py:146
  15.7 24.7 %collective-permute-start.1 = (bf16[512,256]{1,0:T(8,128)(2,1)}, bf16[512,256]{1,0:T(8,128)(2,1)}, u32[]{:S(2)}, u32[]{:S(2)}) collective-permute-start(bf16[512,256]{1,0:T(8,128)(2,1)} %fusion), channel_id=1, source_target_pairs={{0,2},{1,3},{2,0},{3,1},{4,6},{5,7},{6,4},{7,5},{8,10},{9,11},{10,... | collective-permute-start | bytes 786440 | tf_op jit(solution)/shard_map/ppermute | solution.py:146
  15.8 25.3 %collective-permute-start.2 = (bf16[512,256]{1,0:T(8,128)(2,1)}, bf16[512,256]{1,0:T(8,128)(2,1)}, u32[]{:S(2)}, u32[]{:S(2)}) collective-permute-start(bf16[512,256]{1,0:T(8,128)(2,1)} %fusion), channel_id=1, source_target_pairs={{0,1},{1,0},{2,3},{3,2},{4,5},{5,4},{6,7},{7,6},{8,9},{9,8},{10,11... | collective-permute-start | bytes 786440 | tf_op jit(solution)/shard_map/ppermute | solution.py:146
  16.6 17.6 %collective-permute-start.4 = (bf16[504,256]{1,0:T(8,128)(2,1)S(1)}, bf16[504,256]{1,0:T(8,128)(2,1)S(1)}, u32[]{:S(2)}, u32[]{:S(2)}) collective-permute-start(bf16[504,256]{1,0:T(8,128)(2,1)S(1)} %fusion.2.refs_0_), channel_id=1, source_target_pairs={{0,8},{4,12},{8,0},{12,4},{16,24},{20,28},{24,16},{28,20},{1,9},{5... | collective-permute-start | bytes 774152 | tf_op jit(solution)/shard_map/ppermute | solution.py:158
  18.3 15.9 %collective-permute-start.6 = (bf16[504,256]{1,0:T(8,128)(2,1)S(1)}, bf16[504,256]{1,0:T(8,128)(2,1)}, u32[]{:S(2)}, u32[]{:S(2)}) collective-permute-start(bf16[504,256]{1,0:T(8,128)(2,1)S(1)} %fusion.2.refs_0_), channel_id=1, source_target_pairs={{0,16},{4,20},{8,24},{12,28},{16,0},{20,4},{24,8},{28,12},{1,17},{... | collective-permute-start | bytes 774152 | tf_op jit(solution)/shard_map/ppermute | solution.py:158
  20.5 19.2 %all-to-all-start = ((f32[4,6,504]{2,1,0:T(8,128)}), f32[4,6,504]{2,1,0:T(8,128)S(1)}, u32[]{:S(2)}, u32[]{:S(2)}) async-start(f32[4,6,504]{2,1,0:T(8,128)} %broadcast_in_dim.48), calls=%async_computation | async-start | bytes 131072 | tf_op jit(solution)/shard_map/all_to_all | solution.py:97
  34.1 8.7 %collective-permute-start.3 = (bf16[504,256]{1,0:T(8,128)(2,1)S(1)}, bf16[504,256]{1,0:T(8,128)(2,1)S(1)}, u32[]{:S(2)}, u32[]{:S(2)}) collective-permute-start(bf16[504,256]{1,0:T(8,128)(2,1)S(1)} %fusion.2.refs_0_), channel_id=1, source_target_pairs={{0,4},{4,0},{8,12},{12,8},{16,20},{20,16},{24,28},{28,24},{1,5},{5... | collective-permute-start | bytes 774152 | tf_op jit(solution)/shard_map/ppermute | solution.py:169
  34.3 6.7 %collective-permute-start.8 = (bf16[504,256]{1,0:T(8,128)(2,1)S(1)}, bf16[504,256]{1,0:T(8,128)(2,1)S(1)}, u32[]{:S(2)}, u32[]{:S(2)}) collective-permute-start(bf16[504,256]{1,0:T(8,128)(2,1)S(1)} %broadcast_select_fusion.4), channel_id=1, source_target_pairs={{0,16},{4,12},{8,24},{12,4},{16,0},{20,28},{24,8},{28,20},{1,17},{... | collective-permute-start | bytes 774152 | tf_op jit(solution)/shard_map/ppermute | solution.py:163
  43.6 25.6 %collective-permute-start.11 = (bf16[2048,256]{1,0:T(8,128)(2,1)S(1)}, bf16[2048,256]{1,0:T(8,128)(2,1)}, u32[]{:S(2)}, u32[]{:S(2)}) collective-permute-start(bf16[2048,256]{1,0:T(8,128)(2,1)S(1)} %bitcast.93), channel_id=1, source_target_pairs={{0,8},{4,12},{8,0},{12,4},{16,24},{20,28},{24,16},{28,20},{1,9},{5... | collective-permute-start | bytes 3145736 | tf_op jit(solution)/shard_map/ppermute | solution.py:158
  45.1 25.3 %collective-permute-start.12 = (bf16[2048,256]{1,0:T(8,128)(2,1)S(1)}, bf16[2048,256]{1,0:T(8,128)(2,1)}, u32[]{:S(2)}, u32[]{:S(2)}) collective-permute-start(bf16[2048,256]{1,0:T(8,128)(2,1)S(1)} %bitcast.94), channel_id=1, source_target_pairs={{0,16},{4,20},{8,24},{12,28},{16,0},{20,4},{24,8},{28,12},{1,17},{... | collective-permute-start | bytes 3145736 | tf_op jit(solution)/shard_map/ppermute | solution.py:158
  46.6 41.5 %all-to-all-start.1 = ((bf16[4,392,512]{2,1,0:T(8,128)(2,1)}), bf16[4,392,512]{2,1,0:T(8,128)(2,1)S(1)}, u32[]{:S(2)}, u32[]{:S(2)}) async-start(bf16[4,392,512]{2,1,0:T(8,128)(2,1)} %get-tuple-element.201), calls=%async_computation.1 | async-start | bytes 3211264 | tf_op jit(solution)/shard_map/all_to_all | solution.py:142
  71.7 15.0 %collective-permute-start.15 = (bf16[2048,256]{1,0:T(8,128)(2,1)S(1)}, bf16[2048,256]{1,0:T(8,128)(2,1)}, u32[]{:S(2)}, u32[]{:S(2)}) collective-permute-start(bf16[2048,256]{1,0:T(8,128)(2,1)S(1)} %broadcast_select_fusion.1), channel_id=1, source_target_pairs={{0,16},{4,12},{8,24},{12,4},{16,0},{20,28},{24,8},{28,20},{1,17},{... | collective-permute-start | bytes 3145736 | tf_op jit(solution)/shard_map/ppermute | solution.py:163
  73.3 20.0 %collective-permute-start.10 = (bf16[2048,256]{1,0:T(8,128)(2,1)S(1)}, bf16[2048,256]{1,0:T(8,128)(2,1)}, u32[]{:S(2)}, u32[]{:S(2)}) collective-permute-start(bf16[2048,256]{1,0:T(8,128)(2,1)S(1)} %bitcast.95), channel_id=1, source_target_pairs={{0,4},{4,0},{8,12},{12,8},{16,20},{20,16},{24,28},{28,24},{1,5},{5... | collective-permute-start | bytes 3145736 | tf_op jit(solution)/shard_map/ppermute | solution.py:169
  73.3 20.0 %collective-permute-start.13 = (bf16[2048,256]{1,0:T(8,128)(2,1)}, bf16[2048,256]{1,0:T(8,128)(2,1)}, u32[]{:S(2)}, u32[]{:S(2)}) collective-permute-start(bf16[2048,256]{1,0:T(8,128)(2,1)} %collective-permute-done.11.refs_2_), channel_id=1, source_target_pairs={{0,4},{4,0},{8,12},{12,8},{16,20},{20,16},{24,28},{28,24},{1,5},{5... | collective-permute-start | bytes 3145736 | tf_op jit(solution)/shard_map/ppermute | solution.py:169
  73.8 19.5 %collective-permute-start.14 = (bf16[2048,256]{1,0:T(8,128)(2,1)}, bf16[2048,256]{1,0:T(8,128)(2,1)}, u32[]{:S(2)}, u32[]{:S(2)}) collective-permute-start(bf16[2048,256]{1,0:T(8,128)(2,1)} %collective-permute-done.12.refs_4_), channel_id=1, source_target_pairs={{0,4},{4,0},{8,12},{12,8},{16,20},{20,16},{24,28},{28,24},{1,5},{5... | collective-permute-start | bytes 3145736 | tf_op jit(solution)/shard_map/ppermute | solution.py:169
  86.7 6.7 %collective-permute-start.16 = (bf16[2048,256]{1,0:T(8,128)(2,1)}, bf16[2048,256]{1,0:T(8,128)(2,1)}, u32[]{:S(2)}, u32[]{:S(2)}) collective-permute-start(bf16[2048,256]{1,0:T(8,128)(2,1)} %collective-permute-done.15.refs_6_), channel_id=1, source_target_pairs={{0,4},{4,0},{8,12},{12,8},{16,20},{20,16},{24,28},{28,24},{1,5},{5... | collective-permute-start | bytes 3145736 | tf_op jit(solution)/shard_map/ppermute | solution.py:169
  89.2 22.5 %all-to-all-start.2 = ((bf16[4,256,256]{2,1,0:T(8,128)(2,1)}), bf16[4,256,256]{2,1,0:T(8,128)(2,1)}, u32[]{:S(2)}, u32[]{:S(2)}) async-start(bf16[4,256,256]{2,1,0:T(8,128)(2,1)} %broadcast_in_dim.51), calls=%async_computation.2 | async-start | bytes 1048576 | tf_op jit(solution)/shard_map/all_to_all | solution.py:97
  111.7 12.4 %collective-permute-start.22 = (bf16[1024,256]{1,0:T(8,128)(2,1)}, bf16[1024,256]{1,0:T(8,128)(2,1)S(1)}, u32[]{:S(2)}, u32[]{:S(2)}) collective-permute-start(bf16[1024,256]{1,0:T(8,128)(2,1)} %bitcast.16.refs_0_), channel_id=1, source_target_pairs={{0,8},{4,12},{8,0},{12,4},{16,24},{20,28},{24,16},{28,20},{1,9},{5... | collective-permute-start | bytes 1572872 | tf_op jit(solution)/shard_map/ppermute | solution.py:158
  112.3 12.0 %collective-permute-start.23 = (bf16[1024,256]{1,0:T(8,128)(2,1)}, bf16[1024,256]{1,0:T(8,128)(2,1)S(1)}, u32[]{:S(2)}, u32[]{:S(2)}) collective-permute-start(bf16[1024,256]{1,0:T(8,128)(2,1)} %bitcast.16.refs_0_), channel_id=1, source_target_pairs={{0,16},{4,20},{8,24},{12,28},{16,0},{20,4},{24,8},{28,12},{1,17},{... | collective-permute-start | bytes 1572872 | tf_op jit(solution)/shard_map/ppermute | solution.py:158
  117.5 4.7 collective-permute-start.21
  125.4 28.9 %all-to-all-start.3 = ((bf16[4,512,256]{2,1,0:T(8,128)(2,1)}), bf16[4,512,256]{2,1,0:T(8,128)(2,1)S(1)}, u32[]{:S(2)}, u32[]{:S(2)}) async-start(bf16[4,512,256]{2,1,0:T(8,128)(2,1)} %broadcast_in_dim.52), calls=%async_computation.3 | async-start | bytes 2097152 | tf_op jit(solution)/shard_map/all_to_all | solution.py:97
  130.5 14.0 %collective-permute-start.24 = (bf16[1024,256]{1,0:T(8,128)(2,1)S(1)}, bf16[1024,256]{1,0:T(8,128)(2,1)}, u32[]{:S(2)}, u32[]{:S(2)}) collective-permute-start(bf16[1024,256]{1,0:T(8,128)(2,1)S(1)} %broadcast_select_fusion.2), channel_id=1, source_target_pairs={{0,16},{4,12},{8,24},{12,4},{16,0},{20,28},{24,8},{28,20},{1,17},{... | collective-permute-start | bytes 1572872 | tf_op jit(solution)/shard_map/ppermute | solution.py:163
  151.2 12.7 %collective-permute-start.30 = (bf16[1024,256]{1,0:T(8,128)(2,1)}, bf16[1024,256]{1,0:T(8,128)(2,1)}, u32[]{:S(2)}, u32[]{:S(2)}) collective-permute-start(bf16[1024,256]{1,0:T(8,128)(2,1)} %bitcast.16.refs_0_), channel_id=1, source_target_pairs={{0,4},{4,0},{8,12},{12,8},{16,20},{20,16},{24,28},{28,24},{1,5},{5... | collective-permute-start | bytes 1572872 | tf_op jit(solution)/shard_map/ppermute | solution.py:169
  154.4 23.6 %collective-permute-start.34 = (bf16[2048,256]{1,0:T(8,128)(2,1)S(1)}, bf16[2048,256]{1,0:T(8,128)(2,1)S(1)}, u32[]{:S(2)}, u32[]{:S(2)}) collective-permute-start(bf16[2048,256]{1,0:T(8,128)(2,1)S(1)} %bitcast.98), channel_id=1, source_target_pairs={{0,8},{4,12},{8,0},{12,4},{16,24},{20,28},{24,16},{28,20},{1,9},{5... | collective-permute-start | bytes 3145736 | tf_op jit(solution)/shard_map/ppermute | solution.py:158
  155.0 23.1 %collective-permute-start.35 = (bf16[2048,256]{1,0:T(8,128)(2,1)S(1)}, bf16[2048,256]{1,0:T(8,128)(2,1)S(1)}, u32[]{:S(2)}, u32[]{:S(2)}) collective-permute-start(bf16[2048,256]{1,0:T(8,128)(2,1)S(1)} %bitcast.99), channel_id=1, source_target_pairs={{0,16},{4,20},{8,24},{12,28},{16,0},{20,4},{24,8},{28,12},{1,17},{... | collective-permute-start | bytes 3145736 | tf_op jit(solution)/shard_map/ppermute | solution.py:158
  156.7 3.8 collective-permute-start.28
  160.5 4.7 collective-permute-start.29
  179.4 16.6 %collective-permute-start.39 = (bf16[2048,256]{1,0:T(8,128)(2,1)}, bf16[2048,256]{1,0:T(8,128)(2,1)}, u32[]{:S(2)}, u32[]{:S(2)}) collective-permute-start(bf16[2048,256]{1,0:T(8,128)(2,1)} %broadcast_select_fusion), channel_id=1, source_target_pairs={{0,16},{4,12},{8,24},{12,4},{16,0},{20,28},{24,8},{28,20},{1,17},{... | collective-permute-start | bytes 3145736 | tf_op jit(solution)/shard_map/ppermute | solution.py:163
  181.8 14.1 %all-to-all-start.4 = ((bf16[4,208,256]{2,1,0:T(8,128)(2,1)}), bf16[4,208,256]{2,1,0:T(8,128)(2,1)}, u32[]{:S(2)}, u32[]{:S(2)}) async-start(bf16[4,208,256]{2,1,0:T(8,128)(2,1)} %broadcast_in_dim.55), calls=%async_computation.4 | async-start | bytes 851968 | tf_op jit(solution)/shard_map/all_to_all | solution.py:97
  186.6 10.2 %collective-permute-start.36 = (bf16[2048,256]{1,0:T(8,128)(2,1)S(1)}, bf16[2048,256]{1,0:T(8,128)(2,1)}, u32[]{:S(2)}, u32[]{:S(2)}) collective-permute-start(bf16[2048,256]{1,0:T(8,128)(2,1)S(1)} %bitcast.100), channel_id=1, source_target_pairs={{0,4},{4,0},{8,12},{12,8},{16,20},{20,16},{24,28},{28,24},{1,5},{5... | collective-permute-start | bytes 3145736 | tf_op jit(solution)/shard_map/ppermute | solution.py:169
  186.6 11.4 %collective-permute-start.37 = (bf16[2048,256]{1,0:T(8,128)(2,1)S(1)}, bf16[2048,256]{1,0:T(8,128)(2,1)}, u32[]{:S(2)}, u32[]{:S(2)}) collective-permute-start(bf16[2048,256]{1,0:T(8,128)(2,1)S(1)} %collective-permute-done.34.refs_2_), channel_id=1, source_target_pairs={{0,4},{4,0},{8,12},{12,8},{16,20},{20,16},{24,28},{28,24},{1,5},{5... | collective-permute-start | bytes 3145736 | tf_op jit(solution)/shard_map/ppermute | solution.py:169
  187.1 11.4 %collective-permute-start.38 = (bf16[2048,256]{1,0:T(8,128)(2,1)S(1)}, bf16[2048,256]{1,0:T(8,128)(2,1)}, u32[]{:S(2)}, u32[]{:S(2)}) collective-permute-start(bf16[2048,256]{1,0:T(8,128)(2,1)S(1)} %collective-permute-done.35.refs_4_), channel_id=1, source_target_pairs={{0,4},{4,0},{8,12},{12,8},{16,20},{20,16},{24,28},{28,24},{1,5},{5... | collective-permute-start | bytes 3145736 | tf_op jit(solution)/shard_map/ppermute | solution.py:169
  195.9 4.9 collective-permute-start.40
  195.9 13.4 %collective-permute-start.41 = (bf16[832,256]{1,0:T(8,128)(2,1)}, bf16[832,256]{1,0:T(8,128)(2,1)}, u32[]{:S(2)}, u32[]{:S(2)}) collective-permute-start(bf16[832,256]{1,0:T(8,128)(2,1)} %bitcast.28.refs_0_), channel_id=1, source_target_pairs={{0,8},{4,12},{8,0},{12,4},{16,24},{20,28},{24,16},{28,20},{1,9},{5... | collective-permute-start | bytes 1277960 | tf_op jit(solution)/shard_map/ppermute | solution.py:158
  196.8 12.5 %collective-permute-start.42 = (bf16[832,256]{1,0:T(8,128)(2,1)}, bf16[832,256]{1,0:T(8,128)(2,1)S(1)}, u32[]{:S(2)}, u32[]{:S(2)}) collective-permute-start(bf16[832,256]{1,0:T(8,128)(2,1)} %bitcast.28.refs_0_), channel_id=1, source_target_pairs={{0,16},{4,20},{8,24},{12,28},{16,0},{20,4},{24,8},{28,12},{1,17},{... | collective-permute-start | bytes 1277960 | tf_op jit(solution)/shard_map/ppermute | solution.py:158
  197.9 20.3 %collective-permute-start.43 = (bf16[392,512]{1,0:T(8,128)(2,1)}, bf16[392,512]{1,0:T(8,128)(2,1)S(1)}, u32[]{:S(2)}, u32[]{:S(2)}) collective-permute-start(bf16[392,512]{1,0:T(8,128)(2,1)} %get-tuple-element.248), channel_id=1, source_target_pairs={{0,1},{1,0},{2,3},{3,2},{4,5},{5,4},{6,7},{7,6},{8,9},{9,8},{10,11... | collective-permute-start | bytes 1204232 | tf_op jit(solution)/shard_map/ppermute | solution.py:1806
  198.5 20.6 %collective-permute-start.44 = (bf16[392,512]{1,0:T(8,128)(2,1)}, bf16[392,512]{1,0:T(8,128)(2,1)S(1)}, u32[]{:S(2)}, u32[]{:S(2)}) collective-permute-start(bf16[392,512]{1,0:T(8,128)(2,1)} %get-tuple-element.249), channel_id=1, source_target_pairs={{0,2},{1,3},{2,0},{3,1},{4,6},{5,7},{6,4},{7,5},{8,10},{9,11},{10,... | collective-permute-start | bytes 1204232 | tf_op jit(solution)/shard_map/ppermute | solution.py:1807
  220.3 11.9 %collective-permute-start.45 = (bf16[832,256]{1,0:T(8,128)(2,1)S(1)}, bf16[832,256]{1,0:T(8,128)(2,1)S(1)}, u32[]{:S(2)}, u32[]{:S(2)}) collective-permute-start(bf16[832,256]{1,0:T(8,128)(2,1)S(1)} %broadcast_select_fusion.3), channel_id=1, source_target_pairs={{0,16},{4,12},{8,24},{12,4},{16,0},{20,28},{24,8},{28,20},{1,17},{... | collective-permute-start | bytes 1277960 | tf_op jit(solution)/shard_map/ppermute | solution.py:163
  222.1 9.4 %all-to-all-start.6 = ((f32[4,2,2048]{2,1,0:T(2,128)}), f32[4,2,2048]{2,1,0:T(2,128)S(1)}, u32[]{:S(2)}, u32[]{:S(2)}) async-start(f32[4,2,2048]{2,1,0:T(2,128)} %broadcast_in_dim.57), calls=%async_computation.6 | async-start | bytes 131072 | tf_op jit(solution)/shard_map/all_to_all | solution.py:97
  225.8 152.7 %reduce-scatter.4.cloned.1.call-start = ((), (), s32[]{:S(2)}) async-start(), calls=%async_computation.21 | async-start | bytes 9437184 | tf_op jit(solution)/shard_map/reduce_scatter | solution.py:1861
  225.8 11.6 %collective-permute-start.46 = (bf16[832,256]{1,0:T(8,128)(2,1)}, bf16[832,256]{1,0:T(8,128)(2,1)S(1)}, u32[]{:S(2)}, u32[]{:S(2)}) collective-permute-start(bf16[832,256]{1,0:T(8,128)(2,1)} %bitcast.28.refs_0_), channel_id=1, source_target_pairs={{0,4},{4,0},{8,12},{12,8},{16,20},{20,16},{24,28},{28,24},{1,5},{5... | collective-permute-start | bytes 1277960 | tf_op jit(solution)/shard_map/ppermute | solution.py:169
  225.8 11.6 %collective-permute-start.47 = (bf16[832,256]{1,0:T(8,128)(2,1)}, bf16[832,256]{1,0:T(8,128)(2,1)S(1)}, u32[]{:S(2)}, u32[]{:S(2)}) collective-permute-start(bf16[832,256]{1,0:T(8,128)(2,1)} %collective-permute-done.41.refs_2_), channel_id=1, source_target_pairs={{0,4},{4,0},{8,12},{12,8},{16,20},{20,16},{24,28},{28,24},{1,5},{5... | collective-permute-start | bytes 1277960 | tf_op jit(solution)/shard_map/ppermute | solution.py:169
  226.3 11.2 %collective-permute-start.48 = (bf16[832,256]{1,0:T(8,128)(2,1)S(1)}, bf16[832,256]{1,0:T(8,128)(2,1)S(1)}, u32[]{:S(2)}, u32[]{:S(2)}) collective-permute-start(bf16[832,256]{1,0:T(8,128)(2,1)S(1)} %collective-permute-done.42.refs_4_), channel_id=1, source_target_pairs={{0,4},{4,0},{8,12},{12,8},{16,20},{20,16},{24,28},{28,24},{1,5},{5... | collective-permute-start | bytes 1277960 | tf_op jit(solution)/shard_map/ppermute | solution.py:169
  232.2 5.3 collective-permute-start.49
  251.4 17.5 %collective-permute-start.50 = (bf16[392,512]{1,0:T(8,128)(2,1)}, bf16[392,512]{1,0:T(8,128)(2,1)S(1)}, u32[]{:S(2)}, u32[]{:S(2)}) collective-permute-start(bf16[392,512]{1,0:T(8,128)(2,1)} %get-tuple-element.272), channel_id=1, source_target_pairs={{0,3},{1,2},{2,1},{3,0},{4,7},{5,6},{6,5},{7,4},{8,11},{9,10},{10,... | collective-permute-start | bytes 1204232 | tf_op jit(solution)/shard_map/ppermute | solution.py:1834
  253.1 23.2 %collective-permute-start.51 = (bf16[392,512]{1,0:T(8,128)(2,1)}, bf16[392,512]{1,0:T(8,128)(2,1)S(1)}, u32[]{:S(2)}, u32[]{:S(2)}) collective-permute-start(bf16[392,512]{1,0:T(8,128)(2,1)} %get-tuple-element.275), channel_id=1, source_target_pairs={{0,1},{1,0},{2,3},{3,2},{4,5},{5,4},{6,7},{7,6},{8,9},{9,8},{10,11... | collective-permute-start | bytes 1204232 | tf_op jit(solution)/shard_map/ppermute | solution.py:1835
  307.3 22.0 %collective-permute-start.52 = (bf16[392,512]{1,0:T(8,128)(2,1)S(1)}, bf16[392,512]{1,0:T(8,128)(2,1)S(1)}, u32[]{:S(2)}, u32[]{:S(2)}) collective-permute-start(bf16[392,512]{1,0:T(8,128)(2,1)S(1)} %copy-done.47), channel_id=1, source_target_pairs={{0,2},{1,3},{2,0},{3,1},{4,6},{5,7},{6,4},{7,5},{8,10},{9,11},{10,... | collective-permute-start | bytes 1204232 | tf_op jit(solution)/shard_map/ppermute | solution.py:1856
  340.4 9.4 %all-to-all-start.11 = ((f32[4,2,2048]{2,1,0:T(2,128)}), f32[4,2,2048]{2,1,0:T(2,128)S(1)}, u32[]{:S(2)}, u32[]{:S(2)}) async-start(f32[4,2,2048]{2,1,0:T(2,128)} %broadcast_in_dim.62), calls=%async_computation.11 | async-start | bytes 131072 | tf_op jit(solution)/shard_map/all_to_all | solution.py:97
  351.7 25.6 %all-to-all-start.12 = ((bf16[32,2,5120]{2,1,0:T(2,128)(2,1)}), bf16[32,2,5120]{2,1,0:T(2,128)(2,1)S(1)}, u32[]{:S(2)}, u32[]{:S(2)}) async-start(bf16[32,2,5120]{2,1,0:T(2,128)(2,1)} %broadcast_in_dim.63), calls=%async_computation.12 | async-start | bytes 1310720 | tf_op jit(solution)/shard_map/all_to_all | solution.py:121
  354.3 54.5 %reduce-scatter.6.cloned.1.call-start = ((), (), s32[]{:S(2)}) async-start(), calls=%async_computation.22 | async-start | bytes 1310720 | tf_op jit(solution)/shard_map/reduce_scatter | solution.py:1880
  378.5 83.8 %reduce-scatter.8.cloned.1.call-start = ((), (), s32[]{:S(2)}) async-start(), calls=%async_computation.23 | async-start | bytes 2359296 | tf_op jit(solution)/shard_map/reduce_scatter | solution.py:1892
  408.8 7.5 %collective-permute-start.53 = (bf16[4,4,512,256]{3,2,1,0:T(8,128)(2,1)}, bf16[4,4,512,256]{3,2,1,0:T(8,128)(2,1)}, u32[]{:S(2)}, u32[]{:S(2)}) collective-permute-start(bf16[4,4,512,256]{3,2,1,0:T(8,128)(2,1)} %get-tuple-element.305), channel_id=1, source_target_pairs={{0,4},{4,0},{8,12},{12,8},{16,20},{20,16},{24,28},{28,24},{1,5},{5... | collective-permute-start | bytes 12582920 | tf_op jit(solution)/shard_map/ppermute | solution.py:183
  418.7 15.0 %collective-permute-start.54 = (bf16[4,512,256]{2,1,0:T(8,128)(2,1)}, bf16[4,512,256]{2,1,0:T(8,128)(2,1)S(1)}, u32[]{:S(2)}, u32[]{:S(2)}) collective-permute-start(bf16[4,512,256]{2,1,0:T(8,128)(2,1)} %twin_sum.1), channel_id=1, source_target_pairs={{0,16},{4,12},{8,24},{12,4},{16,0},{20,28},{24,8},{28,20},{1,17},{... | collective-permute-start | bytes 3145736 | tf_op jit(solution)/shard_map/ppermute | solution.py:179
  420.3 13.0 %collective-permute-start.55 = (bf16[392,512]{1,0:T(8,128)(2,1)S(1)}, bf16[392,512]{1,0:T(8,128)(2,1)S(1)}, u32[]{:S(2)}, u32[]{:S(2)}) collective-permute-start(bf16[392,512]{1,0:T(8,128)(2,1)S(1)} %copy-done.46), channel_id=1, source_target_pairs={{0,3},{1,2},{2,1},{3,0},{4,7},{5,6},{6,5},{7,4},{8,11},{9,10},{10,... | collective-permute-start | bytes 1204232 | tf_op jit(solution)/shard_map/ppermute | solution.py:1884
  434.7 65.8 %all-to-all-start.15 = ((bf16[4,392,512]{2,1,0:T(8,128)(2,1)}), bf16[4,392,512]{2,1,0:T(8,128)(2,1)S(1)}, u32[]{:S(2)}, u32[]{:S(2)}) async-start(bf16[4,392,512]{2,1,0:T(8,128)(2,1)} %mix_back.3), calls=%async_computation.18 | async-start | bytes 3211264 | tf_op jit(solution)/shard_map/all_to_all | solution.py:142
  447.4 26.9 %collective-permute-start.56 = (bf16[4,512,256]{2,1,0:T(8,128)(2,1)}, bf16[4,512,256]{2,1,0:T(8,128)(2,1)S(1)}, u32[]{:S(2)}, u32[]{:S(2)}) collective-permute-start(bf16[4,512,256]{2,1,0:T(8,128)(2,1)} %get-tuple-element.314), channel_id=1, source_target_pairs={{0,8},{4,12},{8,0},{12,4},{16,24},{20,28},{24,16},{28,20},{1,9},{5... | collective-permute-start | bytes 3145736 | tf_op jit(solution)/shard_map/ppermute | solution.py:187
  448.6 26.7 %collective-permute-start.57 = (bf16[4,512,256]{2,1,0:T(8,128)(2,1)}, bf16[4,512,256]{2,1,0:T(8,128)(2,1)}, u32[]{:S(2)}, u32[]{:S(2)}) collective-permute-start(bf16[4,512,256]{2,1,0:T(8,128)(2,1)} %get-tuple-element.315), channel_id=1, source_target_pairs={{0,16},{4,20},{8,24},{12,28},{16,0},{20,4},{24,8},{28,12},{1,17},{... | collective-permute-start | bytes 3145736 | tf_op jit(solution)/shard_map/ppermute | solution.py:187
  479.8 25.3 %collective-permute-start.58 = (bf16[640,256]{1,0:T(8,128)(2,1)}, bf16[640,256]{1,0:T(8,128)(2,1)S(1)}, u32[]{:S(2)}, u32[]{:S(2)}) collective-permute-start(bf16[640,256]{1,0:T(8,128)(2,1)} %get-tuple-element.329), channel_id=1, source_target_pairs={{0,1},{1,0},{2,3},{3,2},{4,5},{5,4},{6,7},{7,6},{8,9},{9,8},{10,11... | collective-permute-start | bytes 983048 | tf_op jit(solution)/shard_map/ppermute | solution.py:191
  481.7 25.6 %collective-permute-start.59 = (bf16[640,256]{1,0:T(8,128)(2,1)}, bf16[640,256]{1,0:T(8,128)(2,1)S(1)}, u32[]{:S(2)}, u32[]{:S(2)}) collective-permute-start(bf16[640,256]{1,0:T(8,128)(2,1)} %get-tuple-element.330), channel_id=1, source_target_pairs={{0,2},{1,3},{2,0},{3,1},{4,6},{5,7},{6,4},{7,5},{8,10},{9,11},{10,... | collective-permute-start | bytes 983048 | tf_op jit(solution)/shard_map/ppermute | solution.py:191
  483.9 23.5 %collective-permute-start.60 = (bf16[640,256]{1,0:T(8,128)(2,1)}, bf16[640,256]{1,0:T(8,128)(2,1)S(1)}, u32[]{:S(2)}, u32[]{:S(2)}) collective-permute-start(bf16[640,256]{1,0:T(8,128)(2,1)} %get-tuple-element.331), channel_id=1, source_target_pairs={{0,3},{1,2},{2,1},{3,0},{4,7},{5,6},{6,5},{7,4},{8,11},{9,10},{10,... | collective-permute-start | bytes 983048 | tf_op jit(solution)/shard_map/ppermute | solution.py:191
  510.8 15.7 %collective-permute-start.61 = (bf16[128,256]{1,0:T(8,128)(2,1)}, bf16[128,256]{1,0:T(8,128)(2,1)S(1)}, u32[]{:S(2)}, u32[]{:S(2)}) collective-permute-start(bf16[128,256]{1,0:T(8,128)(2,1)} %get-tuple-element.369), channel_id=1, source_target_pairs={{0,1},{1,0},{2,3},{3,2},{4,5},{5,4},{6,7},{7,6},{8,9},{9,8},{10,11... | collective-permute-start | bytes 196616 | tf_op jit(solution)/shard_map/ppermute | solution.py:146
  514.8 11.7 %collective-permute-start.62 = (bf16[128,256]{1,0:T(8,128)(2,1)}, bf16[128,256]{1,0:T(8,128)(2,1)S(1)}, u32[]{:S(2)}, u32[]{:S(2)}) collective-permute-start(bf16[128,256]{1,0:T(8,128)(2,1)} %get-tuple-element.369), channel_id=1, source_target_pairs={{0,2},{1,3},{2,0},{3,1},{4,6},{5,7},{6,4},{7,5},{8,10},{9,11},{10,... | collective-permute-start | bytes 196616 | tf_op jit(solution)/shard_map/ppermute | solution.py:146
  515.6 10.9 %collective-permute-start.63 = (bf16[128,256]{1,0:T(8,128)(2,1)}, bf16[128,256]{1,0:T(8,128)(2,1)S(1)}, u32[]{:S(2)}, u32[]{:S(2)}) collective-permute-start(bf16[128,256]{1,0:T(8,128)(2,1)} %get-tuple-element.369), channel_id=1, source_target_pairs={{0,3},{1,2},{2,1},{3,0},{4,7},{5,6},{6,5},{7,4},{8,11},{9,10},{10,... | collective-permute-start | bytes 196616 | tf_op jit(solution)/shard_map/ppermute | solution.py:146
  527.2 8.9 %all-to-all-start.17 = ((f32[4,2,128]{2,1,0:T(2,128)}), f32[4,2,128]{2,1,0:T(2,128)S(1)}, u32[]{:S(2)}, u32[]{:S(2)}) async-start(f32[4,2,128]{2,1,0:T(2,128)} %broadcast_in_dim.67), calls=%async_computation.20 | async-start | bytes 8192 | tf_op jit(solution)/shard_map/all_to_all | solution.py:97
  (61 other events, 602.2 us)
Sparse Core Ops, SparseCore 0:
  306.5 71.9 reduce-scatter.3
  380.9 27.8 reduce-scatter.5
  420.4 41.8 reduce-scatter.7
